TPU v7x, 32 devices: a whole 2x2x4 slice. The times are simulated.
32 devices in a mesh: dp: 4 (over y, x), tp: 8 (over z, core).
Axes of the slice: x: 2, y: 2, z: 4, core: 2. Of those that a mesh axis runs over, the one named last changes fastest.
Arguments:
- tokens: bfloat16 [512, 4096], P(('dp', 'tp')), may hold values from -6 to 6
- norm_scale_vector: float32 [4096], replicated, may hold values from 0.5 to 1.5
- gate_weight: bfloat16 [4096, 14336], P(None, 'tp'), may hold values from -0.09375 to 0.09375
- up_weight: bfloat16 [4096, 14336], P(None, 'tp'), may hold values from -0.09375 to 0.09375
- down_weight: bfloat16 [14336, 4096], P('tp'), may hold values from -0.046875 to 0.046875
- cotangent: bfloat16 [512, 4096], P(('dp', 'tp')), may hold values from -4 to 4
Outputs:
- mixed: bfloat16 [512, 4096], P(('dp', 'tp'))
- token_gradient: bfloat16 [512, 4096], P(('dp', 'tp'))
- grad_gate: bfloat16 [4096, 14336], P('dp', 'tp')
- grad_up: bfloat16 [4096, 14336], P('dp', 'tp')
- grad_down: bfloat16 [14336, 4096], P('tp', 'dp')
All inputs are finite; a program needn't handle non-finite values.
Results may differ from a plain program's by a relative error of at most 0.025.
Values may be sent and summed in bfloat16 or wider, within the bound.
No kernel may reach another device: no remote copies, remote signals or barrier semaphores. Data moves between devices by JAX's collectives and lax.ppermute only.
A program may use at most 192 MiB of HBM per device.

v0:
```python
import jax
import jax.numpy as jnp
from jax import lax
from jax.sharding import PartitionSpec as P


def contract_rows(left, right):
    return lax.dot_general(
        left, right, (((0,), (0,)), ((), ())), preferred_element_type=jnp.float32
    )


def contract_cols(left, right):
    return lax.dot_general(
        left, right, (((1,), (1,)), ((), ())), preferred_element_type=jnp.float32
    )


def local(tokens, norm_scale_vector, gate_weight, up_weight, down_weight, cotangent):
    expanded_hidden = tokens.astype(jnp.float32)
    reciprocal_root_mean = lax.rsqrt(
        jnp.mean(expanded_hidden * expanded_hidden, axis=-1, keepdims=True) + 1e-05
    )
    unit_input = expanded_hidden * reciprocal_root_mean
    rescaled_input = (unit_input * norm_scale_vector).astype(jnp.bfloat16)
    normed_all = lax.all_gather(rescaled_input, "tp", axis=0, tiled=True)
    gate = jnp.dot(normed_all, gate_weight, preferred_element_type=jnp.float32)
    lifted = jnp.dot(normed_all, up_weight, preferred_element_type=jnp.float32)
    sigmoid_gate = jax.nn.sigmoid(gate)
    activated = gate * sigmoid_gate
    hidden = (activated * lifted).astype(jnp.bfloat16)
    branch = lax.psum_scatter(
        jnp.dot(hidden, down_weight, preferred_element_type=jnp.float32).astype(jnp.bfloat16),
        "tp",
        scatter_dimension=0,
        tiled=True,
    ).astype(jnp.float32)
    mixed = (expanded_hidden + branch).astype(jnp.bfloat16)
    grad_all = lax.all_gather(cotangent, "tp", axis=0, tiled=True)
    grad_hidden = contract_cols(grad_all, down_weight)
    grad_pre = (grad_hidden * lifted * sigmoid_gate * (1.0 + gate * (1.0 - sigmoid_gate))).astype(
        jnp.bfloat16
    )
    grad_lifted = (grad_hidden * activated).astype(jnp.bfloat16)
    grad_normed = lax.psum_scatter(
        (contract_cols(grad_pre, gate_weight) + contract_cols(grad_lifted, up_weight)).astype(
            jnp.bfloat16
        ),
        "tp",
        scatter_dimension=0,
        tiled=True,
    ).astype(jnp.float32)
    gain_applied = grad_normed * norm_scale_vector
    inner_product = jnp.mean(gain_applied * unit_input, axis=-1, keepdims=True)
    token_gradient = (
        cotangent.astype(jnp.float32)
        + reciprocal_root_mean * (gain_applied - unit_input * inner_product)
    ).astype(jnp.bfloat16)
    weight_gate = contract_rows(normed_all, grad_pre).astype(jnp.bfloat16)
    weight_up = contract_rows(normed_all, grad_lifted).astype(jnp.bfloat16)
    weight_down = contract_rows(hidden, grad_all).astype(jnp.bfloat16)
    sum_gate, sum_up, sum_down = (
        lax.psum_scatter(weight_gate, "dp", scatter_dimension=0, tiled=True).astype(jnp.float32),
        lax.psum_scatter(weight_up, "dp", scatter_dimension=0, tiled=True).astype(jnp.float32),
        lax.psum_scatter(weight_down, "dp", scatter_dimension=1, tiled=True).astype(jnp.float32),
    )
    return (
        mixed,
        token_gradient,
        sum_gate.astype(jnp.bfloat16),
        sum_up.astype(jnp.bfloat16),
        sum_down.astype(jnp.bfloat16),
    )


def solution(mesh):
    in_specs = (
        P(("dp", "tp"), None),
        P(),
        P(None, "tp"),
        P(None, "tp"),
        P("tp", None),
        P(("dp", "tp"), None),
    )
    out_specs = (
        P(("dp", "tp"), None),
        P(("dp", "tp"), None),
        P("dp", "tp"),
        P("dp", "tp"),
        P("tp", "dp"),
    )
    return jax.shard_map(local, mesh=mesh, in_specs=in_specs, out_specs=out_specs, check_vma=False)
```

profile of v0, /device:TPU:0, one launch (start us, length us, event | category | flops | bytes accessed | tf_op | source)
XLA Modules:
  0.0 584.8 jit_solution(16484821288710990002)
XLA Ops:
  7.2 0.0 all-gather.3.cloned.1.call-start
  7.2 1.1 fusion.11
  8.3 1.7 fusion.5
  9.9 0.0 all-gather.3.cloned.1.call-update
  10.0 0.0 all-gather.5.cloned.1.call-start
  10.0 0.7 all-gather.5.cloned.1.call-update
  10.7 0.0 reduce-scatter.8.cloned.1.call-start
  10.8 24.2 %all-gather.3.cloned.1.call-done = bf16[128,4096]{1,0:T(8,128)(2,1)} async-done(((bf16[16,4096]{1,0:T(8,128)(2,1)}), bf16[128,4096]{1,0:T(8,128)(2,1)}) %all-gather.3.cloned.1.call-update) | async-done | bytes 1048592 | tf_op jit(solution)/shard_map/all_gather | solution.py:26
  35.0 7.7 %fusion.14 = f32[128,1792]{1,0:T(8,128)S(1)} fusion(bf16[128,4096]{1,0:T(8,128)(2,1)} %all-gather.3.cloned.1.call-done, bf16[4096,1792]{1,0:T(8,128)(2,1)} %param.9), kind=kOutput, calls=%fused_computation.29 | convolution fusion | flops 1879048192 | bytes 16646144 | tf_op jit(solution)/shard_map/dot_general | solution.py:28
  42.7 2.1 copy-done
  44.9 0.2 copy-done.1
  45.1 3.1 fusion.13
  48.2 10.1 %all-gather.5.cloned.1.call-done = bf16[128,4096]{1,0:T(8,128)(2,1)} async-done(((bf16[16,4096]{1,0:T(8,128)(2,1)}), bf16[128,4096]{1,0:T(8,128)(2,1)}) %all-gather.5.cloned.1.call-update) | async-done | bytes 1048592 | tf_op jit(solution)/shard_map/all_gather | solution.py:39
  58.4 10.9 %multiply_convert_fusion = (bf16[128,1792]{1,0:T(8,128)(2,1)S(1)}, bf16[128,1792]{1,0:T(8,128)(2,1)S(1)}, bf16[128,1792]{1,0:T(8,128)(2,1)S(1)}) fusion(f32[128,1792]{1,0:T(8,128)} %fusion.13, f32[128,1792]{1,0:T(8,128)S(1)} %fusion.14, bf16[128,4096]{1,0:T(8,128)(2,1)} %all-gather.5.cloned.1.call-done, bf16[1792,4096]{1,0:T(8,128)(2,1)} %param.10), kind=kOutput, calls=%fused_computation.6 | convolution fusion | flops 1882488832 | bytes 18939904 | tf_op jit(solution)/shard_map/dot_general | solution.py:14
  69.2 9.9 %fusion.15 = f32[128,4096]{1,0:T(8,128)S(1)} fusion(bf16[128,1792]{1,0:T(8,128)(2,1)S(1)} %get-tuple-element.6, bf16[4096,1792]{1,0:T(8,128)(2,1)} %param.8), kind=kOutput, calls=%fused_computation.30 | convolution fusion | flops 1879048192 | bytes 17235968 | tf_op jit(solution)/shard_map/dot_general | solution.py:14
  79.2 11.1 %fusion = bf16[128,4096]{1,0:T(8,128)(2,1)} fusion(f32[128,4096]{1,0:T(8,128)S(1)} %fusion.15, bf16[128,1792]{1,0:T(8,128)(2,1)S(1)} %get-tuple-element.5, bf16[4096,1792]{1,0:T(8,128)(2,1)} %param.9), kind=kOutput, calls=%fused_computation.4 | convolution fusion | flops 1880096768 | bytes 18284544 | tf_op jit(solution)/shard_map/dot_general | solution.py:14
  90.3 0.0 reduce-scatter.8.cloned.1.call-update
  90.3 0.0 reduce-scatter.6.cloned.1.call-start
  90.3 8.3 %convolution_convert_fusion.3 = bf16[128,4096]{1,0:T(8,128)(2,1)} fusion(bf16[128,1792]{1,0:T(8,128)(2,1)S(1)} %get-tuple-element.7, bf16[1792,4096]{1,0:T(8,128)(2,1)} %param.10), kind=kOutput, calls=%fused_computation.5 | convolution fusion | flops 1879572480 | bytes 16187392 | tf_op jit(solution)/shard_map/dot_general | solution.py:33
  98.6 0.0 reduce-scatter.14.cloned.1.call-start
  98.7 7.5 %convolution_convert_fusion = bf16[1792,4096]{1,0:T(8,128)(2,1)} fusion(bf16[128,1792]{1,0:T(8,128)(2,1)S(1)} %get-tuple-element.7, bf16[128,4096]{1,0:T(8,128)(2,1)S(1)} %copy-done.3), kind=kOutput, calls=%fused_computation | convolution fusion | flops 1886388224 | bytes 16187392 | tf_op jit(solution)/shard_map/dot_general | solution.py:8
  106.2 0.0 reduce-scatter.12.cloned.1.call-start
  106.3 7.3 %convolution_convert_fusion.1 = bf16[4096,1792]{1,0:T(8,128)(2,1)} fusion(bf16[128,4096]{1,0:T(8,128)(2,1)S(1)} %copy-done.1, bf16[128,1792]{1,0:T(8,128)(2,1)S(1)} %get-tuple-element.5), kind=kOutput, calls=%fused_computation.1 | convolution fusion | flops 1886388224 | bytes 16187392 | tf_op jit(solution)/shard_map/dot_general | solution.py:8
  113.6 0.0 reduce-scatter.10.cloned.1.call-start
  113.7 7.3 %convolution_convert_fusion.2 = bf16[4096,1792]{1,0:T(8,128)(2,1)} fusion(bf16[128,4096]{1,0:T(8,128)(2,1)S(1)} %copy-done.1, bf16[128,1792]{1,0:T(8,128)(2,1)S(1)} %get-tuple-element.6), kind=kOutput, calls=%fused_computation.2 | convolution fusion | flops 1886388224 | bytes 16187392 | tf_op jit(solution)/shard_map/dot_general | solution.py:8
  121.0 1.5 reduce-scatter.8.cloned.1.call-done
  122.5 1.1 fusion.6
  123.6 31.6 %reduce-scatter.6.cloned.1.call-done = bf16[16,4096]{1,0:T(8,128)(2,1)} async-done(((bf16[128,4096]{1,0:T(8,128)(2,1)}), bf16[16,4096]{1,0:T(8,128)(2,1)}) %reduce-scatter.6.cloned.1.call-update) | async-done | bytes 131088 | tf_op jit(solution)/shard_map/reduce_scatter | solution.py:32
  155.2 1.8 fusion.10
  157.0 137.8 %reduce-scatter.14.cloned.1.call-done = bf16[1792,1024]{1,0:T(8,128)(2,1)} async-done(((bf16[1792,4096]{1,0:T(8,128)(2,1)}), bf16[1792,1024]{1,0:T(8,128)(2,1)}) %reduce-scatter.14.cloned.1.call-update) | async-done | bytes 3670032 | tf_op jit(solution)/shard_map/reduce_scatter | solution.py:65
  294.9 141.5 %reduce-scatter.12.cloned.1.call-done = bf16[1024,1792]{1,0:T(8,128)(2,1)} async-done(((bf16[4096,1792]{1,0:T(8,128)(2,1)}), bf16[1024,1792]{1,0:T(8,128)(2,1)}) %reduce-scatter.12.cloned.1.call-update) | async-done | bytes 3670032 | tf_op jit(solution)/shard_map/reduce_scatter | solution.py:64
  436.3 141.6 %reduce-scatter.10.cloned.1.call-done = bf16[1024,1792]{1,0:T(8,128)(2,1)} async-done(((bf16[4096,1792]{1,0:T(8,128)(2,1)}), bf16[1024,1792]{1,0:T(8,128)(2,1)}) %reduce-scatter.10.cloned.1.call-update) | async-done | bytes 3670032 | tf_op jit(solution)/shard_map/reduce_scatter | solution.py:63
  (16 shorter events, 0.1 us)
Async XLA Ops:
  7.2 27.8 %all-gather.3.cloned.1.call-start = ((), (), s32[]{:S(2)}) async-start(), calls=%async_computation.5 | async-start | bytes 1179648 | tf_op jit(solution)/shard_map/all_gather | solution.py:26
  10.0 48.4 %all-gather.5.cloned.1.call-start = ((), (), s32[]{:S(2)}) async-start(), calls=%async_computation.7 | async-start | bytes 1179648 | tf_op jit(solution)/shard_map/all_gather | solution.py:39
  10.7 111.8 %reduce-scatter.8.cloned.1.call-start = ((), (), s32[]{:S(2)}) async-start(), calls=%async_computation.8 | async-start | bytes 1179648 | tf_op jit(solution)/shard_map/reduce_scatter | solution.py:45
  35.0 9.9 %copy-start = (bf16[4096,1792]{1,0:T(8,128)(2,1)S(1)}, bf16[4096,1792]{1,0:T(8,128)(2,1)}, u32[]{:S(2)}) copy-start(bf16[4096,1792]{1,0:T(8,128)(2,1)} %param.8) | copy-start | bytes 44040196
  35.0 10.1 %copy-start.1 = (bf16[128,4096]{1,0:T(8,128)(2,1)S(1)}, bf16[128,4096]{1,0:T(8,128)(2,1)}, u32[]{:S(2)}) copy-start(bf16[128,4096]{1,0:T(8,128)(2,1)} %all-gather.3.cloned.1.call-done) | copy-start | bytes 3145732
  90.3 8.4 %copy-start.3 = (bf16[128,4096]{1,0:T(8,128)(2,1)S(1)}, bf16[128,4096]{1,0:T(8,128)(2,1)}, u32[]{:S(2)}) copy-start(bf16[128,4096]{1,0:T(8,128)(2,1)} %all-gather.5.cloned.1.call-done) | copy-start | bytes 3145732
  90.3 65.0 %reduce-scatter.6.cloned.1.call-start = ((), (), s32[]{:S(2)}) async-start(), calls=%async_computation.6 | async-start | bytes 1179648 | tf_op jit(solution)/shard_map/reduce_scatter | solution.py:32
  98.6 196.2 %reduce-scatter.14.cloned.1.call-start = ((), (), s32[]{:S(2)}) async-start(), calls=%async_computation.11 | async-start | bytes 18350080 | tf_op jit(solution)/shard_map/reduce_scatter | solution.py:65
  106.2 330.1 %reduce-scatter.12.cloned.1.call-start = ((), (), s32[]{:S(2)}) async-start(), calls=%async_computation.10 | async-start | bytes 18350080 | tf_op jit(solution)/shard_map/reduce_scatter | solution.py:64
  113.6 8.9 %copy-start.2 = (bf16[16,4096]{1,0:T(8,128)(2,1)S(1)}, bf16[16,4096]{1,0:T(8,128)(2,1)}, u32[]{:S(2)}) copy-start(bf16[16,4096]{1,0:T(8,128)(2,1)} %param.6) | copy-start | bytes 393220
  113.6 8.9 %copy-start.5 = (f32[4096]{0:T(1024)S(1)}, f32[4096]{0:T(1024)}, u32[]{:S(2)}) copy-start(f32[4096]{0:T(1024)} %param.7) | copy-start | bytes 49156
  113.6 41.6 %copy-start.4 = (bf16[16,4096]{1,0:T(8,128)(2,1)S(1)}, bf16[16,4096]{1,0:T(8,128)(2,1)}, u32[]{:S(2)}) copy-start(bf16[16,4096]{1,0:T(8,128)(2,1)} %param.11) | copy-start | bytes 393220
  113.6 464.3 %reduce-scatter.10.cloned.1.call-start = ((), (), s32[]{:S(2)}) async-start(), calls=%async_computation.9 | async-start | bytes 18350080 | tf_op jit(solution)/shard_map/reduce_scatter | solution.py:63
Sparse Core Ops, SparseCore 0:
  10.2 24.7 all-gather.2
  36.6 21.7 all-gather.4
  90.4 32.0 reduce-scatter.7
  124.6 30.5 reduce-scatter.5
  158.8 136.0 reduce-scatter.13
  298.4 137.8 reduce-scatter.11
  440.0 137.8 reduce-scatter.9
where the time goes:
time: 585 us
  waiting for transfers between devices  489 us (84%)
  matrix products  73.1 us (12%)
  between operations  14.2 us (2%)
    reduce_scatter x1, waiting for transfers between devices, local(): lax.psum_scatter(weight_gate, 'dp', scatter_dimension=0, tiled=True)  142 us
    reduce_scatter x1, waiting for transfers between devices, local(): lax.psum_scatter(weight_up, 'dp', scatter_dimension=0, tiled=True)  141 us
    reduce_scatter x1, waiting for transfers between devices, local(): lax.psum_scatter(weight_down, 'dp', scatter_dimension=1, tiled=True)  138 us
    dot_general x3, matrix products, contract_cols(): lax.dot_general(left, right, (((1,), (1,)), ((), ())), preferred_element_...  31.9 us
    reduce_scatter x1, waiting for transfers between devices, local(): lax.psum_scatter(jnp.dot(hidden, down_weight, preferred_element_type=jnp....  31.6 us
    all_gather x1, waiting for transfers between devices, local(): normed_all = lax.all_gather(rescaled_input, 'tp', axis=0, tiled=True)  24.2 us
    dot_general x3, matrix products, contract_rows(): lax.dot_general(left, right, (((0,), (0,)), ((), ())), preferred_element_...  22.1 us
  transfers between devices with their start and end apart: 7, of which 7 were waited for; matrix products, arithmetic and copies ran while one was open for 8% of the time, Pallas kernels for 0%

commit v1 on v0

--- a/solution.py
+++ b/solution.py
@@ -16,7 +16,69 @@
     )
 
 
-def local(tokens, norm_scale_vector, gate_weight, up_weight, down_weight, cotangent):
+def gather_tokens(tokens, norm_scale_vector, gate_weight, up_weight, down_weight, cotangent):
+    n_dp = lax.axis_size("dp")
+    n_tp = lax.axis_size("tp")
+    replica = lax.axis_index("dp")
+    rows = tokens.shape[0] * n_tp
+    width = tokens.shape[1] // n_dp
+    expanded_hidden = tokens.astype(jnp.float32)
+    reciprocal_root_mean = lax.rsqrt(
+        jnp.mean(expanded_hidden * expanded_hidden, axis=-1, keepdims=True) + 1e-05
+    )
+    unit_input = expanded_hidden * reciprocal_root_mean
+    rescaled_input = (unit_input * norm_scale_vector).astype(jnp.bfloat16)
+    grad_all = lax.all_gather(cotangent, ("dp", "tp"), axis=0, tiled=True)
+    normed_all = lax.all_gather(rescaled_input, ("dp", "tp"), axis=0, tiled=True)
+    grad_hidden = contract_cols(grad_all, down_weight)
+    gate = jnp.dot(normed_all, gate_weight, preferred_element_type=jnp.float32)
+    lifted = jnp.dot(normed_all, up_weight, preferred_element_type=jnp.float32)
+    sigmoid_gate = jax.nn.sigmoid(gate)
+    activated = gate * sigmoid_gate
+    hidden = (activated * lifted).astype(jnp.bfloat16)
+    grad_pre = (grad_hidden * lifted * sigmoid_gate * (1.0 + gate * (1.0 - sigmoid_gate))).astype(
+        jnp.bfloat16
+    )
+    grad_lifted = (grad_hidden * activated).astype(jnp.bfloat16)
+
+    def mine(array):
+        return lax.dynamic_slice_in_dim(array, replica * rows, rows, 0)
+
+    def columns(array):
+        return lax.dynamic_slice_in_dim(array, replica * width, width, 1)
+
+    branch = lax.psum_scatter(
+        jnp.dot(mine(hidden), down_weight, preferred_element_type=jnp.float32).astype(jnp.bfloat16),
+        "tp",
+        scatter_dimension=0,
+        tiled=True,
+    ).astype(jnp.float32)
+    mixed = (expanded_hidden + branch).astype(jnp.bfloat16)
+    grad_normed = lax.psum_scatter(
+        (
+            contract_cols(mine(grad_pre), gate_weight) + contract_cols(mine(grad_lifted), up_weight)
+        ).astype(jnp.bfloat16),
+        "tp",
+        scatter_dimension=0,
+        tiled=True,
+    ).astype(jnp.float32)
+    gain_applied = grad_normed * norm_scale_vector
+    inner_product = jnp.mean(gain_applied * unit_input, axis=-1, keepdims=True)
+    token_gradient = (
+        cotangent.astype(jnp.float32)
+        + reciprocal_root_mean * (gain_applied - unit_input * inner_product)
+    ).astype(jnp.bfloat16)
+    normed_columns = columns(normed_all)
+    return (
+        mixed,
+        token_gradient,
+        contract_rows(normed_columns, grad_pre).astype(jnp.bfloat16),
+        contract_rows(normed_columns, grad_lifted).astype(jnp.bfloat16),
+        contract_rows(hidden, columns(grad_all)).astype(jnp.bfloat16),
+    )
+
+
+def sum_weight_gradients(tokens, norm_scale_vector, gate_weight, up_weight, down_weight, cotangent):
     expanded_hidden = tokens.astype(jnp.float32)
     reciprocal_root_mean = lax.rsqrt(
         jnp.mean(expanded_hidden * expanded_hidden, axis=-1, keepdims=True) + 1e-05
@@ -74,6 +136,7 @@
 
 
 def solution(mesh):
+    n_tp = mesh.shape["tp"]
     in_specs = (
         P(("dp", "tp"), None),
         P(),
@@ -89,4 +152,13 @@
         P("dp", "tp"),
         P("tp", "dp"),
     )
-    return jax.shard_map(local, mesh=mesh, in_specs=in_specs, out_specs=out_specs, check_vma=False)
+
+    def run(tokens, norm_scale_vector, gate_weight, up_weight, down_weight, cotangent):
+        gathered = tokens.size + cotangent.size
+        weights = (gate_weight.size + up_weight.size + down_weight.size) // n_tp
+        local = gather_tokens if gathered <= weights else sum_weight_gradients
+        return jax.shard_map(
+            local, mesh=mesh, in_specs=in_specs, out_specs=out_specs, check_vma=False
+        )(tokens, norm_scale_vector, gate_weight, up_weight, down_weight, cotangent)
+
+    return run

time: 585 us -> 251 us (0.43)
  waiting for transfers between devices: 489 us -> 138 us
  matrix products: 73.1 us -> 92.8 us
    reduce_scatter x5 -> x2, waiting for transfers between devices: 454 us -> 37.8 us  [the longest x1 31.7 us: gather_tokens(): lax.psum_scatter(jnp.dot(mine(hidden), down_weight, preferred_element_typ...]
    all_gather x2, waiting for transfers between devices: 34.4 us -> 99.7 us  [the longest x1 65.7 us: gather_tokens(): lax.all_gather(rescaled_input, ('dp', 'tp'), axis=0, tiled=True)]
    dot_general x3, matrix products: 19.1 us -> 38 us  [the longest x1 16.8 us: gather_tokens(): gate = jnp.dot(normed_all, gate_weight, preferred_element_type=jnp.float32)]
    dot_general x3, matrix products: 31.9 us -> 38.5 us  [contract_cols(): lax.dot_general(left, right, (((1,), (1,)), ((), ())), preferred_element_...]
  transfers between devices with their start and end apart: 7 -> 4, of which waited for: 7 -> 4; matrix products, arithmetic and copies ran while one was open for 8% -> 22% of each run, Pallas kernels for 0% -> 0%
where the time goes in v1:
time: 251 us
  waiting for transfers between devices  138 us (55%)
  matrix products  92.8 us (37%)
  between operations  13.8 us (5%)
  other arithmetic  5.61 us (2%)
    all_gather x1, waiting for transfers between devices, gather_tokens(): lax.all_gather(rescaled_input, ('dp', 'tp'), axis=0, tiled=True)  65.7 us
    dot_general x3, matrix products, contract_cols(): lax.dot_general(left, right, (((1,), (1,)), ((), ())), preferred_element_...  38.5 us
    all_gather x1, waiting for transfers between devices, gather_tokens(): grad_all = lax.all_gather(cotangent, ('dp', 'tp'), axis=0, tiled=True)  34 us
    reduce_scatter x1, waiting for transfers between devices, gather_tokens(): lax.psum_scatter(jnp.dot(mine(hidden), down_weight, preferred_element_typ...  31.7 us
    dot_general x1, matrix products, gather_tokens(): gate = jnp.dot(normed_all, gate_weight, preferred_element_type=jnp.float32)  16.8 us
    dot_general x3, matrix products, contract_rows(): lax.dot_general(left, right, (((0,), (0,)), ((), ())), preferred_element_...  16.3 us
    dot_general x1, matrix products, gather_tokens(): lifted = jnp.dot(normed_all, up_weight, preferred_element_type=jnp.float32)  12.9 us
    dot_general x1, matrix products, gather_tokens(): jnp.dot(mine(hidden), down_weight, preferred_element_type=jnp.float32)  8.3 us
  transfers between devices with their start and end apart: 4, of which 4 were waited for; matrix products, arithmetic and copies ran while one was open for 22% of the time, Pallas kernels for 0%

profile of v1, /device:TPU:0, one launch (start us, length us, event | category | flops | bytes accessed | tf_op | source)
XLA Modules:
  0.0 250.6 jit_solution(7846577095874448480)
XLA Ops:
  7.2 0.0 all-gather.3.cloned.1.call-start
  7.2 1.1 fusion.18
  8.3 1.7 fusion.12
  9.9 0.0 all-gather.3.cloned.1.call-update
  10.0 0.0 all-gather.5.cloned.1.call-start
  10.0 0.7 all-gather.5.cloned.1.call-update
  10.7 0.0 reduce-scatter.5.cloned.1.call-start
  10.8 65.7 %all-gather.3.cloned.1.call-done = bf16[512,4096]{1,0:T(8,128)(2,1)} async-done(((bf16[16,4096]{1,0:T(8,128)(2,1)}), bf16[512,4096]{1,0:T(8,128)(2,1)}) %all-gather.3.cloned.1.call-update) | async-done | bytes 4194320 | tf_op jit(solution)/shard_map/all_gather | solution.py:32
  76.4 0.0 copy-start.4
  76.4 16.8 %fusion.26 = f32[512,1792]{1,0:T(8,128)} fusion(bf16[512,4096]{1,0:T(8,128)(2,1)} %all-gather.3.cloned.1.call-done, bf16[4096,1792]{1,0:T(8,128)(2,1)} %param.8), kind=kOutput, calls=%fused_computation.41 | convolution fusion | flops 7516192768 | bytes 22544384 | tf_op jit(solution)/shard_map/dot_general | solution.py:34
  93.2 0.0 copy-done.4
  93.2 12.9 %fusion.27 = f32[512,1792]{1,0:T(8,128)} fusion(bf16[512,4096]{1,0:T(8,128)(2,1)S(1)} %copy-done.4, bf16[4096,1792]{1,0:T(8,128)(2,1)} %param.9), kind=kOutput, calls=%fused_computation.42 | convolution fusion | flops 7516192768 | bytes 22544384 | tf_op jit(solution)/shard_map/dot_general | solution.py:35
  106.1 34.0 %all-gather.5.cloned.1.call-done = bf16[512,4096]{1,0:T(8,128)(2,1)} async-done(((bf16[16,4096]{1,0:T(8,128)(2,1)}), bf16[512,4096]{1,0:T(8,128)(2,1)}) %all-gather.5.cloned.1.call-update) | async-done | bytes 4194320 | tf_op jit(solution)/shard_map/all_gather | solution.py:31
  140.1 17.3 %multiply_convert_fusion = (bf16[512,1792]{1,0:T(8,128)(2,1)}, bf16[512,1792]{1,0:T(8,128)(2,1)}, bf16[512,1792]{1,0:T(8,128)(2,1)S(1)}) fusion(f32[512,1792]{1,0:T(8,128)} %fusion.26, f32[512,1792]{1,0:T(8,128)} %fusion.27, bf16[512,4096]{1,0:T(8,128)(2,1)} %all-gather.5.cloned.1.call-done, bf16[1792,4096]{1,0:T(8,128)(2,1)} %param.10), kind=kOutput, calls=%fused_computation.6 | convolution fusion | flops 7529955328 | bytes 31719424 | tf_op jit(solution)/shard_map/dot_general | solution.py:14
  157.5 10.1 %fusion.6 = f32[128,4096]{1,0:T(8,128)S(1)} fusion(bf16[4096,1792]{1,0:T(8,128)(2,1)} %param.8, bf16[512,1792]{1,0:T(8,128)(2,1)} %get-tuple-element.6, s32[]{:T(128)S(6)} %select_n.4), kind=kOutput, calls=%fused_computation.15 | convolution fusion | flops 1879048192 | bytes 17235972 | tf_op jit(solution)/shard_map/dot_general | solution.py:14
  167.6 11.1 %fusion = bf16[128,4096]{1,0:T(8,128)(2,1)} fusion(f32[128,4096]{1,0:T(8,128)S(1)} %fusion.6, bf16[4096,1792]{1,0:T(8,128)(2,1)} %param.9, bf16[512,1792]{1,0:T(8,128)(2,1)} %get-tuple-element.5, s32[]{:T(128)S(6)} %select_n.4), kind=kOutput, calls=%fused_computation.1 | convolution fusion | flops 1880096768 | bytes 18284548 | tf_op jit(solution)/shard_map/dot_general | solution.py:14
  178.7 0.0 reduce-scatter.5.cloned.1.call-update
  178.7 0.0 reduce-scatter.3.cloned.1.call-start
  178.7 8.3 %convolution_convert_fusion = bf16[128,4096]{1,0:T(8,128)(2,1)} fusion(bf16[1792,4096]{1,0:T(8,128)(2,1)} %param.10, bf16[512,1792]{1,0:T(8,128)(2,1)S(1)} %get-tuple-element.7, s32[]{:T(128)S(6)} %select_n.4), kind=kOutput, calls=%fused_computation.2 | convolution fusion | flops 1879572480 | bytes 16187396 | tf_op jit(solution)/shard_map/dot_general | solution.py:51
  187.0 0.0 reduce-scatter.3.cloned.1.call-update
  187.1 0.0 copy-start.3
  187.1 5.9 %convolution_convert_fusion.2 = bf16[1024,1792]{1,0:T(8,128)(2,1)} fusion(bf16[512,1792]{1,0:T(8,128)(2,1)} %get-tuple-element.5, bf16[512,4096]{1,0:T(8,128)(2,1)} %all-gather.3.cloned.1.call-done, s32[]{:T(128)S(6)} %select_n.10), kind=kOutput, calls=%fused_computation.4 | convolution fusion | flops 1880883200 | bytes 6553604 | tf_op jit(solution)/shard_map/dot_general | solution.py:8
  193.0 0.0 copy-done.3
  193.0 5.2 %convolution_convert_fusion.3 = bf16[1024,1792]{1,0:T(8,128)(2,1)} fusion(bf16[512,1792]{1,0:T(8,128)(2,1)S(1)} %copy-done.3, bf16[512,4096]{1,0:T(8,128)(2,1)} %all-gather.3.cloned.1.call-done, s32[]{:T(128)S(6)} %select_n.10), kind=kOutput, calls=%fused_computation.5 | convolution fusion | flops 1880883200 | bytes 6553604 | tf_op jit(solution)/shard_map/dot_general | solution.py:8
  198.2 5.2 %convolution_convert_fusion.1 = bf16[1792,1024]{1,0:T(8,128)(2,1)} fusion(bf16[512,1792]{1,0:T(8,128)(2,1)S(1)} %get-tuple-element.7, bf16[512,4096]{1,0:T(8,128)(2,1)} %all-gather.5.cloned.1.call-done, s32[]{:T(128)S(6)} %select_n.10), kind=kOutput, calls=%fused_computation.3 | convolution fusion | flops 1880883200 | bytes 6553604 | tf_op jit(solution)/shard_map/dot_general | solution.py:8
  203.4 6.1 %reduce-scatter.5.cloned.1.call-done = bf16[16,4096]{1,0:T(8,128)(2,1)} async-done(((bf16[128,4096]{1,0:T(8,128)(2,1)}), bf16[16,4096]{1,0:T(8,128)(2,1)}) %reduce-scatter.5.cloned.1.call-update) | async-done | bytes 131088 | tf_op jit(solution)/shard_map/reduce_scatter | solution.py:57
  209.5 0.0 copy-done
  209.5 0.0 copy-done.2
  209.5 1.1 fusion.13
  210.6 31.7 %reduce-scatter.3.cloned.1.call-done = bf16[16,4096]{1,0:T(8,128)(2,1)} async-done(((bf16[128,4096]{1,0:T(8,128)(2,1)}), bf16[16,4096]{1,0:T(8,128)(2,1)}) %reduce-scatter.3.cloned.1.call-update) | async-done | bytes 131088 | tf_op jit(solution)/shard_map/reduce_scatter | solution.py:50
  242.3 0.0 copy-done.1
  242.3 1.8 fusion.17
  (5 shorter events, 0.0 us)
Async XLA Ops:
  7.2 69.3 %all-gather.3.cloned.1.call-start = ((), (), s32[]{:S(2)}) async-start(), calls=%async_computation.2 | async-start | bytes 4325376 | tf_op jit(solution)/shard_map/all_gather | solution.py:32
  10.0 130.2 %all-gather.5.cloned.1.call-start = ((), (), s32[]{:S(2)}) async-start(), calls=%async_computation.4 | async-start | bytes 4325376 | tf_op jit(solution)/shard_map/all_gather | solution.py:31
  10.7 198.8 %reduce-scatter.5.cloned.1.call-start = ((), (), s32[]{:S(2)}) async-start(), calls=%async_computation.5 | async-start | bytes 1179648 | tf_op jit(solution)/shard_map/reduce_scatter | solution.py:57
  76.4 16.8 %copy-start.4 = (bf16[512,4096]{1,0:T(8,128)(2,1)S(1)}, bf16[512,4096]{1,0:T(8,128)(2,1)}, u32[]{:S(2)}) copy-start(bf16[512,4096]{1,0:T(8,128)(2,1)} %all-gather.3.cloned.1.call-done) | copy-start | bytes 12582916
  178.7 63.6 %reduce-scatter.3.cloned.1.call-start = ((), (), s32[]{:S(2)}) async-start(), calls=%async_computation.3 | async-start | bytes 1179648 | tf_op jit(solution)/shard_map/reduce_scatter | solution.py:50
  187.1 5.9 %copy-start.3 = (bf16[512,1792]{1,0:T(8,128)(2,1)S(1)}, bf16[512,1792]{1,0:T(8,128)(2,1)}, u32[]{:S(2)}) copy-start(bf16[512,1792]{1,0:T(8,128)(2,1)} %get-tuple-element.6) | copy-start | bytes 5505028
  198.2 11.3 %copy-start = (bf16[16,4096]{1,0:T(8,128)(2,1)S(1)}, bf16[16,4096]{1,0:T(8,128)(2,1)}, u32[]{:S(2)}) copy-start(bf16[16,4096]{1,0:T(8,128)(2,1)} %param.6) | copy-start | bytes 393220
  198.2 11.3 %copy-start.2 = (f32[4096]{0:T(1024)S(1)}, f32[4096]{0:T(1024)}, u32[]{:S(2)}) copy-start(f32[4096]{0:T(1024)} %param.7) | copy-start | bytes 49156
  198.2 44.1 %copy-start.1 = (bf16[16,4096]{1,0:T(8,128)(2,1)S(1)}, bf16[16,4096]{1,0:T(8,128)(2,1)}, u32[]{:S(2)}) copy-start(bf16[16,4096]{1,0:T(8,128)(2,1)} %param.11) | copy-start | bytes 393220
Sparse Core Ops, SparseCore 0:
  11.6 64.8 all-gather.2
  79.4 60.6 all-gather.4
  178.8 30.6 reduce-scatter.4
  211.6 30.6 reduce-scatter.2

commit v2 on v0

--- a/solution.py
+++ b/solution.py
@@ -16,7 +16,81 @@
     )
 
 
-def local(tokens, norm_scale_vector, gate_weight, up_weight, down_weight, cotangent):
+def gather_tokens(tokens, norm_scale_vector, gate_weight, up_weight, down_weight, cotangent):
+    n_dp = lax.axis_size("dp")
+    n_tp = lax.axis_size("tp")
+    width = tokens.shape[1] // n_dp
+    first = lax.axis_index("dp") * width
+    rows = tokens.shape[0]
+
+    def swap(array, dp_bits, tp_bits):
+        pairs = [
+            (d * n_tp + t, (d ^ dp_bits) * n_tp + (t ^ tp_bits))
+            for d in range(n_dp)
+            for t in range(n_tp)
+        ]
+        return lax.ppermute(array, ("dp", "tp"), pairs)
+
+    expanded_hidden = tokens.astype(jnp.float32)
+    reciprocal_root_mean = lax.rsqrt(
+        jnp.mean(expanded_hidden * expanded_hidden, axis=-1, keepdims=True) + 1e-05
+    )
+    unit_input = expanded_hidden * reciprocal_root_mean
+    rescaled_input = (unit_input * norm_scale_vector).astype(jnp.bfloat16)
+    shard = jnp.stack([rescaled_input, cotangent])
+    half = jnp.concatenate([shard] + [swap(shard, 0, b) for b in range(2, n_tp, 2)], axis=1)
+    own = jnp.concatenate([half, swap(half, 0, 1)], axis=1)
+    rest = jnp.concatenate([swap(half, b, 0) for b in range(1, n_dp)], axis=1)
+    others = jnp.concatenate([rest, swap(rest, 0, 1)], axis=1)
+
+    def forward(normed, grad_out):
+        gate = jnp.dot(normed, gate_weight, preferred_element_type=jnp.float32)
+        lifted = jnp.dot(normed, up_weight, preferred_element_type=jnp.float32)
+        grad_hidden = contract_cols(grad_out, down_weight)
+        sigmoid_gate = jax.nn.sigmoid(gate)
+        activated = gate * sigmoid_gate
+        hidden = (activated * lifted).astype(jnp.bfloat16)
+        grad_pre = (
+            grad_hidden * lifted * sigmoid_gate * (1.0 + gate * (1.0 - sigmoid_gate))
+        ).astype(jnp.bfloat16)
+        grad_lifted = (grad_hidden * activated).astype(jnp.bfloat16)
+        return hidden, grad_pre, grad_lifted
+
+    hidden, grad_pre, grad_lifted = forward(own[0], own[1])
+    partial_out = jnp.dot(hidden, down_weight, preferred_element_type=jnp.float32)
+    partial_in = contract_cols(grad_pre, gate_weight) + contract_cols(grad_lifted, up_weight)
+    partials = jnp.stack([partial_out.astype(jnp.bfloat16), partial_in.astype(jnp.bfloat16)])
+    kept, sent = jnp.split(partials, 2, axis=1)
+    pair = (kept.astype(jnp.float32) + swap(sent, 0, 1).astype(jnp.float32)).astype(jnp.bfloat16)
+    total = pair[:, :rows].astype(jnp.float32)
+    for k in range(1, n_tp // 2):
+        total += swap(pair[:, k * rows : (k + 1) * rows], 0, 2 * k).astype(jnp.float32)
+    branch, grad_normed = total[0], total[1]
+    mixed = (expanded_hidden + branch).astype(jnp.bfloat16)
+    gain_applied = grad_normed * norm_scale_vector
+    inner_product = jnp.mean(gain_applied * unit_input, axis=-1, keepdims=True)
+    token_gradient = (
+        cotangent.astype(jnp.float32)
+        + reciprocal_root_mean * (gain_applied - unit_input * inner_product)
+    ).astype(jnp.bfloat16)
+
+    more = forward(others[0], others[1])
+    hidden, grad_pre, grad_lifted = (
+        jnp.concatenate(both, axis=0) for both in zip((hidden, grad_pre, grad_lifted), more)
+    )
+    columns = jnp.concatenate(
+        [lax.dynamic_slice_in_dim(part, first, width, 2) for part in (own, others)], axis=1
+    )
+    return (
+        mixed,
+        token_gradient,
+        contract_rows(columns[0], grad_pre).astype(jnp.bfloat16),
+        contract_rows(columns[0], grad_lifted).astype(jnp.bfloat16),
+        contract_rows(hidden, columns[1]).astype(jnp.bfloat16),
+    )
+
+
+def sum_weight_gradients(tokens, norm_scale_vector, gate_weight, up_weight, down_weight, cotangent):
     expanded_hidden = tokens.astype(jnp.float32)
     reciprocal_root_mean = lax.rsqrt(
         jnp.mean(expanded_hidden * expanded_hidden, axis=-1, keepdims=True) + 1e-05
@@ -74,6 +148,7 @@
 
 
 def solution(mesh):
+    n_tp = mesh.shape["tp"]
     in_specs = (
         P(("dp", "tp"), None),
         P(),
@@ -89,4 +164,13 @@
         P("dp", "tp"),
         P("tp", "dp"),
     )
-    return jax.shard_map(local, mesh=mesh, in_specs=in_specs, out_specs=out_specs, check_vma=False)
+
+    def run(tokens, norm_scale_vector, gate_weight, up_weight, down_weight, cotangent):
+        gathered = tokens.size + cotangent.size
+        weights = (gate_weight.size + up_weight.size + down_weight.size) // n_tp
+        local = gather_tokens if gathered <= weights else sum_weight_gradients
+        return jax.shard_map(
+            local, mesh=mesh, in_specs=in_specs, out_specs=out_specs, check_vma=False
+        )(tokens, norm_scale_vector, gate_weight, up_weight, down_weight, cotangent)
+
+    return run

time: 585 us -> 175 us (0.30)
  waiting for transfers between devices: 489 us -> 38.1 us
  matrix products: 73.1 us -> 97.9 us
  starting transfers between devices: 0.29 us -> 16.5 us
  between operations: 14.2 us -> 0.93 us
  local copies, waits for them, and re-layouts: 2.4 us -> 12.3 us
    reduce_scatter x5 -> x0, waiting for transfers between devices: 454 us -> none  [the longest x1 142 us: local(): lax.psum_scatter(weight_gate, 'dp', scatter_dimension=0, tiled=True)]
    ppermute x0 -> x12, waiting for transfers between devices: none -> 38.1 us  [swap(): return lax.ppermute(array, ('dp', 'tp'), pairs)]
    all_gather x2 -> x0, waiting for transfers between devices: 34.4 us -> none  [the longest x1 24.2 us: local(): normed_all = lax.all_gather(rescaled_input, 'tp', axis=0, tiled=True)]
    dot_general x3 -> x5, matrix products: 19.1 us -> 44.5 us  [the longest x2 21.2 us: forward(): lifted = jnp.dot(normed, up_weight, preferred_element_type=jnp.float32)]
    ppermute x0 -> x12, starting transfers between devices: none -> 16.5 us  [swap(): return lax.ppermute(array, ('dp', 'tp'), pairs)]
    dot_general x3, matrix products: 22.1 us -> 11.9 us  [contract_rows(): lax.dot_general(left, right, (((0,), (0,)), ((), ())), preferred_element_...]
    dot_general x3 -> x4, matrix products: 31.9 us -> 41.4 us  [contract_cols(): lax.dot_general(left, right, (((1,), (1,)), ((), ())), preferred_element_...]
    unnamed x12 -> x34, local copies, waits for them, and re-layouts: 2.4 us -> 8.38 us
  transfers between devices with their start and end apart: 7 -> 12, of which waited for: 7 -> 4; matrix products, arithmetic and copies ran while one was open for 8% -> 37% of each run, Pallas kernels for 0% -> 0%
where the time goes in v2:
time: 175 us; the launch traced here: 174 us
  matrix products  97.9 us (56%)
  waiting for transfers between devices  38.1 us (22%)
  starting transfers between devices  16.5 us (9%)
  local copies, waits for them, and re-layouts  12.3 us (7%)
  other arithmetic  8.45 us (5%)
    dot_general x4, matrix products, contract_cols(): lax.dot_general(left, right, (((1,), (1,)), ((), ())), preferred_element_...  41.4 us
    ppermute x12, waiting for transfers between devices, swap(): return lax.ppermute(array, ('dp', 'tp'), pairs)  38.1 us
    dot_general x2, matrix products, forward(): lifted = jnp.dot(normed, up_weight, preferred_element_type=jnp.float32)  21.2 us
    ppermute x12, starting transfers between devices, swap(): return lax.ppermute(array, ('dp', 'tp'), pairs)  16.5 us
    dot_general x2, matrix products, forward(): gate = jnp.dot(normed, gate_weight, preferred_element_type=jnp.float32)  15.9 us
    dot_general x3, matrix products, contract_rows(): lax.dot_general(left, right, (((0,), (0,)), ((), ())), preferred_element_...  11.9 us
    unnamed x34, local copies, waits for them, and re-layouts  8.38 us
    dot_general x1, matrix products, gather_tokens(): jnp.dot(hidden, down_weight, preferred_element_type=jnp.float32)  7.41 us
  transfers between devices with their start and end apart: 12, of which 4 were waited for; matrix products, arithmetic and copies ran while one was open for 37% of the time, Pallas kernels for 0%

profile of v2, /device:TPU:0, one launch (start us, length us, event | category | flops | bytes accessed | tf_op | source)
XLA Modules:
  0.0 174.2 jit_solution(7763363299018201847)
XLA Ops:
  0.6 1.1 fusion.35
  1.7 1.0 fusion.38
  3.6 3.1 %collective-permute-start = (bf16[2,16,4096]{2,1,0:T(8,128)(2,1)S(1)}, bf16[2,16,4096]{2,1,0:T(8,128)(2,1)S(1)}, u32[]{:S(2)}, u32[]{:S(2)}) collective-permute-start(bf16[2,16,4096]{2,1,0:T(8,128)(2,1)S(1)} %get-tuple-element.16), channel_id=1, source_target_pairs={{0,2},{1,3},{2,0},{3,1},{4,6},{5,7},{6,4},{7,5},{8,10},{9,11},{10,... | collective-permute-start | bytes 786440 | tf_op jit(solution)/shard_map/ppermute | solution.py:32
  6.7 2.6 %collective-permute-start.1 = (bf16[2,16,4096]{2,1,0:T(8,128)(2,1)S(1)}, bf16[2,16,4096]{2,1,0:T(8,128)(2,1)S(1)}, u32[]{:S(2)}, u32[]{:S(2)}) collective-permute-start(bf16[2,16,4096]{2,1,0:T(8,128)(2,1)S(1)} %get-tuple-element.16), channel_id=1, source_target_pairs={{0,4},{1,5},{2,6},{3,7},{4,0},{5,1},{6,2},{7,3},{8,12},{9,13},{10,... | collective-permute-start | bytes 786440 | tf_op jit(solution)/shard_map/ppermute | solution.py:32
  9.3 8.6 %collective-permute-done = bf16[2,16,4096]{2,1,0:T(8,128)(2,1)S(1)} collective-permute-done((bf16[2,16,4096]{2,1,0:T(8,128)(2,1)S(1)}, bf16[2,16,4096]{2,1,0:T(8,128)(2,1)S(1)}, u32[]{:S(2)}, u32[]{:S(2)}) %collective-permute-start) | collective-permute-done | bytes 262176 | tf_op jit(solution)/shard_map/ppermute | solution.py:32
  17.9 10.2 %collective-permute-done.1 = bf16[2,16,4096]{2,1,0:T(8,128)(2,1)S(1)} collective-permute-done((bf16[2,16,4096]{2,1,0:T(8,128)(2,1)S(1)}, bf16[2,16,4096]{2,1,0:T(8,128)(2,1)S(1)}, u32[]{:S(2)}, u32[]{:S(2)}) %collective-permute-start.1) | collective-permute-done | bytes 262176 | tf_op jit(solution)/shard_map/ppermute | solution.py:32
  28.1 2.1 %pad_maximum_fusion.3 = bf16[2,64,4096]{2,1,0:T(8,128)(2,1)} fusion(bf16[2,16,4096]{2,1,0:T(8,128)(2,1)S(1)} %collective-permute-done.2, bf16[2,16,4096]{2,1,0:T(8,128)(2,1)S(1)} %collective-permute-done.1, bf16[2,16,4096]{2,1,0:T(8,128)(2,1)S(1)} %collective-permute-done, bf16[1,16,4096]{2,1,0:T(8,128)(2,1)} %bitcast.59, bf16[1,16,4096]{2,1,0:T(8,128)(2,1)S(1)} %fusion.38), kind=kLoop, calls=%fused_computation.43 | loop fusion | flops 5242880 | bytes 2097152 | tf_op jit(solution)/shard_map/concatenate | solution.py:41
  30.2 1.5 collective-permute-start.8
  31.7 1.5 collective-permute-start.9
  33.7 1.0 constant_dynamic-update-slice_fusion.2
  35.8 7.2 %fusion.24 = f32[128,1792]{1,0:T(8,128)S(1)} fusion(bf16[4096,1792]{1,0:T(8,128)(2,1)} %param.8, bf16[2,128,4096]{2,1,0:T(8,128)(2,1)S(1)} %constant_dynamic-update-slice_fusion), kind=kOutput, calls=%fused_computation.45 | convolution fusion | flops 1879048192 | bytes 16646144 | tf_op jit(solution)/shard_map/dot_general | solution.py:47
  43.0 10.1 %fusion.22 = f32[128,1792]{1,0:T(8,128)S(1)} fusion(bf16[1792,4096]{1,0:T(8,128)(2,1)} %param.10, bf16[2,128,4096]{2,1,0:T(8,128)(2,1)S(1)} %constant_dynamic-update-slice_fusion), kind=kOutput, calls=%fused_computation.41 | convolution fusion | flops 1879048192 | bytes 16646144 | tf_op jit(solution)/shard_map/dot_general | solution.py:14
  53.2 8.5 %multiply_convert_fusion.5 = (bf16[128,1792]{1,0:T(8,128)(2,1)}, bf16[128,1792]{1,0:T(8,128)(2,1)S(1)}, bf16[128,1792]{1,0:T(8,128)(2,1)}) fusion(f32[128,1792]{1,0:T(8,128)S(1)} %fusion.24, f32[128,1792]{1,0:T(8,128)S(1)} %fusion.22, bf16[4096,1792]{1,0:T(8,128)(2,1)} %param.9, bf16[2,128,4096]{2,1,0:T(8,128)(2,1)S(1)} %constant_dynamic-update-slice_fusion), kind=kOutput, calls=%fused_computation.48 | convolution fusion | flops 1882488832 | bytes 18939904 | tf_op jit(solution)/shard_map/dot_general | solution.py:48
  61.7 10.1 %fusion.45 = f32[128,4096]{1,0:T(8,128)S(1)} fusion(bf16[128,1792]{1,0:T(8,128)(2,1)S(1)} %get-tuple-element.9, bf16[4096,1792]{1,0:T(8,128)(2,1)} %param.8), kind=kOutput, calls=%fused_computation.88 | convolution fusion | flops 1879048192 | bytes 17235968 | tf_op jit(solution)/shard_map/dot_general | solution.py:14
  71.8 10.3 %fusion.1 = bf16[1,128,4096]{2,1,0:T(8,128)(2,1)S(1)} fusion(f32[128,4096]{1,0:T(8,128)S(1)} %fusion.45, bf16[128,1792]{1,0:T(8,128)(2,1)} %get-tuple-element.10, bf16[4096,1792]{1,0:T(8,128)(2,1)} %param.9), kind=kOutput, calls=%fused_computation.3 | convolution fusion | flops 1880096768 | bytes 18284544 | tf_op jit(solution)/shard_map/dot_general | solution.py:14
  82.1 7.4 %fusion.2 = bf16[1,128,4096]{2,1,0:T(8,128)(2,1)S(1)} fusion(bf16[128,1792]{1,0:T(8,128)(2,1)} %get-tuple-element.8, bf16[1792,4096]{1,0:T(8,128)(2,1)} %param.10), kind=kOutput, calls=%fused_computation.4 | convolution fusion | flops 1879572480 | bytes 16187392 | tf_op jit(solution)/shard_map/dot_general | solution.py:60
  89.8 1.8 %pad_maximum_fusion = bf16[2,192,4096]{2,1,0:T(8,128)(2,1)S(1)} fusion(bf16[2,64,4096]{2,1,0:T(8,128)(2,1)S(1)} %collective-permute-done.10, bf16[2,64,4096]{2,1,0:T(8,128)(2,1)} %collective-permute-done.9, bf16[2,64,4096]{2,1,0:T(8,128)(2,1)} %collective-permute-done.8), kind=kLoop, calls=%fused_computation.11 | loop fusion | flops 9437184 | bytes 6291456 | tf_op jit(solution)/shard_map/concatenate | solution.py:43
  92.5 2.4 %constant_dynamic-update-slice_fusion.8 = bf16[2,384,4096]{2,1,0:T(8,128)(2,1)} fusion(bf16[2,64,4096]{2,1,0:T(8,128)(2,1)} %collective-permute-done.8), kind=kLoop, calls=%fused_computation.79 | loop fusion | bytes 2097152
  94.9 2.3 %constant_dynamic-update-slice_fusion.7 = bf16[2,384,4096]{2,1,0:T(8,128)(2,1)} fusion(bf16[2,384,4096]{2,1,0:T(8,128)(2,1)} %constant_dynamic-update-slice_fusion.8, bf16[2,64,4096]{2,1,0:T(8,128)(2,1)} %collective-permute-done.9), kind=kLoop, calls=%fused_computation.78 | loop fusion | bytes 2097152
  97.6 2.5 %collective-permute-start.7 = (bf16[2,16,4096]{2,1,0:T(8,128)(2,1)S(1)}, bf16[2,16,4096]{2,1,0:T(8,128)(2,1)S(1)}, u32[]{:S(2)}, u32[]{:S(2)}) collective-permute-start(bf16[2,16,4096]{2,1,0:T(8,128)(2,1)S(1)} %get-tuple-element.12), channel_id=1, source_target_pairs={{0,6},{1,7},{2,4},{3,5},{4,2},{5,3},{6,0},{7,1},{8,14},{9,15},{10,... | collective-permute-start | bytes 786440 | tf_op jit(solution)/shard_map/ppermute | solution.py:32
  100.1 3.7 %collective-permute-start.6 = (bf16[2,16,4096]{2,1,0:T(8,128)(2,1)S(1)}, bf16[2,16,4096]{2,1,0:T(8,128)(2,1)S(1)}, u32[]{:S(2)}, u32[]{:S(2)}) collective-permute-start(bf16[2,16,4096]{2,1,0:T(8,128)(2,1)S(1)} %get-tuple-element.13), channel_id=1, source_target_pairs={{0,4},{1,5},{2,6},{3,7},{4,0},{5,1},{6,2},{7,3},{8,12},{9,13},{10,... | collective-permute-start | bytes 786440 | tf_op jit(solution)/shard_map/ppermute | solution.py:32
  104.0 1.1 constant_dynamic-update-slice_fusion.6
  105.1 3.7 %collective-permute-done.7 = bf16[2,16,4096]{2,1,0:T(8,128)(2,1)S(1)} collective-permute-done((bf16[2,16,4096]{2,1,0:T(8,128)(2,1)S(1)}, bf16[2,16,4096]{2,1,0:T(8,128)(2,1)S(1)}, u32[]{:S(2)}, u32[]{:S(2)}) %collective-permute-start.7) | collective-permute-done | bytes 262176 | tf_op jit(solution)/shard_map/ppermute | solution.py:32
  108.8 15.7 %collective-permute-done.6 = bf16[2,16,4096]{2,1,0:T(8,128)(2,1)S(1)} collective-permute-done((bf16[2,16,4096]{2,1,0:T(8,128)(2,1)S(1)}, bf16[2,16,4096]{2,1,0:T(8,128)(2,1)S(1)}, u32[]{:S(2)}, u32[]{:S(2)}) %collective-permute-start.6) | collective-permute-done | bytes 262176 | tf_op jit(solution)/shard_map/ppermute | solution.py:32
  125.6 2.1 %constant_dynamic-update-slice_fusion.5 = bf16[2,384,4096]{2,1,0:T(8,128)(2,1)} fusion(bf16[2,384,4096]{2,1,0:T(8,128)(2,1)} %constant_dynamic-update-slice_fusion.6, bf16[2,192,4096]{2,1,0:T(8,128)(2,1)S(1)} %collective-permute-done.11), kind=kLoop, calls=%fused_computation.76 | loop fusion | bytes 6291456 | tf_op jit(solution)/shard_map/concatenate | solution.py:44
  127.7 8.7 %fusion.4 = f32[384,1792]{1,0:T(8,128)} fusion(bf16[4096,1792]{1,0:T(8,128)(2,1)S(1)} %bitcast.57, bf16[2,384,4096]{2,1,0:T(8,128)(2,1)} %constant_dynamic-update-slice_fusion.5), kind=kOutput, calls=%fused_computation.12 | convolution fusion | flops 5637144576 | bytes 20578304 | tf_op jit(solution)/shard_map/dot_general | solution.py:47
  136.4 10.9 %fusion.3 = f32[384,1792]{1,0:T(8,128)S(1)} fusion(bf16[1792,4096]{1,0:T(8,128)(2,1)} %param.10, bf16[2,384,4096]{2,1,0:T(8,128)(2,1)} %constant_dynamic-update-slice_fusion.5), kind=kOutput, calls=%fused_computation.10 | convolution fusion | flops 5637144576 | bytes 20578304 | tf_op jit(solution)/shard_map/dot_general | solution.py:14
  147.3 1.7 constant_dynamic-slice_fusion
  149.6 12.7 %multiply_convert_fusion = (bf16[384,1792]{1,0:T(8,128)(2,1)S(1)}, bf16[384,1792]{1,0:T(8,128)(2,1)S(1)}, bf16[384,1792]{1,0:T(8,128)(2,1)S(1)}) fusion(f32[384,1792]{1,0:T(8,128)S(1)} %copy-done.9, f32[384,1792]{1,0:T(8,128)S(1)} %fusion.3, bf16[4096,1792]{1,0:T(8,128)(2,1)} %param.9, bf16[2,384,4096]{2,1,0:T(8,128)(2,1)} %constant_dynamic-update-slice_fusion.5), kind=kOutput, calls=%fused_computation.14 | convolution fusion | flops 5647466496 | bytes 27459584 | tf_op jit(solution)/shard_map/dot_general | solution.py:48
  162.3 4.0 %convolution_convert_fusion.3 = bf16[1024,1792]{1,0:T(8,128)(2,1)} fusion(bf16[384,1792]{1,0:T(8,128)(2,1)S(1)} %get-tuple-element.6, bf16[128,1792]{1,0:T(8,128)(2,1)S(1)} %copy-done.7, bf16[2,128,1024]{2,1,0:T(8,128)(2,1)S(1)} %constant_dynamic-slice_fusion.1, bf16[2,384,1024]{2,1,0:T(8,128)(2,1)S(1)} %constant_dynamic-slice_fusion), kind=kOutput, calls=%fused_computation.7 | convolution fusion | flops 1886650368 | bytes 7602176 | tf_op jit(solution)/shard_map/dot_general | solution.py:8
  166.2 4.0 %convolution_convert_fusion.2 = bf16[1024,1792]{1,0:T(8,128)(2,1)} fusion(bf16[384,1792]{1,0:T(8,128)(2,1)S(1)} %get-tuple-element.7, bf16[128,1792]{1,0:T(8,128)(2,1)S(1)} %copy-done.5, bf16[2,128,1024]{2,1,0:T(8,128)(2,1)S(1)} %constant_dynamic-slice_fusion.1, bf16[2,384,1024]{2,1,0:T(8,128)(2,1)S(1)} %constant_dynamic-slice_fusion), kind=kOutput, calls=%fused_computation.6 | convolution fusion | flops 1886650368 | bytes 7602176 | tf_op jit(solution)/shard_map/dot_general | solution.py:8
  170.2 4.0 %convolution_convert_fusion.1 = bf16[1792,1024]{1,0:T(8,128)(2,1)} fusion(bf16[384,1792]{1,0:T(8,128)(2,1)S(1)} %get-tuple-element.5, bf16[128,1792]{1,0:T(8,128)(2,1)S(1)} %copy-done.4, bf16[2,384,1024]{2,1,0:T(8,128)(2,1)S(1)} %constant_dynamic-slice_fusion, bf16[2,128,1024]{2,1,0:T(8,128)(2,1)S(1)} %constant_dynamic-slice_fusion.1), kind=kOutput, calls=%fused_computation.5 | convolution fusion | flops 1886650368 | bytes 7602176 | tf_op jit(solution)/shard_map/dot_general | solution.py:8
  (56 shorter events, 5.8 us)
Async XLA Ops:
  3.6 14.2 %collective-permute-start = (bf16[2,16,4096]{2,1,0:T(8,128)(2,1)S(1)}, bf16[2,16,4096]{2,1,0:T(8,128)(2,1)S(1)}, u32[]{:S(2)}, u32[]{:S(2)}) collective-permute-start(bf16[2,16,4096]{2,1,0:T(8,128)(2,1)S(1)} %get-tuple-element.16), channel_id=1, source_target_pairs={{0,2},{1,3},{2,0},{3,1},{4,6},{5,7},{6,4},{7,5},{8,10},{9,11},{10,... | collective-permute-start | bytes 786440 | tf_op jit(solution)/shard_map/ppermute | solution.py:32
  6.7 21.4 %collective-permute-start.1 = (bf16[2,16,4096]{2,1,0:T(8,128)(2,1)S(1)}, bf16[2,16,4096]{2,1,0:T(8,128)(2,1)S(1)}, u32[]{:S(2)}, u32[]{:S(2)}) collective-permute-start(bf16[2,16,4096]{2,1,0:T(8,128)(2,1)S(1)} %get-tuple-element.16), channel_id=1, source_target_pairs={{0,4},{1,5},{2,6},{3,7},{4,0},{5,1},{6,2},{7,3},{8,12},{9,13},{10,... | collective-permute-start | bytes 786440 | tf_op jit(solution)/shard_map/ppermute | solution.py:32
  9.3 18.8 %collective-permute-start.2 = (bf16[2,16,4096]{2,1,0:T(8,128)(2,1)S(1)}, bf16[2,16,4096]{2,1,0:T(8,128)(2,1)S(1)}, u32[]{:S(2)}, u32[]{:S(2)}) collective-permute-start(bf16[2,16,4096]{2,1,0:T(8,128)(2,1)S(1)} %get-tuple-element.16), channel_id=1, source_target_pairs={{0,6},{1,7},{2,4},{3,5},{4,2},{5,3},{6,0},{7,1},{8,14},{9,15},{10,... | collective-permute-start | bytes 786440 | tf_op jit(solution)/shard_map/ppermute | solution.py:32
  28.1 3.6 %copy-start.2 = (bf16[2,16,4096]{2,1,0:T(8,128)(2,1)}, bf16[2,16,4096]{2,1,0:T(8,128)(2,1)S(1)}, u32[]{:S(2)}) copy-start(bf16[2,16,4096]{2,1,0:T(8,128)(2,1)S(1)} %collective-permute-done.1) | copy-start | bytes 786436
  28.1 3.6 %copy-start.3 = (bf16[2,16,4096]{2,1,0:T(8,128)(2,1)}, bf16[2,16,4096]{2,1,0:T(8,128)(2,1)S(1)}, u32[]{:S(2)}) copy-start(bf16[2,16,4096]{2,1,0:T(8,128)(2,1)S(1)} %collective-permute-done.2) | copy-start | bytes 786436
  30.2 5.5 %collective-permute-start.3 = (bf16[2,64,4096]{2,1,0:T(8,128)(2,1)}, bf16[2,64,4096]{2,1,0:T(8,128)(2,1)S(1)}, u32[]{:S(2)}, u32[]{:S(2)}) collective-permute-start(bf16[2,64,4096]{2,1,0:T(8,128)(2,1)} %pad_maximum_fusion.3), channel_id=1, source_target_pairs={{0,1},{1,0},{2,3},{3,2},{4,5},{5,4},{6,7},{7,6},{8,9},{9,8},{10,11... | collective-permute-start | bytes 3145736 | tf_op jit(solution)/shard_map/ppermute | solution.py:32
  30.2 59.6 %collective-permute-start.8 = (bf16[2,64,4096]{2,1,0:T(8,128)(2,1)}, bf16[2,64,4096]{2,1,0:T(8,128)(2,1)}, u32[]{:S(2)}, u32[]{:S(2)}) collective-permute-start(bf16[2,64,4096]{2,1,0:T(8,128)(2,1)} %pad_maximum_fusion.3), channel_id=1, source_target_pairs={{0,8},{1,9},{2,10},{3,11},{4,12},{5,13},{6,14},{7,15},{8,0},{9,1},... | collective-permute-start | bytes 3145736 | tf_op jit(solution)/shard_map/ppermute | solution.py:32
  31.7 58.1 %collective-permute-start.9 = (bf16[2,64,4096]{2,1,0:T(8,128)(2,1)}, bf16[2,64,4096]{2,1,0:T(8,128)(2,1)}, u32[]{:S(2)}, u32[]{:S(2)}) collective-permute-start(bf16[2,64,4096]{2,1,0:T(8,128)(2,1)} %pad_maximum_fusion.3), channel_id=1, source_target_pairs={{0,16},{1,17},{2,18},{3,19},{4,20},{5,21},{6,22},{7,23},{8,24},{9,... | collective-permute-start | bytes 3145736 | tf_op jit(solution)/shard_map/ppermute | solution.py:32
  33.2 56.6 %collective-permute-start.10 = (bf16[2,64,4096]{2,1,0:T(8,128)(2,1)}, bf16[2,64,4096]{2,1,0:T(8,128)(2,1)S(1)}, u32[]{:S(2)}, u32[]{:S(2)}) collective-permute-start(bf16[2,64,4096]{2,1,0:T(8,128)(2,1)} %pad_maximum_fusion.3), channel_id=1, source_target_pairs={{0,24},{1,25},{2,26},{3,27},{4,28},{5,29},{6,30},{7,31},{8,16},{9,... | collective-permute-start | bytes 3145736 | tf_op jit(solution)/shard_map/ppermute | solution.py:32
  61.7 10.1 %copy-start.6 = (bf16[128,1792]{1,0:T(8,128)(2,1)}, bf16[128,1792]{1,0:T(8,128)(2,1)S(1)}, u32[]{:S(2)}) copy-start(bf16[128,1792]{1,0:T(8,128)(2,1)S(1)} %get-tuple-element.9) | copy-start | bytes 1376260
  89.6 38.1 %slice-start = ((s8[14680064]{0:T(1024)(128)(4,1)}), s8[4194304]{0:T(1024)(128)(4,1)S(1)}, s32[]{:S(2)}) async-start(s8[14680064]{0:T(1024)(128)(4,1)} %bitcast.56), calls=%async_computation | async-start | bytes 8388608
  89.7 38.0 %slice-start.1 = ((s8[14680064]{0:T(1024)(128)(4,1)}), s8[4194304]{0:T(1024)(128)(4,1)S(1)}, s32[]{:S(2)}) async-start(s8[14680064]{0:T(1024)(128)(4,1)} %bitcast.56), calls=%async_computation.1 | async-start | bytes 8388608
  89.7 7.6 %collective-permute-start.4 = (bf16[2,64,4096]{2,1,0:T(8,128)(2,1)S(1)}, bf16[2,64,4096]{2,1,0:T(8,128)(2,1)S(1)}, u32[]{:S(2)}, u32[]{:S(2)}) collective-permute-start(bf16[2,64,4096]{2,1,0:T(8,128)(2,1)S(1)} %pad_maximum_fusion.2), channel_id=1, source_target_pairs={{0,1},{1,0},{2,3},{3,2},{4,5},{5,4},{6,7},{7,6},{8,9},{9,8},{10,11... | collective-permute-start | bytes 3145736 | tf_op jit(solution)/shard_map/ppermute | solution.py:32
  91.7 34.0 %collective-permute-start.11 = (bf16[2,192,4096]{2,1,0:T(8,128)(2,1)S(1)}, bf16[2,192,4096]{2,1,0:T(8,128)(2,1)S(1)}, u32[]{:S(2)}, u32[]{:S(2)}) collective-permute-start(bf16[2,192,4096]{2,1,0:T(8,128)(2,1)S(1)} %pad_maximum_fusion), channel_id=1, source_target_pairs={{0,1},{1,0},{2,3},{3,2},{4,5},{5,4},{6,7},{7,6},{8,9},{9,8},{10,11... | collective-permute-start | bytes 9437192 | tf_op jit(solution)/shard_map/ppermute | solution.py:32
  97.2 30.5 %slice-start.2 = ((s8[14680064]{0:T(1024)(128)(4,1)}), s8[4194304]{0:T(1024)(128)(4,1)S(1)}, s32[]{:S(2)}) async-start(s8[14680064]{0:T(1024)(128)(4,1)} %bitcast.56), calls=%async_computation.2 | async-start | bytes 8388608
  97.6 27.0 %copy-start = (bf16[16,4096]{1,0:T(8,128)(2,1)S(1)}, bf16[16,4096]{1,0:T(8,128)(2,1)}, u32[]{:S(2)}) copy-start(bf16[16,4096]{1,0:T(8,128)(2,1)} %param.6) | copy-start | bytes 393220
  97.6 27.0 %copy-start.8 = (f32[4096]{0:T(1024)S(1)}, f32[4096]{0:T(1024)}, u32[]{:S(2)}) copy-start(f32[4096]{0:T(1024)} %param.7) | copy-start | bytes 49156
  97.6 27.2 %copy-start.1 = (bf16[16,4096]{1,0:T(8,128)(2,1)S(1)}, bf16[16,4096]{1,0:T(8,128)(2,1)}, u32[]{:S(2)}) copy-start(bf16[16,4096]{1,0:T(8,128)(2,1)} %param.11) | copy-start | bytes 393220
  97.6 11.1 %collective-permute-start.7 = (bf16[2,16,4096]{2,1,0:T(8,128)(2,1)S(1)}, bf16[2,16,4096]{2,1,0:T(8,128)(2,1)S(1)}, u32[]{:S(2)}, u32[]{:S(2)}) collective-permute-start(bf16[2,16,4096]{2,1,0:T(8,128)(2,1)S(1)} %get-tuple-element.12), channel_id=1, source_target_pairs={{0,6},{1,7},{2,4},{3,5},{4,2},{5,3},{6,0},{7,1},{8,14},{9,15},{10,... | collective-permute-start | bytes 786440 | tf_op jit(solution)/shard_map/ppermute | solution.py:32
  100.1 24.3 %collective-permute-start.6 = (bf16[2,16,4096]{2,1,0:T(8,128)(2,1)S(1)}, bf16[2,16,4096]{2,1,0:T(8,128)(2,1)S(1)}, u32[]{:S(2)}, u32[]{:S(2)}) collective-permute-start(bf16[2,16,4096]{2,1,0:T(8,128)(2,1)S(1)} %get-tuple-element.13), channel_id=1, source_target_pairs={{0,4},{1,5},{2,6},{3,7},{4,0},{5,1},{6,2},{7,3},{8,12},{9,13},{10,... | collective-permute-start | bytes 786440 | tf_op jit(solution)/shard_map/ppermute | solution.py:32
  103.8 20.6 %collective-permute-start.5 = (bf16[2,16,4096]{2,1,0:T(8,128)(2,1)S(1)}, bf16[2,16,4096]{2,1,0:T(8,128)(2,1)S(1)}, u32[]{:S(2)}, u32[]{:S(2)}) collective-permute-start(bf16[2,16,4096]{2,1,0:T(8,128)(2,1)S(1)} %get-tuple-element.11), channel_id=1, source_target_pairs={{0,2},{1,3},{2,0},{3,1},{4,6},{5,7},{6,4},{7,5},{8,10},{9,11},{10,... | collective-permute-start | bytes 786440 | tf_op jit(solution)/shard_map/ppermute | solution.py:32
  105.1 22.6 %slice-start.3 = ((s8[14680064]{0:T(1024)(128)(4,1)}), s8[2097152]{0:T(1024)(128)(4,1)S(1)}, s32[]{:S(2)}) async-start(s8[14680064]{0:T(1024)(128)(4,1)} %bitcast.56), calls=%async_computation.3 | async-start | bytes 4194304
  147.3 2.3 %copy-start.9 = (f32[384,1792]{1,0:T(8,128)S(1)}, f32[384,1792]{1,0:T(8,128)}, u32[]{:S(2)}) copy-start(f32[384,1792]{1,0:T(8,128)} %fusion.4) | copy-start | bytes 8257540
  149.6 12.7 %copy-start.7 = (bf16[128,1792]{1,0:T(8,128)(2,1)S(1)}, bf16[128,1792]{1,0:T(8,128)(2,1)}, u32[]{:S(2)}) copy-start(bf16[128,1792]{1,0:T(8,128)(2,1)} %copy-done.6) | copy-start | bytes 1376260
  162.3 4.0 %copy-start.5 = (bf16[128,1792]{1,0:T(8,128)(2,1)S(1)}, bf16[128,1792]{1,0:T(8,128)(2,1)}, u32[]{:S(2)}) copy-start(bf16[128,1792]{1,0:T(8,128)(2,1)} %get-tuple-element.10) | copy-start | bytes 1376260
  166.2 4.0 %copy-start.4 = (bf16[128,1792]{1,0:T(8,128)(2,1)S(1)}, bf16[128,1792]{1,0:T(8,128)(2,1)}, u32[]{:S(2)}) copy-start(bf16[128,1792]{1,0:T(8,128)(2,1)} %get-tuple-element.8) | copy-start | bytes 1376260

commit v3 on v2

--- a/solution.py
+++ b/solution.py
@@ -1,6 +1,8 @@
 import jax
 import jax.numpy as jnp
 from jax import lax
+from jax.experimental import pallas as pl
+from jax.experimental.pallas import tpu as pltpu
 from jax.sharding import PartitionSpec as P
 
 
@@ -14,13 +16,191 @@
     return lax.dot_general(
         left, right, (((1,), (1,)), ((), ())), preferred_element_type=jnp.float32
     )
+
+
+TILE = 256
+CHUNK = 1024
+
+
+def activations(normed, grad_out, gate_weight, up_weight, down_weight):
+    gate = jnp.dot(normed, gate_weight, preferred_element_type=jnp.float32)
+    lifted = jnp.dot(normed, up_weight, preferred_element_type=jnp.float32)
+    grad_hidden = contract_cols(grad_out, down_weight)
+    sigmoid_gate = jax.nn.sigmoid(gate)
+    activated = gate * sigmoid_gate
+    hidden = (activated * lifted).astype(jnp.bfloat16)
+    grad_pre = (grad_hidden * lifted * sigmoid_gate * (1.0 + gate * (1.0 - sigmoid_gate))).astype(
+        jnp.bfloat16
+    )
+    grad_lifted = (grad_hidden * activated).astype(jnp.bfloat16)
+    return hidden, grad_pre, grad_lifted
+
+
+def copy_all(copies):
+    for copy in copies:
+        copy.start()
+    for copy in copies:
+        copy.wait()
+
+
+def own_kernel(
+    near, far, gate_weight, up_weight, down_weight,
+    hidden, grad_pre, grad_lifted, kept, sent,
+    rows, out_sum, in_sum, arrived,
+):
+    step = pl.program_id(0)
+    part = near.shape[1]
+
+    @pl.when(step == 0)
+    def _():
+        copy_all([
+            pltpu.make_async_copy(near, rows.at[:, pl.ds(0, part)], arrived.at[0]),
+            pltpu.make_async_copy(far, rows.at[:, pl.ds(part, part)], arrived.at[1]),
+        ])
+        out_sum[...] = jnp.zeros_like(out_sum)
+        in_sum[...] = jnp.zeros_like(in_sum)
+
+    hidden[...], grad_pre[...], grad_lifted[...] = activations(
+        rows[0], rows[1], gate_weight[...], up_weight[...], down_weight[...]
+    )
+    for at in range(0, out_sum.shape[1], CHUNK):
+        here = slice(at, at + CHUNK)
+        out_sum[:, here] += jnp.dot(
+            hidden[...], down_weight[:, here], preferred_element_type=jnp.float32
+        )
+        in_sum[:, here] += contract_cols(grad_pre[...], gate_weight[here]) + contract_cols(
+            grad_lifted[...], up_weight[here]
+        )
+
+    @pl.when(step == pl.num_programs(0) - 1)
+    def _():
+        for index, total in enumerate((out_sum, in_sum)):
+            kept[index] = total[:part].astype(kept.dtype)
+            sent[index] = total[part:].astype(sent.dtype)
+
+
+def own_rows(near, far, gate_weight, up_weight, down_weight):
+    part, depth = near.shape[1:]
+    hidden_units = gate_weight.shape[1]
+    block = (2 * part, TILE)
+    tall = pl.BlockSpec((depth, TILE), lambda i: (0, i))
+    wide = pl.BlockSpec((TILE, depth), lambda i: (i, 0))
+    slim = pl.BlockSpec(block, lambda i: (0, i))
+    whole = pl.BlockSpec((2, part, depth), lambda i: (0, 0, 0))
+    kept = jax.ShapeDtypeStruct((2, part, depth), jnp.bfloat16)
+    unit = jax.ShapeDtypeStruct((2 * part, hidden_units), jnp.bfloat16)
+    return pl.pallas_call(
+        own_kernel,
+        grid=(hidden_units // TILE,),
+        in_specs=[pl.BlockSpec(memory_space=pl.ANY)] * 2 + [tall, tall, wide],
+        out_specs=[slim, slim, slim, whole, whole],
+        out_shape=[unit, unit, unit, kept, kept],
+        scratch_shapes=[
+            pltpu.VMEM((2, 2 * part, depth), jnp.bfloat16),
+            pltpu.VMEM((2 * part, depth), jnp.float32),
+            pltpu.VMEM((2 * part, depth), jnp.float32),
+            pltpu.SemaphoreType.DMA((2,)),
+        ],
+        compiler_params=pltpu.CompilerParams(vmem_limit_bytes=48 * 2**20),
+        cost_estimate=pl.CostEstimate(
+            flops=24 * part * depth * hidden_units,
+            bytes_accessed=6 * depth * hidden_units,
+            transcendentals=2 * part * hidden_units,
+        ),
+        name="own_rows",
+    )(near, far, gate_weight, up_weight, down_weight)
+
+
+def all_kernel(
+    first, near, far, rest_near, rest_far, own_hidden, own_grad_pre, own_grad_lifted,
+    gate_weight, up_weight, down_weight,
+    grad_gate, grad_up, grad_down,
+    rows, own, normed_t, grad_out, hidden, grad_pre, grad_lifted, arrived,
+):
+    step = pl.program_id(0)
+    part, most = near.shape[1], rest_near.shape[1]
+    width = normed_t.shape[0]
+
+    @pl.when(step == 0)
+    def _():
+        columns = pl.ds(pl.multiple_of(first[0], 128), width)
+        copy_all([
+            pltpu.make_async_copy(near.at[:, :, columns], own.at[:, pl.ds(0, part)], arrived.at[0]),
+            pltpu.make_async_copy(far.at[:, :, columns], own.at[:, pl.ds(part, part)], arrived.at[1]),
+            pltpu.make_async_copy(rest_near, rows.at[:, pl.ds(0, most)], arrived.at[2]),
+            pltpu.make_async_copy(rest_far, rows.at[:, pl.ds(most, most)], arrived.at[3]),
+        ])
+        normed_t[:, : 2 * part] = own[0].T
+        normed_t[:, 2 * part :] = rows[0, :, columns].T
+        grad_out[: 2 * part] = own[1]
+        grad_out[2 * part :] = rows[1, :, columns]
+
+    hidden[: 2 * part] = own_hidden[...]
+    grad_pre[: 2 * part] = own_grad_pre[...]
+    grad_lifted[: 2 * part] = own_grad_lifted[...]
+    hidden[2 * part :], grad_pre[2 * part :], grad_lifted[2 * part :] = activations(
+        rows[0], rows[1], gate_weight[...], up_weight[...], down_weight[...]
+    )
+    grad_gate[...] = jnp.dot(
+        normed_t[...], grad_pre[...], preferred_element_type=jnp.float32
+    ).astype(grad_gate.dtype)
+    grad_up[...] = jnp.dot(
+        normed_t[...], grad_lifted[...], preferred_element_type=jnp.float32
+    ).astype(grad_up.dtype)
+    grad_down[...] = jnp.dot(
+        hidden[...].T, grad_out[...], preferred_element_type=jnp.float32
+    ).astype(grad_down.dtype)
+
+
+def all_rows(first, near, far, rest_near, rest_far, units, gate_weight, up_weight, down_weight, width):
+    part, depth = near.shape[1:]
+    most = rest_near.shape[1]
+    count = 2 * (part + most)
+    hidden_units = gate_weight.shape[1]
+    tall = pl.BlockSpec((depth, TILE), lambda i: (0, i))
+    wide = pl.BlockSpec((TILE, depth), lambda i: (i, 0))
+    slim = pl.BlockSpec((2 * part, TILE), lambda i: (0, i))
+    return pl.pallas_call(
+        all_kernel,
+        grid=(hidden_units // TILE,),
+        in_specs=[pl.BlockSpec(memory_space=pltpu.SMEM)]
+        + [pl.BlockSpec(memory_space=pl.ANY)] * 4
+        + [slim, slim, slim, tall, tall, wide],
+        out_specs=[
+            pl.BlockSpec((width, TILE), lambda i: (0, i)),
+            pl.BlockSpec((width, TILE), lambda i: (0, i)),
+            pl.BlockSpec((TILE, width), lambda i: (i, 0)),
+        ],
+        out_shape=[
+            jax.ShapeDtypeStruct((width, hidden_units), jnp.bfloat16),
+            jax.ShapeDtypeStruct((width, hidden_units), jnp.bfloat16),
+            jax.ShapeDtypeStruct((hidden_units, width), jnp.bfloat16),
+        ],
+        scratch_shapes=[
+            pltpu.VMEM((2, 2 * most, depth), jnp.bfloat16),
+            pltpu.VMEM((2, 2 * part, width), jnp.bfloat16),
+            pltpu.VMEM((width, count), jnp.bfloat16),
+            pltpu.VMEM((count, width), jnp.bfloat16),
+            pltpu.VMEM((count, TILE), jnp.bfloat16),
+            pltpu.VMEM((count, TILE), jnp.bfloat16),
+            pltpu.VMEM((count, TILE), jnp.bfloat16),
+            pltpu.SemaphoreType.DMA((4,)),
+        ],
+        compiler_params=pltpu.CompilerParams(vmem_limit_bytes=48 * 2**20),
+        cost_estimate=pl.CostEstimate(
+            flops=12 * most * depth * hidden_units + 6 * count * width * hidden_units,
+            bytes_accessed=6 * (depth + width) * hidden_units,
+            transcendentals=2 * most * hidden_units,
+        ),
+        name="all_rows",
+    )(first, near, far, rest_near, rest_far, *units, gate_weight, up_weight, down_weight)
 
 
 def gather_tokens(tokens, norm_scale_vector, gate_weight, up_weight, down_weight, cotangent):
     n_dp = lax.axis_size("dp")
     n_tp = lax.axis_size("tp")
     width = tokens.shape[1] // n_dp
-    first = lax.axis_index("dp") * width
+    first = (lax.axis_index("dp") * width).astype(jnp.int32).reshape(1)
     rows = tokens.shape[0]
 
     def swap(array, dp_bits, tp_bits):
@@ -38,33 +218,18 @@
     unit_input = expanded_hidden * reciprocal_root_mean
     rescaled_input = (unit_input * norm_scale_vector).astype(jnp.bfloat16)
     shard = jnp.stack([rescaled_input, cotangent])
-    half = jnp.concatenate([shard] + [swap(shard, 0, b) for b in range(2, n_tp, 2)], axis=1)
-    own = jnp.concatenate([half, swap(half, 0, 1)], axis=1)
-    rest = jnp.concatenate([swap(half, b, 0) for b in range(1, n_dp)], axis=1)
-    others = jnp.concatenate([rest, swap(rest, 0, 1)], axis=1)
-
-    def forward(normed, grad_out):
-        gate = jnp.dot(normed, gate_weight, preferred_element_type=jnp.float32)
-        lifted = jnp.dot(normed, up_weight, preferred_element_type=jnp.float32)
-        grad_hidden = contract_cols(grad_out, down_weight)
-        sigmoid_gate = jax.nn.sigmoid(gate)
-        activated = gate * sigmoid_gate
-        hidden = (activated * lifted).astype(jnp.bfloat16)
-        grad_pre = (
-            grad_hidden * lifted * sigmoid_gate * (1.0 + gate * (1.0 - sigmoid_gate))
-        ).astype(jnp.bfloat16)
-        grad_lifted = (grad_hidden * activated).astype(jnp.bfloat16)
-        return hidden, grad_pre, grad_lifted
-
-    hidden, grad_pre, grad_lifted = forward(own[0], own[1])
-    partial_out = jnp.dot(hidden, down_weight, preferred_element_type=jnp.float32)
-    partial_in = contract_cols(grad_pre, gate_weight) + contract_cols(grad_lifted, up_weight)
-    partials = jnp.stack([partial_out.astype(jnp.bfloat16), partial_in.astype(jnp.bfloat16)])
-    kept, sent = jnp.split(partials, 2, axis=1)
+    near = jnp.concatenate([shard] + [swap(shard, 0, b) for b in range(2, n_tp, 2)], axis=1)
+    far = swap(near, 0, 1)
+    rest_near = jnp.concatenate([swap(near, b, 0) for b in range(1, n_dp)], axis=1)
+    *units, kept, sent = own_rows(near, far, gate_weight, up_weight, down_weight)
+    rest_far = swap(rest_near, 0, 1)
+
     pair = (kept.astype(jnp.float32) + swap(sent, 0, 1).astype(jnp.float32)).astype(jnp.bfloat16)
-    total = pair[:, :rows].astype(jnp.float32)
-    for k in range(1, n_tp // 2):
-        total += swap(pair[:, k * rows : (k + 1) * rows], 0, 2 * k).astype(jnp.float32)
+    parts = [swap(pair[:, k * rows : (k + 1) * rows], 0, 2 * k) for k in range(1, n_tp // 2)]
+    weight_gradients = all_rows(
+        first, near, far, rest_near, rest_far, units, gate_weight, up_weight, down_weight, width
+    )
+    total = pair[:, :rows].astype(jnp.float32) + sum(part.astype(jnp.float32) for part in parts)
     branch, grad_normed = total[0], total[1]
     mixed = (expanded_hidden + branch).astype(jnp.bfloat16)
     gain_applied = grad_normed * norm_scale_vector
@@ -73,21 +238,7 @@
         cotangent.astype(jnp.float32)
         + reciprocal_root_mean * (gain_applied - unit_input * inner_product)
     ).astype(jnp.bfloat16)
-
-    more = forward(others[0], others[1])
-    hidden, grad_pre, grad_lifted = (
-        jnp.concatenate(both, axis=0) for both in zip((hidden, grad_pre, grad_lifted), more)
-    )
-    columns = jnp.concatenate(
-        [lax.dynamic_slice_in_dim(part, first, width, 2) for part in (own, others)], axis=1
-    )
-    return (
-        mixed,
-        token_gradient,
-        contract_rows(columns[0], grad_pre).astype(jnp.bfloat16),
-        contract_rows(columns[0], grad_lifted).astype(jnp.bfloat16),
-        contract_rows(hidden, columns[1]).astype(jnp.bfloat16),
-    )
+    return mixed, token_gradient, *weight_gradients
 
 
 def sum_weight_gradients(tokens, norm_scale_vector, gate_weight, up_weight, down_weight, cotangent):

time: 175 us -> 162 us (0.926)
  matrix products: 97.9 us -> 0 us
  Pallas kernels: 0 us -> 74.2 us
  waiting for transfers between devices: 38.1 us -> 60.6 us
  local copies, waits for them, and re-layouts: 12.3 us -> 5.15 us
  starting transfers between devices: 16.5 us -> 12.9 us
    dot_general x12 -> x0, matrix products: 97.9 us -> none  [the longest x4 41.4 us: contract_cols(): lax.dot_general(left, right, (((1,), (1,)), ((), ())), preferred_element_...]
    pallas_call x0 -> x2, Pallas kernels: none -> 74.2 us  [the longest x1 44.1 us: all_rows(): pl.pallas_call(all_kernel, grid=(hidden_units // TILE,), in_specs=[pl.Blo...]
    ppermute x12, waiting for transfers between devices: 38.1 us -> 60.6 us  [swap(): return lax.ppermute(array, ('dp', 'tp'), pairs)]
    unnamed x34 -> x6, local copies, waits for them, and re-layouts: 8.38 us -> 3.2 us
    ppermute x12, starting transfers between devices: 16.5 us -> 12.9 us  [swap(): return lax.ppermute(array, ('dp', 'tp'), pairs)]
    concatenate x1 -> x0, other arithmetic: 1.85 us -> none  [gather_tokens(): rest = jnp.concatenate([swap(half, b, 0) for b in range(1, n_dp)], axis=1)]
  transfers between devices with their start and end apart: 12 -> 12, of which waited for: 4 -> 6; matrix products, arithmetic and copies ran while one was open for 37% -> 5% of each run, Pallas kernels for 0% -> 19%
where the time goes in v3:
time: 162 us
  Pallas kernels  74.2 us (46%)
  waiting for transfers between devices  60.6 us (37%)
  starting transfers between devices  12.9 us (8%)
  other arithmetic  8.45 us (5%)
  local copies, waits for them, and re-layouts  5.15 us (3%)
    ppermute x12, waiting for transfers between devices, swap(): return lax.ppermute(array, ('dp', 'tp'), pairs)  60.6 us
    pallas_call x1, Pallas kernels, all_rows(): pl.pallas_call(all_kernel, grid=(hidden_units // TILE,), in_specs=[pl.Blo...  44.1 us
    pallas_call x1, Pallas kernels, own_rows(): pl.pallas_call(own_kernel, grid=(hidden_units // TILE,), in_specs=[pl.Blo...  30.1 us
    ppermute x12, starting transfers between devices, swap(): return lax.ppermute(array, ('dp', 'tp'), pairs)  12.9 us
  transfers between devices with their start and end apart: 12, of which 6 were waited for; matrix products, arithmetic and copies ran while one was open for 5% of the time, Pallas kernels for 19%

profile of v3, /device:TPU:0, one launch (start us, length us, event | category | flops | bytes accessed | tf_op | source)
XLA Modules:
  0.0 162.0 jit_solution(6807147155046798430)
XLA Ops:
  0.6 1.1 fusion.9
  1.7 1.0 fusion.12
  2.7 0.9 pad_maximum_fusion.1
  3.6 5.1 %collective-permute-start.2 = (bf16[2,16,4096]{2,1,0:T(8,128)(2,1)S(1)}, bf16[2,16,4096]{2,1,0:T(8,128)(2,1)S(1)}, u32[]{:S(2)}, u32[]{:S(2)}) collective-permute-start(bf16[2,16,4096]{2,1,0:T(8,128)(2,1)S(1)} %pad_maximum_fusion.1), channel_id=1, source_target_pairs={{0,6},{1,7},{2,4},{3,5},{4,2},{5,3},{6,0},{7,1},{8,14},{9,15},{10,... | collective-permute-start | bytes 786440 | tf_op jit(solution)/shard_map/ppermute | solution.py:212
  8.8 0.0 collective-permute-start.1
  8.8 0.6 collective-permute-start
  9.4 6.6 %collective-permute-done.2 = bf16[2,16,4096]{2,1,0:T(8,128)(2,1)S(1)} collective-permute-done((bf16[2,16,4096]{2,1,0:T(8,128)(2,1)S(1)}, bf16[2,16,4096]{2,1,0:T(8,128)(2,1)S(1)}, u32[]{:S(2)}, u32[]{:S(2)}) %collective-permute-start.2) | collective-permute-done | bytes 262176 | tf_op jit(solution)/shard_map/ppermute | solution.py:212
  16.0 15.0 %collective-permute-done.1 = bf16[2,16,4096]{2,1,0:T(8,128)(2,1)S(1)} collective-permute-done((bf16[2,16,4096]{2,1,0:T(8,128)(2,1)S(1)}, bf16[2,16,4096]{2,1,0:T(8,128)(2,1)S(1)}, u32[]{:S(2)}, u32[]{:S(2)}) %collective-permute-start.1) | collective-permute-done | bytes 262176 | tf_op jit(solution)/shard_map/ppermute | solution.py:212
  31.1 1.0 pad_maximum_fusion.near
  32.1 0.1 collective-permute-start.3
  32.1 2.5 %collective-permute-start.10 = (bf16[2,64,4096]{2,1,0:T(8,128)(2,1)S(1)}, bf16[2,64,4096]{2,1,0:T(8,128)(2,1)S(1)}, u32[]{:S(2)}, u32[]{:S(2)}) collective-permute-start(bf16[2,64,4096]{2,1,0:T(8,128)(2,1)S(1)} %pad_maximum_fusion.near), channel_id=1, source_target_pairs={{0,24},{1,25},{2,26},{3,27},{4,28},{5,29},{6,30},{7,31},{8,16},{9,... | collective-permute-start | bytes 3145736 | tf_op jit(solution)/shard_map/ppermute | solution.py:212
  34.7 0.5 collective-permute-start.9
  35.2 0.5 collective-permute-start.8
  35.7 30.1 %own_rows.1 = (bf16[128,1792]{1,0:T(8,128)(2,1)S(1)}, bf16[128,1792]{1,0:T(8,128)(2,1)S(1)}, bf16[128,1792]{1,0:T(8,128)(2,1)S(1)}, bf16[2,64,4096]{2,1,0:T(8,128)(2,1)S(1)}, bf16[2,64,4096]{2,1,0:T(8,128)(2,1)S(1)}) custom-call(bf16[2,64,4096]{2,1,0:T(8,128)(2,1)S(1)} %pad_maximum_fusion.near, bf16[2,64,4096]{2,1,0:T(8,128)(2,1)S(1)} %collective-permute-done.3.far, ...), custom_call_target="tpu_custom_call" | custom-call | flops 11274289152 | bytes 44040192 | tf_op jit(solution)/shard_map/own_rows/pallas_call | solution.py:92
  65.8 0.1 collective-permute-start.4
  65.9 15.3 %collective-permute-done.8 = bf16[2,64,4096]{2,1,0:T(8,128)(2,1)S(1)} collective-permute-done((bf16[2,64,4096]{2,1,0:T(8,128)(2,1)S(1)}, bf16[2,64,4096]{2,1,0:T(8,128)(2,1)S(1)}, u32[]{:S(2)}, u32[]{:S(2)}) %collective-permute-start.8) | collective-permute-done | bytes 1048608 | tf_op jit(solution)/shard_map/ppermute | solution.py:212
  81.2 1.1 constant_dynamic-update-slice_fusion.2
  82.3 1.1 constant_dynamic-update-slice_fusion.1
  83.4 1.1 constant_dynamic-update-slice_fusion.rest_near
  84.5 0.2 add_convert_fusion
  84.8 0.0 copy-start
  84.8 1.0 copy-done
  85.7 0.9 fusion.13
  86.6 2.5 %collective-permute-start.7 = (bf16[2,16,4096]{2,1,0:T(8,128)(2,1)}, bf16[2,16,4096]{2,1,0:T(8,128)(2,1)}, u32[]{:S(2)}, u32[]{:S(2)}) collective-permute-start(bf16[2,16,4096]{2,1,0:T(8,128)(2,1)} %get-tuple-element.22), channel_id=1, source_target_pairs={{0,6},{1,7},{2,4},{3,5},{4,2},{5,3},{6,0},{7,1},{8,14},{9,15},{10,... | collective-permute-start | bytes 786440 | tf_op jit(solution)/shard_map/ppermute | solution.py:212
  89.1 1.0 collective-permute-start.6
  90.1 5.5 %collective-permute-done.5 = bf16[2,16,4096]{2,1,0:T(8,128)(2,1)} collective-permute-done((bf16[2,16,4096]{2,1,0:T(8,128)(2,1)}, bf16[2,16,4096]{2,1,0:T(8,128)(2,1)}, u32[]{:S(2)}, u32[]{:S(2)}) %collective-permute-start.5) | collective-permute-done | bytes 262176 | tf_op jit(solution)/shard_map/ppermute | solution.py:212
  95.7 6.6 %collective-permute-done.7 = bf16[2,16,4096]{2,1,0:T(8,128)(2,1)} collective-permute-done((bf16[2,16,4096]{2,1,0:T(8,128)(2,1)}, bf16[2,16,4096]{2,1,0:T(8,128)(2,1)}, u32[]{:S(2)}, u32[]{:S(2)}) %collective-permute-start.7) | collective-permute-done | bytes 262176 | tf_op jit(solution)/shard_map/ppermute | solution.py:212
  102.3 11.4 %collective-permute-done.6 = bf16[2,16,4096]{2,1,0:T(8,128)(2,1)} collective-permute-done((bf16[2,16,4096]{2,1,0:T(8,128)(2,1)}, bf16[2,16,4096]{2,1,0:T(8,128)(2,1)}, u32[]{:S(2)}, u32[]{:S(2)}) %collective-permute-start.6) | collective-permute-done | bytes 262176 | tf_op jit(solution)/shard_map/ppermute | solution.py:212
  113.7 1.3 add_add_fusion
  115.0 1.1 fusion.4
  116.1 1.8 %fusion.8 = (bf16[16,4096]{1,0:T(8,128)(2,1)}, bf16[16,4096]{1,0:T(8,128)(2,1)}) fusion(bf16[16,4096]{1,0:T(8,128)(2,1)} %param.6, bf16[16,4096]{1,0:T(8,128)(2,1)} %param.11, f32[2,16,4096]{2,1,0:T(8,128)S(1)} %add_add_fusion, f32[16]{0:T(128)S(1)} %broadcast_multiply_fusion, f32[4096]{0:T(1024)S(1)} %copy-done.1, f32[16]{0:T(128)S(1)} %add_rsqrt_fusion), kind=kLoop, calls=%fused_computation.14 | loop fusion | flops 720896 | bytes 1065088 | tf_op jit(solution)/shard_map/convert_element_type | solution.py:240
  117.9 44.1 %all_rows.1 = (bf16[1024,1792]{1,0:T(8,128)(2,1)}, bf16[1024,1792]{1,0:T(8,128)(2,1)}, bf16[1792,1024]{1,0:T(8,128)(2,1)}) custom-call(s32[1]{0:T(128)} %bitcast.4.first, bf16[2,64,4096]{2,1,0:T(8,128)(2,1)S(1)} %pad_maximum_fusion.near, bf16[2,64,4096]{2,1,0:T(8,128)(2,1)S(1)} %collective-permute-done.3.far, ...), custom_call_target="tpu_custom_call" | custom-call | flops 22548578304 | bytes 55050240 | tf_op jit(solution)/shard_map/all_rows/pallas_call | solution.py:163
  (12 shorter events, 0.0 us)
Async XLA Ops:
  3.6 12.4 %collective-permute-start.2 = (bf16[2,16,4096]{2,1,0:T(8,128)(2,1)S(1)}, bf16[2,16,4096]{2,1,0:T(8,128)(2,1)S(1)}, u32[]{:S(2)}, u32[]{:S(2)}) collective-permute-start(bf16[2,16,4096]{2,1,0:T(8,128)(2,1)S(1)} %pad_maximum_fusion.1), channel_id=1, source_target_pairs={{0,6},{1,7},{2,4},{3,5},{4,2},{5,3},{6,0},{7,1},{8,14},{9,15},{10,... | collective-permute-start | bytes 786440 | tf_op jit(solution)/shard_map/ppermute | solution.py:212
  8.8 22.3 %collective-permute-start.1 = (bf16[2,16,4096]{2,1,0:T(8,128)(2,1)S(1)}, bf16[2,16,4096]{2,1,0:T(8,128)(2,1)S(1)}, u32[]{:S(2)}, u32[]{:S(2)}) collective-permute-start(bf16[2,16,4096]{2,1,0:T(8,128)(2,1)S(1)} %pad_maximum_fusion.1), channel_id=1, source_target_pairs={{0,4},{1,5},{2,6},{3,7},{4,0},{5,1},{6,2},{7,3},{8,12},{9,13},{10,... | collective-permute-start | bytes 786440 | tf_op jit(solution)/shard_map/ppermute | solution.py:212
  8.8 22.3 %collective-permute-start = (bf16[2,16,4096]{2,1,0:T(8,128)(2,1)S(1)}, bf16[2,16,4096]{2,1,0:T(8,128)(2,1)S(1)}, u32[]{:S(2)}, u32[]{:S(2)}) collective-permute-start(bf16[2,16,4096]{2,1,0:T(8,128)(2,1)S(1)} %pad_maximum_fusion.1), channel_id=1, source_target_pairs={{0,2},{1,3},{2,0},{3,1},{4,6},{5,7},{6,4},{7,5},{8,10},{9,11},{10,... | collective-permute-start | bytes 786440 | tf_op jit(solution)/shard_map/ppermute | solution.py:212
  32.1 3.6 %collective-permute-start.3 = (bf16[2,64,4096]{2,1,0:T(8,128)(2,1)S(1)}, bf16[2,64,4096]{2,1,0:T(8,128)(2,1)S(1)}, u32[]{:S(2)}, u32[]{:S(2)}) collective-permute-start(bf16[2,64,4096]{2,1,0:T(8,128)(2,1)S(1)} %pad_maximum_fusion.near), channel_id=1, source_target_pairs={{0,1},{1,0},{2,3},{3,2},{4,5},{5,4},{6,7},{7,6},{8,9},{9,8},{10,11... | collective-permute-start | bytes 3145736 | tf_op jit(solution)/shard_map/ppermute | solution.py:212
  32.1 51.3 %collective-permute-start.10 = (bf16[2,64,4096]{2,1,0:T(8,128)(2,1)S(1)}, bf16[2,64,4096]{2,1,0:T(8,128)(2,1)S(1)}, u32[]{:S(2)}, u32[]{:S(2)}) collective-permute-start(bf16[2,64,4096]{2,1,0:T(8,128)(2,1)S(1)} %pad_maximum_fusion.near), channel_id=1, source_target_pairs={{0,24},{1,25},{2,26},{3,27},{4,28},{5,29},{6,30},{7,31},{8,16},{9,... | collective-permute-start | bytes 3145736 | tf_op jit(solution)/shard_map/ppermute | solution.py:212
  34.7 47.7 %collective-permute-start.9 = (bf16[2,64,4096]{2,1,0:T(8,128)(2,1)S(1)}, bf16[2,64,4096]{2,1,0:T(8,128)(2,1)S(1)}, u32[]{:S(2)}, u32[]{:S(2)}) collective-permute-start(bf16[2,64,4096]{2,1,0:T(8,128)(2,1)S(1)} %pad_maximum_fusion.near), channel_id=1, source_target_pairs={{0,16},{1,17},{2,18},{3,19},{4,20},{5,21},{6,22},{7,23},{8,24},{9,... | collective-permute-start | bytes 3145736 | tf_op jit(solution)/shard_map/ppermute | solution.py:212
  35.2 46.0 %collective-permute-start.8 = (bf16[2,64,4096]{2,1,0:T(8,128)(2,1)S(1)}, bf16[2,64,4096]{2,1,0:T(8,128)(2,1)S(1)}, u32[]{:S(2)}, u32[]{:S(2)}) collective-permute-start(bf16[2,64,4096]{2,1,0:T(8,128)(2,1)S(1)} %pad_maximum_fusion.near), channel_id=1, source_target_pairs={{0,8},{1,9},{2,10},{3,11},{4,12},{5,13},{6,14},{7,15},{8,0},{9,1},... | collective-permute-start | bytes 3145736 | tf_op jit(solution)/shard_map/ppermute | solution.py:212
  65.8 18.7 %collective-permute-start.4 = (bf16[2,64,4096]{2,1,0:T(8,128)(2,1)S(1)}, bf16[2,64,4096]{2,1,0:T(8,128)(2,1)S(1)}, u32[]{:S(2)}, u32[]{:S(2)}) collective-permute-start(bf16[2,64,4096]{2,1,0:T(8,128)(2,1)S(1)} %get-tuple-element.14), channel_id=1, source_target_pairs={{0,1},{1,0},{2,3},{3,2},{4,5},{5,4},{6,7},{7,6},{8,9},{9,8},{10,11... | collective-permute-start | bytes 3145736 | tf_op jit(solution)/shard_map/ppermute | solution.py:212
  84.5 33.4 %collective-permute-start.11 = (bf16[2,192,4096]{2,1,0:T(8,128)(2,1)}, bf16[2,192,4096]{2,1,0:T(8,128)(2,1)}, u32[]{:S(2)}, u32[]{:S(2)}) collective-permute-start(bf16[2,192,4096]{2,1,0:T(8,128)(2,1)} %constant_dynamic-update-slice_fusion.rest_near), channel_id=1, source_target_pairs={{0,1},{1,0},{2,3},{3,2},{4,5},{5,4},{6,7},{7,6},{8,9},{9,8},{10,11... | collective-permute-start | bytes 9437192 | tf_op jit(solution)/shard_map/ppermute | solution.py:212
  84.5 30.5 %copy-start.1 = (f32[4096]{0:T(1024)S(1)}, f32[4096]{0:T(1024)}, u32[]{:S(2)}) copy-start(f32[4096]{0:T(1024)} %param.7) | copy-start | bytes 49156
  84.8 1.0 copy-start
  86.6 9.0 %collective-permute-start.5 = (bf16[2,16,4096]{2,1,0:T(8,128)(2,1)}, bf16[2,16,4096]{2,1,0:T(8,128)(2,1)}, u32[]{:S(2)}, u32[]{:S(2)}) collective-permute-start(bf16[2,16,4096]{2,1,0:T(8,128)(2,1)} %get-tuple-element.21), channel_id=1, source_target_pairs={{0,2},{1,3},{2,0},{3,1},{4,6},{5,7},{6,4},{7,5},{8,10},{9,11},{10,... | collective-permute-start | bytes 786440 | tf_op jit(solution)/shard_map/ppermute | solution.py:212
  86.6 15.7 %collective-permute-start.7 = (bf16[2,16,4096]{2,1,0:T(8,128)(2,1)}, bf16[2,16,4096]{2,1,0:T(8,128)(2,1)}, u32[]{:S(2)}, u32[]{:S(2)}) collective-permute-start(bf16[2,16,4096]{2,1,0:T(8,128)(2,1)} %get-tuple-element.22), channel_id=1, source_target_pairs={{0,6},{1,7},{2,4},{3,5},{4,2},{5,3},{6,0},{7,1},{8,14},{9,15},{10,... | collective-permute-start | bytes 786440 | tf_op jit(solution)/shard_map/ppermute | solution.py:212
  89.1 24.6 %collective-permute-start.6 = (bf16[2,16,4096]{2,1,0:T(8,128)(2,1)}, bf16[2,16,4096]{2,1,0:T(8,128)(2,1)}, u32[]{:S(2)}, u32[]{:S(2)}) collective-permute-start(bf16[2,16,4096]{2,1,0:T(8,128)(2,1)} %get-tuple-element.23), channel_id=1, source_target_pairs={{0,4},{1,5},{2,6},{3,7},{4,0},{5,1},{6,2},{7,3},{8,12},{9,13},{10,... | collective-permute-start | bytes 786440 | tf_op jit(solution)/shard_map/ppermute | solution.py:212

commit v4 on v3

--- a/solution.py
+++ b/solution.py
@@ -1,3 +1,5 @@
+import functools
+
 import jax
 import jax.numpy as jnp
 from jax import lax
@@ -19,13 +21,12 @@
 
 
 TILE = 256
-CHUNK = 1024
-
-
-def activations(normed, grad_out, gate_weight, up_weight, down_weight):
+COLUMNS = 512
+
+
+def activations(normed, grad_hidden, gate_weight, up_weight):
     gate = jnp.dot(normed, gate_weight, preferred_element_type=jnp.float32)
     lifted = jnp.dot(normed, up_weight, preferred_element_type=jnp.float32)
-    grad_hidden = contract_cols(grad_out, down_weight)
     sigmoid_gate = jax.nn.sigmoid(gate)
     activated = gate * sigmoid_gate
     hidden = (activated * lifted).astype(jnp.bfloat16)
@@ -43,103 +44,128 @@
         copy.wait()
 
 
-def own_kernel(
-    near, far, gate_weight, up_weight, down_weight,
-    hidden, grad_pre, grad_lifted, kept, sent,
-    rows, out_sum, in_sum, arrived,
-):
-    step = pl.program_id(0)
-    part = near.shape[1]
-
-    @pl.when(step == 0)
+def pack(pieces, rows, arrived):
+    height = pieces[0].shape[1]
+    copy_all([
+        pltpu.make_async_copy(piece, rows.at[:, pl.ds(i * height, height)], arrived.at[i])
+        for i, piece in enumerate(pieces)
+    ])
+
+
+def own_kernel(n_pieces, *refs):
+    pieces, refs = refs[:n_pieces], refs[n_pieces:]
+    gate_weight, up_weight, down_weight, hidden, grad_pre, grad_lifted, rows, arrived = refs
+
+    @pl.when(pl.program_id(0) == 0)
     def _():
-        copy_all([
-            pltpu.make_async_copy(near, rows.at[:, pl.ds(0, part)], arrived.at[0]),
-            pltpu.make_async_copy(far, rows.at[:, pl.ds(part, part)], arrived.at[1]),
-        ])
-        out_sum[...] = jnp.zeros_like(out_sum)
-        in_sum[...] = jnp.zeros_like(in_sum)
-
+        pack(pieces, rows, arrived)
+
+    grad_hidden = contract_cols(rows[1], down_weight[...])
     hidden[...], grad_pre[...], grad_lifted[...] = activations(
-        rows[0], rows[1], gate_weight[...], up_weight[...], down_weight[...]
-    )
-    for at in range(0, out_sum.shape[1], CHUNK):
-        here = slice(at, at + CHUNK)
-        out_sum[:, here] += jnp.dot(
-            hidden[...], down_weight[:, here], preferred_element_type=jnp.float32
-        )
-        in_sum[:, here] += contract_cols(grad_pre[...], gate_weight[here]) + contract_cols(
-            grad_lifted[...], up_weight[here]
-        )
-
-    @pl.when(step == pl.num_programs(0) - 1)
-    def _():
-        for index, total in enumerate((out_sum, in_sum)):
-            kept[index] = total[:part].astype(kept.dtype)
-            sent[index] = total[part:].astype(sent.dtype)
-
-
-def own_rows(near, far, gate_weight, up_weight, down_weight):
-    part, depth = near.shape[1:]
-    hidden_units = gate_weight.shape[1]
-    block = (2 * part, TILE)
+        rows[0], grad_hidden, gate_weight[...], up_weight[...]
+    )
+
+
+def own_rows(pieces, gate_weight, up_weight, down_weight):
+    depth, hidden_units = gate_weight.shape
+    count = sum(piece.shape[1] for piece in pieces)
     tall = pl.BlockSpec((depth, TILE), lambda i: (0, i))
     wide = pl.BlockSpec((TILE, depth), lambda i: (i, 0))
-    slim = pl.BlockSpec(block, lambda i: (0, i))
-    whole = pl.BlockSpec((2, part, depth), lambda i: (0, 0, 0))
-    kept = jax.ShapeDtypeStruct((2, part, depth), jnp.bfloat16)
-    unit = jax.ShapeDtypeStruct((2 * part, hidden_units), jnp.bfloat16)
+    slim = pl.BlockSpec((count, TILE), lambda i: (0, i))
+    unit = jax.ShapeDtypeStruct((count, hidden_units), jnp.bfloat16)
     return pl.pallas_call(
-        own_kernel,
+        functools.partial(own_kernel, len(pieces)),
         grid=(hidden_units // TILE,),
-        in_specs=[pl.BlockSpec(memory_space=pl.ANY)] * 2 + [tall, tall, wide],
-        out_specs=[slim, slim, slim, whole, whole],
-        out_shape=[unit, unit, unit, kept, kept],
+        in_specs=[pl.BlockSpec(memory_space=pl.ANY)] * len(pieces) + [tall, tall, wide],
+        out_specs=[slim, slim, slim],
+        out_shape=[unit, unit, unit],
         scratch_shapes=[
-            pltpu.VMEM((2, 2 * part, depth), jnp.bfloat16),
-            pltpu.VMEM((2 * part, depth), jnp.float32),
-            pltpu.VMEM((2 * part, depth), jnp.float32),
-            pltpu.SemaphoreType.DMA((2,)),
+            pltpu.VMEM((2, count, depth), jnp.bfloat16),
+            pltpu.SemaphoreType.DMA((len(pieces),)),
         ],
-        compiler_params=pltpu.CompilerParams(vmem_limit_bytes=48 * 2**20),
+        compiler_params=pltpu.CompilerParams(vmem_limit_bytes=24 * 2**20),
         cost_estimate=pl.CostEstimate(
-            flops=24 * part * depth * hidden_units,
+            flops=6 * count * depth * hidden_units,
             bytes_accessed=6 * depth * hidden_units,
-            transcendentals=2 * part * hidden_units,
+            transcendentals=count * hidden_units,
         ),
         name="own_rows",
-    )(near, far, gate_weight, up_weight, down_weight)
-
-
-def all_kernel(
-    first, near, far, rest_near, rest_far, own_hidden, own_grad_pre, own_grad_lifted,
-    gate_weight, up_weight, down_weight,
-    grad_gate, grad_up, grad_down,
-    rows, own, normed_t, grad_out, hidden, grad_pre, grad_lifted, arrived,
+    )(*pieces, gate_weight, up_weight, down_weight)
+
+
+def partial_kernel(
+    hidden, grad_pre, grad_lifted, gate_weight, up_weight, down_weight,
+    kept, sent, grad_pre_t, grad_lifted_t,
 ):
+    part = kept.shape[1]
+
+    @pl.when(pl.program_id(0) == 0)
+    def _():
+        grad_pre_t[...] = grad_pre[...].T
+        grad_lifted_t[...] = grad_lifted[...].T
+
+    partial_out = jnp.dot(hidden[...], down_weight[...], preferred_element_type=jnp.float32)
+    partial_in = (
+        jnp.dot(gate_weight[...], grad_pre_t[...], preferred_element_type=jnp.float32)
+        + jnp.dot(up_weight[...], grad_lifted_t[...], preferred_element_type=jnp.float32)
+    ).T
+    for index, total in enumerate((partial_out, partial_in)):
+        kept[index] = total[:part].astype(kept.dtype)
+        sent[index] = total[part:].astype(sent.dtype)
+
+
+def partial_sums(units, gate_weight, up_weight, down_weight):
+    depth, hidden_units = gate_weight.shape
+    count = units[0].shape[0]
+    whole = pl.BlockSpec((count, hidden_units), lambda i: (0, 0))
+    wide = pl.BlockSpec((COLUMNS, hidden_units), lambda i: (i, 0))
+    tall = pl.BlockSpec((hidden_units, COLUMNS), lambda i: (0, i))
+    slim = pl.BlockSpec((2, count // 2, COLUMNS), lambda i: (0, 0, i))
+    kept = jax.ShapeDtypeStruct((2, count // 2, depth), jnp.bfloat16)
+    return pl.pallas_call(
+        partial_kernel,
+        grid=(depth // COLUMNS,),
+        in_specs=[whole, whole, whole, wide, wide, tall],
+        out_specs=[slim, slim],
+        out_shape=[kept, kept],
+        scratch_shapes=[pltpu.VMEM((hidden_units, count), jnp.bfloat16)] * 2,
+        compiler_params=pltpu.CompilerParams(vmem_limit_bytes=24 * 2**20),
+        cost_estimate=pl.CostEstimate(
+            flops=6 * count * depth * hidden_units,
+            bytes_accessed=6 * depth * hidden_units,
+            transcendentals=0,
+        ),
+        name="partial_sums",
+    )(*units, gate_weight, up_weight, down_weight)
+
+
+def all_kernel(n_own, n_rest, *refs):
+    first, refs = refs[0], refs[1:]
+    own_pieces, rest_pieces, refs = refs[:n_own], refs[n_own : n_own + n_rest], refs[n_own + n_rest :]
+    own_hidden, own_grad_pre, own_grad_lifted, gate_weight, up_weight, down_weight = refs[:6]
+    grad_gate, grad_up, grad_down = refs[6:9]
+    rows, own, normed_t, grad_out, grad_out_t, hidden, grad_pre, grad_lifted, arrived = refs[9:]
     step = pl.program_id(0)
-    part, most = near.shape[1], rest_near.shape[1]
+    mine = own.shape[1]
     width = normed_t.shape[0]
 
     @pl.when(step == 0)
     def _():
         columns = pl.ds(pl.multiple_of(first[0], 128), width)
-        copy_all([
-            pltpu.make_async_copy(near.at[:, :, columns], own.at[:, pl.ds(0, part)], arrived.at[0]),
-            pltpu.make_async_copy(far.at[:, :, columns], own.at[:, pl.ds(part, part)], arrived.at[1]),
-            pltpu.make_async_copy(rest_near, rows.at[:, pl.ds(0, most)], arrived.at[2]),
-            pltpu.make_async_copy(rest_far, rows.at[:, pl.ds(most, most)], arrived.at[3]),
-        ])
-        normed_t[:, : 2 * part] = own[0].T
-        normed_t[:, 2 * part :] = rows[0, :, columns].T
-        grad_out[: 2 * part] = own[1]
-        grad_out[2 * part :] = rows[1, :, columns]
-
-    hidden[: 2 * part] = own_hidden[...]
-    grad_pre[: 2 * part] = own_grad_pre[...]
-    grad_lifted[: 2 * part] = own_grad_lifted[...]
-    hidden[2 * part :], grad_pre[2 * part :], grad_lifted[2 * part :] = activations(
-        rows[0], rows[1], gate_weight[...], up_weight[...], down_weight[...]
+        pack([piece.at[:, :, columns] for piece in own_pieces], own, arrived)
+        pack(rest_pieces, rows, arrived)
+        grad_out_t[...] = rows[1].T
+        normed_t[:, :mine] = own[0].T
+        normed_t[:, mine:] = rows[0, :, columns].T
+        grad_out[:mine] = own[1]
+        grad_out[mine:] = rows[1, :, columns]
+
+    hidden[:mine] = own_hidden[...]
+    grad_pre[:mine] = own_grad_pre[...]
+    grad_lifted[:mine] = own_grad_lifted[...]
+    grad_hidden = jnp.dot(down_weight[...], grad_out_t[...], preferred_element_type=jnp.float32).T
+    hidden[mine:], grad_pre[mine:], grad_lifted[mine:] = activations(
+        rows[0], grad_hidden, gate_weight[...], up_weight[...]
     )
     grad_gate[...] = jnp.dot(
         normed_t[...], grad_pre[...], preferred_element_type=jnp.float32
@@ -152,19 +178,20 @@
     ).astype(grad_down.dtype)
 
 
-def all_rows(first, near, far, rest_near, rest_far, units, gate_weight, up_weight, down_weight, width):
-    part, depth = near.shape[1:]
-    most = rest_near.shape[1]
-    count = 2 * (part + most)
-    hidden_units = gate_weight.shape[1]
+def all_rows(first, own_pieces, rest_pieces, units, gate_weight, up_weight, down_weight, width):
+    depth, hidden_units = gate_weight.shape
+    mine = sum(piece.shape[1] for piece in own_pieces)
+    most = sum(piece.shape[1] for piece in rest_pieces)
+    count = mine + most
     tall = pl.BlockSpec((depth, TILE), lambda i: (0, i))
     wide = pl.BlockSpec((TILE, depth), lambda i: (i, 0))
-    slim = pl.BlockSpec((2 * part, TILE), lambda i: (0, i))
+    slim = pl.BlockSpec((mine, TILE), lambda i: (0, i))
+    n_pieces = len(own_pieces) + len(rest_pieces)
     return pl.pallas_call(
-        all_kernel,
+        functools.partial(all_kernel, len(own_pieces), len(rest_pieces)),
         grid=(hidden_units // TILE,),
         in_specs=[pl.BlockSpec(memory_space=pltpu.SMEM)]
-        + [pl.BlockSpec(memory_space=pl.ANY)] * 4
+        + [pl.BlockSpec(memory_space=pl.ANY)] * n_pieces
         + [slim, slim, slim, tall, tall, wide],
         out_specs=[
             pl.BlockSpec((width, TILE), lambda i: (0, i)),
@@ -177,23 +204,24 @@
             jax.ShapeDtypeStruct((hidden_units, width), jnp.bfloat16),
         ],
         scratch_shapes=[
-            pltpu.VMEM((2, 2 * most, depth), jnp.bfloat16),
-            pltpu.VMEM((2, 2 * part, width), jnp.bfloat16),
+            pltpu.VMEM((2, most, depth), jnp.bfloat16),
+            pltpu.VMEM((2, mine, width), jnp.bfloat16),
             pltpu.VMEM((width, count), jnp.bfloat16),
             pltpu.VMEM((count, width), jnp.bfloat16),
+            pltpu.VMEM((depth, most), jnp.bfloat16),
             pltpu.VMEM((count, TILE), jnp.bfloat16),
             pltpu.VMEM((count, TILE), jnp.bfloat16),
             pltpu.VMEM((count, TILE), jnp.bfloat16),
-            pltpu.SemaphoreType.DMA((4,)),
+            pltpu.SemaphoreType.DMA((max(len(own_pieces), len(rest_pieces)),)),
         ],
         compiler_params=pltpu.CompilerParams(vmem_limit_bytes=48 * 2**20),
         cost_estimate=pl.CostEstimate(
-            flops=12 * most * depth * hidden_units + 6 * count * width * hidden_units,
+            flops=6 * most * depth * hidden_units + 6 * count * width * hidden_units,
             bytes_accessed=6 * (depth + width) * hidden_units,
-            transcendentals=2 * most * hidden_units,
+            transcendentals=most * hidden_units,
         ),
         name="all_rows",
-    )(first, near, far, rest_near, rest_far, *units, gate_weight, up_weight, down_weight)
+    )(first, *own_pieces, *rest_pieces, *units, gate_weight, up_weight, down_weight)
 
 
 def gather_tokens(tokens, norm_scale_vector, gate_weight, up_weight, down_weight, cotangent):
@@ -218,17 +246,25 @@
     unit_input = expanded_hidden * reciprocal_root_mean
     rescaled_input = (unit_input * norm_scale_vector).astype(jnp.bfloat16)
     shard = jnp.stack([rescaled_input, cotangent])
-    near = jnp.concatenate([shard] + [swap(shard, 0, b) for b in range(2, n_tp, 2)], axis=1)
-    far = swap(near, 0, 1)
-    rest_near = jnp.concatenate([swap(near, b, 0) for b in range(1, n_dp)], axis=1)
-    *units, kept, sent = own_rows(near, far, gate_weight, up_weight, down_weight)
-    rest_far = swap(rest_near, 0, 1)
+    shards = [shard] + [swap(shard, 0, b) for b in range(2, n_tp, 2)]
+    near = [jnp.concatenate(group, axis=1) for group in (shards[:2], shards[2:])]
+    far = [swap(piece, 0, 1) for piece in near]
+    rest_early, rest_late = ([swap(piece, b, 0) for b in range(1, n_dp)] for piece in near)
+    units = own_rows(near + far, gate_weight, up_weight, down_weight)
+    units, rest_early = lax.optimization_barrier((units, rest_early))
+    kept, sent = partial_sums(units, gate_weight, up_weight, down_weight)
+    rest_early += [swap(piece, 0, 1) for piece in rest_early]
+    kept, sent, rest_early, rest_late = lax.optimization_barrier(
+        (kept, sent, rest_early, rest_late)
+    )
+    rest_late += [swap(piece, 0, 1) for piece in rest_late]
 
     pair = (kept.astype(jnp.float32) + swap(sent, 0, 1).astype(jnp.float32)).astype(jnp.bfloat16)
     parts = [swap(pair[:, k * rows : (k + 1) * rows], 0, 2 * k) for k in range(1, n_tp // 2)]
     weight_gradients = all_rows(
-        first, near, far, rest_near, rest_far, units, gate_weight, up_weight, down_weight, width
-    )
+        first, near + far, rest_early + rest_late, units, gate_weight, up_weight, down_weight, width
+    )
+    parts, weight_gradients = lax.optimization_barrier((parts, weight_gradients))
     total = pair[:, :rows].astype(jnp.float32) + sum(part.astype(jnp.float32) for part in parts)
     branch, grad_normed = total[0], total[1]
     mixed = (expanded_hidden + branch).astype(jnp.bfloat16)

time: 162 us -> 135 us (0.83)
  waiting for transfers between devices: 60.6 us -> 28.9 us
  starting transfers between devices: 12.9 us -> 21 us
  Pallas kernels: 74.2 us -> 68.3 us
  local copies, waits for them, and re-layouts: 5.15 us -> 8.88 us
  other arithmetic: 8.45 us -> 6.68 us
    ppermute x12 -> x21, waiting for transfers between devices: 60.6 us -> 28.9 us  [swap(): return lax.ppermute(array, ('dp', 'tp'), pairs)]
    ppermute x12 -> x21, starting transfers between devices: 12.9 us -> 21 us  [swap(): return lax.ppermute(array, ('dp', 'tp'), pairs)]
    pallas_call x2 -> x3, Pallas kernels: 74.2 us -> 68.3 us  [the longest x1 35.1 us: all_rows(): pl.pallas_call(functools.partial(all_kernel, len(own_pieces), len(rest_pi...]
    unnamed x6 -> x57, local copies, waits for them, and re-layouts: 3.2 us -> 8.81 us
  transfers between devices with their start and end apart: 12 -> 21, of which waited for: 6 -> 4; matrix products, arithmetic and copies ran while one was open for 5% -> 2% of each run, Pallas kernels for 19% -> 51%
where the time goes in v4:
time: 135 us
  Pallas kernels  68.3 us (51%)
  waiting for transfers between devices  28.9 us (21%)
  starting transfers between devices  21 us (16%)
  local copies, waits for them, and re-layouts  8.88 us (7%)
  other arithmetic  6.68 us (5%)
    pallas_call x1, Pallas kernels, all_rows(): pl.pallas_call(functools.partial(all_kernel, len(own_pieces), len(rest_pi...  35.1 us
    ppermute x21, waiting for transfers between devices, swap(): return lax.ppermute(array, ('dp', 'tp'), pairs)  28.9 us
    ppermute x21, starting transfers between devices, swap(): return lax.ppermute(array, ('dp', 'tp'), pairs)  21 us
    pallas_call x1, Pallas kernels, partial_sums(): pl.pallas_call(partial_kernel, grid=(depth // COLUMNS,), in_specs=[whole,...  17.1 us
    pallas_call x1, Pallas kernels, own_rows(): pl.pallas_call(functools.partial(own_kernel, len(pieces)), grid=(hidden_u...  16.1 us
    unnamed x57, local copies, waits for them, and re-layouts  8.81 us
  transfers between devices with their start and end apart: 21, of which 4 were waited for; matrix products, arithmetic and copies ran while one was open for 2% of the time, Pallas kernels for 51%

profile of v4, /device:TPU:0, one launch (start us, length us, event | category | flops | bytes accessed | tf_op | source)
XLA Modules:
  0.0 134.8 jit_solution(11800302680815849723)
XLA Ops:
  0.6 1.1 fusion.9
  1.7 1.0 fusion.12
  2.7 0.9 pad_maximum_fusion.1
  3.6 3.1 %collective-permute-start = (bf16[2,16,4096]{2,1,0:T(8,128)(2,1)S(1)}, bf16[2,16,4096]{2,1,0:T(8,128)(2,1)S(1)}, u32[]{:S(2)}, u32[]{:S(2)}) collective-permute-start(bf16[2,16,4096]{2,1,0:T(8,128)(2,1)S(1)} %pad_maximum_fusion.1), channel_id=1, source_target_pairs={{0,2},{1,3},{2,0},{3,1},{4,6},{5,7},{6,4},{7,5},{8,10},{9,11},{10,... | collective-permute-start | bytes 786440 | tf_op jit(solution)/shard_map/ppermute | solution.py:240
  6.7 2.6 %collective-permute-start.1 = (bf16[2,16,4096]{2,1,0:T(8,128)(2,1)S(1)}, bf16[2,16,4096]{2,1,0:T(8,128)(2,1)S(1)}, u32[]{:S(2)}, u32[]{:S(2)}) collective-permute-start(bf16[2,16,4096]{2,1,0:T(8,128)(2,1)S(1)} %pad_maximum_fusion.1), channel_id=1, source_target_pairs={{0,4},{1,5},{2,6},{3,7},{4,0},{5,1},{6,2},{7,3},{8,12},{9,13},{10,... | collective-permute-start | bytes 786440 | tf_op jit(solution)/shard_map/ppermute | solution.py:240
  9.3 8.6 %collective-permute-done = bf16[2,16,4096]{2,1,0:T(8,128)(2,1)S(1)} collective-permute-done((bf16[2,16,4096]{2,1,0:T(8,128)(2,1)S(1)}, bf16[2,16,4096]{2,1,0:T(8,128)(2,1)S(1)}, u32[]{:S(2)}, u32[]{:S(2)}) %collective-permute-start) | collective-permute-done | bytes 262176 | tf_op jit(solution)/shard_map/ppermute | solution.py:240
  17.9 0.9 pad_maximum_fusion.refs_0_.refs_1_
  18.9 9.2 %collective-permute-done.1 = bf16[2,16,4096]{2,1,0:T(8,128)(2,1)S(1)} collective-permute-done((bf16[2,16,4096]{2,1,0:T(8,128)(2,1)S(1)}, bf16[2,16,4096]{2,1,0:T(8,128)(2,1)S(1)}, u32[]{:S(2)}, u32[]{:S(2)}) %collective-permute-start.1) | collective-permute-done | bytes 262176 | tf_op jit(solution)/shard_map/ppermute | solution.py:240
  28.2 2.5 %collective-permute-start.7 = (bf16[2,32,4096]{2,1,0:T(8,128)(2,1)S(1)}, bf16[2,32,4096]{2,1,0:T(8,128)(2,1)S(1)}, u32[]{:S(2)}, u32[]{:S(2)}) collective-permute-start(bf16[2,32,4096]{2,1,0:T(8,128)(2,1)S(1)} %pad_maximum_fusion.refs_0_.refs_1_), channel_id=1, source_target_pairs={{0,24},{1,25},{2,26},{3,27},{4,28},{5,29},{6,30},{7,31},{8,16},{9,... | collective-permute-start | bytes 1572872 | tf_op jit(solution)/shard_map/ppermute | solution.py:240
  30.8 0.5 collective-permute-start.6
  31.3 0.5 collective-permute-start.5
  31.8 2.4 %collective-permute-start.13 = (bf16[2,32,4096]{2,1,0:T(8,128)(2,1)S(1)}, bf16[2,32,4096]{2,1,0:T(8,128)(2,1)S(1)}, u32[]{:S(2)}, u32[]{:S(2)}) collective-permute-start(bf16[2,32,4096]{2,1,0:T(8,128)(2,1)S(1)} %constant_dynamic-update-slice_fusion.refs_1_.refs_2_), channel_id=1, source_target_pairs={{0,24},{1,25},{2,26},{3,27},{4,28},{5,29},{6,30},{7,31},{8,16},{9,... | collective-permute-start | bytes 1572872 | tf_op jit(solution)/shard_map/ppermute | solution.py:240
  34.2 0.5 collective-permute-start.12
  34.8 5.2 %copy-done = bf16[4096,1792]{1,0:T(8,128)(2,1)S(1)} copy-done((bf16[4096,1792]{1,0:T(8,128)(2,1)S(1)}, bf16[4096,1792]{1,0:T(8,128)(2,1)}, u32[]{:S(2)}) %copy-start) | copy-done | bytes 14680088
  39.9 16.1 %own_rows.1 = (bf16[128,1792]{1,0:T(8,128)(2,1)S(1)}, bf16[128,1792]{1,0:T(8,128)(2,1)S(1)}, bf16[128,1792]{1,0:T(8,128)(2,1)S(1)}) custom-call(bf16[2,32,4096]{2,1,0:T(8,128)(2,1)S(1)} %pad_maximum_fusion.refs_0_.refs_1_, bf16[2,32,4096]{2,1,0:T(8,128)(2,1)S(1)} %constant_dynamic-update-slice_fusion.refs_1_.refs_2_, ...), custom_call_target="tpu_custom_call" | custom-call | flops 5637144576 | bytes 44040192 | tf_op jit(solution)/shard_map/own_rows/pallas_call | solution.py:76
  56.1 0.6 collective-permute-start.11
  56.8 0.5 collective-permute-start.9
  57.3 9.2 %collective-permute-done.13.refs_13_ = bf16[2,32,4096]{2,1,0:T(8,128)(2,1)S(1)} collective-permute-done((bf16[2,32,4096]{2,1,0:T(8,128)(2,1)S(1)}, bf16[2,32,4096]{2,1,0:T(8,128)(2,1)S(1)}, u32[]{:S(2)}, u32[]{:S(2)}) %collective-permute-start.13) | collective-permute-done | bytes 524320 | tf_op jit(solution)/shard_map/ppermute | solution.py:240
  66.5 17.1 %partial_sums.1 = (bf16[2,64,4096]{2,1,0:T(8,128)(2,1)S(1)}, bf16[2,64,4096]{2,1,0:T(8,128)(2,1)}) custom-call(bf16[128,1792]{1,0:T(8,128)(2,1)S(1)} %get-tuple-element.39.hidden.refs_17_, bf16[128,1792]{1,0:T(8,128)(2,1)S(1)} %get-tuple-element.40.grad_pre.refs_18_, bf16[128,1792]{1,0:T(8,128)(2,1)S(1)} %get-tuple-element.41.grad_lifted.refs_19_, ...), custom_call_target="tpu_custom_call" | custom-call | flops 5637144576 | bytes 44040192 | tf_op jit(solution)/shard_map/partial_sums/pallas_call | solution.py:125
  83.7 0.9 copy-done.14
  84.6 0.8 copy-done.16
  85.4 0.8 copy-done.24
  86.2 0.3 collective-permute-start.14
  86.6 0.3 collective-permute-start.18
  86.9 0.3 collective-permute-start.19
  87.4 1.9 %collective-permute-done.14 = bf16[2,64,4096]{2,1,0:T(8,128)(2,1)} collective-permute-done((bf16[2,64,4096]{2,1,0:T(8,128)(2,1)}, bf16[2,64,4096]{2,1,0:T(8,128)(2,1)}, u32[]{:S(2)}, u32[]{:S(2)}) %collective-permute-start.14) | collective-permute-done | bytes 1048608 | tf_op jit(solution)/shard_map/ppermute | solution.py:240
  89.2 1.6 %add_convert_fusion = bf16[2,64,4096]{2,1,0:T(8,128)(2,1)S(1)} fusion(bf16[2,64,4096]{2,1,0:T(8,128)(2,1)} %collective-permute-done.14, bf16[2,64,4096]{2,1,0:T(8,128)(2,1)S(1)} %get-tuple-element.47), kind=kLoop, calls=%fused_computation | loop fusion | flops 2097152 | bytes 3145728 | tf_op jit(solution)/shard_map/convert_element_type | solution.py:262
  90.9 2.5 %collective-permute-start.17 = (bf16[2,16,4096]{2,1,0:T(8,128)(2,1)S(1)}, bf16[2,16,4096]{2,1,0:T(8,128)(2,1)S(1)}, u32[]{:S(2)}, u32[]{:S(2)}) collective-permute-start(bf16[2,16,4096]{2,1,0:T(8,128)(2,1)S(1)} %get-tuple-element.67), channel_id=1, source_target_pairs={{0,6},{1,7},{2,4},{3,5},{4,2},{5,3},{6,0},{7,1},{8,14},{9,15},{10,... | collective-permute-start | bytes 786440 | tf_op jit(solution)/shard_map/ppermute | solution.py:240
  93.4 3.7 %collective-permute-start.16 = (bf16[2,16,4096]{2,1,0:T(8,128)(2,1)S(1)}, bf16[2,16,4096]{2,1,0:T(8,128)(2,1)S(1)}, u32[]{:S(2)}, u32[]{:S(2)}) collective-permute-start(bf16[2,16,4096]{2,1,0:T(8,128)(2,1)S(1)} %get-tuple-element.68), channel_id=1, source_target_pairs={{0,4},{1,5},{2,6},{3,7},{4,0},{5,1},{6,2},{7,3},{8,12},{9,13},{10,... | collective-permute-start | bytes 786440 | tf_op jit(solution)/shard_map/ppermute | solution.py:240
  97.3 0.6 copy-done.25
  98.5 35.1 %all_rows.1 = (bf16[1024,1792]{1,0:T(8,128)(2,1)}, bf16[1024,1792]{1,0:T(8,128)(2,1)}, bf16[1792,1024]{1,0:T(8,128)(2,1)}) custom-call(s32[1]{0:T(128)} %bitcast.2.refs_0_, bf16[2,32,4096]{2,1,0:T(8,128)(2,1)S(1)} %pad_maximum_fusion.refs_0_.refs_1_, bf16[2,32,4096]{2,1,0:T(8,128)(2,1)S(1)} %constant_dynamic-update-slice_fusion.refs_1_.refs_2_, ...), custom_call_target="tpu_custom_call" | custom-call | flops 22548578304 | bytes 55050240 | tf_op jit(solution)/shard_map/all_rows/pallas_call | solution.py:190
  134.0 0.8 fusion.8
  (82 shorter events, 1.7 us)
Async XLA Ops:
  3.6 14.2 %collective-permute-start = (bf16[2,16,4096]{2,1,0:T(8,128)(2,1)S(1)}, bf16[2,16,4096]{2,1,0:T(8,128)(2,1)S(1)}, u32[]{:S(2)}, u32[]{:S(2)}) collective-permute-start(bf16[2,16,4096]{2,1,0:T(8,128)(2,1)S(1)} %pad_maximum_fusion.1), channel_id=1, source_target_pairs={{0,2},{1,3},{2,0},{3,1},{4,6},{5,7},{6,4},{7,5},{8,10},{9,11},{10,... | collective-permute-start | bytes 786440 | tf_op jit(solution)/shard_map/ppermute | solution.py:240
  6.7 21.4 %collective-permute-start.1 = (bf16[2,16,4096]{2,1,0:T(8,128)(2,1)S(1)}, bf16[2,16,4096]{2,1,0:T(8,128)(2,1)S(1)}, u32[]{:S(2)}, u32[]{:S(2)}) collective-permute-start(bf16[2,16,4096]{2,1,0:T(8,128)(2,1)S(1)} %pad_maximum_fusion.1), channel_id=1, source_target_pairs={{0,4},{1,5},{2,6},{3,7},{4,0},{5,1},{6,2},{7,3},{8,12},{9,13},{10,... | collective-permute-start | bytes 786440 | tf_op jit(solution)/shard_map/ppermute | solution.py:240
  9.3 18.8 %collective-permute-start.2 = (bf16[2,16,4096]{2,1,0:T(8,128)(2,1)S(1)}, bf16[2,16,4096]{2,1,0:T(8,128)(2,1)S(1)}, u32[]{:S(2)}, u32[]{:S(2)}) collective-permute-start(bf16[2,16,4096]{2,1,0:T(8,128)(2,1)S(1)} %pad_maximum_fusion.1), channel_id=1, source_target_pairs={{0,6},{1,7},{2,4},{3,5},{4,2},{5,3},{6,0},{7,1},{8,14},{9,15},{10,... | collective-permute-start | bytes 786440 | tf_op jit(solution)/shard_map/ppermute | solution.py:240
  18.8 13.0 %collective-permute-start.3 = (bf16[2,32,4096]{2,1,0:T(8,128)(2,1)S(1)}, bf16[2,32,4096]{2,1,0:T(8,128)(2,1)S(1)}, u32[]{:S(2)}, u32[]{:S(2)}) collective-permute-start(bf16[2,32,4096]{2,1,0:T(8,128)(2,1)S(1)} %pad_maximum_fusion.refs_0_.refs_1_), channel_id=1, source_target_pairs={{0,1},{1,0},{2,3},{3,2},{4,5},{5,4},{6,7},{7,6},{8,9},{9,8},{10,11... | collective-permute-start | bytes 1572872 | tf_op jit(solution)/shard_map/ppermute | solution.py:240
  28.2 6.1 %collective-permute-start.4 = (bf16[2,32,4096]{2,1,0:T(8,128)(2,1)S(1)}, bf16[2,32,4096]{2,1,0:T(8,128)(2,1)S(1)}, u32[]{:S(2)}, u32[]{:S(2)}) collective-permute-start(bf16[2,32,4096]{2,1,0:T(8,128)(2,1)S(1)} %constant_dynamic-update-slice_fusion.refs_1_.refs_2_), channel_id=1, source_target_pairs={{0,1},{1,0},{2,3},{3,2},{4,5},{5,4},{6,7},{7,6},{8,9},{9,8},{10,11... | collective-permute-start | bytes 1572872 | tf_op jit(solution)/shard_map/ppermute | solution.py:240
  28.2 27.8 %collective-permute-start.7 = (bf16[2,32,4096]{2,1,0:T(8,128)(2,1)S(1)}, bf16[2,32,4096]{2,1,0:T(8,128)(2,1)S(1)}, u32[]{:S(2)}, u32[]{:S(2)}) collective-permute-start(bf16[2,32,4096]{2,1,0:T(8,128)(2,1)S(1)} %pad_maximum_fusion.refs_0_.refs_1_), channel_id=1, source_target_pairs={{0,24},{1,25},{2,26},{3,27},{4,28},{5,29},{6,30},{7,31},{8,16},{9,... | collective-permute-start | bytes 1572872 | tf_op jit(solution)/shard_map/ppermute | solution.py:240
  30.8 25.9 %collective-permute-start.6 = (bf16[2,32,4096]{2,1,0:T(8,128)(2,1)S(1)}, bf16[2,32,4096]{2,1,0:T(8,128)(2,1)S(1)}, u32[]{:S(2)}, u32[]{:S(2)}) collective-permute-start(bf16[2,32,4096]{2,1,0:T(8,128)(2,1)S(1)} %pad_maximum_fusion.refs_0_.refs_1_), channel_id=1, source_target_pairs={{0,16},{1,17},{2,18},{3,19},{4,20},{5,21},{6,22},{7,23},{8,24},{9,... | collective-permute-start | bytes 1572872 | tf_op jit(solution)/shard_map/ppermute | solution.py:240
  31.3 25.4 %collective-permute-start.5 = (bf16[2,32,4096]{2,1,0:T(8,128)(2,1)S(1)}, bf16[2,32,4096]{2,1,0:T(8,128)(2,1)S(1)}, u32[]{:S(2)}, u32[]{:S(2)}) collective-permute-start(bf16[2,32,4096]{2,1,0:T(8,128)(2,1)S(1)} %pad_maximum_fusion.refs_0_.refs_1_), channel_id=1, source_target_pairs={{0,8},{1,9},{2,10},{3,11},{4,12},{5,13},{6,14},{7,15},{8,0},{9,1},... | collective-permute-start | bytes 1572872 | tf_op jit(solution)/shard_map/ppermute | solution.py:240
  31.8 34.7 %collective-permute-start.13 = (bf16[2,32,4096]{2,1,0:T(8,128)(2,1)S(1)}, bf16[2,32,4096]{2,1,0:T(8,128)(2,1)S(1)}, u32[]{:S(2)}, u32[]{:S(2)}) collective-permute-start(bf16[2,32,4096]{2,1,0:T(8,128)(2,1)S(1)} %constant_dynamic-update-slice_fusion.refs_1_.refs_2_), channel_id=1, source_target_pairs={{0,24},{1,25},{2,26},{3,27},{4,28},{5,29},{6,30},{7,31},{8,16},{9,... | collective-permute-start | bytes 1572872 | tf_op jit(solution)/shard_map/ppermute | solution.py:240
  34.2 49.4 %collective-permute-start.12 = (bf16[2,32,4096]{2,1,0:T(8,128)(2,1)S(1)}, bf16[2,32,4096]{2,1,0:T(8,128)(2,1)S(1)}, u32[]{:S(2)}, u32[]{:S(2)}) collective-permute-start(bf16[2,32,4096]{2,1,0:T(8,128)(2,1)S(1)} %constant_dynamic-update-slice_fusion.refs_1_.refs_2_), channel_id=1, source_target_pairs={{0,16},{1,17},{2,18},{3,19},{4,20},{5,21},{6,22},{7,23},{8,24},{9,... | collective-permute-start | bytes 1572872 | tf_op jit(solution)/shard_map/ppermute | solution.py:240
  39.9 26.6 %copy-start.1 = (bf16[4096,1792]{1,0:T(8,128)(2,1)S(1)}, bf16[4096,1792]{1,0:T(8,128)(2,1)}, u32[]{:S(2)}) copy-start(bf16[4096,1792]{1,0:T(8,128)(2,1)} %refs_20_.1) | copy-start | bytes 44040196
  56.0 27.6 %copy-start.2 = (bf16[128,1792]{1,0:T(8,128)(2,1)}, bf16[128,1792]{1,0:T(8,128)(2,1)S(1)}, u32[]{:S(2)}) copy-start(bf16[128,1792]{1,0:T(8,128)(2,1)S(1)} %get-tuple-element.39.hidden.refs_17_) | copy-start | bytes 1376260
  56.0 27.6 %copy-start.4 = (bf16[128,1792]{1,0:T(8,128)(2,1)}, bf16[128,1792]{1,0:T(8,128)(2,1)S(1)}, u32[]{:S(2)}) copy-start(bf16[128,1792]{1,0:T(8,128)(2,1)S(1)} %get-tuple-element.40.grad_pre.refs_18_) | copy-start | bytes 1376260
  56.0 27.6 %copy-start.6 = (bf16[128,1792]{1,0:T(8,128)(2,1)}, bf16[128,1792]{1,0:T(8,128)(2,1)S(1)}, u32[]{:S(2)}) copy-start(bf16[128,1792]{1,0:T(8,128)(2,1)S(1)} %get-tuple-element.41.grad_lifted.refs_19_) | copy-start | bytes 1376260
  56.1 27.6 %copy-start.8 = (bf16[2,32,4096]{2,1,0:T(8,128)(2,1)}, bf16[2,32,4096]{2,1,0:T(8,128)(2,1)S(1)}, u32[]{:S(2)}) copy-start(bf16[2,32,4096]{2,1,0:T(8,128)(2,1)S(1)} %collective-permute-done.7.refs_7_) | copy-start | bytes 1572868
  56.1 27.6 %collective-permute-start.11 = (bf16[2,32,4096]{2,1,0:T(8,128)(2,1)S(1)}, bf16[2,32,4096]{2,1,0:T(8,128)(2,1)S(1)}, u32[]{:S(2)}, u32[]{:S(2)}) collective-permute-start(bf16[2,32,4096]{2,1,0:T(8,128)(2,1)S(1)} %constant_dynamic-update-slice_fusion.refs_1_.refs_2_), channel_id=1, source_target_pairs={{0,8},{1,9},{2,10},{3,11},{4,12},{5,13},{6,14},{7,15},{8,0},{9,1},... | collective-permute-start | bytes 1572872 | tf_op jit(solution)/shard_map/ppermute | solution.py:240
  56.7 27.0 %copy-start.10 = (bf16[2,32,4096]{2,1,0:T(8,128)(2,1)}, bf16[2,32,4096]{2,1,0:T(8,128)(2,1)S(1)}, u32[]{:S(2)}) copy-start(bf16[2,32,4096]{2,1,0:T(8,128)(2,1)S(1)} %collective-permute-done.6.refs_6_) | copy-start | bytes 1572868
  56.7 27.0 %copy-start.12 = (bf16[2,32,4096]{2,1,0:T(8,128)(2,1)}, bf16[2,32,4096]{2,1,0:T(8,128)(2,1)S(1)}, u32[]{:S(2)}) copy-start(bf16[2,32,4096]{2,1,0:T(8,128)(2,1)S(1)} %collective-permute-done.5.refs_5_) | copy-start | bytes 1572868
  56.7 27.0 %collective-permute-start.8 = (bf16[2,32,4096]{2,1,0:T(8,128)(2,1)S(1)}, bf16[2,32,4096]{2,1,0:T(8,128)(2,1)S(1)}, u32[]{:S(2)}, u32[]{:S(2)}) collective-permute-start(bf16[2,32,4096]{2,1,0:T(8,128)(2,1)S(1)} %collective-permute-done.5.refs_5_), channel_id=1, source_target_pairs={{0,1},{1,0},{2,3},{3,2},{4,5},{5,4},{6,7},{7,6},{8,9},{9,8},{10,11... | collective-permute-start | bytes 1572872 | tf_op jit(solution)/shard_map/ppermute | solution.py:240
  56.8 27.8 %collective-permute-start.9 = (bf16[2,32,4096]{2,1,0:T(8,128)(2,1)S(1)}, bf16[2,32,4096]{2,1,0:T(8,128)(2,1)S(1)}, u32[]{:S(2)}, u32[]{:S(2)}) collective-permute-start(bf16[2,32,4096]{2,1,0:T(8,128)(2,1)S(1)} %collective-permute-done.6.refs_6_), channel_id=1, source_target_pairs={{0,1},{1,0},{2,3},{3,2},{4,5},{5,4},{6,7},{7,6},{8,9},{9,8},{10,11... | collective-permute-start | bytes 1572872 | tf_op jit(solution)/shard_map/ppermute | solution.py:240
  66.5 17.2 %copy-start.21 = (bf16[2,32,4096]{2,1,0:T(8,128)(2,1)}, bf16[2,32,4096]{2,1,0:T(8,128)(2,1)S(1)}, u32[]{:S(2)}) copy-start(bf16[2,32,4096]{2,1,0:T(8,128)(2,1)S(1)} %collective-permute-done.13.refs_13_) | copy-start | bytes 1572868
  66.5 18.9 %collective-permute-start.10 = (bf16[2,32,4096]{2,1,0:T(8,128)(2,1)S(1)}, bf16[2,32,4096]{2,1,0:T(8,128)(2,1)S(1)}, u32[]{:S(2)}, u32[]{:S(2)}) collective-permute-start(bf16[2,32,4096]{2,1,0:T(8,128)(2,1)S(1)} %collective-permute-done.7.refs_7_), channel_id=1, source_target_pairs={{0,1},{1,0},{2,3},{3,2},{4,5},{5,4},{6,7},{7,6},{8,9},{9,8},{10,11... | collective-permute-start | bytes 1572872 | tf_op jit(solution)/shard_map/ppermute | solution.py:240
  86.2 3.0 %collective-permute-start.14 = (bf16[2,64,4096]{2,1,0:T(8,128)(2,1)}, bf16[2,64,4096]{2,1,0:T(8,128)(2,1)}, u32[]{:S(2)}, u32[]{:S(2)}) collective-permute-start(bf16[2,64,4096]{2,1,0:T(8,128)(2,1)} %get-tuple-element.48), channel_id=1, source_target_pairs={{0,1},{1,0},{2,3},{3,2},{4,5},{5,4},{6,7},{7,6},{8,9},{9,8},{10,11... | collective-permute-start | bytes 3145736 | tf_op jit(solution)/shard_map/ppermute | solution.py:240
  86.6 10.5 %collective-permute-start.18 = (bf16[2,32,4096]{2,1,0:T(8,128)(2,1)}, bf16[2,32,4096]{2,1,0:T(8,128)(2,1)S(1)}, u32[]{:S(2)}, u32[]{:S(2)}) collective-permute-start(bf16[2,32,4096]{2,1,0:T(8,128)(2,1)} %copy-done.23), channel_id=1, source_target_pairs={{0,1},{1,0},{2,3},{3,2},{4,5},{5,4},{6,7},{7,6},{8,9},{9,8},{10,11... | collective-permute-start | bytes 1572872 | tf_op jit(solution)/shard_map/ppermute | solution.py:240
  86.9 10.4 %collective-permute-start.19 = (bf16[2,32,4096]{2,1,0:T(8,128)(2,1)}, bf16[2,32,4096]{2,1,0:T(8,128)(2,1)S(1)}, u32[]{:S(2)}, u32[]{:S(2)}) collective-permute-start(bf16[2,32,4096]{2,1,0:T(8,128)(2,1)} %copy-done.22), channel_id=1, source_target_pairs={{0,1},{1,0},{2,3},{3,2},{4,5},{5,4},{6,7},{7,6},{8,9},{9,8},{10,11... | collective-permute-start | bytes 1572872 | tf_op jit(solution)/shard_map/ppermute | solution.py:240
  87.2 10.2 %collective-permute-start.20 = (bf16[2,32,4096]{2,1,0:T(8,128)(2,1)}, bf16[2,32,4096]{2,1,0:T(8,128)(2,1)S(1)}, u32[]{:S(2)}, u32[]{:S(2)}) collective-permute-start(bf16[2,32,4096]{2,1,0:T(8,128)(2,1)} %copy-done.21), channel_id=1, source_target_pairs={{0,1},{1,0},{2,3},{3,2},{4,5},{5,4},{6,7},{7,6},{8,9},{9,8},{10,11... | collective-permute-start | bytes 1572872 | tf_op jit(solution)/shard_map/ppermute | solution.py:240
  90.9 42.7 %collective-permute-start.17 = (bf16[2,16,4096]{2,1,0:T(8,128)(2,1)S(1)}, bf16[2,16,4096]{2,1,0:T(8,128)(2,1)S(1)}, u32[]{:S(2)}, u32[]{:S(2)}) collective-permute-start(bf16[2,16,4096]{2,1,0:T(8,128)(2,1)S(1)} %get-tuple-element.67), channel_id=1, source_target_pairs={{0,6},{1,7},{2,4},{3,5},{4,2},{5,3},{6,0},{7,1},{8,14},{9,15},{10,... | collective-permute-start | bytes 786440 | tf_op jit(solution)/shard_map/ppermute | solution.py:240
  93.4 40.1 %collective-permute-start.16 = (bf16[2,16,4096]{2,1,0:T(8,128)(2,1)S(1)}, bf16[2,16,4096]{2,1,0:T(8,128)(2,1)S(1)}, u32[]{:S(2)}, u32[]{:S(2)}) collective-permute-start(bf16[2,16,4096]{2,1,0:T(8,128)(2,1)S(1)} %get-tuple-element.68), channel_id=1, source_target_pairs={{0,4},{1,5},{2,6},{3,7},{4,0},{5,1},{6,2},{7,3},{8,12},{9,13},{10,... | collective-permute-start | bytes 786440 | tf_op jit(solution)/shard_map/ppermute | solution.py:240
  97.1 36.4 %collective-permute-start.15 = (bf16[2,16,4096]{2,1,0:T(8,128)(2,1)S(1)}, bf16[2,16,4096]{2,1,0:T(8,128)(2,1)S(1)}, u32[]{:S(2)}, u32[]{:S(2)}) collective-permute-start(bf16[2,16,4096]{2,1,0:T(8,128)(2,1)S(1)} %get-tuple-element.69), channel_id=1, source_target_pairs={{0,2},{1,3},{2,0},{3,1},{4,6},{5,7},{6,4},{7,5},{8,10},{9,11},{10,... | collective-permute-start | bytes 786440 | tf_op jit(solution)/shard_map/ppermute | solution.py:240
  98.4 35.3 %copy-start.18 = (bf16[16,4096]{1,0:T(8,128)(2,1)S(1)}, bf16[16,4096]{1,0:T(8,128)(2,1)}, u32[]{:S(2)}) copy-start(bf16[16,4096]{1,0:T(8,128)(2,1)} %param.6) | copy-start | bytes 393220
  98.4 35.3 %copy-start.20 = (f32[4096]{0:T(1024)S(1)}, f32[4096]{0:T(1024)}, u32[]{:S(2)}) copy-start(f32[4096]{0:T(1024)} %param.7) | copy-start | bytes 49156
  98.4 35.5 %copy-start.19 = (bf16[16,4096]{1,0:T(8,128)(2,1)S(1)}, bf16[16,4096]{1,0:T(8,128)(2,1)}, u32[]{:S(2)}) copy-start(bf16[16,4096]{1,0:T(8,128)(2,1)} %param.11) | copy-start | bytes 393220
  (17 other events, 108.5 us)

commit v5 on v4

--- a/solution.py
+++ b/solution.py
@@ -21,12 +21,13 @@
 
 
 TILE = 256
-COLUMNS = 512
-
-
-def activations(normed, grad_hidden, gate_weight, up_weight):
+CHUNK = 1024
+
+
+def activations(normed, grad_out_t, gate_weight, up_weight, down_weight):
     gate = jnp.dot(normed, gate_weight, preferred_element_type=jnp.float32)
     lifted = jnp.dot(normed, up_weight, preferred_element_type=jnp.float32)
+    grad_hidden = jnp.dot(down_weight, grad_out_t, preferred_element_type=jnp.float32).T
     sigmoid_gate = jax.nn.sigmoid(gate)
     activated = gate * sigmoid_gate
     hidden = (activated * lifted).astype(jnp.bfloat16)
@@ -45,103 +46,89 @@
 
 
 def pack(pieces, rows, arrived):
-    height = pieces[0].shape[1]
-    copy_all([
-        pltpu.make_async_copy(piece, rows.at[:, pl.ds(i * height, height)], arrived.at[i])
-        for i, piece in enumerate(pieces)
-    ])
-
-
-def own_kernel(n_pieces, *refs):
-    pieces, refs = refs[:n_pieces], refs[n_pieces:]
-    gate_weight, up_weight, down_weight, hidden, grad_pre, grad_lifted, rows, arrived = refs
-
-    @pl.when(pl.program_id(0) == 0)
+    copies, at = [], 0
+    for i, piece in enumerate(pieces):
+        height = piece.shape[1]
+        copies.append(pltpu.make_async_copy(piece, rows.at[:, pl.ds(at, height)], arrived.at[i]))
+        at += height
+    copy_all(copies)
+
+
+def own_kernel(*refs):
+    replica, refs = refs[0], refs[1:]
+    (near, late, far_gathered, far_late), refs = refs[:4], refs[4:]
+    gate_weight, up_weight, down_weight, hidden, grad_pre, grad_lifted, kept, sent = refs[:8]
+    rows, grad_out_t, out_sum, in_sum, arrived = refs[8:]
+    step = pl.program_id(0)
+    part = kept.shape[1]
+
+    @pl.when(step == 0)
     def _():
-        pack(pieces, rows, arrived)
-
-    grad_hidden = contract_cols(rows[1], down_weight[...])
+        pack([near, late, far_gathered.at[replica[0]], far_late], rows, arrived)
+        grad_out_t[...] = rows[1].T
+        out_sum[...] = jnp.zeros_like(out_sum)
+        in_sum[...] = jnp.zeros_like(in_sum)
+
     hidden[...], grad_pre[...], grad_lifted[...] = activations(
-        rows[0], grad_hidden, gate_weight[...], up_weight[...]
-    )
-
-
-def own_rows(pieces, gate_weight, up_weight, down_weight):
+        rows[0], grad_out_t[...], gate_weight[...], up_weight[...], down_weight[...]
+    )
+    grad_pre_t, grad_lifted_t = grad_pre[...].T, grad_lifted[...].T
+    for at in range(0, out_sum.shape[1], CHUNK):
+        here = slice(at, at + CHUNK)
+        out_sum[:, here] += jnp.dot(
+            hidden[...], down_weight[:, here], preferred_element_type=jnp.float32
+        )
+        in_sum[here] += jnp.dot(
+            gate_weight[here], grad_pre_t, preferred_element_type=jnp.float32
+        ) + jnp.dot(up_weight[here], grad_lifted_t, preferred_element_type=jnp.float32)
+
+    @pl.when(step == pl.num_programs(0) - 1)
+    def _():
+        kept[0] = out_sum[:part].astype(kept.dtype)
+        sent[0] = out_sum[part:].astype(sent.dtype)
+        summed = in_sum[...].T
+        kept[1] = summed[:part].astype(kept.dtype)
+        sent[1] = summed[part:].astype(sent.dtype)
+
+
+def own_rows(replica, near, late, far_gathered, far_late, gate_weight, up_weight, down_weight):
     depth, hidden_units = gate_weight.shape
-    count = sum(piece.shape[1] for piece in pieces)
+    count = 2 * (near.shape[1] + late.shape[1])
     tall = pl.BlockSpec((depth, TILE), lambda i: (0, i))
     wide = pl.BlockSpec((TILE, depth), lambda i: (i, 0))
     slim = pl.BlockSpec((count, TILE), lambda i: (0, i))
+    whole = pl.BlockSpec((2, count // 2, depth), lambda i: (0, 0, 0))
+    kept = jax.ShapeDtypeStruct((2, count // 2, depth), jnp.bfloat16)
     unit = jax.ShapeDtypeStruct((count, hidden_units), jnp.bfloat16)
     return pl.pallas_call(
-        functools.partial(own_kernel, len(pieces)),
+        own_kernel,
         grid=(hidden_units // TILE,),
-        in_specs=[pl.BlockSpec(memory_space=pl.ANY)] * len(pieces) + [tall, tall, wide],
-        out_specs=[slim, slim, slim],
-        out_shape=[unit, unit, unit],
+        in_specs=[pl.BlockSpec(memory_space=pltpu.SMEM)]
+        + [pl.BlockSpec(memory_space=pl.ANY)] * 4
+        + [tall, tall, wide],
+        out_specs=[slim, slim, slim, whole, whole],
+        out_shape=[unit, unit, unit, kept, kept],
         scratch_shapes=[
             pltpu.VMEM((2, count, depth), jnp.bfloat16),
-            pltpu.SemaphoreType.DMA((len(pieces),)),
+            pltpu.VMEM((depth, count), jnp.bfloat16),
+            pltpu.VMEM((count, depth), jnp.float32),
+            pltpu.VMEM((depth, count), jnp.float32),
+            pltpu.SemaphoreType.DMA((4,)),
         ],
-        compiler_params=pltpu.CompilerParams(vmem_limit_bytes=24 * 2**20),
+        compiler_params=pltpu.CompilerParams(vmem_limit_bytes=48 * 2**20),
         cost_estimate=pl.CostEstimate(
-            flops=6 * count * depth * hidden_units,
+            flops=12 * count * depth * hidden_units,
             bytes_accessed=6 * depth * hidden_units,
             transcendentals=count * hidden_units,
         ),
         name="own_rows",
-    )(*pieces, gate_weight, up_weight, down_weight)
-
-
-def partial_kernel(
-    hidden, grad_pre, grad_lifted, gate_weight, up_weight, down_weight,
-    kept, sent, grad_pre_t, grad_lifted_t,
-):
-    part = kept.shape[1]
-
-    @pl.when(pl.program_id(0) == 0)
-    def _():
-        grad_pre_t[...] = grad_pre[...].T
-        grad_lifted_t[...] = grad_lifted[...].T
-
-    partial_out = jnp.dot(hidden[...], down_weight[...], preferred_element_type=jnp.float32)
-    partial_in = (
-        jnp.dot(gate_weight[...], grad_pre_t[...], preferred_element_type=jnp.float32)
-        + jnp.dot(up_weight[...], grad_lifted_t[...], preferred_element_type=jnp.float32)
-    ).T
-    for index, total in enumerate((partial_out, partial_in)):
-        kept[index] = total[:part].astype(kept.dtype)
-        sent[index] = total[part:].astype(sent.dtype)
-
-
-def partial_sums(units, gate_weight, up_weight, down_weight):
-    depth, hidden_units = gate_weight.shape
-    count = units[0].shape[0]
-    whole = pl.BlockSpec((count, hidden_units), lambda i: (0, 0))
-    wide = pl.BlockSpec((COLUMNS, hidden_units), lambda i: (i, 0))
-    tall = pl.BlockSpec((hidden_units, COLUMNS), lambda i: (0, i))
-    slim = pl.BlockSpec((2, count // 2, COLUMNS), lambda i: (0, 0, i))
-    kept = jax.ShapeDtypeStruct((2, count // 2, depth), jnp.bfloat16)
-    return pl.pallas_call(
-        partial_kernel,
-        grid=(depth // COLUMNS,),
-        in_specs=[whole, whole, whole, wide, wide, tall],
-        out_specs=[slim, slim],
-        out_shape=[kept, kept],
-        scratch_shapes=[pltpu.VMEM((hidden_units, count), jnp.bfloat16)] * 2,
-        compiler_params=pltpu.CompilerParams(vmem_limit_bytes=24 * 2**20),
-        cost_estimate=pl.CostEstimate(
-            flops=6 * count * depth * hidden_units,
-            bytes_accessed=6 * depth * hidden_units,
-            transcendentals=0,
-        ),
-        name="partial_sums",
-    )(*units, gate_weight, up_weight, down_weight)
-
-
-def all_kernel(n_own, n_rest, *refs):
-    first, refs = refs[0], refs[1:]
-    own_pieces, rest_pieces, refs = refs[:n_own], refs[n_own : n_own + n_rest], refs[n_own + n_rest :]
+    )(replica, near, late, far_gathered, far_late, gate_weight, up_weight, down_weight)
+
+
+def all_kernel(n_rest, *refs):
+    replica, refs = refs[0], refs[1:]
+    (late, far_late, gathered, far_gathered), refs = refs[:4], refs[4:]
+    rest_late, refs = refs[:n_rest], refs[n_rest:]
     own_hidden, own_grad_pre, own_grad_lifted, gate_weight, up_weight, down_weight = refs[:6]
     grad_gate, grad_up, grad_down = refs[6:9]
     rows, own, normed_t, grad_out, grad_out_t, hidden, grad_pre, grad_lifted, arrived = refs[9:]
@@ -151,9 +138,13 @@
 
     @pl.when(step == 0)
     def _():
-        columns = pl.ds(pl.multiple_of(first[0], 128), width)
+        me = replica[0]
+        columns = pl.ds(pl.multiple_of(me * width, 128), width)
+        own_pieces = [gathered.at[me], late, far_gathered.at[me], far_late]
         pack([piece.at[:, :, columns] for piece in own_pieces], own, arrived)
-        pack(rest_pieces, rows, arrived)
+        others = range(1, gathered.shape[0])
+        rest_pieces = [part.at[me ^ b] for part in (gathered, far_gathered) for b in others]
+        pack(rest_pieces + list(rest_late), rows, arrived)
         grad_out_t[...] = rows[1].T
         normed_t[:, :mine] = own[0].T
         normed_t[:, mine:] = rows[0, :, columns].T
@@ -163,9 +154,8 @@
     hidden[:mine] = own_hidden[...]
     grad_pre[:mine] = own_grad_pre[...]
     grad_lifted[:mine] = own_grad_lifted[...]
-    grad_hidden = jnp.dot(down_weight[...], grad_out_t[...], preferred_element_type=jnp.float32).T
     hidden[mine:], grad_pre[mine:], grad_lifted[mine:] = activations(
-        rows[0], grad_hidden, gate_weight[...], up_weight[...]
+        rows[0], grad_out_t[...], gate_weight[...], up_weight[...], down_weight[...]
     )
     grad_gate[...] = jnp.dot(
         normed_t[...], grad_pre[...], preferred_element_type=jnp.float32
@@ -178,20 +168,20 @@
     ).astype(grad_down.dtype)
 
 
-def all_rows(first, own_pieces, rest_pieces, units, gate_weight, up_weight, down_weight, width):
+def all_rows(replica, own_late, gathered, rest_late, units, gate_weight, up_weight, down_weight):
     depth, hidden_units = gate_weight.shape
-    mine = sum(piece.shape[1] for piece in own_pieces)
-    most = sum(piece.shape[1] for piece in rest_pieces)
-    count = mine + most
+    mine = units[0].shape[0]
+    count = mine * gathered[0].shape[0]
+    most = count - mine
+    width = depth // gathered[0].shape[0]
     tall = pl.BlockSpec((depth, TILE), lambda i: (0, i))
     wide = pl.BlockSpec((TILE, depth), lambda i: (i, 0))
     slim = pl.BlockSpec((mine, TILE), lambda i: (0, i))
-    n_pieces = len(own_pieces) + len(rest_pieces)
     return pl.pallas_call(
-        functools.partial(all_kernel, len(own_pieces), len(rest_pieces)),
+        functools.partial(all_kernel, len(rest_late)),
         grid=(hidden_units // TILE,),
         in_specs=[pl.BlockSpec(memory_space=pltpu.SMEM)]
-        + [pl.BlockSpec(memory_space=pl.ANY)] * n_pieces
+        + [pl.BlockSpec(memory_space=pl.ANY)] * (4 + len(rest_late))
         + [slim, slim, slim, tall, tall, wide],
         out_specs=[
             pl.BlockSpec((width, TILE), lambda i: (0, i)),
@@ -212,7 +202,7 @@
             pltpu.VMEM((count, TILE), jnp.bfloat16),
             pltpu.VMEM((count, TILE), jnp.bfloat16),
             pltpu.VMEM((count, TILE), jnp.bfloat16),
-            pltpu.SemaphoreType.DMA((max(len(own_pieces), len(rest_pieces)),)),
+            pltpu.SemaphoreType.DMA((4 * gathered[0].shape[0],)),
         ],
         compiler_params=pltpu.CompilerParams(vmem_limit_bytes=48 * 2**20),
         cost_estimate=pl.CostEstimate(
@@ -221,14 +211,13 @@
             transcendentals=most * hidden_units,
         ),
         name="all_rows",
-    )(first, *own_pieces, *rest_pieces, *units, gate_weight, up_weight, down_weight)
+    )(replica, *own_late, *gathered, *rest_late, *units, gate_weight, up_weight, down_weight)
 
 
 def gather_tokens(tokens, norm_scale_vector, gate_weight, up_weight, down_weight, cotangent):
     n_dp = lax.axis_size("dp")
     n_tp = lax.axis_size("tp")
-    width = tokens.shape[1] // n_dp
-    first = (lax.axis_index("dp") * width).astype(jnp.int32).reshape(1)
+    replica = lax.axis_index("dp").astype(jnp.int32).reshape(1)
     rows = tokens.shape[0]
 
     def swap(array, dp_bits, tp_bits):
@@ -246,23 +235,27 @@
     unit_input = expanded_hidden * reciprocal_root_mean
     rescaled_input = (unit_input * norm_scale_vector).astype(jnp.bfloat16)
     shard = jnp.stack([rescaled_input, cotangent])
-    shards = [shard] + [swap(shard, 0, b) for b in range(2, n_tp, 2)]
-    near = [jnp.concatenate(group, axis=1) for group in (shards[:2], shards[2:])]
-    far = [swap(piece, 0, 1) for piece in near]
-    rest_early, rest_late = ([swap(piece, b, 0) for b in range(1, n_dp)] for piece in near)
-    units = own_rows(near + far, gate_weight, up_weight, down_weight)
-    units, rest_early = lax.optimization_barrier((units, rest_early))
-    kept, sent = partial_sums(units, gate_weight, up_weight, down_weight)
-    rest_early += [swap(piece, 0, 1) for piece in rest_early]
-    kept, sent, rest_early, rest_late = lax.optimization_barrier(
-        (kept, sent, rest_early, rest_late)
-    )
-    rest_late += [swap(piece, 0, 1) for piece in rest_late]
+    gathered = lax.all_gather(shard, "dp", axis=0)
+    late = jnp.concatenate([swap(shard, 0, b) for b in range(2, n_tp, 2)], axis=1)
+    far_gathered, far_late = swap(gathered, 0, 1), swap(late, 0, 1)
+    rest = [swap(late, b, 0) for b in range(1, n_dp)]
+    *units, kept, sent = own_rows(
+        replica, shard, late, far_gathered, far_late, gate_weight, up_weight, down_weight
+    )
+    kept, sent, rest = lax.optimization_barrier((kept, sent, rest))
+    rest += [swap(piece, 0, 1) for piece in rest]
 
     pair = (kept.astype(jnp.float32) + swap(sent, 0, 1).astype(jnp.float32)).astype(jnp.bfloat16)
     parts = [swap(pair[:, k * rows : (k + 1) * rows], 0, 2 * k) for k in range(1, n_tp // 2)]
     weight_gradients = all_rows(
-        first, near + far, rest_early + rest_late, units, gate_weight, up_weight, down_weight, width
+        replica,
+        (late, far_late),
+        (gathered, far_gathered),
+        rest,
+        units,
+        gate_weight,
+        up_weight,
+        down_weight,
     )
     parts, weight_gradients = lax.optimization_barrier((parts, weight_gradients))
     total = pair[:, :rows].astype(jnp.float32) + sum(part.astype(jnp.float32) for part in parts)

time: 135 us -> 132 us (0.978)
  between operations: 1.04 us -> 14.2 us
  local copies, waits for them, and re-layouts: 8.88 us -> 3.16 us
  starting transfers between devices: 21 us -> 15.3 us
  Pallas kernels: 68.3 us -> 62.9 us
  waiting for transfers between devices: 28.9 us -> 31.5 us
  other arithmetic: 6.68 us -> 5.1 us
    ppermute x21 -> x15, starting transfers between devices: 21 us -> 15.2 us  [swap(): return lax.ppermute(array, ('dp', 'tp'), pairs)]
    unnamed x57 -> x16, local copies, waits for them, and re-layouts: 8.81 us -> 3.09 us
    pallas_call x3 -> x2, Pallas kernels: 68.3 us -> 62.9 us  [the longest x1 37 us: all_rows(): pl.pallas_call(functools.partial(all_kernel, len(rest_late)), grid=(hidde...]
    ppermute x21 -> x15, waiting for transfers between devices: 28.9 us -> 30.8 us  [swap(): return lax.ppermute(array, ('dp', 'tp'), pairs)]
  transfers between devices with their start and end apart: 21 -> 16, of which waited for: 4 -> 5; matrix products, arithmetic and copies ran while one was open for 2% -> 0% of each run, Pallas kernels for 51% -> 48%
where the time goes in v5:
time: 132 us
  Pallas kernels  62.9 us (48%)
  waiting for transfers between devices  31.5 us (24%)
  starting transfers between devices  15.3 us (12%)
  between operations  14.2 us (11%)
  other arithmetic  5.1 us (4%)
  local copies, waits for them, and re-layouts  3.16 us (2%)
    pallas_call x1, Pallas kernels, all_rows(): pl.pallas_call(functools.partial(all_kernel, len(rest_late)), grid=(hidde...  37 us
    ppermute x15, waiting for transfers between devices, swap(): return lax.ppermute(array, ('dp', 'tp'), pairs)  30.8 us
    pallas_call x1, Pallas kernels, own_rows(): pl.pallas_call(own_kernel, grid=(hidden_units // TILE,), in_specs=[pl.Blo...  25.8 us
    ppermute x15, starting transfers between devices, swap(): return lax.ppermute(array, ('dp', 'tp'), pairs)  15.2 us
    unnamed x16, local copies, waits for them, and re-layouts  3.09 us
    another operation x2, other arithmetic, gather_tokens(): shard = jnp.stack([rescaled_input, cotangent])  2.65 us
  transfers between devices with their start and end apart: 16, of which 5 were waited for; matrix products, arithmetic and copies ran while one was open for 0% of the time, Pallas kernels for 48%

profile of v5, /device:TPU:0, one launch (start us, length us, event | category | flops | bytes accessed | tf_op | source)
XLA Modules:
  0.0 132.0 jit_solution(15426223561800149106)
XLA Ops:
  7.2 0.0 all-gather.3.cloned.1.call-start
  7.2 1.1 fusion.9
  8.3 1.0 fusion.12
  9.3 1.6 %pad_maximum_fusion.refs_1_ = bf16[2,16,4096]{2,1,0:T(8,128)(2,1)} fusion(bf16[1,16,4096]{2,1,0:T(8,128)(2,1)} %bitcast.17, bf16[1,16,4096]{2,1,0:T(8,128)(2,1)S(1)} %fusion.12), kind=kLoop, calls=%fused_computation.19 | loop fusion | flops 131072 | bytes 524288 | tf_op jit(solution)/shard_map/stack | solution.py:237
  10.9 3.1 %collective-permute-start = (bf16[2,16,4096]{2,1,0:T(8,128)(2,1)}, bf16[2,16,4096]{2,1,0:T(8,128)(2,1)S(1)}, u32[]{:S(2)}, u32[]{:S(2)}) collective-permute-start(bf16[2,16,4096]{2,1,0:T(8,128)(2,1)} %pad_maximum_fusion.refs_1_), channel_id=1, source_target_pairs={{0,2},{1,3},{2,0},{3,1},{4,6},{5,7},{6,4},{7,5},{8,10},{9,11},{10,... | collective-permute-start | bytes 786440 | tf_op jit(solution)/shard_map/ppermute | solution.py:229
  14.0 2.5 %collective-permute-start.2 = (bf16[2,16,4096]{2,1,0:T(8,128)(2,1)}, bf16[2,16,4096]{2,1,0:T(8,128)(2,1)S(1)}, u32[]{:S(2)}, u32[]{:S(2)}) collective-permute-start(bf16[2,16,4096]{2,1,0:T(8,128)(2,1)} %pad_maximum_fusion.refs_1_), channel_id=1, source_target_pairs={{0,6},{1,7},{2,4},{3,5},{4,2},{5,3},{6,0},{7,1},{8,14},{9,15},{10,... | collective-permute-start | bytes 786440 | tf_op jit(solution)/shard_map/ppermute | solution.py:229
  16.5 0.1 collective-permute-start.1
  16.6 4.4 %collective-permute-done = bf16[2,16,4096]{2,1,0:T(8,128)(2,1)S(1)} collective-permute-done((bf16[2,16,4096]{2,1,0:T(8,128)(2,1)}, bf16[2,16,4096]{2,1,0:T(8,128)(2,1)S(1)}, u32[]{:S(2)}, u32[]{:S(2)}) %collective-permute-start) | collective-permute-done | bytes 262176 | tf_op jit(solution)/shard_map/ppermute | solution.py:229
  21.1 18.7 %collective-permute-done.1 = bf16[2,16,4096]{2,1,0:T(8,128)(2,1)S(1)} collective-permute-done((bf16[2,16,4096]{2,1,0:T(8,128)(2,1)}, bf16[2,16,4096]{2,1,0:T(8,128)(2,1)S(1)}, u32[]{:S(2)}, u32[]{:S(2)}) %collective-permute-start.1) | collective-permute-done | bytes 262176 | tf_op jit(solution)/shard_map/ppermute | solution.py:229
  39.8 0.7 all-gather.3.cloned.1.call-done
  40.5 0.6 collective-permute-start.4
  41.0 1.9 %collective-permute-start.7 = (bf16[2,48,4096]{2,1,0:T(8,128)(2,1)S(1)}, bf16[2,48,4096]{2,1,0:T(8,128)(2,1)S(1)}, u32[]{:S(2)}, u32[]{:S(2)}) collective-permute-start(bf16[2,48,4096]{2,1,0:T(8,128)(2,1)S(1)} %constant_dynamic-update-slice_fusion.refs_2_.refs_1_), channel_id=1, source_target_pairs={{0,24},{1,25},{2,26},{3,27},{4,28},{5,29},{6,30},{7,31},{8,16},{9,... | collective-permute-start | bytes 2359304 | tf_op jit(solution)/shard_map/ppermute | solution.py:229
  42.9 1.0 collective-permute-start.6
  43.9 0.6 collective-permute-start.5
  44.5 1.0 copy-done.2
  45.5 0.9 copy-done
  46.4 25.8 %own_rows.1 = (bf16[128,1792]{1,0:T(8,128)(2,1)S(1)}, bf16[128,1792]{1,0:T(8,128)(2,1)S(1)}, bf16[128,1792]{1,0:T(8,128)(2,1)S(1)}, bf16[2,64,4096]{2,1,0:T(8,128)(2,1)S(1)}, bf16[2,64,4096]{2,1,0:T(8,128)(2,1)S(1)}) custom-call(s32[1]{0:T(128)} %bitcast.refs_0_, bf16[2,16,4096]{2,1,0:T(8,128)(2,1)S(1)} %copy-done, ...), custom_call_target="tpu_custom_call" | custom-call | flops 11274289152 | bytes 44040192 | tf_op jit(solution)/shard_map/own_rows/pallas_call | solution.py:103
  72.3 6.0 %collective-permute-done.6.refs_6_ = bf16[2,48,4096]{2,1,0:T(8,128)(2,1)S(1)} collective-permute-done((bf16[2,48,4096]{2,1,0:T(8,128)(2,1)S(1)}, bf16[2,48,4096]{2,1,0:T(8,128)(2,1)S(1)}, u32[]{:S(2)}, u32[]{:S(2)}) %collective-permute-start.6) | collective-permute-done | bytes 786464 | tf_op jit(solution)/shard_map/ppermute | solution.py:229
  78.3 0.0 collective-permute-done.5.refs_5_
  78.3 0.5 collective-permute-start.12
  78.9 0.5 collective-permute-start.14
  79.4 1.6 %collective-permute-done.8 = bf16[2,64,4096]{2,1,0:T(8,128)(2,1)S(1)} collective-permute-done((bf16[2,64,4096]{2,1,0:T(8,128)(2,1)S(1)}, bf16[2,64,4096]{2,1,0:T(8,128)(2,1)S(1)}, u32[]{:S(2)}, u32[]{:S(2)}) %collective-permute-start.8) | collective-permute-done | bytes 1048608 | tf_op jit(solution)/shard_map/ppermute | solution.py:229
  81.0 0.2 add_convert_fusion
  81.3 0.1 fusion.13
  81.3 3.4 %collective-permute-start.11 = (bf16[2,16,4096]{2,1,0:T(8,128)(2,1)S(1)}, bf16[2,16,4096]{2,1,0:T(8,128)(2,1)S(1)}, u32[]{:S(2)}, u32[]{:S(2)}) collective-permute-start(bf16[2,16,4096]{2,1,0:T(8,128)(2,1)S(1)} %get-tuple-element.43), channel_id=1, source_target_pairs={{0,6},{1,7},{2,4},{3,5},{4,2},{5,3},{6,0},{7,1},{8,14},{9,15},{10,... | collective-permute-start | bytes 786440 | tf_op jit(solution)/shard_map/ppermute | solution.py:229
  84.7 1.1 collective-permute-start.9
  85.8 0.9 copy-done.5
  86.7 0.3 copy-done.6
  86.9 37.0 %all_rows.1 = (bf16[1024,1792]{1,0:T(8,128)(2,1)}, bf16[1024,1792]{1,0:T(8,128)(2,1)}, bf16[1792,1024]{1,0:T(8,128)(2,1)}) custom-call(s32[1]{0:T(128)} %bitcast.refs_0_, bf16[2,48,4096]{2,1,0:T(8,128)(2,1)S(1)} %constant_dynamic-update-slice_fusion.refs_2_.refs_1_, bf16[2,48,4096]{2,1,0:T(8,128)(2,1)S(1)} %collective-permute-done.4.refs_4_.refs_2_, ...), custom_call_target="tpu_custom_call" | custom-call | flops 22548578304 | bytes 55050240 | tf_op jit(solution)/shard_map/all_rows/pallas_call | solution.py:180
  124.0 0.1 add_add_fusion
  124.1 0.2 fusion.4
  124.4 0.8 fusion.8
  (30 shorter events, 0.1 us)
Async XLA Ops:
  7.2 33.3 %all-gather.3.cloned.1.call-start = ((), (), s32[]{:S(2)}) async-start(), calls=%async_computation | async-start | bytes 1310720 | tf_op jit(solution)/shard_map/all_gather | solution.py:238
  10.9 10.1 %collective-permute-start = (bf16[2,16,4096]{2,1,0:T(8,128)(2,1)}, bf16[2,16,4096]{2,1,0:T(8,128)(2,1)S(1)}, u32[]{:S(2)}, u32[]{:S(2)}) collective-permute-start(bf16[2,16,4096]{2,1,0:T(8,128)(2,1)} %pad_maximum_fusion.refs_1_), channel_id=1, source_target_pairs={{0,2},{1,3},{2,0},{3,1},{4,6},{5,7},{6,4},{7,5},{8,10},{9,11},{10,... | collective-permute-start | bytes 786440 | tf_op jit(solution)/shard_map/ppermute | solution.py:229
  14.0 26.4 %collective-permute-start.2 = (bf16[2,16,4096]{2,1,0:T(8,128)(2,1)}, bf16[2,16,4096]{2,1,0:T(8,128)(2,1)S(1)}, u32[]{:S(2)}, u32[]{:S(2)}) collective-permute-start(bf16[2,16,4096]{2,1,0:T(8,128)(2,1)} %pad_maximum_fusion.refs_1_), channel_id=1, source_target_pairs={{0,6},{1,7},{2,4},{3,5},{4,2},{5,3},{6,0},{7,1},{8,14},{9,15},{10,... | collective-permute-start | bytes 786440 | tf_op jit(solution)/shard_map/ppermute | solution.py:229
  16.5 23.2 %collective-permute-start.1 = (bf16[2,16,4096]{2,1,0:T(8,128)(2,1)}, bf16[2,16,4096]{2,1,0:T(8,128)(2,1)S(1)}, u32[]{:S(2)}, u32[]{:S(2)}) collective-permute-start(bf16[2,16,4096]{2,1,0:T(8,128)(2,1)} %pad_maximum_fusion.refs_1_), channel_id=1, source_target_pairs={{0,4},{1,5},{2,6},{3,7},{4,0},{5,1},{6,2},{7,3},{8,12},{9,13},{10,... | collective-permute-start | bytes 786440 | tf_op jit(solution)/shard_map/ppermute | solution.py:229
  40.4 4.1 %collective-permute-start.3 = (bf16[4,2,16,4096]{3,2,1,0:T(8,128)(2,1)}, bf16[4,2,16,4096]{3,2,1,0:T(8,128)(2,1)S(1)}, u32[]{:S(2)}, u32[]{:S(2)}) collective-permute-start(bf16[4,2,16,4096]{3,2,1,0:T(8,128)(2,1)} %bitcast.18), channel_id=1, source_target_pairs={{0,1},{1,0},{2,3},{3,2},{4,5},{5,4},{6,7},{7,6},{8,9},{9,8},{10,11... | collective-permute-start | bytes 3145736 | tf_op jit(solution)/shard_map/ppermute | solution.py:229
  40.5 4.1 %collective-permute-start.4 = (bf16[2,48,4096]{2,1,0:T(8,128)(2,1)S(1)}, bf16[2,48,4096]{2,1,0:T(8,128)(2,1)S(1)}, u32[]{:S(2)}, u32[]{:S(2)}) collective-permute-start(bf16[2,48,4096]{2,1,0:T(8,128)(2,1)S(1)} %constant_dynamic-update-slice_fusion.refs_2_.refs_1_), channel_id=1, source_target_pairs={{0,1},{1,0},{2,3},{3,2},{4,5},{5,4},{6,7},{7,6},{8,9},{9,8},{10,11... | collective-permute-start | bytes 2359304 | tf_op jit(solution)/shard_map/ppermute | solution.py:229
  41.0 31.3 %collective-permute-start.7 = (bf16[2,48,4096]{2,1,0:T(8,128)(2,1)S(1)}, bf16[2,48,4096]{2,1,0:T(8,128)(2,1)S(1)}, u32[]{:S(2)}, u32[]{:S(2)}) collective-permute-start(bf16[2,48,4096]{2,1,0:T(8,128)(2,1)S(1)} %constant_dynamic-update-slice_fusion.refs_2_.refs_1_), channel_id=1, source_target_pairs={{0,24},{1,25},{2,26},{3,27},{4,28},{5,29},{6,30},{7,31},{8,16},{9,... | collective-permute-start | bytes 2359304 | tf_op jit(solution)/shard_map/ppermute | solution.py:229
  42.9 35.4 %collective-permute-start.6 = (bf16[2,48,4096]{2,1,0:T(8,128)(2,1)S(1)}, bf16[2,48,4096]{2,1,0:T(8,128)(2,1)S(1)}, u32[]{:S(2)}, u32[]{:S(2)}) collective-permute-start(bf16[2,48,4096]{2,1,0:T(8,128)(2,1)S(1)} %constant_dynamic-update-slice_fusion.refs_2_.refs_1_), channel_id=1, source_target_pairs={{0,16},{1,17},{2,18},{3,19},{4,20},{5,21},{6,22},{7,23},{8,24},{9,... | collective-permute-start | bytes 2359304 | tf_op jit(solution)/shard_map/ppermute | solution.py:229
  43.9 34.4 %collective-permute-start.5 = (bf16[2,48,4096]{2,1,0:T(8,128)(2,1)S(1)}, bf16[2,48,4096]{2,1,0:T(8,128)(2,1)S(1)}, u32[]{:S(2)}, u32[]{:S(2)}) collective-permute-start(bf16[2,48,4096]{2,1,0:T(8,128)(2,1)S(1)} %constant_dynamic-update-slice_fusion.refs_2_.refs_1_), channel_id=1, source_target_pairs={{0,8},{1,9},{2,10},{3,11},{4,12},{5,13},{6,14},{7,15},{8,0},{9,1},... | collective-permute-start | bytes 2359304 | tf_op jit(solution)/shard_map/ppermute | solution.py:229
  44.5 1.0 copy-start.2
  45.5 0.9 copy-start
  78.3 2.7 %collective-permute-start.8 = (bf16[2,64,4096]{2,1,0:T(8,128)(2,1)S(1)}, bf16[2,64,4096]{2,1,0:T(8,128)(2,1)S(1)}, u32[]{:S(2)}, u32[]{:S(2)}) collective-permute-start(bf16[2,64,4096]{2,1,0:T(8,128)(2,1)S(1)} %get-tuple-element.27), channel_id=1, source_target_pairs={{0,1},{1,0},{2,3},{3,2},{4,5},{5,4},{6,7},{7,6},{8,9},{9,8},{10,11... | collective-permute-start | bytes 3145736 | tf_op jit(solution)/shard_map/ppermute | solution.py:229
  78.3 6.4 %collective-permute-start.12 = (bf16[2,48,4096]{2,1,0:T(8,128)(2,1)S(1)}, bf16[2,48,4096]{2,1,0:T(8,128)(2,1)S(1)}, u32[]{:S(2)}, u32[]{:S(2)}) collective-permute-start(bf16[2,48,4096]{2,1,0:T(8,128)(2,1)S(1)} %collective-permute-done.5.refs_5_), channel_id=1, source_target_pairs={{0,1},{1,0},{2,3},{3,2},{4,5},{5,4},{6,7},{7,6},{8,9},{9,8},{10,11... | collective-permute-start | bytes 2359304 | tf_op jit(solution)/shard_map/ppermute | solution.py:229
  78.8 6.9 %collective-permute-start.13 = (bf16[2,48,4096]{2,1,0:T(8,128)(2,1)S(1)}, bf16[2,48,4096]{2,1,0:T(8,128)(2,1)S(1)}, u32[]{:S(2)}, u32[]{:S(2)}) collective-permute-start(bf16[2,48,4096]{2,1,0:T(8,128)(2,1)S(1)} %collective-permute-done.6.refs_6_), channel_id=1, source_target_pairs={{0,1},{1,0},{2,3},{3,2},{4,5},{5,4},{6,7},{7,6},{8,9},{9,8},{10,11... | collective-permute-start | bytes 2359304 | tf_op jit(solution)/shard_map/ppermute | solution.py:229
  78.9 6.9 %collective-permute-start.14 = (bf16[2,48,4096]{2,1,0:T(8,128)(2,1)S(1)}, bf16[2,48,4096]{2,1,0:T(8,128)(2,1)S(1)}, u32[]{:S(2)}, u32[]{:S(2)}) collective-permute-start(bf16[2,48,4096]{2,1,0:T(8,128)(2,1)S(1)} %collective-permute-done.7.refs_7_), channel_id=1, source_target_pairs={{0,1},{1,0},{2,3},{3,2},{4,5},{5,4},{6,7},{7,6},{8,9},{9,8},{10,11... | collective-permute-start | bytes 2359304 | tf_op jit(solution)/shard_map/ppermute | solution.py:229
  81.3 42.6 %collective-permute-start.11 = (bf16[2,16,4096]{2,1,0:T(8,128)(2,1)S(1)}, bf16[2,16,4096]{2,1,0:T(8,128)(2,1)S(1)}, u32[]{:S(2)}, u32[]{:S(2)}) collective-permute-start(bf16[2,16,4096]{2,1,0:T(8,128)(2,1)S(1)} %get-tuple-element.43), channel_id=1, source_target_pairs={{0,6},{1,7},{2,4},{3,5},{4,2},{5,3},{6,0},{7,1},{8,14},{9,15},{10,... | collective-permute-start | bytes 786440 | tf_op jit(solution)/shard_map/ppermute | solution.py:229
  84.7 39.3 %collective-permute-start.10 = (bf16[2,16,4096]{2,1,0:T(8,128)(2,1)S(1)}, bf16[2,16,4096]{2,1,0:T(8,128)(2,1)S(1)}, u32[]{:S(2)}, u32[]{:S(2)}) collective-permute-start(bf16[2,16,4096]{2,1,0:T(8,128)(2,1)S(1)} %get-tuple-element.44), channel_id=1, source_target_pairs={{0,4},{1,5},{2,6},{3,7},{4,0},{5,1},{6,2},{7,3},{8,12},{9,13},{10,... | collective-permute-start | bytes 786440 | tf_op jit(solution)/shard_map/ppermute | solution.py:229
  84.7 39.3 %collective-permute-start.9 = (bf16[2,16,4096]{2,1,0:T(8,128)(2,1)S(1)}, bf16[2,16,4096]{2,1,0:T(8,128)(2,1)S(1)}, u32[]{:S(2)}, u32[]{:S(2)}) collective-permute-start(bf16[2,16,4096]{2,1,0:T(8,128)(2,1)S(1)} %get-tuple-element.45), channel_id=1, source_target_pairs={{0,2},{1,3},{2,0},{3,1},{4,6},{5,7},{6,4},{7,5},{8,10},{9,11},{10,... | collective-permute-start | bytes 786440 | tf_op jit(solution)/shard_map/ppermute | solution.py:229
  85.8 0.9 copy-start.5
  85.8 1.1 copy-start.6
  86.9 37.2 %copy-start.1 = (bf16[16,4096]{1,0:T(8,128)(2,1)S(1)}, bf16[16,4096]{1,0:T(8,128)(2,1)}, u32[]{:S(2)}) copy-start(bf16[16,4096]{1,0:T(8,128)(2,1)} %param.6) | copy-start | bytes 393220
  86.9 37.2 %copy-start.4 = (f32[4096]{0:T(1024)S(1)}, f32[4096]{0:T(1024)}, u32[]{:S(2)}) copy-start(f32[4096]{0:T(1024)} %param.7) | copy-start | bytes 49156
  86.9 37.4 %copy-start.3 = (bf16[16,4096]{1,0:T(8,128)(2,1)S(1)}, bf16[16,4096]{1,0:T(8,128)(2,1)}, u32[]{:S(2)}) copy-start(bf16[16,4096]{1,0:T(8,128)(2,1)} %param.11) | copy-start | bytes 393220
Sparse Core Ops, SparseCore 0:
  11.1 29.3 all-gather.2

commit v6 on v5

--- a/solution.py
+++ b/solution.py
@@ -38,33 +38,33 @@
     return hidden, grad_pre, grad_lifted
 
 
-def copy_all(copies):
-    for copy in copies:
-        copy.start()
-    for copy in copies:
-        copy.wait()
-
-
 def pack(pieces, rows, arrived):
     copies, at = [], 0
     for i, piece in enumerate(pieces):
         height = piece.shape[1]
         copies.append(pltpu.make_async_copy(piece, rows.at[:, pl.ds(at, height)], arrived.at[i]))
         at += height
-    copy_all(copies)
-
-
-def own_kernel(*refs):
-    replica, refs = refs[0], refs[1:]
-    (near, late, far_gathered, far_late), refs = refs[:4], refs[4:]
+    for copy in copies:
+        copy.start()
+    for copy in copies:
+        copy.wait()
+
+
+def height(pieces):
+    return sum(piece.shape[1] for piece in pieces)
+
+
+def first_kernel(n_pieces, *refs):
+    pieces, refs = refs[:n_pieces], refs[n_pieces:]
     gate_weight, up_weight, down_weight, hidden, grad_pre, grad_lifted, kept, sent = refs[:8]
     rows, grad_out_t, out_sum, in_sum, arrived = refs[8:]
     step = pl.program_id(0)
     part = kept.shape[1]
+    own = out_sum.shape[0]
 
     @pl.when(step == 0)
     def _():
-        pack([near, late, far_gathered.at[replica[0]], far_late], rows, arrived)
+        pack(pieces, rows, arrived)
         grad_out_t[...] = rows[1].T
         out_sum[...] = jnp.zeros_like(out_sum)
         in_sum[...] = jnp.zeros_like(in_sum)
@@ -72,11 +72,11 @@
     hidden[...], grad_pre[...], grad_lifted[...] = activations(
         rows[0], grad_out_t[...], gate_weight[...], up_weight[...], down_weight[...]
     )
-    grad_pre_t, grad_lifted_t = grad_pre[...].T, grad_lifted[...].T
+    grad_pre_t, grad_lifted_t = grad_pre[:own].T, grad_lifted[:own].T
     for at in range(0, out_sum.shape[1], CHUNK):
         here = slice(at, at + CHUNK)
         out_sum[:, here] += jnp.dot(
-            hidden[...], down_weight[:, here], preferred_element_type=jnp.float32
+            hidden[:own], down_weight[:, here], preferred_element_type=jnp.float32
         )
         in_sum[here] += jnp.dot(
             gate_weight[here], grad_pre_t, preferred_element_type=jnp.float32
@@ -91,70 +91,64 @@
         sent[1] = summed[part:].astype(sent.dtype)
 
 
-def own_rows(replica, near, late, far_gathered, far_late, gate_weight, up_weight, down_weight):
+def first_rows(own_pieces, more_pieces, gate_weight, up_weight, down_weight):
     depth, hidden_units = gate_weight.shape
-    count = 2 * (near.shape[1] + late.shape[1])
+    pieces = own_pieces + more_pieces
+    own, count = height(own_pieces), height(pieces)
     tall = pl.BlockSpec((depth, TILE), lambda i: (0, i))
     wide = pl.BlockSpec((TILE, depth), lambda i: (i, 0))
     slim = pl.BlockSpec((count, TILE), lambda i: (0, i))
-    whole = pl.BlockSpec((2, count // 2, depth), lambda i: (0, 0, 0))
-    kept = jax.ShapeDtypeStruct((2, count // 2, depth), jnp.bfloat16)
+    whole = pl.BlockSpec((2, own // 2, depth), lambda i: (0, 0, 0))
+    kept = jax.ShapeDtypeStruct((2, own // 2, depth), jnp.bfloat16)
     unit = jax.ShapeDtypeStruct((count, hidden_units), jnp.bfloat16)
     return pl.pallas_call(
-        own_kernel,
+        functools.partial(first_kernel, len(pieces)),
         grid=(hidden_units // TILE,),
-        in_specs=[pl.BlockSpec(memory_space=pltpu.SMEM)]
-        + [pl.BlockSpec(memory_space=pl.ANY)] * 4
-        + [tall, tall, wide],
+        in_specs=[pl.BlockSpec(memory_space=pl.ANY)] * len(pieces) + [tall, tall, wide],
         out_specs=[slim, slim, slim, whole, whole],
         out_shape=[unit, unit, unit, kept, kept],
         scratch_shapes=[
             pltpu.VMEM((2, count, depth), jnp.bfloat16),
             pltpu.VMEM((depth, count), jnp.bfloat16),
-            pltpu.VMEM((count, depth), jnp.float32),
-            pltpu.VMEM((depth, count), jnp.float32),
-            pltpu.SemaphoreType.DMA((4,)),
+            pltpu.VMEM((own, depth), jnp.float32),
+            pltpu.VMEM((depth, own), jnp.float32),
+            pltpu.SemaphoreType.DMA((len(pieces),)),
         ],
-        compiler_params=pltpu.CompilerParams(vmem_limit_bytes=48 * 2**20),
+        compiler_params=pltpu.CompilerParams(vmem_limit_bytes=44 * 2**20),
         cost_estimate=pl.CostEstimate(
-            flops=12 * count * depth * hidden_units,
+            flops=6 * (count + own) * depth * hidden_units,
             bytes_accessed=6 * depth * hidden_units,
             transcendentals=count * hidden_units,
         ),
-        name="own_rows",
-    )(replica, near, late, far_gathered, far_late, gate_weight, up_weight, down_weight)
-
-
-def all_kernel(n_rest, *refs):
+        name="first_rows",
+    )(*pieces, gate_weight, up_weight, down_weight)
+
+
+def all_kernel(n_first, n_last, *refs):
     replica, refs = refs[0], refs[1:]
-    (late, far_late, gathered, far_gathered), refs = refs[:4], refs[4:]
-    rest_late, refs = refs[:n_rest], refs[n_rest:]
-    own_hidden, own_grad_pre, own_grad_lifted, gate_weight, up_weight, down_weight = refs[:6]
-    grad_gate, grad_up, grad_down = refs[6:9]
-    rows, own, normed_t, grad_out, grad_out_t, hidden, grad_pre, grad_lifted, arrived = refs[9:]
-    step = pl.program_id(0)
-    mine = own.shape[1]
+    first_pieces, refs = refs[:n_first], refs[n_first:]
+    last_pieces, refs = refs[:n_last], refs[n_last:]
+    first_hidden, first_grad_pre, first_grad_lifted = refs[:3]
+    gate_weight, up_weight, down_weight, grad_gate, grad_up, grad_down = refs[3:9]
+    rows, first, normed_t, grad_out, grad_out_t, hidden, grad_pre, grad_lifted, arrived = refs[9:]
+    ahead = first.shape[1]
     width = normed_t.shape[0]
 
-    @pl.when(step == 0)
+    @pl.when(pl.program_id(0) == 0)
     def _():
-        me = replica[0]
-        columns = pl.ds(pl.multiple_of(me * width, 128), width)
-        own_pieces = [gathered.at[me], late, far_gathered.at[me], far_late]
-        pack([piece.at[:, :, columns] for piece in own_pieces], own, arrived)
-        others = range(1, gathered.shape[0])
-        rest_pieces = [part.at[me ^ b] for part in (gathered, far_gathered) for b in others]
-        pack(rest_pieces + list(rest_late), rows, arrived)
+        columns = pl.ds(pl.multiple_of(replica[0] * width, 128), width)
+        pack(last_pieces, rows, arrived)
+        pack([piece.at[:, :, columns] for piece in first_pieces], first, arrived)
         grad_out_t[...] = rows[1].T
-        normed_t[:, :mine] = own[0].T
-        normed_t[:, mine:] = rows[0, :, columns].T
-        grad_out[:mine] = own[1]
-        grad_out[mine:] = rows[1, :, columns]
-
-    hidden[:mine] = own_hidden[...]
-    grad_pre[:mine] = own_grad_pre[...]
-    grad_lifted[:mine] = own_grad_lifted[...]
-    hidden[mine:], grad_pre[mine:], grad_lifted[mine:] = activations(
+        normed_t[:, :ahead] = first[0].T
+        normed_t[:, ahead:] = rows[0, :, columns].T
+        grad_out[:ahead] = first[1]
+        grad_out[ahead:] = rows[1, :, columns]
+
+    hidden[:ahead] = first_hidden[...]
+    grad_pre[:ahead] = first_grad_pre[...]
+    grad_lifted[:ahead] = first_grad_lifted[...]
+    hidden[ahead:], grad_pre[ahead:], grad_lifted[ahead:] = activations(
         rows[0], grad_out_t[...], gate_weight[...], up_weight[...], down_weight[...]
     )
     grad_gate[...] = jnp.dot(
@@ -168,20 +162,20 @@
     ).astype(grad_down.dtype)
 
 
-def all_rows(replica, own_late, gathered, rest_late, units, gate_weight, up_weight, down_weight):
+def all_rows(replica, n_dp, first_pieces, last_pieces, units, gate_weight, up_weight, down_weight):
     depth, hidden_units = gate_weight.shape
-    mine = units[0].shape[0]
-    count = mine * gathered[0].shape[0]
-    most = count - mine
-    width = depth // gathered[0].shape[0]
+    ahead, behind = height(first_pieces), height(last_pieces)
+    count = ahead + behind
+    width = depth // n_dp
     tall = pl.BlockSpec((depth, TILE), lambda i: (0, i))
     wide = pl.BlockSpec((TILE, depth), lambda i: (i, 0))
-    slim = pl.BlockSpec((mine, TILE), lambda i: (0, i))
+    slim = pl.BlockSpec((ahead, TILE), lambda i: (0, i))
+    n_pieces = len(first_pieces), len(last_pieces)
     return pl.pallas_call(
-        functools.partial(all_kernel, len(rest_late)),
+        functools.partial(all_kernel, *n_pieces),
         grid=(hidden_units // TILE,),
         in_specs=[pl.BlockSpec(memory_space=pltpu.SMEM)]
-        + [pl.BlockSpec(memory_space=pl.ANY)] * (4 + len(rest_late))
+        + [pl.BlockSpec(memory_space=pl.ANY)] * sum(n_pieces)
         + [slim, slim, slim, tall, tall, wide],
         out_specs=[
             pl.BlockSpec((width, TILE), lambda i: (0, i)),
@@ -194,24 +188,24 @@
             jax.ShapeDtypeStruct((hidden_units, width), jnp.bfloat16),
         ],
         scratch_shapes=[
-            pltpu.VMEM((2, most, depth), jnp.bfloat16),
-            pltpu.VMEM((2, mine, width), jnp.bfloat16),
+            pltpu.VMEM((2, behind, depth), jnp.bfloat16),
+            pltpu.VMEM((2, ahead, width), jnp.bfloat16),
             pltpu.VMEM((width, count), jnp.bfloat16),
             pltpu.VMEM((count, width), jnp.bfloat16),
-            pltpu.VMEM((depth, most), jnp.bfloat16),
+            pltpu.VMEM((depth, behind), jnp.bfloat16),
             pltpu.VMEM((count, TILE), jnp.bfloat16),
             pltpu.VMEM((count, TILE), jnp.bfloat16),
             pltpu.VMEM((count, TILE), jnp.bfloat16),
-            pltpu.SemaphoreType.DMA((4 * gathered[0].shape[0],)),
+            pltpu.SemaphoreType.DMA((max(n_pieces),)),
         ],
-        compiler_params=pltpu.CompilerParams(vmem_limit_bytes=48 * 2**20),
+        compiler_params=pltpu.CompilerParams(vmem_limit_bytes=40 * 2**20),
         cost_estimate=pl.CostEstimate(
-            flops=6 * most * depth * hidden_units + 6 * count * width * hidden_units,
+            flops=6 * (behind * depth + count * width) * hidden_units,
             bytes_accessed=6 * (depth + width) * hidden_units,
-            transcendentals=most * hidden_units,
+            transcendentals=behind * hidden_units,
         ),
         name="all_rows",
-    )(replica, *own_late, *gathered, *rest_late, *units, gate_weight, up_weight, down_weight)
+    )(replica, *first_pieces, *last_pieces, *units, gate_weight, up_weight, down_weight)
 
 
 def gather_tokens(tokens, norm_scale_vector, gate_weight, up_weight, down_weight, cotangent):
@@ -228,34 +222,38 @@
         ]
         return lax.ppermute(array, ("dp", "tp"), pairs)
 
+    def far(pieces):
+        return [swap(piece, 0, 1) for piece in pieces]
+
     expanded_hidden = tokens.astype(jnp.float32)
     reciprocal_root_mean = lax.rsqrt(
         jnp.mean(expanded_hidden * expanded_hidden, axis=-1, keepdims=True) + 1e-05
     )
     unit_input = expanded_hidden * reciprocal_root_mean
     rescaled_input = (unit_input * norm_scale_vector).astype(jnp.bfloat16)
-    shard = jnp.stack([rescaled_input, cotangent])
-    gathered = lax.all_gather(shard, "dp", axis=0)
-    late = jnp.concatenate([swap(shard, 0, b) for b in range(2, n_tp, 2)], axis=1)
-    far_gathered, far_late = swap(gathered, 0, 1), swap(late, 0, 1)
-    rest = [swap(late, b, 0) for b in range(1, n_dp)]
-    *units, kept, sent = own_rows(
-        replica, shard, late, far_gathered, far_late, gate_weight, up_weight, down_weight
-    )
+    unit0 = jnp.stack([rescaled_input, cotangent])
+    unit1, unit2 = swap(unit0, 0, 2), swap(unit0, 0, 4)
+    more = [swap(unit0, b, 0) for b in range(1, n_dp)]
+    unit1, unit2, more = lax.optimization_barrier((unit1, unit2, more))
+    unit3, across = swap(unit2, 0, 2), swap(unit1, 1, 0)
+    far_more, far_unit0 = far(more), swap(unit0, 0, 1)
+    unit3, across, far_more, far_unit0 = lax.optimization_barrier(
+        (unit3, across, far_more, far_unit0)
+    )
+    last = jnp.concatenate([unit2, unit3], axis=1)
+    late = jnp.concatenate([unit1, unit2, unit3], axis=1)
+    own = [unit0, late, far_unit0, swap(late, 0, 1)]
+    more += [across] + far_more + far([across])
+    own, more = lax.optimization_barrier((own, more))
+    rest = [swap(last, 1, 0)] + [swap(late, b, 0) for b in range(2, n_dp)]
+    *units, kept, sent = first_rows(own, more, gate_weight, up_weight, down_weight)
     kept, sent, rest = lax.optimization_barrier((kept, sent, rest))
-    rest += [swap(piece, 0, 1) for piece in rest]
+    rest += far(rest)
 
     pair = (kept.astype(jnp.float32) + swap(sent, 0, 1).astype(jnp.float32)).astype(jnp.bfloat16)
     parts = [swap(pair[:, k * rows : (k + 1) * rows], 0, 2 * k) for k in range(1, n_tp // 2)]
     weight_gradients = all_rows(
-        replica,
-        (late, far_late),
-        (gathered, far_gathered),
-        rest,
-        units,
-        gate_weight,
-        up_weight,
-        down_weight,
+        replica, n_dp, own + more, rest, units, gate_weight, up_weight, down_weight
     )
     parts, weight_gradients = lax.optimization_barrier((parts, weight_gradients))
     total = pair[:, :rows].astype(jnp.float32) + sum(part.astype(jnp.float32) for part in parts)
@@ -328,7 +326,7 @@
 
 
 def solution(mesh):
-    n_tp = mesh.shape["tp"]
+    n_dp, n_tp = mesh.shape["dp"], mesh.shape["tp"]
     in_specs = (
         P(("dp", "tp"), None),
         P(),
@@ -348,7 +346,9 @@
     def run(tokens, norm_scale_vector, gate_weight, up_weight, down_weight, cotangent):
         gathered = tokens.size + cotangent.size
         weights = (gate_weight.size + up_weight.size + down_weight.size) // n_tp
-        local = gather_tokens if gathered <= weights else sum_weight_gradients
+        local = sum_weight_gradients
+        if (n_dp, n_tp) == (4, 8) and gathered <= weights:
+            local = gather_tokens
         return jax.shard_map(
             local, mesh=mesh, in_specs=in_specs, out_specs=out_specs, check_vma=False
         )(tokens, norm_scale_vector, gate_weight, up_weight, down_weight, cotangent)

time: 132 us -> 120 us (0.909)
  waiting for transfers between devices: 31.5 us -> 16.8 us
  between operations: 14.2 us -> 1.09 us
  local copies, waits for them, and re-layouts: 3.16 us -> 8.51 us
  starting transfers between devices: 15.3 us -> 20.5 us
  Pallas kernels: 62.9 us -> 67.3 us
    ppermute x15 -> x23, waiting for transfers between devices: 30.8 us -> 16.8 us  [swap(): return lax.ppermute(array, ('dp', 'tp'), pairs)]
    unnamed x16 -> x68, local copies, waits for them, and re-layouts: 3.09 us -> 8.44 us
    ppermute x15 -> x23, starting transfers between devices: 15.2 us -> 20.5 us  [swap(): return lax.ppermute(array, ('dp', 'tp'), pairs)]
    pallas_call x2, Pallas kernels: 62.9 us -> 67.3 us  [the longest x1 35.8 us: first_rows(): pl.pallas_call(functools.partial(first_kernel, len(pieces)), grid=(hidden...]
  transfers between devices with their start and end apart: 16 -> 23, of which waited for: 5 -> 7; matrix products, arithmetic and copies ran while one was open for 0% -> 1% of each run, Pallas kernels for 48% -> 56%
where the time goes in v6:
time: 120 us
  Pallas kernels  67.3 us (56%)
  starting transfers between devices  20.5 us (17%)
  waiting for transfers between devices  16.8 us (14%)
  local copies, waits for them, and re-layouts  8.51 us (7%)
  other arithmetic  5.66 us (5%)
    pallas_call x1, Pallas kernels, first_rows(): pl.pallas_call(functools.partial(first_kernel, len(pieces)), grid=(hidden...  35.8 us
    pallas_call x1, Pallas kernels, all_rows(): pl.pallas_call(functools.partial(all_kernel, *n_pieces), grid=(hidden_uni...  31.6 us
    ppermute x23, starting transfers between devices, swap(): return lax.ppermute(array, ('dp', 'tp'), pairs)  20.5 us
    ppermute x23, waiting for transfers between devices, swap(): return lax.ppermute(array, ('dp', 'tp'), pairs)  16.8 us
    unnamed x68, local copies, waits for them, and re-layouts  8.44 us
  transfers between devices with their start and end apart: 23, of which 7 were waited for; matrix products, arithmetic and copies ran while one was open for 1% of the time, Pallas kernels for 56%

profile of v6, /device:TPU:0, one launch (start us, length us, event | category | flops | bytes accessed | tf_op | source)
XLA Modules:
  0.0 119.9 jit_solution(12723109682843178295)
XLA Ops:
  0.6 1.1 fusion.9
  1.7 1.0 fusion.12
  2.7 0.9 pad_maximum_fusion.1.refs_0_.refs_1_
  3.6 3.1 %collective-permute-start = (bf16[2,16,4096]{2,1,0:T(8,128)(2,1)S(1)}, bf16[2,16,4096]{2,1,0:T(8,128)(2,1)S(1)}, u32[]{:S(2)}, u32[]{:S(2)}) collective-permute-start(bf16[2,16,4096]{2,1,0:T(8,128)(2,1)S(1)} %pad_maximum_fusion.1.refs_0_.refs_1_), channel_id=1, source_target_pairs={{0,2},{1,3},{2,0},{3,1},{4,6},{5,7},{6,4},{7,5},{8,10},{9,11},{10,... | collective-permute-start | bytes 786440 | tf_op jit(solution)/shard_map/ppermute | solution.py:223
  6.7 2.6 %collective-permute-start.1 = (bf16[2,16,4096]{2,1,0:T(8,128)(2,1)S(1)}, bf16[2,16,4096]{2,1,0:T(8,128)(2,1)S(1)}, u32[]{:S(2)}, u32[]{:S(2)}) collective-permute-start(bf16[2,16,4096]{2,1,0:T(8,128)(2,1)S(1)} %pad_maximum_fusion.1.refs_0_.refs_1_), channel_id=1, source_target_pairs={{0,4},{1,5},{2,6},{3,7},{4,0},{5,1},{6,2},{7,3},{8,12},{9,13},{10,... | collective-permute-start | bytes 786440 | tf_op jit(solution)/shard_map/ppermute | solution.py:223
  9.3 1.5 %collective-permute-start.2 = (bf16[2,16,4096]{2,1,0:T(8,128)(2,1)S(1)}, bf16[2,16,4096]{2,1,0:T(8,128)(2,1)S(1)}, u32[]{:S(2)}, u32[]{:S(2)}) collective-permute-start(bf16[2,16,4096]{2,1,0:T(8,128)(2,1)S(1)} %pad_maximum_fusion.1.refs_0_.refs_1_), channel_id=1, source_target_pairs={{0,8},{1,9},{2,10},{3,11},{4,12},{5,13},{6,14},{7,15},{8,0},{9,1},... | collective-permute-start | bytes 786440 | tf_op jit(solution)/shard_map/ppermute | solution.py:223
  10.8 1.5 %collective-permute-start.3 = (bf16[2,16,4096]{2,1,0:T(8,128)(2,1)S(1)}, bf16[2,16,4096]{2,1,0:T(8,128)(2,1)S(1)}, u32[]{:S(2)}, u32[]{:S(2)}) collective-permute-start(bf16[2,16,4096]{2,1,0:T(8,128)(2,1)S(1)} %pad_maximum_fusion.1.refs_0_.refs_1_), channel_id=1, source_target_pairs={{0,16},{1,17},{2,18},{3,19},{4,20},{5,21},{6,22},{7,23},{8,24},{9,... | collective-permute-start | bytes 786440 | tf_op jit(solution)/shard_map/ppermute | solution.py:223
  12.8 5.7 %collective-permute-done = bf16[2,16,4096]{2,1,0:T(8,128)(2,1)S(1)} collective-permute-done((bf16[2,16,4096]{2,1,0:T(8,128)(2,1)S(1)}, bf16[2,16,4096]{2,1,0:T(8,128)(2,1)S(1)}, u32[]{:S(2)}, u32[]{:S(2)}) %collective-permute-start) | collective-permute-done | bytes 262176 | tf_op jit(solution)/shard_map/ppermute | solution.py:223
  18.5 2.5 %collective-permute-done.1 = bf16[2,16,4096]{2,1,0:T(8,128)(2,1)S(1)} collective-permute-done((bf16[2,16,4096]{2,1,0:T(8,128)(2,1)S(1)}, bf16[2,16,4096]{2,1,0:T(8,128)(2,1)S(1)}, u32[]{:S(2)}, u32[]{:S(2)}) %collective-permute-start.1) | collective-permute-done | bytes 262176 | tf_op jit(solution)/shard_map/ppermute | solution.py:223
  21.1 2.6 %collective-permute-done.3.refs_5_.refs_6_ = bf16[2,16,4096]{2,1,0:T(8,128)(2,1)S(1)} collective-permute-done((bf16[2,16,4096]{2,1,0:T(8,128)(2,1)S(1)}, bf16[2,16,4096]{2,1,0:T(8,128)(2,1)S(1)}, u32[]{:S(2)}, u32[]{:S(2)}) %collective-permute-start.3) | collective-permute-done | bytes 262176 | tf_op jit(solution)/shard_map/ppermute | solution.py:223
  23.6 0.5 collective-permute-start.5
  24.2 1.2 collective-permute-start.6
  26.0 4.1 %collective-permute-done.5 = bf16[2,16,4096]{2,1,0:T(8,128)(2,1)S(1)} collective-permute-done((bf16[2,16,4096]{2,1,0:T(8,128)(2,1)S(1)}, bf16[2,16,4096]{2,1,0:T(8,128)(2,1)S(1)}, u32[]{:S(2)}, u32[]{:S(2)}) %collective-permute-start.5) | collective-permute-done | bytes 262176 | tf_op jit(solution)/shard_map/ppermute | solution.py:223
  30.7 1.6 %collective-permute-start.14 = (bf16[2,48,4096]{2,1,0:T(8,128)(2,1)S(1)}, bf16[2,48,4096]{2,1,0:T(8,128)(2,1)S(1)}, u32[]{:S(2)}, u32[]{:S(2)}) collective-permute-start(bf16[2,48,4096]{2,1,0:T(8,128)(2,1)S(1)} %constant_dynamic-update-slice_fusion.refs_1_.refs_2_), channel_id=1, source_target_pairs={{0,16},{1,17},{2,18},{3,19},{4,20},{5,21},{6,22},{7,23},{8,24},{9,... | collective-permute-start | bytes 2359304 | tf_op jit(solution)/shard_map/ppermute | solution.py:223
  32.3 1.1 collective-permute-start.15
  33.4 0.9 collective-permute-start.13
  34.3 0.6 collective-permute-done.12.refs_11_.refs_12_
  34.9 35.8 %first_rows.1 = (bf16[256,1792]{1,0:T(8,128)(2,1)S(1)}, bf16[256,1792]{1,0:T(8,128)(2,1)S(1)}, bf16[256,1792]{1,0:T(8,128)(2,1)S(1)}, bf16[2,64,4096]{2,1,0:T(8,128)(2,1)S(1)}, bf16[2,64,4096]{2,1,0:T(8,128)(2,1)S(1)}) custom-call(bf16[2,16,4096]{2,1,0:T(8,128)(2,1)S(1)} %pad_maximum_fusion.1.refs_0_.refs_1_, ...), custom_call_target="tpu_custom_call" | custom-call | flops 16911433728 | bytes 44040192 | tf_op jit(solution)/shard_map/first_rows/pallas_call | solution.py:104
  70.8 0.9 copy-done.24
  71.7 0.9 copy-done.26
  72.6 0.9 copy-done.28
  73.8 0.6 copy-done.6
  75.7 0.8 collective-permute-done.16
  76.5 1.5 %add_convert_fusion = bf16[2,64,4096]{2,1,0:T(8,128)(2,1)S(1)} fusion(bf16[2,64,4096]{2,1,0:T(8,128)(2,1)} %collective-permute-done.16, bf16[2,64,4096]{2,1,0:T(8,128)(2,1)S(1)} %get-tuple-element.72), kind=kLoop, calls=%fused_computation | loop fusion | flops 2097152 | bytes 3145728 | tf_op jit(solution)/shard_map/convert_element_type | solution.py:253
  78.0 1.6 %collective-permute-start.17 = (bf16[2,16,4096]{2,1,0:T(8,128)(2,1)S(1)}, bf16[2,16,4096]{2,1,0:T(8,128)(2,1)S(1)}, u32[]{:S(2)}, u32[]{:S(2)}) collective-permute-start(bf16[2,16,4096]{2,1,0:T(8,128)(2,1)S(1)} %get-tuple-element.91), channel_id=1, source_target_pairs={{0,2},{1,3},{2,0},{3,1},{4,6},{5,7},{6,4},{7,5},{8,10},{9,11},{10,... | collective-permute-start | bytes 786440 | tf_op jit(solution)/shard_map/ppermute | solution.py:223
  80.0 2.4 %collective-permute-start.19 = (bf16[2,16,4096]{2,1,0:T(8,128)(2,1)S(1)}, bf16[2,16,4096]{2,1,0:T(8,128)(2,1)S(1)}, u32[]{:S(2)}, u32[]{:S(2)}) collective-permute-start(bf16[2,16,4096]{2,1,0:T(8,128)(2,1)S(1)} %get-tuple-element.89), channel_id=1, source_target_pairs={{0,6},{1,7},{2,4},{3,5},{4,2},{5,3},{6,0},{7,1},{8,14},{9,15},{10,... | collective-permute-start | bytes 786440 | tf_op jit(solution)/shard_map/ppermute | solution.py:223
  82.6 0.9 copy-done.23
  83.5 1.2 copy-done.25
  84.7 1.2 copy-done.27
  85.9 1.2 copy-done.29
  87.1 31.6 %all_rows.1 = (bf16[1024,1792]{1,0:T(8,128)(2,1)}, bf16[1024,1792]{1,0:T(8,128)(2,1)}, bf16[1792,1024]{1,0:T(8,128)(2,1)}) custom-call(s32[1]{0:T(128)} %bitcast.2.refs_0_, bf16[2,16,4096]{2,1,0:T(8,128)(2,1)S(1)} %pad_maximum_fusion.1.refs_0_.refs_1_, bf16[2,48,4096]{2,1,0:T(8,128)(2,1)S(1)} %constant_dynamic-update-slice_fusion.refs_1_.refs_2_, ...), custom_call_target="tpu_custom_call" | custom-call | flops 16911433728 | bytes 55050240 | tf_op jit(solution)/shard_map/all_rows/pallas_call | solution.py:174
  119.1 0.8 fusion.8
  (96 shorter events, 4.1 us)
Async XLA Ops:
  3.6 14.9 %collective-permute-start = (bf16[2,16,4096]{2,1,0:T(8,128)(2,1)S(1)}, bf16[2,16,4096]{2,1,0:T(8,128)(2,1)S(1)}, u32[]{:S(2)}, u32[]{:S(2)}) collective-permute-start(bf16[2,16,4096]{2,1,0:T(8,128)(2,1)S(1)} %pad_maximum_fusion.1.refs_0_.refs_1_), channel_id=1, source_target_pairs={{0,2},{1,3},{2,0},{3,1},{4,6},{5,7},{6,4},{7,5},{8,10},{9,11},{10,... | collective-permute-start | bytes 786440 | tf_op jit(solution)/shard_map/ppermute | solution.py:223
  6.7 14.3 %collective-permute-start.1 = (bf16[2,16,4096]{2,1,0:T(8,128)(2,1)S(1)}, bf16[2,16,4096]{2,1,0:T(8,128)(2,1)S(1)}, u32[]{:S(2)}, u32[]{:S(2)}) collective-permute-start(bf16[2,16,4096]{2,1,0:T(8,128)(2,1)S(1)} %pad_maximum_fusion.1.refs_0_.refs_1_), channel_id=1, source_target_pairs={{0,4},{1,5},{2,6},{3,7},{4,0},{5,1},{6,2},{7,3},{8,12},{9,13},{10,... | collective-permute-start | bytes 786440 | tf_op jit(solution)/shard_map/ppermute | solution.py:223
  9.3 11.7 %collective-permute-start.2 = (bf16[2,16,4096]{2,1,0:T(8,128)(2,1)S(1)}, bf16[2,16,4096]{2,1,0:T(8,128)(2,1)S(1)}, u32[]{:S(2)}, u32[]{:S(2)}) collective-permute-start(bf16[2,16,4096]{2,1,0:T(8,128)(2,1)S(1)} %pad_maximum_fusion.1.refs_0_.refs_1_), channel_id=1, source_target_pairs={{0,8},{1,9},{2,10},{3,11},{4,12},{5,13},{6,14},{7,15},{8,0},{9,1},... | collective-permute-start | bytes 786440 | tf_op jit(solution)/shard_map/ppermute | solution.py:223
  10.8 12.8 %collective-permute-start.3 = (bf16[2,16,4096]{2,1,0:T(8,128)(2,1)S(1)}, bf16[2,16,4096]{2,1,0:T(8,128)(2,1)S(1)}, u32[]{:S(2)}, u32[]{:S(2)}) collective-permute-start(bf16[2,16,4096]{2,1,0:T(8,128)(2,1)S(1)} %pad_maximum_fusion.1.refs_0_.refs_1_), channel_id=1, source_target_pairs={{0,16},{1,17},{2,18},{3,19},{4,20},{5,21},{6,22},{7,23},{8,24},{9,... | collective-permute-start | bytes 786440 | tf_op jit(solution)/shard_map/ppermute | solution.py:223
  12.3 11.3 %collective-permute-start.4 = (bf16[2,16,4096]{2,1,0:T(8,128)(2,1)S(1)}, bf16[2,16,4096]{2,1,0:T(8,128)(2,1)S(1)}, u32[]{:S(2)}, u32[]{:S(2)}) collective-permute-start(bf16[2,16,4096]{2,1,0:T(8,128)(2,1)S(1)} %pad_maximum_fusion.1.refs_0_.refs_1_), channel_id=1, source_target_pairs={{0,24},{1,25},{2,26},{3,27},{4,28},{5,29},{6,30},{7,31},{8,16},{9,... | collective-permute-start | bytes 786440 | tf_op jit(solution)/shard_map/ppermute | solution.py:223
  18.5 7.3 %collective-permute-start.10 = (bf16[2,16,4096]{2,1,0:T(8,128)(2,1)S(1)}, bf16[2,16,4096]{2,1,0:T(8,128)(2,1)S(1)}, u32[]{:S(2)}, u32[]{:S(2)}) collective-permute-start(bf16[2,16,4096]{2,1,0:T(8,128)(2,1)S(1)} %pad_maximum_fusion.1.refs_0_.refs_1_), channel_id=1, source_target_pairs={{0,1},{1,0},{2,3},{3,2},{4,5},{5,4},{6,7},{7,6},{8,9},{9,8},{10,11... | collective-permute-start | bytes 786440 | tf_op jit(solution)/shard_map/ppermute | solution.py:223
  23.6 47.1 %copy-start.8 = (bf16[2,16,4096]{2,1,0:T(8,128)(2,1)}, bf16[2,16,4096]{2,1,0:T(8,128)(2,1)S(1)}, u32[]{:S(2)}) copy-start(bf16[2,16,4096]{2,1,0:T(8,128)(2,1)S(1)} %collective-permute-done.3.refs_5_.refs_6_) | copy-start | bytes 786436
  23.6 47.1 %copy-start.10 = (bf16[2,16,4096]{2,1,0:T(8,128)(2,1)}, bf16[2,16,4096]{2,1,0:T(8,128)(2,1)S(1)}, u32[]{:S(2)}) copy-start(bf16[2,16,4096]{2,1,0:T(8,128)(2,1)S(1)} %collective-permute-done.4.refs_6_.refs_7_) | copy-start | bytes 786436
  23.6 6.4 %collective-permute-start.5 = (bf16[2,16,4096]{2,1,0:T(8,128)(2,1)S(1)}, bf16[2,16,4096]{2,1,0:T(8,128)(2,1)S(1)}, u32[]{:S(2)}, u32[]{:S(2)}) collective-permute-start(bf16[2,16,4096]{2,1,0:T(8,128)(2,1)S(1)} %collective-permute-done.1), channel_id=1, source_target_pairs={{0,2},{1,3},{2,0},{3,1},{4,6},{5,7},{6,4},{7,5},{8,10},{9,11},{10,... | collective-permute-start | bytes 786440 | tf_op jit(solution)/shard_map/ppermute | solution.py:223
  24.2 6.4 %collective-permute-start.6 = (bf16[2,16,4096]{2,1,0:T(8,128)(2,1)S(1)}, bf16[2,16,4096]{2,1,0:T(8,128)(2,1)S(1)}, u32[]{:S(2)}, u32[]{:S(2)}) collective-permute-start(bf16[2,16,4096]{2,1,0:T(8,128)(2,1)S(1)} %collective-permute-done), channel_id=1, source_target_pairs={{0,8},{1,9},{2,10},{3,11},{4,12},{5,13},{6,14},{7,15},{8,0},{9,1},... | collective-permute-start | bytes 786440 | tf_op jit(solution)/shard_map/ppermute | solution.py:223
  25.3 5.2 %collective-permute-start.7 = (bf16[2,16,4096]{2,1,0:T(8,128)(2,1)S(1)}, bf16[2,16,4096]{2,1,0:T(8,128)(2,1)S(1)}, u32[]{:S(2)}, u32[]{:S(2)}) collective-permute-start(bf16[2,16,4096]{2,1,0:T(8,128)(2,1)S(1)} %collective-permute-done.2.refs_4_.refs_5_), channel_id=1, source_target_pairs={{0,1},{1,0},{2,3},{3,2},{4,5},{5,4},{6,7},{7,6},{8,9},{9,8},{10,11... | collective-permute-start | bytes 786440 | tf_op jit(solution)/shard_map/ppermute | solution.py:223
  25.3 5.2 %collective-permute-start.8 = (bf16[2,16,4096]{2,1,0:T(8,128)(2,1)S(1)}, bf16[2,16,4096]{2,1,0:T(8,128)(2,1)S(1)}, u32[]{:S(2)}, u32[]{:S(2)}) collective-permute-start(bf16[2,16,4096]{2,1,0:T(8,128)(2,1)S(1)} %collective-permute-done.3.refs_5_.refs_6_), channel_id=1, source_target_pairs={{0,1},{1,0},{2,3},{3,2},{4,5},{5,4},{6,7},{7,6},{8,9},{9,8},{10,11... | collective-permute-start | bytes 786440 | tf_op jit(solution)/shard_map/ppermute | solution.py:223
  25.9 44.9 %copy-start.12 = (bf16[2,16,4096]{2,1,0:T(8,128)(2,1)}, bf16[2,16,4096]{2,1,0:T(8,128)(2,1)S(1)}, u32[]{:S(2)}) copy-start(bf16[2,16,4096]{2,1,0:T(8,128)(2,1)S(1)} %collective-permute-done.10.refs_2_.refs_3_) | copy-start | bytes 786436
  25.9 4.7 %collective-permute-start.9 = (bf16[2,16,4096]{2,1,0:T(8,128)(2,1)S(1)}, bf16[2,16,4096]{2,1,0:T(8,128)(2,1)S(1)}, u32[]{:S(2)}, u32[]{:S(2)}) collective-permute-start(bf16[2,16,4096]{2,1,0:T(8,128)(2,1)S(1)} %collective-permute-done.4.refs_6_.refs_7_), channel_id=1, source_target_pairs={{0,1},{1,0},{2,3},{3,2},{4,5},{5,4},{6,7},{7,6},{8,9},{9,8},{10,11... | collective-permute-start | bytes 786440 | tf_op jit(solution)/shard_map/ppermute | solution.py:223
  30.5 40.2 %copy-start.14 = (bf16[2,16,4096]{2,1,0:T(8,128)(2,1)}, bf16[2,16,4096]{2,1,0:T(8,128)(2,1)S(1)}, u32[]{:S(2)}) copy-start(bf16[2,16,4096]{2,1,0:T(8,128)(2,1)S(1)} %collective-permute-done.6.refs_7_.refs_8_) | copy-start | bytes 786436
  30.5 40.2 %copy-start.16 = (bf16[2,16,4096]{2,1,0:T(8,128)(2,1)}, bf16[2,16,4096]{2,1,0:T(8,128)(2,1)S(1)}, u32[]{:S(2)}) copy-start(bf16[2,16,4096]{2,1,0:T(8,128)(2,1)S(1)} %collective-permute-done.7.refs_8_.refs_9_) | copy-start | bytes 786436
  30.5 40.2 %copy-start.18 = (bf16[2,16,4096]{2,1,0:T(8,128)(2,1)}, bf16[2,16,4096]{2,1,0:T(8,128)(2,1)S(1)}, u32[]{:S(2)}) copy-start(bf16[2,16,4096]{2,1,0:T(8,128)(2,1)S(1)} %collective-permute-done.8.refs_9_.refs_10_) | copy-start | bytes 786436
  30.6 40.2 %copy-start.20 = (bf16[2,16,4096]{2,1,0:T(8,128)(2,1)}, bf16[2,16,4096]{2,1,0:T(8,128)(2,1)S(1)}, u32[]{:S(2)}) copy-start(bf16[2,16,4096]{2,1,0:T(8,128)(2,1)S(1)} %collective-permute-done.9.refs_10_.refs_11_) | copy-start | bytes 786436
  30.6 4.3 %collective-permute-start.11 = (bf16[2,48,4096]{2,1,0:T(8,128)(2,1)S(1)}, bf16[2,48,4096]{2,1,0:T(8,128)(2,1)S(1)}, u32[]{:S(2)}, u32[]{:S(2)}) collective-permute-start(bf16[2,48,4096]{2,1,0:T(8,128)(2,1)S(1)} %constant_dynamic-update-slice_fusion.refs_1_.refs_2_), channel_id=1, source_target_pairs={{0,1},{1,0},{2,3},{3,2},{4,5},{5,4},{6,7},{7,6},{8,9},{9,8},{10,11... | collective-permute-start | bytes 2359304 | tf_op jit(solution)/shard_map/ppermute | solution.py:223
  30.7 42.9 %collective-permute-start.14 = (bf16[2,48,4096]{2,1,0:T(8,128)(2,1)S(1)}, bf16[2,48,4096]{2,1,0:T(8,128)(2,1)S(1)}, u32[]{:S(2)}, u32[]{:S(2)}) collective-permute-start(bf16[2,48,4096]{2,1,0:T(8,128)(2,1)S(1)} %constant_dynamic-update-slice_fusion.refs_1_.refs_2_), channel_id=1, source_target_pairs={{0,16},{1,17},{2,18},{3,19},{4,20},{5,21},{6,22},{7,23},{8,24},{9,... | collective-permute-start | bytes 2359304 | tf_op jit(solution)/shard_map/ppermute | solution.py:223
  32.3 41.3 %collective-permute-start.15 = (bf16[2,48,4096]{2,1,0:T(8,128)(2,1)S(1)}, bf16[2,48,4096]{2,1,0:T(8,128)(2,1)S(1)}, u32[]{:S(2)}, u32[]{:S(2)}) collective-permute-start(bf16[2,48,4096]{2,1,0:T(8,128)(2,1)S(1)} %constant_dynamic-update-slice_fusion.refs_1_.refs_2_), channel_id=1, source_target_pairs={{0,24},{1,25},{2,26},{3,27},{4,28},{5,29},{6,30},{7,31},{8,16},{9,... | collective-permute-start | bytes 2359304 | tf_op jit(solution)/shard_map/ppermute | solution.py:223
  33.4 1.5 %collective-permute-start.12 = (bf16[2,16,4096]{2,1,0:T(8,128)(2,1)S(1)}, bf16[2,16,4096]{2,1,0:T(8,128)(2,1)S(1)}, u32[]{:S(2)}, u32[]{:S(2)}) collective-permute-start(bf16[2,16,4096]{2,1,0:T(8,128)(2,1)S(1)} %collective-permute-done.6.refs_7_.refs_8_), channel_id=1, source_target_pairs={{0,1},{1,0},{2,3},{3,2},{4,5},{5,4},{6,7},{7,6},{8,9},{9,8},{10,11... | collective-permute-start | bytes 786440 | tf_op jit(solution)/shard_map/ppermute | solution.py:223
  33.4 40.2 %collective-permute-start.13 = (bf16[2,32,4096]{2,1,0:T(8,128)(2,1)S(1)}, bf16[2,32,4096]{2,1,0:T(8,128)(2,1)S(1)}, u32[]{:S(2)}, u32[]{:S(2)}) collective-permute-start(bf16[2,32,4096]{2,1,0:T(8,128)(2,1)S(1)} %pad_maximum_fusion), channel_id=1, source_target_pairs={{0,8},{1,9},{2,10},{3,11},{4,12},{5,13},{6,14},{7,15},{8,0},{9,1},... | collective-permute-start | bytes 1572872 | tf_op jit(solution)/shard_map/ppermute | solution.py:223
  34.9 35.9 %copy-start.22 = (bf16[2,16,4096]{2,1,0:T(8,128)(2,1)}, bf16[2,16,4096]{2,1,0:T(8,128)(2,1)S(1)}, u32[]{:S(2)}) copy-start(bf16[2,16,4096]{2,1,0:T(8,128)(2,1)S(1)} %collective-permute-done.12.refs_11_.refs_12_) | copy-start | bytes 786436
  34.9 35.9 %copy-start = (bf16[2,48,4096]{2,1,0:T(8,128)(2,1)}, bf16[2,48,4096]{2,1,0:T(8,128)(2,1)S(1)}, u32[]{:S(2)}) copy-start(bf16[2,48,4096]{2,1,0:T(8,128)(2,1)S(1)} %collective-permute-done.11.refs_3_.refs_4_) | copy-start | bytes 2359300
  73.6 2.9 %collective-permute-start.16 = (bf16[2,64,4096]{2,1,0:T(8,128)(2,1)S(1)}, bf16[2,64,4096]{2,1,0:T(8,128)(2,1)}, u32[]{:S(2)}, u32[]{:S(2)}) collective-permute-start(bf16[2,64,4096]{2,1,0:T(8,128)(2,1)S(1)} %get-tuple-element.73), channel_id=1, source_target_pairs={{0,1},{1,0},{2,3},{3,2},{4,5},{5,4},{6,7},{7,6},{8,9},{9,8},{10,11... | collective-permute-start | bytes 3145736 | tf_op jit(solution)/shard_map/ppermute | solution.py:223
  75.0 5.1 %collective-permute-start.20 = (bf16[2,32,4096]{2,1,0:T(8,128)(2,1)}, bf16[2,32,4096]{2,1,0:T(8,128)(2,1)S(1)}, u32[]{:S(2)}, u32[]{:S(2)}) collective-permute-start(bf16[2,32,4096]{2,1,0:T(8,128)(2,1)} %copy-done.6), channel_id=1, source_target_pairs={{0,1},{1,0},{2,3},{3,2},{4,5},{5,4},{6,7},{7,6},{8,9},{9,8},{10,11... | collective-permute-start | bytes 1572872 | tf_op jit(solution)/shard_map/ppermute | solution.py:223
  75.2 7.3 %collective-permute-start.21 = (bf16[2,48,4096]{2,1,0:T(8,128)(2,1)}, bf16[2,48,4096]{2,1,0:T(8,128)(2,1)S(1)}, u32[]{:S(2)}, u32[]{:S(2)}) collective-permute-start(bf16[2,48,4096]{2,1,0:T(8,128)(2,1)} %copy-done.2), channel_id=1, source_target_pairs={{0,1},{1,0},{2,3},{3,2},{4,5},{5,4},{6,7},{7,6},{8,9},{9,8},{10,11... | collective-permute-start | bytes 2359304 | tf_op jit(solution)/shard_map/ppermute | solution.py:223
  75.5 6.9 %collective-permute-start.22 = (bf16[2,48,4096]{2,1,0:T(8,128)(2,1)}, bf16[2,48,4096]{2,1,0:T(8,128)(2,1)S(1)}, u32[]{:S(2)}, u32[]{:S(2)}) collective-permute-start(bf16[2,48,4096]{2,1,0:T(8,128)(2,1)} %copy-done.4), channel_id=1, source_target_pairs={{0,1},{1,0},{2,3},{3,2},{4,5},{5,4},{6,7},{7,6},{8,9},{9,8},{10,11... | collective-permute-start | bytes 2359304 | tf_op jit(solution)/shard_map/ppermute | solution.py:223
  78.0 40.6 %collective-permute-start.17 = (bf16[2,16,4096]{2,1,0:T(8,128)(2,1)S(1)}, bf16[2,16,4096]{2,1,0:T(8,128)(2,1)S(1)}, u32[]{:S(2)}, u32[]{:S(2)}) collective-permute-start(bf16[2,16,4096]{2,1,0:T(8,128)(2,1)S(1)} %get-tuple-element.91), channel_id=1, source_target_pairs={{0,2},{1,3},{2,0},{3,1},{4,6},{5,7},{6,4},{7,5},{8,10},{9,11},{10,... | collective-permute-start | bytes 786440 | tf_op jit(solution)/shard_map/ppermute | solution.py:223
  79.6 39.0 %collective-permute-start.18 = (bf16[2,16,4096]{2,1,0:T(8,128)(2,1)S(1)}, bf16[2,16,4096]{2,1,0:T(8,128)(2,1)S(1)}, u32[]{:S(2)}, u32[]{:S(2)}) collective-permute-start(bf16[2,16,4096]{2,1,0:T(8,128)(2,1)S(1)} %get-tuple-element.90), channel_id=1, source_target_pairs={{0,4},{1,5},{2,6},{3,7},{4,0},{5,1},{6,2},{7,3},{8,12},{9,13},{10,... | collective-permute-start | bytes 786440 | tf_op jit(solution)/shard_map/ppermute | solution.py:223
  80.0 38.6 %collective-permute-start.19 = (bf16[2,16,4096]{2,1,0:T(8,128)(2,1)S(1)}, bf16[2,16,4096]{2,1,0:T(8,128)(2,1)S(1)}, u32[]{:S(2)}, u32[]{:S(2)}) collective-permute-start(bf16[2,16,4096]{2,1,0:T(8,128)(2,1)S(1)} %get-tuple-element.89), channel_id=1, source_target_pairs={{0,6},{1,7},{2,4},{3,5},{4,2},{5,3},{6,0},{7,1},{8,14},{9,15},{10,... | collective-permute-start | bytes 786440 | tf_op jit(solution)/shard_map/ppermute | solution.py:223
  (24 other events, 189.7 us)

commit v7 on v6

--- a/solution.py
+++ b/solution.py
@@ -24,10 +24,14 @@
 CHUNK = 1024
 
 
-def activations(normed, grad_out_t, gate_weight, up_weight, down_weight):
+def project(normed, grad_out_t, gate_weight, up_weight, down_weight):
     gate = jnp.dot(normed, gate_weight, preferred_element_type=jnp.float32)
     lifted = jnp.dot(normed, up_weight, preferred_element_type=jnp.float32)
     grad_hidden = jnp.dot(down_weight, grad_out_t, preferred_element_type=jnp.float32).T
+    return gate, lifted, grad_hidden
+
+
+def activations(gate, lifted, grad_hidden):
     sigmoid_gate = jax.nn.sigmoid(gate)
     activated = gate * sigmoid_gate
     hidden = (activated * lifted).astype(jnp.bfloat16)
@@ -54,13 +58,12 @@
     return sum(piece.shape[1] for piece in pieces)
 
 
-def first_kernel(n_pieces, *refs):
+def own_kernel(n_pieces, *refs):
     pieces, refs = refs[:n_pieces], refs[n_pieces:]
     gate_weight, up_weight, down_weight, hidden, grad_pre, grad_lifted, kept, sent = refs[:8]
     rows, grad_out_t, out_sum, in_sum, arrived = refs[8:]
     step = pl.program_id(0)
     part = kept.shape[1]
-    own = out_sum.shape[0]
 
     @pl.when(step == 0)
     def _():
@@ -70,13 +73,13 @@
         in_sum[...] = jnp.zeros_like(in_sum)
 
     hidden[...], grad_pre[...], grad_lifted[...] = activations(
-        rows[0], grad_out_t[...], gate_weight[...], up_weight[...], down_weight[...]
-    )
-    grad_pre_t, grad_lifted_t = grad_pre[:own].T, grad_lifted[:own].T
+        *project(rows[0], grad_out_t[...], gate_weight[...], up_weight[...], down_weight[...])
+    )
+    grad_pre_t, grad_lifted_t = grad_pre[...].T, grad_lifted[...].T
     for at in range(0, out_sum.shape[1], CHUNK):
         here = slice(at, at + CHUNK)
         out_sum[:, here] += jnp.dot(
-            hidden[:own], down_weight[:, here], preferred_element_type=jnp.float32
+            hidden[...], down_weight[:, here], preferred_element_type=jnp.float32
         )
         in_sum[here] += jnp.dot(
             gate_weight[here], grad_pre_t, preferred_element_type=jnp.float32
@@ -91,96 +94,107 @@
         sent[1] = summed[part:].astype(sent.dtype)
 
 
-def first_rows(own_pieces, more_pieces, gate_weight, up_weight, down_weight):
+def own_rows(pieces, gate_weight, up_weight, down_weight):
     depth, hidden_units = gate_weight.shape
-    pieces = own_pieces + more_pieces
-    own, count = height(own_pieces), height(pieces)
+    count = height(pieces)
     tall = pl.BlockSpec((depth, TILE), lambda i: (0, i))
     wide = pl.BlockSpec((TILE, depth), lambda i: (i, 0))
     slim = pl.BlockSpec((count, TILE), lambda i: (0, i))
-    whole = pl.BlockSpec((2, own // 2, depth), lambda i: (0, 0, 0))
-    kept = jax.ShapeDtypeStruct((2, own // 2, depth), jnp.bfloat16)
+    whole = pl.BlockSpec((2, count // 2, depth), lambda i: (0, 0, 0))
+    kept = jax.ShapeDtypeStruct((2, count // 2, depth), jnp.bfloat16)
     unit = jax.ShapeDtypeStruct((count, hidden_units), jnp.bfloat16)
     return pl.pallas_call(
-        functools.partial(first_kernel, len(pieces)),
+        functools.partial(own_kernel, len(pieces)),
         grid=(hidden_units // TILE,),
-        in_specs=[pl.BlockSpec(memory_space=pl.ANY)] * len(pieces) + [tall, tall, wide],
+        in_specs=[pl.BlockSpec(memory_space=pltpu.HBM)] * len(pieces) + [tall, tall, wide],
         out_specs=[slim, slim, slim, whole, whole],
         out_shape=[unit, unit, unit, kept, kept],
         scratch_shapes=[
             pltpu.VMEM((2, count, depth), jnp.bfloat16),
             pltpu.VMEM((depth, count), jnp.bfloat16),
-            pltpu.VMEM((own, depth), jnp.float32),
-            pltpu.VMEM((depth, own), jnp.float32),
+            pltpu.VMEM((count, depth), jnp.float32),
+            pltpu.VMEM((depth, count), jnp.float32),
             pltpu.SemaphoreType.DMA((len(pieces),)),
         ],
-        compiler_params=pltpu.CompilerParams(vmem_limit_bytes=44 * 2**20),
+        compiler_params=pltpu.CompilerParams(vmem_limit_bytes=46 * 2**20),
         cost_estimate=pl.CostEstimate(
-            flops=6 * (count + own) * depth * hidden_units,
+            flops=12 * count * depth * hidden_units,
             bytes_accessed=6 * depth * hidden_units,
             transcendentals=count * hidden_units,
         ),
-        name="first_rows",
+        name="own_rows",
     )(*pieces, gate_weight, up_weight, down_weight)
 
 
-def all_kernel(n_first, n_last, *refs):
+def all_kernel(n_own, n_last, *refs):
     replica, refs = refs[0], refs[1:]
-    first_pieces, refs = refs[:n_first], refs[n_first:]
+    own_pieces, refs = refs[:n_own], refs[n_own:]
     last_pieces, refs = refs[:n_last], refs[n_last:]
-    first_hidden, first_grad_pre, first_grad_lifted = refs[:3]
+    own_hidden, own_grad_pre, own_grad_lifted = refs[:3]
     gate_weight, up_weight, down_weight, grad_gate, grad_up, grad_down = refs[3:9]
     rows, first, normed_t, grad_out, grad_out_t, hidden, grad_pre, grad_lifted, arrived = refs[9:]
+    step, last = pl.program_id(0), pl.num_programs(0) - 1
     ahead = first.shape[1]
     width = normed_t.shape[0]
 
-    @pl.when(pl.program_id(0) == 0)
+    @pl.when(step == 0)
     def _():
         columns = pl.ds(pl.multiple_of(replica[0] * width, 128), width)
         pack(last_pieces, rows, arrived)
-        pack([piece.at[:, :, columns] for piece in first_pieces], first, arrived)
+        pack([piece.at[:, :, columns] for piece in own_pieces], first, arrived)
         grad_out_t[...] = rows[1].T
         normed_t[:, :ahead] = first[0].T
         normed_t[:, ahead:] = rows[0, :, columns].T
         grad_out[:ahead] = first[1]
         grad_out[ahead:] = rows[1, :, columns]
 
-    hidden[:ahead] = first_hidden[...]
-    grad_pre[:ahead] = first_grad_pre[...]
-    grad_lifted[:ahead] = first_grad_lifted[...]
-    hidden[ahead:], grad_pre[ahead:], grad_lifted[ahead:] = activations(
-        rows[0], grad_out_t[...], gate_weight[...], up_weight[...], down_weight[...]
-    )
-    grad_gate[...] = jnp.dot(
-        normed_t[...], grad_pre[...], preferred_element_type=jnp.float32
-    ).astype(grad_gate.dtype)
-    grad_up[...] = jnp.dot(
-        normed_t[...], grad_lifted[...], preferred_element_type=jnp.float32
-    ).astype(grad_up.dtype)
-    grad_down[...] = jnp.dot(
-        hidden[...].T, grad_out[...], preferred_element_type=jnp.float32
-    ).astype(grad_down.dtype)
-
-
-def all_rows(replica, n_dp, first_pieces, last_pieces, units, gate_weight, up_weight, down_weight):
+    def weight_gradients():
+        grad_gate[...] = jnp.dot(
+            normed_t[...], grad_pre[...], preferred_element_type=jnp.float32
+        ).astype(grad_gate.dtype)
+        grad_up[...] = jnp.dot(
+            normed_t[...], grad_lifted[...], preferred_element_type=jnp.float32
+        ).astype(grad_up.dtype)
+        grad_down[...] = jnp.dot(
+            hidden[...].T, grad_out[...], preferred_element_type=jnp.float32
+        ).astype(grad_down.dtype)
+
+    @pl.when(step < last)
+    def _():
+        products = project(
+            rows[0], grad_out_t[...], gate_weight[...], up_weight[...], down_weight[...]
+        )
+        weight_gradients()
+        hidden[:ahead] = own_hidden[...]
+        grad_pre[:ahead] = own_grad_pre[...]
+        grad_lifted[:ahead] = own_grad_lifted[...]
+        hidden[ahead:], grad_pre[ahead:], grad_lifted[ahead:] = activations(*products)
+
+    @pl.when(step == last)
+    def _():
+        weight_gradients()
+
+
+def all_rows(replica, n_dp, own_pieces, last_pieces, units, gate_weight, up_weight, down_weight):
     depth, hidden_units = gate_weight.shape
-    ahead, behind = height(first_pieces), height(last_pieces)
+    ahead, behind = height(own_pieces), height(last_pieces)
     count = ahead + behind
     width = depth // n_dp
-    tall = pl.BlockSpec((depth, TILE), lambda i: (0, i))
-    wide = pl.BlockSpec((TILE, depth), lambda i: (i, 0))
-    slim = pl.BlockSpec((ahead, TILE), lambda i: (0, i))
-    n_pieces = len(first_pieces), len(last_pieces)
+    tiles = hidden_units // TILE
+    tall = pl.BlockSpec((depth, TILE), lambda i: (0, jnp.minimum(i, tiles - 1)))
+    wide = pl.BlockSpec((TILE, depth), lambda i: (jnp.minimum(i, tiles - 1), 0))
+    slim = pl.BlockSpec((ahead, TILE), lambda i: (0, jnp.minimum(i, tiles - 1)))
+    n_pieces = len(own_pieces), len(last_pieces)
     return pl.pallas_call(
         functools.partial(all_kernel, *n_pieces),
-        grid=(hidden_units // TILE,),
+        grid=(tiles + 1,),
         in_specs=[pl.BlockSpec(memory_space=pltpu.SMEM)]
-        + [pl.BlockSpec(memory_space=pl.ANY)] * sum(n_pieces)
+        + [pl.BlockSpec(memory_space=pltpu.HBM)] * sum(n_pieces)
         + [slim, slim, slim, tall, tall, wide],
         out_specs=[
-            pl.BlockSpec((width, TILE), lambda i: (0, i)),
-            pl.BlockSpec((width, TILE), lambda i: (0, i)),
-            pl.BlockSpec((TILE, width), lambda i: (i, 0)),
+            pl.BlockSpec((width, TILE), lambda i: (0, jnp.maximum(i - 1, 0))),
+            pl.BlockSpec((width, TILE), lambda i: (0, jnp.maximum(i - 1, 0))),
+            pl.BlockSpec((TILE, width), lambda i: (jnp.maximum(i - 1, 0), 0)),
         ],
         out_shape=[
             jax.ShapeDtypeStruct((width, hidden_units), jnp.bfloat16),
@@ -198,14 +212,14 @@
             pltpu.VMEM((count, TILE), jnp.bfloat16),
             pltpu.SemaphoreType.DMA((max(n_pieces),)),
         ],
-        compiler_params=pltpu.CompilerParams(vmem_limit_bytes=40 * 2**20),
+        compiler_params=pltpu.CompilerParams(vmem_limit_bytes=46 * 2**20),
         cost_estimate=pl.CostEstimate(
             flops=6 * (behind * depth + count * width) * hidden_units,
             bytes_accessed=6 * (depth + width) * hidden_units,
             transcendentals=behind * hidden_units,
         ),
         name="all_rows",
-    )(replica, *first_pieces, *last_pieces, *units, gate_weight, up_weight, down_weight)
+    )(replica, *own_pieces, *last_pieces, *units, gate_weight, up_weight, down_weight)
 
 
 def gather_tokens(tokens, norm_scale_vector, gate_weight, up_weight, down_weight, cotangent):
@@ -233,27 +247,23 @@
     rescaled_input = (unit_input * norm_scale_vector).astype(jnp.bfloat16)
     unit0 = jnp.stack([rescaled_input, cotangent])
     unit1, unit2 = swap(unit0, 0, 2), swap(unit0, 0, 4)
-    more = [swap(unit0, b, 0) for b in range(1, n_dp)]
-    unit1, unit2, more = lax.optimization_barrier((unit1, unit2, more))
-    unit3, across = swap(unit2, 0, 2), swap(unit1, 1, 0)
-    far_more, far_unit0 = far(more), swap(unit0, 0, 1)
-    unit3, across, far_more, far_unit0 = lax.optimization_barrier(
-        (unit3, across, far_more, far_unit0)
-    )
-    last = jnp.concatenate([unit2, unit3], axis=1)
+    more = [swap(unit0, b, 0) for b in reversed(range(1, n_dp))]
+    *more, unit1, unit2 = lax.optimization_barrier((*more, unit1, unit2))
+    unit3, far_unit0, far_more = swap(unit2, 0, 2), swap(unit0, 0, 1), far(more)
+    far_more, far_unit0, unit3 = lax.optimization_barrier((far_more, far_unit0, unit3))
     late = jnp.concatenate([unit1, unit2, unit3], axis=1)
     own = [unit0, late, far_unit0, swap(late, 0, 1)]
-    more += [across] + far_more + far([across])
+    more += far_more
     own, more = lax.optimization_barrier((own, more))
-    rest = [swap(last, 1, 0)] + [swap(late, b, 0) for b in range(2, n_dp)]
-    *units, kept, sent = first_rows(own, more, gate_weight, up_weight, down_weight)
+    rest = [swap(late, b, 0) for b in range(1, n_dp)]
+    *units, kept, sent = own_rows(own, gate_weight, up_weight, down_weight)
     kept, sent, rest = lax.optimization_barrier((kept, sent, rest))
-    rest += far(rest)
+    rest += far(rest) + more
 
     pair = (kept.astype(jnp.float32) + swap(sent, 0, 1).astype(jnp.float32)).astype(jnp.bfloat16)
     parts = [swap(pair[:, k * rows : (k + 1) * rows], 0, 2 * k) for k in range(1, n_tp // 2)]
     weight_gradients = all_rows(
-        replica, n_dp, own + more, rest, units, gate_weight, up_weight, down_weight
+        replica, n_dp, own, rest, units, gate_weight, up_weight, down_weight
     )
     parts, weight_gradients = lax.optimization_barrier((parts, weight_gradients))
     total = pair[:, :rows].astype(jnp.float32) + sum(part.astype(jnp.float32) for part in parts)

time: 120 us -> 119 us (level)
  waiting for transfers between devices: 16.8 us -> 25 us
  Pallas kernels: 67.3 us -> 60.6 us
    ppermute x23 -> x21, waiting for transfers between devices: 16.8 us -> 25 us  [swap(): return lax.ppermute(array, ('dp', 'tp'), pairs)]
    pallas_call x2, Pallas kernels: 67.3 us -> 60.6 us  [the longest x1 35.7 us: all_rows(): pl.pallas_call(functools.partial(all_kernel, *n_pieces), grid=(tiles + 1,...]
    unnamed x68 -> x56, local copies, waits for them, and re-layouts: 8.44 us -> 7.3 us
    ppermute x23 -> x21, starting transfers between devices: 20.5 us -> 19.4 us  [swap(): return lax.ppermute(array, ('dp', 'tp'), pairs)]
  transfers between devices with their start and end apart: 23 -> 21, of which waited for: 7 -> 7; matrix products, arithmetic and copies ran while one was open for 1% -> 1% of each run, Pallas kernels for 56% -> 51%
where the time goes in v7:
time: 119 us
  Pallas kernels  60.6 us (51%)
  waiting for transfers between devices  25 us (21%)
  starting transfers between devices  19.4 us (16%)
  local copies, waits for them, and re-layouts  7.37 us (6%)
  other arithmetic  5.64 us (5%)
    pallas_call x1, Pallas kernels, all_rows(): pl.pallas_call(functools.partial(all_kernel, *n_pieces), grid=(tiles + 1,...  35.7 us
    ppermute x21, waiting for transfers between devices, swap(): return lax.ppermute(array, ('dp', 'tp'), pairs)  25 us
    pallas_call x1, Pallas kernels, own_rows(): pl.pallas_call(functools.partial(own_kernel, len(pieces)), grid=(hidden_u...  25 us
    ppermute x21, starting transfers between devices, swap(): return lax.ppermute(array, ('dp', 'tp'), pairs)  19.4 us
    unnamed x56, local copies, waits for them, and re-layouts  7.3 us
  transfers between devices with their start and end apart: 21, of which 7 were waited for; matrix products, arithmetic and copies ran while one was open for 1% of the time, Pallas kernels for 51%

profile of v7, /device:TPU:0, one launch (start us, length us, event | category | flops | bytes accessed | tf_op | source)
XLA Modules:
  0.0 118.9 jit_solution(16786554669761268673)
XLA Ops:
  0.6 1.1 fusion.9
  1.7 1.0 fusion.12
  2.7 0.9 pad_maximum_fusion.refs_0_.refs_1_
  3.6 4.1 %collective-permute-start.4 = (bf16[2,16,4096]{2,1,0:T(8,128)(2,1)S(1)}, bf16[2,16,4096]{2,1,0:T(8,128)(2,1)S(1)}, u32[]{:S(2)}, u32[]{:S(2)}) collective-permute-start(bf16[2,16,4096]{2,1,0:T(8,128)(2,1)S(1)} %pad_maximum_fusion.refs_0_.refs_1_), channel_id=1, source_target_pairs={{0,4},{1,5},{2,6},{3,7},{4,0},{5,1},{6,2},{7,3},{8,12},{9,13},{10,... | collective-permute-start | bytes 786440 | tf_op jit(solution)/shard_map/ppermute | solution.py:237
  7.7 1.6 %collective-permute-start.3 = (bf16[2,16,4096]{2,1,0:T(8,128)(2,1)S(1)}, bf16[2,16,4096]{2,1,0:T(8,128)(2,1)S(1)}, u32[]{:S(2)}, u32[]{:S(2)}) collective-permute-start(bf16[2,16,4096]{2,1,0:T(8,128)(2,1)S(1)} %pad_maximum_fusion.refs_0_.refs_1_), channel_id=1, source_target_pairs={{0,2},{1,3},{2,0},{3,1},{4,6},{5,7},{6,4},{7,5},{8,10},{9,11},{10,... | collective-permute-start | bytes 786440 | tf_op jit(solution)/shard_map/ppermute | solution.py:237
  9.3 1.5 %collective-permute-start.2 = (bf16[2,16,4096]{2,1,0:T(8,128)(2,1)S(1)}, bf16[2,16,4096]{2,1,0:T(8,128)(2,1)S(1)}, u32[]{:S(2)}, u32[]{:S(2)}) collective-permute-start(bf16[2,16,4096]{2,1,0:T(8,128)(2,1)S(1)} %pad_maximum_fusion.refs_0_.refs_1_), channel_id=1, source_target_pairs={{0,8},{1,9},{2,10},{3,11},{4,12},{5,13},{6,14},{7,15},{8,0},{9,1},... | collective-permute-start | bytes 786440 | tf_op jit(solution)/shard_map/ppermute | solution.py:237
  10.8 1.5 %collective-permute-start.1 = (bf16[2,16,4096]{2,1,0:T(8,128)(2,1)S(1)}, bf16[2,16,4096]{2,1,0:T(8,128)(2,1)S(1)}, u32[]{:S(2)}, u32[]{:S(2)}) collective-permute-start(bf16[2,16,4096]{2,1,0:T(8,128)(2,1)S(1)} %pad_maximum_fusion.refs_0_.refs_1_), channel_id=1, source_target_pairs={{0,16},{1,17},{2,18},{3,19},{4,20},{5,21},{6,22},{7,23},{8,24},{9,... | collective-permute-start | bytes 786440 | tf_op jit(solution)/shard_map/ppermute | solution.py:237
  12.8 7.0 %collective-permute-done.4 = bf16[2,16,4096]{2,1,0:T(8,128)(2,1)S(1)} collective-permute-done((bf16[2,16,4096]{2,1,0:T(8,128)(2,1)S(1)}, bf16[2,16,4096]{2,1,0:T(8,128)(2,1)S(1)}, u32[]{:S(2)}, u32[]{:S(2)}) %collective-permute-start.4) | collective-permute-done | bytes 262176 | tf_op jit(solution)/shard_map/ppermute | solution.py:237
  20.0 3.7 %collective-permute-done.1.refs_12_ = bf16[2,16,4096]{2,1,0:T(8,128)(2,1)S(1)} collective-permute-done((bf16[2,16,4096]{2,1,0:T(8,128)(2,1)S(1)}, bf16[2,16,4096]{2,1,0:T(8,128)(2,1)S(1)}, u32[]{:S(2)}, u32[]{:S(2)}) %collective-permute-start.1) | collective-permute-done | bytes 262176 | tf_op jit(solution)/shard_map/ppermute | solution.py:237
  23.6 0.5 collective-permute-start.9
  24.2 0.5 collective-permute-start.6
  24.7 5.3 %collective-permute-done.9 = bf16[2,16,4096]{2,1,0:T(8,128)(2,1)S(1)} collective-permute-done((bf16[2,16,4096]{2,1,0:T(8,128)(2,1)S(1)}, bf16[2,16,4096]{2,1,0:T(8,128)(2,1)S(1)}, u32[]{:S(2)}, u32[]{:S(2)}) %collective-permute-start.9) | collective-permute-done | bytes 262176 | tf_op jit(solution)/shard_map/ppermute | solution.py:237
  30.1 0.8 copy-done.20
  31.0 1.6 %collective-permute-start.13 = (bf16[2,48,4096]{2,1,0:T(8,128)(2,1)S(1)}, bf16[2,48,4096]{2,1,0:T(8,128)(2,1)S(1)}, u32[]{:S(2)}, u32[]{:S(2)}) collective-permute-start(bf16[2,48,4096]{2,1,0:T(8,128)(2,1)S(1)} %constant_dynamic-update-slice_fusion.refs_1_.refs_2_), channel_id=1, source_target_pairs={{0,24},{1,25},{2,26},{3,27},{4,28},{5,29},{6,30},{7,31},{8,16},{9,... | collective-permute-start | bytes 2359304 | tf_op jit(solution)/shard_map/ppermute | solution.py:237
  32.6 1.3 %collective-permute-start.12 = (bf16[2,48,4096]{2,1,0:T(8,128)(2,1)S(1)}, bf16[2,48,4096]{2,1,0:T(8,128)(2,1)S(1)}, u32[]{:S(2)}, u32[]{:S(2)}) collective-permute-start(bf16[2,48,4096]{2,1,0:T(8,128)(2,1)S(1)} %constant_dynamic-update-slice_fusion.refs_1_.refs_2_), channel_id=1, source_target_pairs={{0,16},{1,17},{2,18},{3,19},{4,20},{5,21},{6,22},{7,23},{8,24},{9,... | collective-permute-start | bytes 2359304 | tf_op jit(solution)/shard_map/ppermute | solution.py:237
  33.9 0.7 collective-permute-start.11
  34.6 25.0 %own_rows.1 = (bf16[128,1792]{1,0:T(8,128)(2,1)S(1)}, bf16[128,1792]{1,0:T(8,128)(2,1)S(1)}, bf16[128,1792]{1,0:T(8,128)(2,1)S(1)}, bf16[2,64,4096]{2,1,0:T(8,128)(2,1)S(1)}, bf16[2,64,4096]{2,1,0:T(8,128)(2,1)}) custom-call(bf16[2,16,4096]{2,1,0:T(8,128)(2,1)S(1)} %pad_maximum_fusion.refs_0_.refs_1_, ...), custom_call_target="tpu_custom_call" | custom-call | flops 11274289152 | bytes 44040192 | tf_op jit(solution)/shard_map/own_rows/pallas_call | solution.py:106
  59.6 0.8 copy-done.6
  60.3 0.8 copy-done.8
  61.1 0.8 copy-done.10
  61.9 6.9 %collective-permute-done.12.refs_6_ = bf16[2,48,4096]{2,1,0:T(8,128)(2,1)S(1)} collective-permute-done((bf16[2,48,4096]{2,1,0:T(8,128)(2,1)S(1)}, bf16[2,48,4096]{2,1,0:T(8,128)(2,1)S(1)}, u32[]{:S(2)}, u32[]{:S(2)}) %collective-permute-start.12) | collective-permute-done | bytes 786464 | tf_op jit(solution)/shard_map/ppermute | solution.py:237
  68.8 0.8 copy-done.2
  70.0 0.5 collective-permute-start.18
  71.0 1.9 %collective-permute-done.14 = bf16[2,64,4096]{2,1,0:T(8,128)(2,1)} collective-permute-done((bf16[2,64,4096]{2,1,0:T(8,128)(2,1)}, bf16[2,64,4096]{2,1,0:T(8,128)(2,1)}, u32[]{:S(2)}, u32[]{:S(2)}) %collective-permute-start.14) | collective-permute-done | bytes 1048608 | tf_op jit(solution)/shard_map/ppermute | solution.py:237
  72.9 1.5 %add_convert_fusion = bf16[2,64,4096]{2,1,0:T(8,128)(2,1)S(1)} fusion(bf16[2,64,4096]{2,1,0:T(8,128)(2,1)} %collective-permute-done.14, bf16[2,64,4096]{2,1,0:T(8,128)(2,1)S(1)} %get-tuple-element.60), kind=kLoop, calls=%fused_computation | loop fusion | flops 2097152 | bytes 3145728 | tf_op jit(solution)/shard_map/convert_element_type | solution.py:263
  74.4 2.0 %collective-permute-start.17 = (bf16[2,16,4096]{2,1,0:T(8,128)(2,1)S(1)}, bf16[2,16,4096]{2,1,0:T(8,128)(2,1)S(1)}, u32[]{:S(2)}, u32[]{:S(2)}) collective-permute-start(bf16[2,16,4096]{2,1,0:T(8,128)(2,1)S(1)} %get-tuple-element.83), channel_id=1, source_target_pairs={{0,6},{1,7},{2,4},{3,5},{4,2},{5,3},{6,0},{7,1},{8,14},{9,15},{10,... | collective-permute-start | bytes 786440 | tf_op jit(solution)/shard_map/ppermute | solution.py:237
  76.5 2.4 %collective-permute-start.15 = (bf16[2,16,4096]{2,1,0:T(8,128)(2,1)S(1)}, bf16[2,16,4096]{2,1,0:T(8,128)(2,1)S(1)}, u32[]{:S(2)}, u32[]{:S(2)}) collective-permute-start(bf16[2,16,4096]{2,1,0:T(8,128)(2,1)S(1)} %get-tuple-element.85), channel_id=1, source_target_pairs={{0,2},{1,3},{2,0},{3,1},{4,6},{5,7},{6,4},{7,5},{8,10},{9,11},{10,... | collective-permute-start | bytes 786440 | tf_op jit(solution)/shard_map/ppermute | solution.py:237
  78.9 0.9 copy-done.25
  80.1 0.9 copy-done.19
  81.1 0.9 copy-done.21
  82.0 35.7 %all_rows.1 = (bf16[1024,1792]{1,0:T(8,128)(2,1)}, bf16[1024,1792]{1,0:T(8,128)(2,1)}, bf16[1792,1024]{1,0:T(8,128)(2,1)}) custom-call(s32[1]{0:T(128)} %bitcast.2.refs_0_, bf16[2,16,4096]{2,1,0:T(8,128)(2,1)S(1)} %pad_maximum_fusion.refs_0_.refs_1_, bf16[2,48,4096]{2,1,0:T(8,128)(2,1)S(1)} %constant_dynamic-update-slice_fusion.refs_1_.refs_2_, ...), custom_call_target="tpu_custom_call" | custom-call | flops 22548578304 | bytes 55050240 | tf_op jit(solution)/shard_map/all_rows/pallas_call | solution.py:188
  118.2 0.8 fusion.8
  (79 shorter events, 2.5 us)
Async XLA Ops:
  3.6 16.1 %collective-permute-start.4 = (bf16[2,16,4096]{2,1,0:T(8,128)(2,1)S(1)}, bf16[2,16,4096]{2,1,0:T(8,128)(2,1)S(1)}, u32[]{:S(2)}, u32[]{:S(2)}) collective-permute-start(bf16[2,16,4096]{2,1,0:T(8,128)(2,1)S(1)} %pad_maximum_fusion.refs_0_.refs_1_), channel_id=1, source_target_pairs={{0,4},{1,5},{2,6},{3,7},{4,0},{5,1},{6,2},{7,3},{8,12},{9,13},{10,... | collective-permute-start | bytes 786440 | tf_op jit(solution)/shard_map/ppermute | solution.py:237
  7.7 12.2 %collective-permute-start.3 = (bf16[2,16,4096]{2,1,0:T(8,128)(2,1)S(1)}, bf16[2,16,4096]{2,1,0:T(8,128)(2,1)S(1)}, u32[]{:S(2)}, u32[]{:S(2)}) collective-permute-start(bf16[2,16,4096]{2,1,0:T(8,128)(2,1)S(1)} %pad_maximum_fusion.refs_0_.refs_1_), channel_id=1, source_target_pairs={{0,2},{1,3},{2,0},{3,1},{4,6},{5,7},{6,4},{7,5},{8,10},{9,11},{10,... | collective-permute-start | bytes 786440 | tf_op jit(solution)/shard_map/ppermute | solution.py:237
  9.3 10.6 %collective-permute-start.2 = (bf16[2,16,4096]{2,1,0:T(8,128)(2,1)S(1)}, bf16[2,16,4096]{2,1,0:T(8,128)(2,1)S(1)}, u32[]{:S(2)}, u32[]{:S(2)}) collective-permute-start(bf16[2,16,4096]{2,1,0:T(8,128)(2,1)S(1)} %pad_maximum_fusion.refs_0_.refs_1_), channel_id=1, source_target_pairs={{0,8},{1,9},{2,10},{3,11},{4,12},{5,13},{6,14},{7,15},{8,0},{9,1},... | collective-permute-start | bytes 786440 | tf_op jit(solution)/shard_map/ppermute | solution.py:237
  10.8 12.8 %collective-permute-start.1 = (bf16[2,16,4096]{2,1,0:T(8,128)(2,1)S(1)}, bf16[2,16,4096]{2,1,0:T(8,128)(2,1)S(1)}, u32[]{:S(2)}, u32[]{:S(2)}) collective-permute-start(bf16[2,16,4096]{2,1,0:T(8,128)(2,1)S(1)} %pad_maximum_fusion.refs_0_.refs_1_), channel_id=1, source_target_pairs={{0,16},{1,17},{2,18},{3,19},{4,20},{5,21},{6,22},{7,23},{8,24},{9,... | collective-permute-start | bytes 786440 | tf_op jit(solution)/shard_map/ppermute | solution.py:237
  12.3 11.3 %collective-permute-start = (bf16[2,16,4096]{2,1,0:T(8,128)(2,1)S(1)}, bf16[2,16,4096]{2,1,0:T(8,128)(2,1)S(1)}, u32[]{:S(2)}, u32[]{:S(2)}) collective-permute-start(bf16[2,16,4096]{2,1,0:T(8,128)(2,1)S(1)} %pad_maximum_fusion.refs_0_.refs_1_), channel_id=1, source_target_pairs={{0,24},{1,25},{2,26},{3,27},{4,28},{5,29},{6,30},{7,31},{8,16},{9,... | collective-permute-start | bytes 786440 | tf_op jit(solution)/shard_map/ppermute | solution.py:237
  19.8 4.9 %collective-permute-start.8 = (bf16[2,16,4096]{2,1,0:T(8,128)(2,1)S(1)}, bf16[2,16,4096]{2,1,0:T(8,128)(2,1)S(1)}, u32[]{:S(2)}, u32[]{:S(2)}) collective-permute-start(bf16[2,16,4096]{2,1,0:T(8,128)(2,1)S(1)} %pad_maximum_fusion.refs_0_.refs_1_), channel_id=1, source_target_pairs={{0,1},{1,0},{2,3},{3,2},{4,5},{5,4},{6,7},{7,6},{8,9},{9,8},{10,11... | collective-permute-start | bytes 786440 | tf_op jit(solution)/shard_map/ppermute | solution.py:237
  23.6 11.0 %copy-start.12 = (bf16[2,16,4096]{2,1,0:T(8,128)(2,1)}, bf16[2,16,4096]{2,1,0:T(8,128)(2,1)S(1)}, u32[]{:S(2)}) copy-start(bf16[2,16,4096]{2,1,0:T(8,128)(2,1)S(1)} %collective-permute-done.1.refs_12_) | copy-start | bytes 786436
  23.6 10.9 %copy-start.14 = (bf16[2,16,4096]{2,1,0:T(8,128)(2,1)}, bf16[2,16,4096]{2,1,0:T(8,128)(2,1)S(1)}, u32[]{:S(2)}) copy-start(bf16[2,16,4096]{2,1,0:T(8,128)(2,1)S(1)} %collective-permute-done.refs_11_) | copy-start | bytes 786436
  23.6 6.4 %collective-permute-start.9 = (bf16[2,16,4096]{2,1,0:T(8,128)(2,1)S(1)}, bf16[2,16,4096]{2,1,0:T(8,128)(2,1)S(1)}, u32[]{:S(2)}, u32[]{:S(2)}) collective-permute-start(bf16[2,16,4096]{2,1,0:T(8,128)(2,1)S(1)} %collective-permute-done.4), channel_id=1, source_target_pairs={{0,2},{1,3},{2,0},{3,1},{4,6},{5,7},{6,4},{7,5},{8,10},{9,11},{10,... | collective-permute-start | bytes 786440 | tf_op jit(solution)/shard_map/ppermute | solution.py:237
  24.2 5.9 %collective-permute-start.5 = (bf16[2,16,4096]{2,1,0:T(8,128)(2,1)S(1)}, bf16[2,16,4096]{2,1,0:T(8,128)(2,1)S(1)}, u32[]{:S(2)}, u32[]{:S(2)}) collective-permute-start(bf16[2,16,4096]{2,1,0:T(8,128)(2,1)S(1)} %collective-permute-done.refs_11_), channel_id=1, source_target_pairs={{0,1},{1,0},{2,3},{3,2},{4,5},{5,4},{6,7},{7,6},{8,9},{9,8},{10,11... | collective-permute-start | bytes 786440 | tf_op jit(solution)/shard_map/ppermute | solution.py:237
  24.2 5.9 %collective-permute-start.6 = (bf16[2,16,4096]{2,1,0:T(8,128)(2,1)S(1)}, bf16[2,16,4096]{2,1,0:T(8,128)(2,1)S(1)}, u32[]{:S(2)}, u32[]{:S(2)}) collective-permute-start(bf16[2,16,4096]{2,1,0:T(8,128)(2,1)S(1)} %collective-permute-done.1.refs_12_), channel_id=1, source_target_pairs={{0,1},{1,0},{2,3},{3,2},{4,5},{5,4},{6,7},{7,6},{8,9},{9,8},{10,11... | collective-permute-start | bytes 786440 | tf_op jit(solution)/shard_map/ppermute | solution.py:237
  24.7 5.4 %collective-permute-start.7 = (bf16[2,16,4096]{2,1,0:T(8,128)(2,1)S(1)}, bf16[2,16,4096]{2,1,0:T(8,128)(2,1)S(1)}, u32[]{:S(2)}, u32[]{:S(2)}) collective-permute-start(bf16[2,16,4096]{2,1,0:T(8,128)(2,1)S(1)} %collective-permute-done.2.refs_13_), channel_id=1, source_target_pairs={{0,1},{1,0},{2,3},{3,2},{4,5},{5,4},{6,7},{7,6},{8,9},{9,8},{10,11... | collective-permute-start | bytes 786440 | tf_op jit(solution)/shard_map/ppermute | solution.py:237
  31.0 3.6 %collective-permute-start.10 = (bf16[2,48,4096]{2,1,0:T(8,128)(2,1)S(1)}, bf16[2,48,4096]{2,1,0:T(8,128)(2,1)S(1)}, u32[]{:S(2)}, u32[]{:S(2)}) collective-permute-start(bf16[2,48,4096]{2,1,0:T(8,128)(2,1)S(1)} %constant_dynamic-update-slice_fusion.refs_1_.refs_2_), channel_id=1, source_target_pairs={{0,1},{1,0},{2,3},{3,2},{4,5},{5,4},{6,7},{7,6},{8,9},{9,8},{10,11... | collective-permute-start | bytes 2359304 | tf_op jit(solution)/shard_map/ppermute | solution.py:237
  31.0 30.8 %collective-permute-start.13 = (bf16[2,48,4096]{2,1,0:T(8,128)(2,1)S(1)}, bf16[2,48,4096]{2,1,0:T(8,128)(2,1)S(1)}, u32[]{:S(2)}, u32[]{:S(2)}) collective-permute-start(bf16[2,48,4096]{2,1,0:T(8,128)(2,1)S(1)} %constant_dynamic-update-slice_fusion.refs_1_.refs_2_), channel_id=1, source_target_pairs={{0,24},{1,25},{2,26},{3,27},{4,28},{5,29},{6,30},{7,31},{8,16},{9,... | collective-permute-start | bytes 2359304 | tf_op jit(solution)/shard_map/ppermute | solution.py:237
  32.6 36.2 %collective-permute-start.12 = (bf16[2,48,4096]{2,1,0:T(8,128)(2,1)S(1)}, bf16[2,48,4096]{2,1,0:T(8,128)(2,1)S(1)}, u32[]{:S(2)}, u32[]{:S(2)}) collective-permute-start(bf16[2,48,4096]{2,1,0:T(8,128)(2,1)S(1)} %constant_dynamic-update-slice_fusion.refs_1_.refs_2_), channel_id=1, source_target_pairs={{0,16},{1,17},{2,18},{3,19},{4,20},{5,21},{6,22},{7,23},{8,24},{9,... | collective-permute-start | bytes 2359304 | tf_op jit(solution)/shard_map/ppermute | solution.py:237
  33.9 34.9 %collective-permute-start.11 = (bf16[2,48,4096]{2,1,0:T(8,128)(2,1)S(1)}, bf16[2,48,4096]{2,1,0:T(8,128)(2,1)S(1)}, u32[]{:S(2)}, u32[]{:S(2)}) collective-permute-start(bf16[2,48,4096]{2,1,0:T(8,128)(2,1)S(1)} %constant_dynamic-update-slice_fusion.refs_1_.refs_2_), channel_id=1, source_target_pairs={{0,8},{1,9},{2,10},{3,11},{4,12},{5,13},{6,14},{7,15},{8,0},{9,1},... | collective-permute-start | bytes 2359304 | tf_op jit(solution)/shard_map/ppermute | solution.py:237
  69.9 3.0 %collective-permute-start.14 = (bf16[2,64,4096]{2,1,0:T(8,128)(2,1)}, bf16[2,64,4096]{2,1,0:T(8,128)(2,1)}, u32[]{:S(2)}, u32[]{:S(2)}) collective-permute-start(bf16[2,64,4096]{2,1,0:T(8,128)(2,1)} %get-tuple-element.61), channel_id=1, source_target_pairs={{0,1},{1,0},{2,3},{3,2},{4,5},{5,4},{6,7},{7,6},{8,9},{9,8},{10,11... | collective-permute-start | bytes 3145736 | tf_op jit(solution)/shard_map/ppermute | solution.py:237
  69.9 10.2 %copy-start.7 = (bf16[128,1792]{1,0:T(8,128)(2,1)S(1)}, bf16[128,1792]{1,0:T(8,128)(2,1)}, u32[]{:S(2)}) copy-start(bf16[128,1792]{1,0:T(8,128)(2,1)} %copy-done.6) | copy-start | bytes 1376260
  69.9 10.2 %copy-start.9 = (bf16[128,1792]{1,0:T(8,128)(2,1)S(1)}, bf16[128,1792]{1,0:T(8,128)(2,1)}, u32[]{:S(2)}) copy-start(bf16[128,1792]{1,0:T(8,128)(2,1)} %copy-done.8) | copy-start | bytes 1376260
  69.9 10.2 %copy-start.11 = (bf16[128,1792]{1,0:T(8,128)(2,1)S(1)}, bf16[128,1792]{1,0:T(8,128)(2,1)}, u32[]{:S(2)}) copy-start(bf16[128,1792]{1,0:T(8,128)(2,1)} %copy-done.10) | copy-start | bytes 1376260
  69.9 10.2 %copy-start.13 = (bf16[2,16,4096]{2,1,0:T(8,128)(2,1)S(1)}, bf16[2,16,4096]{2,1,0:T(8,128)(2,1)}, u32[]{:S(2)}) copy-start(bf16[2,16,4096]{2,1,0:T(8,128)(2,1)} %copy-done.12) | copy-start | bytes 786436
  70.0 10.2 %copy-start.15 = (bf16[2,16,4096]{2,1,0:T(8,128)(2,1)S(1)}, bf16[2,16,4096]{2,1,0:T(8,128)(2,1)}, u32[]{:S(2)}) copy-start(bf16[2,16,4096]{2,1,0:T(8,128)(2,1)} %copy-done.14) | copy-start | bytes 786436
  70.0 10.2 %copy-start.17 = (bf16[2,16,4096]{2,1,0:T(8,128)(2,1)S(1)}, bf16[2,16,4096]{2,1,0:T(8,128)(2,1)}, u32[]{:S(2)}) copy-start(bf16[2,16,4096]{2,1,0:T(8,128)(2,1)} %copy-done.16) | copy-start | bytes 786436
  70.0 6.5 %collective-permute-start.18 = (bf16[2,48,4096]{2,1,0:T(8,128)(2,1)}, bf16[2,48,4096]{2,1,0:T(8,128)(2,1)S(1)}, u32[]{:S(2)}, u32[]{:S(2)}) collective-permute-start(bf16[2,48,4096]{2,1,0:T(8,128)(2,1)} %copy-done.4), channel_id=1, source_target_pairs={{0,1},{1,0},{2,3},{3,2},{4,5},{5,4},{6,7},{7,6},{8,9},{9,8},{10,11... | collective-permute-start | bytes 2359304 | tf_op jit(solution)/shard_map/ppermute | solution.py:237
  70.5 8.4 %collective-permute-start.19 = (bf16[2,48,4096]{2,1,0:T(8,128)(2,1)}, bf16[2,48,4096]{2,1,0:T(8,128)(2,1)S(1)}, u32[]{:S(2)}, u32[]{:S(2)}) collective-permute-start(bf16[2,48,4096]{2,1,0:T(8,128)(2,1)} %copy-done.2), channel_id=1, source_target_pairs={{0,1},{1,0},{2,3},{3,2},{4,5},{5,4},{6,7},{7,6},{8,9},{9,8},{10,11... | collective-permute-start | bytes 2359304 | tf_op jit(solution)/shard_map/ppermute | solution.py:237
  70.6 8.3 %collective-permute-start.20 = (bf16[2,48,4096]{2,1,0:T(8,128)(2,1)}, bf16[2,48,4096]{2,1,0:T(8,128)(2,1)S(1)}, u32[]{:S(2)}, u32[]{:S(2)}) collective-permute-start(bf16[2,48,4096]{2,1,0:T(8,128)(2,1)} %copy-done), channel_id=1, source_target_pairs={{0,1},{1,0},{2,3},{3,2},{4,5},{5,4},{6,7},{7,6},{8,9},{9,8},{10,11... | collective-permute-start | bytes 2359304 | tf_op jit(solution)/shard_map/ppermute | solution.py:237
  74.4 43.3 %collective-permute-start.17 = (bf16[2,16,4096]{2,1,0:T(8,128)(2,1)S(1)}, bf16[2,16,4096]{2,1,0:T(8,128)(2,1)S(1)}, u32[]{:S(2)}, u32[]{:S(2)}) collective-permute-start(bf16[2,16,4096]{2,1,0:T(8,128)(2,1)S(1)} %get-tuple-element.83), channel_id=1, source_target_pairs={{0,6},{1,7},{2,4},{3,5},{4,2},{5,3},{6,0},{7,1},{8,14},{9,15},{10,... | collective-permute-start | bytes 786440 | tf_op jit(solution)/shard_map/ppermute | solution.py:237
  76.5 41.3 %collective-permute-start.16 = (bf16[2,16,4096]{2,1,0:T(8,128)(2,1)S(1)}, bf16[2,16,4096]{2,1,0:T(8,128)(2,1)S(1)}, u32[]{:S(2)}, u32[]{:S(2)}) collective-permute-start(bf16[2,16,4096]{2,1,0:T(8,128)(2,1)S(1)} %get-tuple-element.84), channel_id=1, source_target_pairs={{0,4},{1,5},{2,6},{3,7},{4,0},{5,1},{6,2},{7,3},{8,12},{9,13},{10,... | collective-permute-start | bytes 786440 | tf_op jit(solution)/shard_map/ppermute | solution.py:237
  76.5 41.3 %collective-permute-start.15 = (bf16[2,16,4096]{2,1,0:T(8,128)(2,1)S(1)}, bf16[2,16,4096]{2,1,0:T(8,128)(2,1)S(1)}, u32[]{:S(2)}, u32[]{:S(2)}) collective-permute-start(bf16[2,16,4096]{2,1,0:T(8,128)(2,1)S(1)} %get-tuple-element.85), channel_id=1, source_target_pairs={{0,2},{1,3},{2,0},{3,1},{4,6},{5,7},{6,4},{7,5},{8,10},{9,11},{10,... | collective-permute-start | bytes 786440 | tf_op jit(solution)/shard_map/ppermute | solution.py:237
  82.0 35.9 %copy-start.22 = (bf16[16,4096]{1,0:T(8,128)(2,1)S(1)}, bf16[16,4096]{1,0:T(8,128)(2,1)}, u32[]{:S(2)}) copy-start(bf16[16,4096]{1,0:T(8,128)(2,1)} %param.6) | copy-start | bytes 393220
  82.0 35.9 %copy-start.24 = (f32[4096]{0:T(1024)S(1)}, f32[4096]{0:T(1024)}, u32[]{:S(2)}) copy-start(f32[4096]{0:T(1024)} %param.7) | copy-start | bytes 49156
  82.0 36.1 %copy-start.23 = (bf16[16,4096]{1,0:T(8,128)(2,1)S(1)}, bf16[16,4096]{1,0:T(8,128)(2,1)}, u32[]{:S(2)}) copy-start(bf16[16,4096]{1,0:T(8,128)(2,1)} %param.11) | copy-start | bytes 393220
  (16 other events, 55.5 us)

commit v8 on v7

--- a/solution.py
+++ b/solution.py
@@ -52,6 +52,10 @@
         copy.start()
     for copy in copies:
         copy.wait()
+
+
+def in_hbm(*arrays):
+    return [pltpu.with_memory_space_constraint(array, pltpu.HBM) for array in arrays]
 
 
 def height(pieces):
@@ -106,7 +110,7 @@
     return pl.pallas_call(
         functools.partial(own_kernel, len(pieces)),
         grid=(hidden_units // TILE,),
-        in_specs=[pl.BlockSpec(memory_space=pltpu.HBM)] * len(pieces) + [tall, tall, wide],
+        in_specs=[pl.BlockSpec(memory_space=pl.ANY)] * len(pieces) + [tall, tall, wide],
         out_specs=[slim, slim, slim, whole, whole],
         out_shape=[unit, unit, unit, kept, kept],
         scratch_shapes=[
@@ -116,14 +120,14 @@
             pltpu.VMEM((depth, count), jnp.float32),
             pltpu.SemaphoreType.DMA((len(pieces),)),
         ],
-        compiler_params=pltpu.CompilerParams(vmem_limit_bytes=46 * 2**20),
+        compiler_params=pltpu.CompilerParams(vmem_limit_bytes=28 * 2**20),
         cost_estimate=pl.CostEstimate(
             flops=12 * count * depth * hidden_units,
             bytes_accessed=6 * depth * hidden_units,
             transcendentals=count * hidden_units,
         ),
         name="own_rows",
-    )(*pieces, gate_weight, up_weight, down_weight)
+    )(*pieces, *in_hbm(gate_weight, up_weight, down_weight))
 
 
 def all_kernel(n_own, n_last, *refs):
@@ -189,7 +193,7 @@
         functools.partial(all_kernel, *n_pieces),
         grid=(tiles + 1,),
         in_specs=[pl.BlockSpec(memory_space=pltpu.SMEM)]
-        + [pl.BlockSpec(memory_space=pltpu.HBM)] * sum(n_pieces)
+        + [pl.BlockSpec(memory_space=pl.ANY)] * sum(n_pieces)
         + [slim, slim, slim, tall, tall, wide],
         out_specs=[
             pl.BlockSpec((width, TILE), lambda i: (0, jnp.maximum(i - 1, 0))),
@@ -212,14 +216,14 @@
             pltpu.VMEM((count, TILE), jnp.bfloat16),
             pltpu.SemaphoreType.DMA((max(n_pieces),)),
         ],
-        compiler_params=pltpu.CompilerParams(vmem_limit_bytes=46 * 2**20),
+        compiler_params=pltpu.CompilerParams(vmem_limit_bytes=32 * 2**20),
         cost_estimate=pl.CostEstimate(
             flops=6 * (behind * depth + count * width) * hidden_units,
             bytes_accessed=6 * (depth + width) * hidden_units,
             transcendentals=behind * hidden_units,
         ),
         name="all_rows",
-    )(replica, *own_pieces, *last_pieces, *units, gate_weight, up_weight, down_weight)
+    )(replica, *own_pieces, *last_pieces, *units, *in_hbm(gate_weight, up_weight, down_weight))
 
 
 def gather_tokens(tokens, norm_scale_vector, gate_weight, up_weight, down_weight, cotangent):
@@ -247,20 +251,23 @@
     rescaled_input = (unit_input * norm_scale_vector).astype(jnp.bfloat16)
     unit0 = jnp.stack([rescaled_input, cotangent])
     unit1, unit2 = swap(unit0, 0, 2), swap(unit0, 0, 4)
-    more = [swap(unit0, b, 0) for b in reversed(range(1, n_dp))]
-    *more, unit1, unit2 = lax.optimization_barrier((*more, unit1, unit2))
-    unit3, far_unit0, far_more = swap(unit2, 0, 2), swap(unit0, 0, 1), far(more)
-    far_more, far_unit0, unit3 = lax.optimization_barrier((far_more, far_unit0, unit3))
-    late = jnp.concatenate([unit1, unit2, unit3], axis=1)
-    own = [unit0, late, far_unit0, swap(late, 0, 1)]
-    more += far_more
+    across0 = [swap(unit0, b, 0) for b in range(1, n_dp)]
+    unit3 = swap(unit2, 0, 2)
+    across0, unit1 = lax.optimization_barrier((across0, unit1))
+    across1 = [swap(unit1, 1, 0), swap(unit1, 2, 0)]
+    far_units, far_across0 = far([unit0, unit1]), far(across0)
+    far_across0, far_units, across1, unit3 = lax.optimization_barrier(
+        (far_across0, far_units, across1, unit3)
+    )
+    last = jnp.concatenate([unit2, unit3], axis=1)
+    own = [unit0, unit1, last] + far_units + [swap(last, 0, 1)]
+    more = across0 + far_across0 + across1
     own, more = lax.optimization_barrier((own, more))
-    rest = [swap(late, b, 0) for b in range(1, n_dp)]
+    rest = [swap(unit1, 3, 0)] + [swap(last, b, 0) for b in range(1, n_dp)]
     *units, kept, sent = own_rows(own, gate_weight, up_weight, down_weight)
     kept, sent, rest = lax.optimization_barrier((kept, sent, rest))
-    rest += far(rest) + more
-
     pair = (kept.astype(jnp.float32) + swap(sent, 0, 1).astype(jnp.float32)).astype(jnp.bfloat16)
+    rest += more + far(across1 + rest)
     parts = [swap(pair[:, k * rows : (k + 1) * rows], 0, 2 * k) for k in range(1, n_tp // 2)]
     weight_gradients = all_rows(
         replica, n_dp, own, rest, units, gate_weight, up_weight, down_weight

time: 119 us -> 115 us (0.966)
  waiting for transfers between devices: 25 us -> 15.8 us
  starting transfers between devices: 19.4 us -> 24.8 us
  Pallas kernels: 60.6 us -> 58.7 us
  local copies, waits for them, and re-layouts: 7.37 us -> 8.79 us
    ppermute x21 -> x28, waiting for transfers between devices: 25 us -> 15.8 us  [swap(): return lax.ppermute(array, ('dp', 'tp'), pairs)]
    ppermute x21 -> x28, starting transfers between devices: 19.4 us -> 24.8 us  [swap(): return lax.ppermute(array, ('dp', 'tp'), pairs)]
    pallas_call x1, Pallas kernels: 35.7 us -> 33.8 us  [all_rows(): pl.pallas_call(functools.partial(all_kernel, *n_pieces), grid=(tiles + 1,...]
    unnamed x56 -> x63, local copies, waits for them, and re-layouts: 7.3 us -> 8.72 us
  transfers between devices with their start and end apart: 21 -> 28, of which waited for: 7 -> 10; matrix products, arithmetic and copies ran while one was open for 1% -> 1% of each run, Pallas kernels for 51% -> 51%
where the time goes in v8:
time: 115 us
  Pallas kernels  58.7 us (51%)
  starting transfers between devices  24.8 us (22%)
  waiting for transfers between devices  15.8 us (14%)
  local copies, waits for them, and re-layouts  8.79 us (8%)
  other arithmetic  5.63 us (5%)
    pallas_call x1, Pallas kernels, all_rows(): pl.pallas_call(functools.partial(all_kernel, *n_pieces), grid=(tiles + 1,...  33.8 us
    pallas_call x1, Pallas kernels, own_rows(): pl.pallas_call(functools.partial(own_kernel, len(pieces)), grid=(hidden_u...  25 us
    ppermute x28, starting transfers between devices, swap(): return lax.ppermute(array, ('dp', 'tp'), pairs)  24.8 us
    ppermute x28, waiting for transfers between devices, swap(): return lax.ppermute(array, ('dp', 'tp'), pairs)  15.8 us
    unnamed x63, local copies, waits for them, and re-layouts  8.72 us
  transfers between devices with their start and end apart: 28, of which 10 were waited for; matrix products, arithmetic and copies ran while one was open for 1% of the time, Pallas kernels for 51%

profile of v8, /device:TPU:0, one launch (start us, length us, event | category | flops | bytes accessed | tf_op | source)
XLA Modules:
  0.0 114.8 jit_solution(15647465822396888822)
XLA Ops:
  0.6 1.1 fusion.9
  1.7 1.0 fusion.12
  2.7 0.9 pad_maximum_fusion.refs_0_.refs_1_
  3.6 4.1 %collective-permute-start.4 = (bf16[2,16,4096]{2,1,0:T(8,128)(2,1)S(1)}, bf16[2,16,4096]{2,1,0:T(8,128)(2,1)S(1)}, u32[]{:S(2)}, u32[]{:S(2)}) collective-permute-start(bf16[2,16,4096]{2,1,0:T(8,128)(2,1)S(1)} %pad_maximum_fusion.refs_0_.refs_1_), channel_id=1, source_target_pairs={{0,4},{1,5},{2,6},{3,7},{4,0},{5,1},{6,2},{7,3},{8,12},{9,13},{10,... | collective-permute-start | bytes 786440 | tf_op jit(solution)/shard_map/ppermute | solution.py:241
  7.7 1.6 %collective-permute-start.3 = (bf16[2,16,4096]{2,1,0:T(8,128)(2,1)S(1)}, bf16[2,16,4096]{2,1,0:T(8,128)(2,1)S(1)}, u32[]{:S(2)}, u32[]{:S(2)}) collective-permute-start(bf16[2,16,4096]{2,1,0:T(8,128)(2,1)S(1)} %pad_maximum_fusion.refs_0_.refs_1_), channel_id=1, source_target_pairs={{0,2},{1,3},{2,0},{3,1},{4,6},{5,7},{6,4},{7,5},{8,10},{9,11},{10,... | collective-permute-start | bytes 786440 | tf_op jit(solution)/shard_map/ppermute | solution.py:241
  9.3 2.4 %collective-permute-start.2 = (bf16[2,16,4096]{2,1,0:T(8,128)(2,1)S(1)}, bf16[2,16,4096]{2,1,0:T(8,128)(2,1)S(1)}, u32[]{:S(2)}, u32[]{:S(2)}) collective-permute-start(bf16[2,16,4096]{2,1,0:T(8,128)(2,1)S(1)} %pad_maximum_fusion.refs_0_.refs_1_), channel_id=1, source_target_pairs={{0,24},{1,25},{2,26},{3,27},{4,28},{5,29},{6,30},{7,31},{8,16},{9,... | collective-permute-start | bytes 786440 | tf_op jit(solution)/shard_map/ppermute | solution.py:241
  12.8 7.0 %collective-permute-done.4 = bf16[2,16,4096]{2,1,0:T(8,128)(2,1)S(1)} collective-permute-done((bf16[2,16,4096]{2,1,0:T(8,128)(2,1)S(1)}, bf16[2,16,4096]{2,1,0:T(8,128)(2,1)S(1)}, u32[]{:S(2)}, u32[]{:S(2)}) %collective-permute-start.4) | collective-permute-done | bytes 262176 | tf_op jit(solution)/shard_map/ppermute | solution.py:241
  20.0 1.5 %collective-permute-start.12 = (bf16[2,16,4096]{2,1,0:T(8,128)(2,1)S(1)}, bf16[2,16,4096]{2,1,0:T(8,128)(2,1)S(1)}, u32[]{:S(2)}, u32[]{:S(2)}) collective-permute-start(bf16[2,16,4096]{2,1,0:T(8,128)(2,1)S(1)} %collective-permute-done.4), channel_id=1, source_target_pairs={{0,2},{1,3},{2,0},{3,1},{4,6},{5,7},{6,4},{7,5},{8,10},{9,11},{10,... | collective-permute-start | bytes 786440 | tf_op jit(solution)/shard_map/ppermute | solution.py:241
  21.5 1.9 %collective-permute-done.1.refs_12_ = bf16[2,16,4096]{2,1,0:T(8,128)(2,1)S(1)} collective-permute-done((bf16[2,16,4096]{2,1,0:T(8,128)(2,1)S(1)}, bf16[2,16,4096]{2,1,0:T(8,128)(2,1)S(1)}, u32[]{:S(2)}, u32[]{:S(2)}) %collective-permute-start.1) | collective-permute-done | bytes 262176 | tf_op jit(solution)/shard_map/ppermute | solution.py:241
  24.1 1.5 %collective-permute-start.11 = (bf16[2,16,4096]{2,1,0:T(8,128)(2,1)S(1)}, bf16[2,16,4096]{2,1,0:T(8,128)(2,1)S(1)}, u32[]{:S(2)}, u32[]{:S(2)}) collective-permute-start(bf16[2,16,4096]{2,1,0:T(8,128)(2,1)S(1)} %collective-permute-done.3.refs_1_.refs_2_), channel_id=1, source_target_pairs={{0,16},{1,17},{2,18},{3,19},{4,20},{5,21},{6,22},{7,23},{8,24},{9,... | collective-permute-start | bytes 786440 | tf_op jit(solution)/shard_map/ppermute | solution.py:241
  25.6 0.8 collective-permute-start.10
  26.4 2.1 %collective-permute-done.12 = bf16[2,16,4096]{2,1,0:T(8,128)(2,1)S(1)} collective-permute-done((bf16[2,16,4096]{2,1,0:T(8,128)(2,1)S(1)}, bf16[2,16,4096]{2,1,0:T(8,128)(2,1)S(1)}, u32[]{:S(2)}, u32[]{:S(2)}) %collective-permute-start.12) | collective-permute-done | bytes 262176 | tf_op jit(solution)/shard_map/ppermute | solution.py:241
  28.5 0.7 copy-done.16
  30.0 0.7 copy-done.22
  31.6 1.3 %collective-permute-done.11.refs_18_ = bf16[2,16,4096]{2,1,0:T(8,128)(2,1)S(1)} collective-permute-done((bf16[2,16,4096]{2,1,0:T(8,128)(2,1)S(1)}, bf16[2,16,4096]{2,1,0:T(8,128)(2,1)S(1)}, u32[]{:S(2)}, u32[]{:S(2)}) %collective-permute-start.11) | collective-permute-done | bytes 262176 | tf_op jit(solution)/shard_map/ppermute | solution.py:241
  32.8 1.1 collective-permute-done.10.refs_17_
  34.1 1.6 %collective-permute-start.14 = (bf16[2,16,4096]{2,1,0:T(8,128)(2,1)S(1)}, bf16[2,16,4096]{2,1,0:T(8,128)(2,1)S(1)}, u32[]{:S(2)}, u32[]{:S(2)}) collective-permute-start(bf16[2,16,4096]{2,1,0:T(8,128)(2,1)S(1)} %collective-permute-done.3.refs_1_.refs_2_), channel_id=1, source_target_pairs={{0,24},{1,25},{2,26},{3,27},{4,28},{5,29},{6,30},{7,31},{8,16},{9,... | collective-permute-start | bytes 786440 | tf_op jit(solution)/shard_map/ppermute | solution.py:241
  35.7 1.4 %collective-permute-start.17 = (bf16[2,32,4096]{2,1,0:T(8,128)(2,1)S(1)}, bf16[2,32,4096]{2,1,0:T(8,128)(2,1)S(1)}, u32[]{:S(2)}, u32[]{:S(2)}) collective-permute-start(bf16[2,32,4096]{2,1,0:T(8,128)(2,1)S(1)} %constant_dynamic-update-slice_fusion.refs_2_.refs_3_), channel_id=1, source_target_pairs={{0,24},{1,25},{2,26},{3,27},{4,28},{5,29},{6,30},{7,31},{8,16},{9,... | collective-permute-start | bytes 1572872 | tf_op jit(solution)/shard_map/ppermute | solution.py:241
  37.7 1.5 %collective-permute-start.15 = (bf16[2,32,4096]{2,1,0:T(8,128)(2,1)S(1)}, bf16[2,32,4096]{2,1,0:T(8,128)(2,1)S(1)}, u32[]{:S(2)}, u32[]{:S(2)}) collective-permute-start(bf16[2,32,4096]{2,1,0:T(8,128)(2,1)S(1)} %constant_dynamic-update-slice_fusion.refs_2_.refs_3_), channel_id=1, source_target_pairs={{0,8},{1,9},{2,10},{3,11},{4,12},{5,13},{6,14},{7,15},{8,0},{9,1},... | collective-permute-start | bytes 1572872 | tf_op jit(solution)/shard_map/ppermute | solution.py:241
  39.2 25.0 %own_rows.1 = (bf16[128,1792]{1,0:T(8,128)(2,1)S(1)}, bf16[128,1792]{1,0:T(8,128)(2,1)S(1)}, bf16[128,1792]{1,0:T(8,128)(2,1)S(1)}, bf16[2,64,4096]{2,1,0:T(8,128)(2,1)S(1)}, bf16[2,64,4096]{2,1,0:T(8,128)(2,1)}) custom-call(bf16[2,16,4096]{2,1,0:T(8,128)(2,1)S(1)} %pad_maximum_fusion.refs_0_.refs_1_, ...), custom_call_target="tpu_custom_call" | custom-call | flops 11274289152 | bytes 44040192 | tf_op jit(solution)/shard_map/own_rows/pallas_call | solution.py:110
  64.2 0.8 copy-done.6
  64.9 0.8 copy-done.8
  65.7 0.8 copy-done.10
  66.6 0.8 copy-done
  69.4 1.7 %collective-permute-done.18 = bf16[2,64,4096]{2,1,0:T(8,128)(2,1)} collective-permute-done((bf16[2,64,4096]{2,1,0:T(8,128)(2,1)}, bf16[2,64,4096]{2,1,0:T(8,128)(2,1)}, u32[]{:S(2)}, u32[]{:S(2)}) %collective-permute-start.18) | collective-permute-done | bytes 1048608 | tf_op jit(solution)/shard_map/ppermute | solution.py:241
  71.3 1.5 %add_convert_fusion = bf16[2,64,4096]{2,1,0:T(8,128)(2,1)S(1)} fusion(bf16[2,64,4096]{2,1,0:T(8,128)(2,1)} %collective-permute-done.18, bf16[2,64,4096]{2,1,0:T(8,128)(2,1)S(1)} %get-tuple-element.71), kind=kLoop, calls=%fused_computation | loop fusion | flops 2097152 | bytes 3145728 | tf_op jit(solution)/shard_map/convert_element_type | solution.py:269
  73.3 2.3 %collective-permute-start.21 = (bf16[2,16,4096]{2,1,0:T(8,128)(2,1)S(1)}, bf16[2,16,4096]{2,1,0:T(8,128)(2,1)S(1)}, u32[]{:S(2)}, u32[]{:S(2)}) collective-permute-start(bf16[2,16,4096]{2,1,0:T(8,128)(2,1)S(1)} %get-tuple-element.97), channel_id=1, source_target_pairs={{0,6},{1,7},{2,4},{3,5},{4,2},{5,3},{6,0},{7,1},{8,14},{9,15},{10,... | collective-permute-start | bytes 786440 | tf_op jit(solution)/shard_map/ppermute | solution.py:241
  75.6 2.1 %collective-permute-start.19 = (bf16[2,16,4096]{2,1,0:T(8,128)(2,1)S(1)}, bf16[2,16,4096]{2,1,0:T(8,128)(2,1)S(1)}, u32[]{:S(2)}, u32[]{:S(2)}) collective-permute-start(bf16[2,16,4096]{2,1,0:T(8,128)(2,1)S(1)} %get-tuple-element.99), channel_id=1, source_target_pairs={{0,2},{1,3},{2,0},{3,1},{4,6},{5,7},{6,4},{7,5},{8,10},{9,11},{10,... | collective-permute-start | bytes 786440 | tf_op jit(solution)/shard_map/ppermute | solution.py:241
  77.9 0.9 copy-done.25
  78.8 0.9 copy-done.27
  79.8 33.8 %all_rows.1 = (bf16[1024,1792]{1,0:T(8,128)(2,1)}, bf16[1024,1792]{1,0:T(8,128)(2,1)}, bf16[1792,1024]{1,0:T(8,128)(2,1)}) custom-call(s32[1]{0:T(128)} %bitcast.2.refs_0_, bf16[2,16,4096]{2,1,0:T(8,128)(2,1)S(1)} %pad_maximum_fusion.refs_0_.refs_1_, bf16[2,16,4096]{2,1,0:T(8,128)(2,1)S(1)} %collective-permute-done.3.refs_1_.refs_2_, ...), custom_call_target="tpu_custom_call" | custom-call | flops 22548578304 | bytes 55050240 | tf_op jit(solution)/shard_map/all_rows/pallas_call | solution.py:192
  114.0 0.8 fusion.8
  (100 shorter events, 7.4 us)
Async XLA Ops:
  3.6 16.1 %collective-permute-start.4 = (bf16[2,16,4096]{2,1,0:T(8,128)(2,1)S(1)}, bf16[2,16,4096]{2,1,0:T(8,128)(2,1)S(1)}, u32[]{:S(2)}, u32[]{:S(2)}) collective-permute-start(bf16[2,16,4096]{2,1,0:T(8,128)(2,1)S(1)} %pad_maximum_fusion.refs_0_.refs_1_), channel_id=1, source_target_pairs={{0,4},{1,5},{2,6},{3,7},{4,0},{5,1},{6,2},{7,3},{8,12},{9,13},{10,... | collective-permute-start | bytes 786440 | tf_op jit(solution)/shard_map/ppermute | solution.py:241
  7.7 12.2 %collective-permute-start.3 = (bf16[2,16,4096]{2,1,0:T(8,128)(2,1)S(1)}, bf16[2,16,4096]{2,1,0:T(8,128)(2,1)S(1)}, u32[]{:S(2)}, u32[]{:S(2)}) collective-permute-start(bf16[2,16,4096]{2,1,0:T(8,128)(2,1)S(1)} %pad_maximum_fusion.refs_0_.refs_1_), channel_id=1, source_target_pairs={{0,2},{1,3},{2,0},{3,1},{4,6},{5,7},{6,4},{7,5},{8,10},{9,11},{10,... | collective-permute-start | bytes 786440 | tf_op jit(solution)/shard_map/ppermute | solution.py:241
  9.3 12.1 %collective-permute-start.2 = (bf16[2,16,4096]{2,1,0:T(8,128)(2,1)S(1)}, bf16[2,16,4096]{2,1,0:T(8,128)(2,1)S(1)}, u32[]{:S(2)}, u32[]{:S(2)}) collective-permute-start(bf16[2,16,4096]{2,1,0:T(8,128)(2,1)S(1)} %pad_maximum_fusion.refs_0_.refs_1_), channel_id=1, source_target_pairs={{0,24},{1,25},{2,26},{3,27},{4,28},{5,29},{6,30},{7,31},{8,16},{9,... | collective-permute-start | bytes 786440 | tf_op jit(solution)/shard_map/ppermute | solution.py:241
  11.8 11.6 %collective-permute-start.1 = (bf16[2,16,4096]{2,1,0:T(8,128)(2,1)S(1)}, bf16[2,16,4096]{2,1,0:T(8,128)(2,1)S(1)}, u32[]{:S(2)}, u32[]{:S(2)}) collective-permute-start(bf16[2,16,4096]{2,1,0:T(8,128)(2,1)S(1)} %pad_maximum_fusion.refs_0_.refs_1_), channel_id=1, source_target_pairs={{0,16},{1,17},{2,18},{3,19},{4,20},{5,21},{6,22},{7,23},{8,24},{9,... | collective-permute-start | bytes 786440 | tf_op jit(solution)/shard_map/ppermute | solution.py:241
  12.3 11.1 %collective-permute-start = (bf16[2,16,4096]{2,1,0:T(8,128)(2,1)S(1)}, bf16[2,16,4096]{2,1,0:T(8,128)(2,1)S(1)}, u32[]{:S(2)}, u32[]{:S(2)}) collective-permute-start(bf16[2,16,4096]{2,1,0:T(8,128)(2,1)S(1)} %pad_maximum_fusion.refs_0_.refs_1_), channel_id=1, source_target_pairs={{0,8},{1,9},{2,10},{3,11},{4,12},{5,13},{6,14},{7,15},{8,0},{9,1},... | collective-permute-start | bytes 786440 | tf_op jit(solution)/shard_map/ppermute | solution.py:241
  19.8 6.6 %collective-permute-start.8 = (bf16[2,16,4096]{2,1,0:T(8,128)(2,1)S(1)}, bf16[2,16,4096]{2,1,0:T(8,128)(2,1)S(1)}, u32[]{:S(2)}, u32[]{:S(2)}) collective-permute-start(bf16[2,16,4096]{2,1,0:T(8,128)(2,1)S(1)} %pad_maximum_fusion.refs_0_.refs_1_), channel_id=1, source_target_pairs={{0,1},{1,0},{2,3},{3,2},{4,5},{5,4},{6,7},{7,6},{8,9},{9,8},{10,11... | collective-permute-start | bytes 786440 | tf_op jit(solution)/shard_map/ppermute | solution.py:241
  20.0 8.5 %collective-permute-start.12 = (bf16[2,16,4096]{2,1,0:T(8,128)(2,1)S(1)}, bf16[2,16,4096]{2,1,0:T(8,128)(2,1)S(1)}, u32[]{:S(2)}, u32[]{:S(2)}) collective-permute-start(bf16[2,16,4096]{2,1,0:T(8,128)(2,1)S(1)} %collective-permute-done.4), channel_id=1, source_target_pairs={{0,2},{1,3},{2,0},{3,1},{4,6},{5,7},{6,4},{7,5},{8,10},{9,11},{10,... | collective-permute-start | bytes 786440 | tf_op jit(solution)/shard_map/ppermute | solution.py:241
  23.3 15.9 %copy-start.12 = (bf16[2,16,4096]{2,1,0:T(8,128)(2,1)}, bf16[2,16,4096]{2,1,0:T(8,128)(2,1)S(1)}, u32[]{:S(2)}) copy-start(bf16[2,16,4096]{2,1,0:T(8,128)(2,1)S(1)} %collective-permute-done.1.refs_12_) | copy-start | bytes 786436
  23.4 5.1 %collective-permute-start.5 = (bf16[2,16,4096]{2,1,0:T(8,128)(2,1)S(1)}, bf16[2,16,4096]{2,1,0:T(8,128)(2,1)S(1)}, u32[]{:S(2)}, u32[]{:S(2)}) collective-permute-start(bf16[2,16,4096]{2,1,0:T(8,128)(2,1)S(1)} %collective-permute-done.refs_11_), channel_id=1, source_target_pairs={{0,1},{1,0},{2,3},{3,2},{4,5},{5,4},{6,7},{7,6},{8,9},{9,8},{10,11... | collective-permute-start | bytes 786440 | tf_op jit(solution)/shard_map/ppermute | solution.py:241
  24.1 8.7 %collective-permute-start.11 = (bf16[2,16,4096]{2,1,0:T(8,128)(2,1)S(1)}, bf16[2,16,4096]{2,1,0:T(8,128)(2,1)S(1)}, u32[]{:S(2)}, u32[]{:S(2)}) collective-permute-start(bf16[2,16,4096]{2,1,0:T(8,128)(2,1)S(1)} %collective-permute-done.3.refs_1_.refs_2_), channel_id=1, source_target_pairs={{0,16},{1,17},{2,18},{3,19},{4,20},{5,21},{6,22},{7,23},{8,24},{9,... | collective-permute-start | bytes 786440 | tf_op jit(solution)/shard_map/ppermute | solution.py:241
  25.6 8.4 %collective-permute-start.10 = (bf16[2,16,4096]{2,1,0:T(8,128)(2,1)S(1)}, bf16[2,16,4096]{2,1,0:T(8,128)(2,1)S(1)}, u32[]{:S(2)}, u32[]{:S(2)}) collective-permute-start(bf16[2,16,4096]{2,1,0:T(8,128)(2,1)S(1)} %collective-permute-done.3.refs_1_.refs_2_), channel_id=1, source_target_pairs={{0,8},{1,9},{2,10},{3,11},{4,12},{5,13},{6,14},{7,15},{8,0},{9,1},... | collective-permute-start | bytes 786440 | tf_op jit(solution)/shard_map/ppermute | solution.py:241
  26.4 7.6 %collective-permute-start.9 = (bf16[2,16,4096]{2,1,0:T(8,128)(2,1)S(1)}, bf16[2,16,4096]{2,1,0:T(8,128)(2,1)S(1)}, u32[]{:S(2)}, u32[]{:S(2)}) collective-permute-start(bf16[2,16,4096]{2,1,0:T(8,128)(2,1)S(1)} %collective-permute-done.3.refs_1_.refs_2_), channel_id=1, source_target_pairs={{0,1},{1,0},{2,3},{3,2},{4,5},{5,4},{6,7},{7,6},{8,9},{9,8},{10,11... | collective-permute-start | bytes 786440 | tf_op jit(solution)/shard_map/ppermute | solution.py:241
  28.5 1.5 %collective-permute-start.6 = (bf16[2,16,4096]{2,1,0:T(8,128)(2,1)S(1)}, bf16[2,16,4096]{2,1,0:T(8,128)(2,1)S(1)}, u32[]{:S(2)}, u32[]{:S(2)}) collective-permute-start(bf16[2,16,4096]{2,1,0:T(8,128)(2,1)S(1)} %collective-permute-done.1.refs_12_), channel_id=1, source_target_pairs={{0,1},{1,0},{2,3},{3,2},{4,5},{5,4},{6,7},{7,6},{8,9},{9,8},{10,11... | collective-permute-start | bytes 786440 | tf_op jit(solution)/shard_map/ppermute | solution.py:241
  29.2 1.7 %collective-permute-start.7 = (bf16[2,16,4096]{2,1,0:T(8,128)(2,1)S(1)}, bf16[2,16,4096]{2,1,0:T(8,128)(2,1)S(1)}, u32[]{:S(2)}, u32[]{:S(2)}) collective-permute-start(bf16[2,16,4096]{2,1,0:T(8,128)(2,1)S(1)} %collective-permute-done.2.refs_13_), channel_id=1, source_target_pairs={{0,1},{1,0},{2,3},{3,2},{4,5},{5,4},{6,7},{7,6},{8,9},{9,8},{10,11... | collective-permute-start | bytes 786440 | tf_op jit(solution)/shard_map/ppermute | solution.py:241
  34.0 5.2 %collective-permute-start.13 = (bf16[2,32,4096]{2,1,0:T(8,128)(2,1)S(1)}, bf16[2,32,4096]{2,1,0:T(8,128)(2,1)S(1)}, u32[]{:S(2)}, u32[]{:S(2)}) collective-permute-start(bf16[2,32,4096]{2,1,0:T(8,128)(2,1)S(1)} %constant_dynamic-update-slice_fusion.refs_2_.refs_3_), channel_id=1, source_target_pairs={{0,1},{1,0},{2,3},{3,2},{4,5},{5,4},{6,7},{7,6},{8,9},{9,8},{10,11... | collective-permute-start | bytes 1572872 | tf_op jit(solution)/shard_map/ppermute | solution.py:241
  34.1 32.4 %collective-permute-start.14 = (bf16[2,16,4096]{2,1,0:T(8,128)(2,1)S(1)}, bf16[2,16,4096]{2,1,0:T(8,128)(2,1)S(1)}, u32[]{:S(2)}, u32[]{:S(2)}) collective-permute-start(bf16[2,16,4096]{2,1,0:T(8,128)(2,1)S(1)} %collective-permute-done.3.refs_1_.refs_2_), channel_id=1, source_target_pairs={{0,24},{1,25},{2,26},{3,27},{4,28},{5,29},{6,30},{7,31},{8,16},{9,... | collective-permute-start | bytes 786440 | tf_op jit(solution)/shard_map/ppermute | solution.py:241
  35.7 30.8 %collective-permute-start.17 = (bf16[2,32,4096]{2,1,0:T(8,128)(2,1)S(1)}, bf16[2,32,4096]{2,1,0:T(8,128)(2,1)S(1)}, u32[]{:S(2)}, u32[]{:S(2)}) collective-permute-start(bf16[2,32,4096]{2,1,0:T(8,128)(2,1)S(1)} %constant_dynamic-update-slice_fusion.refs_2_.refs_3_), channel_id=1, source_target_pairs={{0,24},{1,25},{2,26},{3,27},{4,28},{5,29},{6,30},{7,31},{8,16},{9,... | collective-permute-start | bytes 1572872 | tf_op jit(solution)/shard_map/ppermute | solution.py:241
  37.1 29.5 %collective-permute-start.16 = (bf16[2,32,4096]{2,1,0:T(8,128)(2,1)S(1)}, bf16[2,32,4096]{2,1,0:T(8,128)(2,1)S(1)}, u32[]{:S(2)}, u32[]{:S(2)}) collective-permute-start(bf16[2,32,4096]{2,1,0:T(8,128)(2,1)S(1)} %constant_dynamic-update-slice_fusion.refs_2_.refs_3_), channel_id=1, source_target_pairs={{0,16},{1,17},{2,18},{3,19},{4,20},{5,21},{6,22},{7,23},{8,24},{9,... | collective-permute-start | bytes 1572872 | tf_op jit(solution)/shard_map/ppermute | solution.py:241
  37.7 28.9 %collective-permute-start.15 = (bf16[2,32,4096]{2,1,0:T(8,128)(2,1)S(1)}, bf16[2,32,4096]{2,1,0:T(8,128)(2,1)S(1)}, u32[]{:S(2)}, u32[]{:S(2)}) collective-permute-start(bf16[2,32,4096]{2,1,0:T(8,128)(2,1)S(1)} %constant_dynamic-update-slice_fusion.refs_2_.refs_3_), channel_id=1, source_target_pairs={{0,8},{1,9},{2,10},{3,11},{4,12},{5,13},{6,14},{7,15},{8,0},{9,1},... | collective-permute-start | bytes 1572872 | tf_op jit(solution)/shard_map/ppermute | solution.py:241
  68.2 3.0 %collective-permute-start.18 = (bf16[2,64,4096]{2,1,0:T(8,128)(2,1)}, bf16[2,64,4096]{2,1,0:T(8,128)(2,1)}, u32[]{:S(2)}, u32[]{:S(2)}) collective-permute-start(bf16[2,64,4096]{2,1,0:T(8,128)(2,1)} %get-tuple-element.72), channel_id=1, source_target_pairs={{0,1},{1,0},{2,3},{3,2},{4,5},{5,4},{6,7},{7,6},{8,9},{9,8},{10,11... | collective-permute-start | bytes 3145736 | tf_op jit(solution)/shard_map/ppermute | solution.py:241
  68.3 4.5 %collective-permute-start.22 = (bf16[2,16,4096]{2,1,0:T(8,128)(2,1)}, bf16[2,16,4096]{2,1,0:T(8,128)(2,1)S(1)}, u32[]{:S(2)}, u32[]{:S(2)}) collective-permute-start(bf16[2,16,4096]{2,1,0:T(8,128)(2,1)} %copy-done.20), channel_id=1, source_target_pairs={{0,1},{1,0},{2,3},{3,2},{4,5},{5,4},{6,7},{7,6},{8,9},{9,8},{10,11... | collective-permute-start | bytes 786440 | tf_op jit(solution)/shard_map/ppermute | solution.py:241
  68.8 4.5 %collective-permute-start.23 = (bf16[2,16,4096]{2,1,0:T(8,128)(2,1)}, bf16[2,16,4096]{2,1,0:T(8,128)(2,1)S(1)}, u32[]{:S(2)}, u32[]{:S(2)}) collective-permute-start(bf16[2,16,4096]{2,1,0:T(8,128)(2,1)} %copy-done.18), channel_id=1, source_target_pairs={{0,1},{1,0},{2,3},{3,2},{4,5},{5,4},{6,7},{7,6},{8,9},{9,8},{10,11... | collective-permute-start | bytes 786440 | tf_op jit(solution)/shard_map/ppermute | solution.py:241
  68.9 6.7 %collective-permute-start.24 = (bf16[2,16,4096]{2,1,0:T(8,128)(2,1)}, bf16[2,16,4096]{2,1,0:T(8,128)(2,1)S(1)}, u32[]{:S(2)}, u32[]{:S(2)}) collective-permute-start(bf16[2,16,4096]{2,1,0:T(8,128)(2,1)} %copy-done.26), channel_id=1, source_target_pairs={{0,1},{1,0},{2,3},{3,2},{4,5},{5,4},{6,7},{7,6},{8,9},{9,8},{10,11... | collective-permute-start | bytes 786440 | tf_op jit(solution)/shard_map/ppermute | solution.py:241
  69.3 6.3 %collective-permute-start.25 = (bf16[2,32,4096]{2,1,0:T(8,128)(2,1)}, bf16[2,32,4096]{2,1,0:T(8,128)(2,1)S(1)}, u32[]{:S(2)}, u32[]{:S(2)}) collective-permute-start(bf16[2,32,4096]{2,1,0:T(8,128)(2,1)} %copy-done.4), channel_id=1, source_target_pairs={{0,1},{1,0},{2,3},{3,2},{4,5},{5,4},{6,7},{7,6},{8,9},{9,8},{10,11... | collective-permute-start | bytes 1572872 | tf_op jit(solution)/shard_map/ppermute | solution.py:241
  71.2 6.6 %collective-permute-start.26 = (bf16[2,32,4096]{2,1,0:T(8,128)(2,1)}, bf16[2,32,4096]{2,1,0:T(8,128)(2,1)S(1)}, u32[]{:S(2)}, u32[]{:S(2)}) collective-permute-start(bf16[2,32,4096]{2,1,0:T(8,128)(2,1)} %copy-done.2), channel_id=1, source_target_pairs={{0,1},{1,0},{2,3},{3,2},{4,5},{5,4},{6,7},{7,6},{8,9},{9,8},{10,11... | collective-permute-start | bytes 1572872 | tf_op jit(solution)/shard_map/ppermute | solution.py:241
  72.8 5.0 %collective-permute-start.27 = (bf16[2,32,4096]{2,1,0:T(8,128)(2,1)}, bf16[2,32,4096]{2,1,0:T(8,128)(2,1)S(1)}, u32[]{:S(2)}, u32[]{:S(2)}) collective-permute-start(bf16[2,32,4096]{2,1,0:T(8,128)(2,1)} %copy-done), channel_id=1, source_target_pairs={{0,1},{1,0},{2,3},{3,2},{4,5},{5,4},{6,7},{7,6},{8,9},{9,8},{10,11... | collective-permute-start | bytes 1572872 | tf_op jit(solution)/shard_map/ppermute | solution.py:241
  73.3 40.3 %collective-permute-start.21 = (bf16[2,16,4096]{2,1,0:T(8,128)(2,1)S(1)}, bf16[2,16,4096]{2,1,0:T(8,128)(2,1)S(1)}, u32[]{:S(2)}, u32[]{:S(2)}) collective-permute-start(bf16[2,16,4096]{2,1,0:T(8,128)(2,1)S(1)} %get-tuple-element.97), channel_id=1, source_target_pairs={{0,6},{1,7},{2,4},{3,5},{4,2},{5,3},{6,0},{7,1},{8,14},{9,15},{10,... | collective-permute-start | bytes 786440 | tf_op jit(solution)/shard_map/ppermute | solution.py:241
  75.6 37.9 %collective-permute-start.20 = (bf16[2,16,4096]{2,1,0:T(8,128)(2,1)S(1)}, bf16[2,16,4096]{2,1,0:T(8,128)(2,1)S(1)}, u32[]{:S(2)}, u32[]{:S(2)}) collective-permute-start(bf16[2,16,4096]{2,1,0:T(8,128)(2,1)S(1)} %get-tuple-element.98), channel_id=1, source_target_pairs={{0,4},{1,5},{2,6},{3,7},{4,0},{5,1},{6,2},{7,3},{8,12},{9,13},{10,... | collective-permute-start | bytes 786440 | tf_op jit(solution)/shard_map/ppermute | solution.py:241
  75.6 37.9 %collective-permute-start.19 = (bf16[2,16,4096]{2,1,0:T(8,128)(2,1)S(1)}, bf16[2,16,4096]{2,1,0:T(8,128)(2,1)S(1)}, u32[]{:S(2)}, u32[]{:S(2)}) collective-permute-start(bf16[2,16,4096]{2,1,0:T(8,128)(2,1)S(1)} %get-tuple-element.99), channel_id=1, source_target_pairs={{0,2},{1,3},{2,0},{3,1},{4,6},{5,7},{6,4},{7,5},{8,10},{9,11},{10,... | collective-permute-start | bytes 786440 | tf_op jit(solution)/shard_map/ppermute | solution.py:241
  79.8 33.9 %copy-start.28 = (bf16[16,4096]{1,0:T(8,128)(2,1)S(1)}, bf16[16,4096]{1,0:T(8,128)(2,1)}, u32[]{:S(2)}) copy-start(bf16[16,4096]{1,0:T(8,128)(2,1)} %param.6) | copy-start | bytes 393220
  79.8 34.0 %copy-start.30 = (f32[4096]{0:T(1024)S(1)}, f32[4096]{0:T(1024)}, u32[]{:S(2)}) copy-start(f32[4096]{0:T(1024)} %param.7) | copy-start | bytes 49156
  79.8 34.2 %copy-start.29 = (bf16[16,4096]{1,0:T(8,128)(2,1)S(1)}, bf16[16,4096]{1,0:T(8,128)(2,1)}, u32[]{:S(2)}) copy-start(bf16[16,4096]{1,0:T(8,128)(2,1)} %param.11) | copy-start | bytes 393220
  (27 other events, 138.1 us)

commit v9 on v8

--- a/solution.py
+++ b/solution.py
@@ -62,16 +62,36 @@
     return sum(piece.shape[1] for piece in pieces)
 
 
+def norm_kernel(tokens, norm_scale_vector, cotangent, unit):
+    expanded_hidden = tokens[...].astype(jnp.float32)
+    reciprocal_root_mean = lax.rsqrt(
+        jnp.mean(expanded_hidden * expanded_hidden, axis=-1, keepdims=True) + 1e-05
+    )
+    rescaled_input = expanded_hidden * reciprocal_root_mean * norm_scale_vector[...]
+    unit[0] = rescaled_input.astype(unit.dtype)
+    unit[1] = cotangent[...]
+
+
+def normalize(tokens, norm_scale_vector, cotangent):
+    return pl.pallas_call(
+        norm_kernel,
+        out_shape=jax.ShapeDtypeStruct((2, *tokens.shape), jnp.bfloat16),
+        name="normalize",
+    )(*in_hbm(tokens, norm_scale_vector.reshape(1, -1), cotangent))
+
+
 def own_kernel(n_pieces, *refs):
-    pieces, refs = refs[:n_pieces], refs[n_pieces:]
-    gate_weight, up_weight, down_weight, hidden, grad_pre, grad_lifted, kept, sent = refs[:8]
-    rows, grad_out_t, out_sum, in_sum, arrived = refs[8:]
+    replica, pieces, refs = refs[0], refs[1 : n_pieces + 1], refs[n_pieces + 1 :]
+    gate_weight, up_weight, down_weight, hidden, grad_pre, grad_lifted = refs[:6]
+    columns, kept, sent, rows, grad_out_t, out_sum, in_sum, arrived = refs[6:]
     step = pl.program_id(0)
     part = kept.shape[1]
 
     @pl.when(step == 0)
     def _():
         pack(pieces, rows, arrived)
+        width = columns.shape[2]
+        columns[...] = rows[:, :, pl.ds(pl.multiple_of(replica[0] * width, 128), width)]
         grad_out_t[...] = rows[1].T
         out_sum[...] = jnp.zeros_like(out_sum)
         in_sum[...] = jnp.zeros_like(in_sum)
@@ -98,7 +118,7 @@
         sent[1] = summed[part:].astype(sent.dtype)
 
 
-def own_rows(pieces, gate_weight, up_weight, down_weight):
+def own_rows(replica, n_dp, pieces, gate_weight, up_weight, down_weight):
     depth, hidden_units = gate_weight.shape
     count = height(pieces)
     tall = pl.BlockSpec((depth, TILE), lambda i: (0, i))
@@ -106,13 +126,16 @@
     slim = pl.BlockSpec((count, TILE), lambda i: (0, i))
     whole = pl.BlockSpec((2, count // 2, depth), lambda i: (0, 0, 0))
     kept = jax.ShapeDtypeStruct((2, count // 2, depth), jnp.bfloat16)
-    unit = jax.ShapeDtypeStruct((count, hidden_units), jnp.bfloat16)
+    columns = (2, count, depth // n_dp)
+    unit = pltpu.HBM((count, hidden_units), jnp.bfloat16)
     return pl.pallas_call(
         functools.partial(own_kernel, len(pieces)),
         grid=(hidden_units // TILE,),
-        in_specs=[pl.BlockSpec(memory_space=pl.ANY)] * len(pieces) + [tall, tall, wide],
-        out_specs=[slim, slim, slim, whole, whole],
-        out_shape=[unit, unit, unit, kept, kept],
+        in_specs=[pl.BlockSpec(memory_space=pltpu.SMEM)]
+        + [pl.BlockSpec(memory_space=pl.ANY)] * len(pieces)
+        + [tall, tall, wide],
+        out_specs=[slim, slim, slim, pl.BlockSpec(columns, lambda i: (0, 0, 0)), whole, whole],
+        out_shape=[unit, unit, unit, pltpu.HBM(columns, jnp.bfloat16), kept, kept],
         scratch_shapes=[
             pltpu.VMEM((2, count, depth), jnp.bfloat16),
             pltpu.VMEM((depth, count), jnp.bfloat16),
@@ -127,29 +150,26 @@
             transcendentals=count * hidden_units,
         ),
         name="own_rows",
-    )(*pieces, *in_hbm(gate_weight, up_weight, down_weight))
-
-
-def all_kernel(n_own, n_last, *refs):
-    replica, refs = refs[0], refs[1:]
-    own_pieces, refs = refs[:n_own], refs[n_own:]
-    last_pieces, refs = refs[:n_last], refs[n_last:]
-    own_hidden, own_grad_pre, own_grad_lifted = refs[:3]
-    gate_weight, up_weight, down_weight, grad_gate, grad_up, grad_down = refs[3:9]
-    rows, first, normed_t, grad_out, grad_out_t, hidden, grad_pre, grad_lifted, arrived = refs[9:]
+    )(replica, *pieces, *in_hbm(gate_weight, up_weight, down_weight))
+
+
+def all_kernel(n_pieces, *refs):
+    replica, pieces, refs = refs[0], refs[1 : n_pieces + 1], refs[n_pieces + 1 :]
+    own_hidden, own_grad_pre, own_grad_lifted, own_columns = refs[:4]
+    gate_weight, up_weight, down_weight, grad_gate, grad_up, grad_down = refs[4:10]
+    rows, normed_t, grad_out, grad_out_t, hidden, grad_pre, grad_lifted, arrived = refs[10:]
     step, last = pl.program_id(0), pl.num_programs(0) - 1
-    ahead = first.shape[1]
+    ahead = own_columns.shape[1]
     width = normed_t.shape[0]
 
     @pl.when(step == 0)
     def _():
         columns = pl.ds(pl.multiple_of(replica[0] * width, 128), width)
-        pack(last_pieces, rows, arrived)
-        pack([piece.at[:, :, columns] for piece in own_pieces], first, arrived)
+        pack(pieces, rows, arrived)
         grad_out_t[...] = rows[1].T
-        normed_t[:, :ahead] = first[0].T
+        normed_t[:, :ahead] = own_columns[0].T
         normed_t[:, ahead:] = rows[0, :, columns].T
-        grad_out[:ahead] = first[1]
+        grad_out[:ahead] = own_columns[1]
         grad_out[ahead:] = rows[1, :, columns]
 
     def weight_gradients():
@@ -179,22 +199,22 @@
         weight_gradients()
 
 
-def all_rows(replica, n_dp, own_pieces, last_pieces, units, gate_weight, up_weight, down_weight):
+def all_rows(replica, pieces, units, own_columns, gate_weight, up_weight, down_weight):
     depth, hidden_units = gate_weight.shape
-    ahead, behind = height(own_pieces), height(last_pieces)
+    ahead, width = own_columns.shape[1:]
+    behind = height(pieces)
     count = ahead + behind
-    width = depth // n_dp
     tiles = hidden_units // TILE
     tall = pl.BlockSpec((depth, TILE), lambda i: (0, jnp.minimum(i, tiles - 1)))
     wide = pl.BlockSpec((TILE, depth), lambda i: (jnp.minimum(i, tiles - 1), 0))
     slim = pl.BlockSpec((ahead, TILE), lambda i: (0, jnp.minimum(i, tiles - 1)))
-    n_pieces = len(own_pieces), len(last_pieces)
     return pl.pallas_call(
-        functools.partial(all_kernel, *n_pieces),
+        functools.partial(all_kernel, len(pieces)),
         grid=(tiles + 1,),
         in_specs=[pl.BlockSpec(memory_space=pltpu.SMEM)]
-        + [pl.BlockSpec(memory_space=pl.ANY)] * sum(n_pieces)
-        + [slim, slim, slim, tall, tall, wide],
+        + [pl.BlockSpec(memory_space=pl.ANY)] * len(pieces)
+        + [slim, slim, slim, pl.BlockSpec(own_columns.shape, lambda i: (0, 0, 0))]
+        + [tall, tall, wide],
         out_specs=[
             pl.BlockSpec((width, TILE), lambda i: (0, jnp.maximum(i - 1, 0))),
             pl.BlockSpec((width, TILE), lambda i: (0, jnp.maximum(i - 1, 0))),
@@ -207,14 +227,13 @@
         ],
         scratch_shapes=[
             pltpu.VMEM((2, behind, depth), jnp.bfloat16),
-            pltpu.VMEM((2, ahead, width), jnp.bfloat16),
             pltpu.VMEM((width, count), jnp.bfloat16),
             pltpu.VMEM((count, width), jnp.bfloat16),
             pltpu.VMEM((depth, behind), jnp.bfloat16),
             pltpu.VMEM((count, TILE), jnp.bfloat16),
             pltpu.VMEM((count, TILE), jnp.bfloat16),
             pltpu.VMEM((count, TILE), jnp.bfloat16),
-            pltpu.SemaphoreType.DMA((max(n_pieces),)),
+            pltpu.SemaphoreType.DMA((len(pieces),)),
         ],
         compiler_params=pltpu.CompilerParams(vmem_limit_bytes=32 * 2**20),
         cost_estimate=pl.CostEstimate(
@@ -223,7 +242,7 @@
             transcendentals=behind * hidden_units,
         ),
         name="all_rows",
-    )(replica, *own_pieces, *last_pieces, *units, *in_hbm(gate_weight, up_weight, down_weight))
+    )(replica, *in_hbm(*pieces, *units, own_columns, gate_weight, up_weight, down_weight))
 
 
 def gather_tokens(tokens, norm_scale_vector, gate_weight, up_weight, down_weight, cotangent):
@@ -248,29 +267,25 @@
         jnp.mean(expanded_hidden * expanded_hidden, axis=-1, keepdims=True) + 1e-05
     )
     unit_input = expanded_hidden * reciprocal_root_mean
-    rescaled_input = (unit_input * norm_scale_vector).astype(jnp.bfloat16)
-    unit0 = jnp.stack([rescaled_input, cotangent])
-    unit1, unit2 = swap(unit0, 0, 2), swap(unit0, 0, 4)
-    across0 = [swap(unit0, b, 0) for b in range(1, n_dp)]
+    unit0 = normalize(tokens, norm_scale_vector, cotangent)
+    unit2, unit1 = swap(unit0, 0, 4), swap(unit0, 0, 2)
+    across = [swap(unit0, b, 0) for b in range(1, n_dp)]
     unit3 = swap(unit2, 0, 2)
-    across0, unit1 = lax.optimization_barrier((across0, unit1))
-    across1 = [swap(unit1, 1, 0), swap(unit1, 2, 0)]
-    far_units, far_across0 = far([unit0, unit1]), far(across0)
-    far_across0, far_units, across1, unit3 = lax.optimization_barrier(
-        (far_across0, far_units, across1, unit3)
-    )
+    far_units, far_across = far([unit0, unit1]), far(across)
+    across, far_units, unit3 = lax.optimization_barrier((across, far_units, unit3))
     last = jnp.concatenate([unit2, unit3], axis=1)
+    late = jnp.concatenate([unit1, unit2, unit3], axis=1)
     own = [unit0, unit1, last] + far_units + [swap(last, 0, 1)]
-    more = across0 + far_across0 + across1
-    own, more = lax.optimization_barrier((own, more))
-    rest = [swap(unit1, 3, 0)] + [swap(last, b, 0) for b in range(1, n_dp)]
-    *units, kept, sent = own_rows(own, gate_weight, up_weight, down_weight)
+    rest = [swap(late, b, 0) for b in range(1, n_dp)]
+    *units, own_columns, kept, sent = own_rows(
+        replica, n_dp, own, gate_weight, up_weight, down_weight
+    )
     kept, sent, rest = lax.optimization_barrier((kept, sent, rest))
     pair = (kept.astype(jnp.float32) + swap(sent, 0, 1).astype(jnp.float32)).astype(jnp.bfloat16)
-    rest += more + far(across1 + rest)
+    rest += far(rest) + across + far_across
     parts = [swap(pair[:, k * rows : (k + 1) * rows], 0, 2 * k) for k in range(1, n_tp // 2)]
     weight_gradients = all_rows(
-        replica, n_dp, own, rest, units, gate_weight, up_weight, down_weight
+        replica, rest, units, own_columns, gate_weight, up_weight, down_weight
     )
     parts, weight_gradients = lax.optimization_barrier((parts, weight_gradients))
     total = pair[:, :rows].astype(jnp.float32) + sum(part.astype(jnp.float32) for part in parts)

time: 115 us -> 115 us (level)
  waiting for transfers between devices: 15.8 us -> 26.4 us
  local copies, waits for them, and re-layouts: 8.79 us -> 2.2 us
  starting transfers between devices: 24.8 us -> 19.5 us
  Pallas kernels: 58.7 us -> 63.9 us
  other arithmetic: 5.63 us -> 1.62 us
    ppermute x28 -> x22, waiting for transfers between devices: 15.8 us -> 26.4 us  [swap(): return lax.ppermute(array, ('dp', 'tp'), pairs)]
    unnamed x63 -> x34, local copies, waits for them, and re-layouts: 8.72 us -> 2.11 us
    ppermute x28 -> x22, starting transfers between devices: 24.8 us -> 19.5 us  [swap(): return lax.ppermute(array, ('dp', 'tp'), pairs)]
    pallas_call x1 -> x2, Pallas kernels: 33.8 us -> 38.9 us  [the longest x1 37 us: all_rows(): pl.pallas_call(functools.partial(all_kernel, len(pieces)), grid=(tiles +...]
    another operation x2 -> x0, other arithmetic: 1.94 us -> none  [gather_tokens(): unit0 = jnp.stack([rescaled_input, cotangent])]
    convert_element_type x1, other arithmetic: 1.48 us -> 0.31 us  [gather_tokens(): (kept.astype(jnp.float32) + swap(sent, 0, 1).astype(jnp.float32)).astype(...]
  transfers between devices with their start and end apart: 28 -> 22, of which waited for: 10 -> 6; matrix products, arithmetic and copies ran while one was open for 1% -> 0% of each run, Pallas kernels for 51% -> 54%
where the time goes in v9:
time: 115 us
  Pallas kernels  63.9 us (56%)
  waiting for transfers between devices  26.4 us (23%)
  starting transfers between devices  19.5 us (17%)
  local copies, waits for them, and re-layouts  2.2 us (2%)
  other arithmetic  1.62 us (1%)
    pallas_call x1, Pallas kernels, all_rows(): pl.pallas_call(functools.partial(all_kernel, len(pieces)), grid=(tiles +...  37 us
    ppermute x22, waiting for transfers between devices, swap(): return lax.ppermute(array, ('dp', 'tp'), pairs)  26.4 us
    pallas_call x1, Pallas kernels, own_rows(): pl.pallas_call(functools.partial(own_kernel, len(pieces)), grid=(hidden_u...  25 us
    ppermute x22, starting transfers between devices, swap(): return lax.ppermute(array, ('dp', 'tp'), pairs)  19.5 us
  transfers between devices with their start and end apart: 22, of which 6 were waited for; matrix products, arithmetic and copies ran while one was open for 0% of the time, Pallas kernels for 54%

profile of v9, /device:TPU:0, one launch (start us, length us, event | category | flops | bytes accessed | tf_op | source)
XLA Modules:
  0.0 114.5 jit_solution(14492984555492186880)
XLA Ops:
  0.6 1.8 %normalize.1.refs_1_ = bf16[2,16,4096]{2,1,0:T(8,128)(2,1)} custom-call(bf16[16,4096]{1,0:T(8,128)(2,1)} %tokens.1, f32[1,4096]{1,0:T(1,128)} %bitcast.14, bf16[16,4096]{1,0:T(8,128)(2,1)} %cotangent.1), custom_call_target="tpu_custom_call" | custom-call | tf_op jit(solution)/shard_map/normalize/pallas_call | solution.py:76
  2.5 3.0 %collective-permute-start = (bf16[2,16,4096]{2,1,0:T(8,128)(2,1)}, bf16[2,16,4096]{2,1,0:T(8,128)(2,1)S(1)}, u32[]{:S(2)}, u32[]{:S(2)}) collective-permute-start(bf16[2,16,4096]{2,1,0:T(8,128)(2,1)} %normalize.1.refs_1_), channel_id=1, source_target_pairs={{0,2},{1,3},{2,0},{3,1},{4,6},{5,7},{6,4},{7,5},{8,10},{9,11},{10,... | collective-permute-start | bytes 786440 | tf_op jit(solution)/shard_map/ppermute | solution.py:260
  5.5 2.6 %collective-permute-start.1 = (bf16[2,16,4096]{2,1,0:T(8,128)(2,1)}, bf16[2,16,4096]{2,1,0:T(8,128)(2,1)S(1)}, u32[]{:S(2)}, u32[]{:S(2)}) collective-permute-start(bf16[2,16,4096]{2,1,0:T(8,128)(2,1)} %normalize.1.refs_1_), channel_id=1, source_target_pairs={{0,4},{1,5},{2,6},{3,7},{4,0},{5,1},{6,2},{7,3},{8,12},{9,13},{10,... | collective-permute-start | bytes 786440 | tf_op jit(solution)/shard_map/ppermute | solution.py:260
  8.1 1.5 %collective-permute-start.2 = (bf16[2,16,4096]{2,1,0:T(8,128)(2,1)}, bf16[2,16,4096]{2,1,0:T(8,128)(2,1)S(1)}, u32[]{:S(2)}, u32[]{:S(2)}) collective-permute-start(bf16[2,16,4096]{2,1,0:T(8,128)(2,1)} %normalize.1.refs_1_), channel_id=1, source_target_pairs={{0,8},{1,9},{2,10},{3,11},{4,12},{5,13},{6,14},{7,15},{8,0},{9,1},... | collective-permute-start | bytes 786440 | tf_op jit(solution)/shard_map/ppermute | solution.py:260
  9.6 1.5 %collective-permute-start.3 = (bf16[2,16,4096]{2,1,0:T(8,128)(2,1)}, bf16[2,16,4096]{2,1,0:T(8,128)(2,1)S(1)}, u32[]{:S(2)}, u32[]{:S(2)}) collective-permute-start(bf16[2,16,4096]{2,1,0:T(8,128)(2,1)} %normalize.1.refs_1_), channel_id=1, source_target_pairs={{0,16},{1,17},{2,18},{3,19},{4,20},{5,21},{6,22},{7,23},{8,24},{9,... | collective-permute-start | bytes 786440 | tf_op jit(solution)/shard_map/ppermute | solution.py:260
  11.1 0.5 collective-permute-start.4
  11.6 5.9 %collective-permute-done.refs_2_ = bf16[2,16,4096]{2,1,0:T(8,128)(2,1)S(1)} collective-permute-done((bf16[2,16,4096]{2,1,0:T(8,128)(2,1)}, bf16[2,16,4096]{2,1,0:T(8,128)(2,1)S(1)}, u32[]{:S(2)}, u32[]{:S(2)}) %collective-permute-start) | collective-permute-done | bytes 262176 | tf_op jit(solution)/shard_map/ppermute | solution.py:260
  17.5 2.5 %collective-permute-done.1 = bf16[2,16,4096]{2,1,0:T(8,128)(2,1)S(1)} collective-permute-done((bf16[2,16,4096]{2,1,0:T(8,128)(2,1)}, bf16[2,16,4096]{2,1,0:T(8,128)(2,1)S(1)}, u32[]{:S(2)}, u32[]{:S(2)}) %collective-permute-start.1) | collective-permute-done | bytes 262176 | tf_op jit(solution)/shard_map/ppermute | solution.py:260
  20.1 0.5 collective-permute-start.7
  20.6 2.0 %collective-permute-done.3.refs_8_ = bf16[2,16,4096]{2,1,0:T(8,128)(2,1)S(1)} collective-permute-done((bf16[2,16,4096]{2,1,0:T(8,128)(2,1)}, bf16[2,16,4096]{2,1,0:T(8,128)(2,1)S(1)}, u32[]{:S(2)}, u32[]{:S(2)}) %collective-permute-start.3) | collective-permute-done | bytes 262176 | tf_op jit(solution)/shard_map/ppermute | solution.py:260
  22.6 6.1 %collective-permute-done.7 = bf16[2,16,4096]{2,1,0:T(8,128)(2,1)S(1)} collective-permute-done((bf16[2,16,4096]{2,1,0:T(8,128)(2,1)S(1)}, bf16[2,16,4096]{2,1,0:T(8,128)(2,1)S(1)}, u32[]{:S(2)}, u32[]{:S(2)}) %collective-permute-start.7) | collective-permute-done | bytes 262176 | tf_op jit(solution)/shard_map/ppermute | solution.py:260
  28.9 1.6 %collective-permute-start.9 = (bf16[2,48,4096]{2,1,0:T(8,128)(2,1)S(1)}, bf16[2,48,4096]{2,1,0:T(8,128)(2,1)S(1)}, u32[]{:S(2)}, u32[]{:S(2)}) collective-permute-start(bf16[2,48,4096]{2,1,0:T(8,128)(2,1)S(1)} %get-tuple-element.62), channel_id=1, source_target_pairs={{0,8},{1,9},{2,10},{3,11},{4,12},{5,13},{6,14},{7,15},{8,0},{9,1},... | collective-permute-start | bytes 2359304 | tf_op jit(solution)/shard_map/ppermute | solution.py:260
  30.5 1.5 %collective-permute-start.10 = (bf16[2,48,4096]{2,1,0:T(8,128)(2,1)S(1)}, bf16[2,48,4096]{2,1,0:T(8,128)(2,1)S(1)}, u32[]{:S(2)}, u32[]{:S(2)}) collective-permute-start(bf16[2,48,4096]{2,1,0:T(8,128)(2,1)S(1)} %get-tuple-element.62), channel_id=1, source_target_pairs={{0,16},{1,17},{2,18},{3,19},{4,20},{5,21},{6,22},{7,23},{8,24},{9,... | collective-permute-start | bytes 2359304 | tf_op jit(solution)/shard_map/ppermute | solution.py:260
  32.0 0.5 collective-permute-start.11
  32.5 0.9 copy-done
  33.4 25.0 %own_rows.1 = (bf16[128,1792]{1,0:T(8,128)(2,1)}, bf16[128,1792]{1,0:T(8,128)(2,1)}, bf16[128,1792]{1,0:T(8,128)(2,1)}, bf16[2,128,1024]{2,1,0:T(8,128)(2,1)}, b...) custom-call(s32[1]{0:T(128)} %bitcast.refs_0_, bf16[2,16,4096]{2,1,0:T(8,128)(2,1)S(1)} %copy-done, ...), custom_call_target="tpu_custom_call" | custom-call | flops 11274289152 | bytes 44040192 | tf_op jit(solution)/shard_map/own_rows/pallas_call | solution.py:131
  58.4 8.5 %collective-permute-done.10.refs_2_ = bf16[2,48,4096]{2,1,0:T(8,128)(2,1)S(1)} collective-permute-done((bf16[2,48,4096]{2,1,0:T(8,128)(2,1)S(1)}, bf16[2,48,4096]{2,1,0:T(8,128)(2,1)S(1)}, u32[]{:S(2)}, u32[]{:S(2)}) %collective-permute-start.10) | collective-permute-done | bytes 786464 | tf_op jit(solution)/shard_map/ppermute | solution.py:260
  67.0 0.1 fusion.8
  67.2 0.6 collective-permute-start.19
  67.8 0.4 collective-permute-start.21
  68.3 1.3 %collective-permute-done.12 = bf16[2,64,4096]{2,1,0:T(8,128)(2,1)S(1)} collective-permute-done((bf16[2,64,4096]{2,1,0:T(8,128)(2,1)S(1)}, bf16[2,64,4096]{2,1,0:T(8,128)(2,1)S(1)}, u32[]{:S(2)}, u32[]{:S(2)}) %collective-permute-start.12) | collective-permute-done | bytes 1048608 | tf_op jit(solution)/shard_map/ppermute | solution.py:260
  69.6 0.1 collective-permute-start.17
  69.8 0.3 add_convert_fusion
  70.1 0.4 collective-permute-start.18
  70.6 0.5 collective-permute-start.13
  71.1 2.6 %collective-permute-start.14 = (bf16[2,16,4096]{2,1,0:T(8,128)(2,1)S(1)}, bf16[2,16,4096]{2,1,0:T(8,128)(2,1)S(1)}, u32[]{:S(2)}, u32[]{:S(2)}) collective-permute-start(bf16[2,16,4096]{2,1,0:T(8,128)(2,1)S(1)} %get-tuple-element.58), channel_id=1, source_target_pairs={{0,4},{1,5},{2,6},{3,7},{4,0},{5,1},{6,2},{7,3},{8,12},{9,13},{10,... | collective-permute-start | bytes 786440 | tf_op jit(solution)/shard_map/ppermute | solution.py:260
  73.7 1.4 %collective-permute-start.15 = (bf16[2,16,4096]{2,1,0:T(8,128)(2,1)S(1)}, bf16[2,16,4096]{2,1,0:T(8,128)(2,1)S(1)}, u32[]{:S(2)}, u32[]{:S(2)}) collective-permute-start(bf16[2,16,4096]{2,1,0:T(8,128)(2,1)S(1)} %get-tuple-element.57), channel_id=1, source_target_pairs={{0,6},{1,7},{2,4},{3,5},{4,2},{5,3},{6,0},{7,1},{8,14},{9,15},{10,... | collective-permute-start | bytes 786440 | tf_op jit(solution)/shard_map/ppermute | solution.py:260
  75.2 0.8 copy-done.8
  76.0 0.3 copy-done.9
  76.3 37.0 %all_rows.1 = (bf16[1024,1792]{1,0:T(8,128)(2,1)}, bf16[1024,1792]{1,0:T(8,128)(2,1)}, bf16[1792,1024]{1,0:T(8,128)(2,1)}) custom-call(s32[1]{0:T(128)} %bitcast.refs_0_, bf16[2,48,4096]{2,1,0:T(8,128)(2,1)} %copy-done.4, bf16[2,48,4096]{2,1,0:T(8,128)(2,1)} %copy-done.5, bf16[2,48,4096]{2,1,0:T(8,128)(2,1)} %copy-done.6, bf16[2,48,4096]{2,1,0:T(8,128)(2,1)} %copy-done.7, ...), custom_call_target="tpu_custom_call" | custom-call | flops 22548578304 | bytes 55050240 | tf_op jit(solution)/shard_map/all_rows/pallas_call | solution.py:211
  113.5 0.2 fusion.2
  113.7 0.8 fusion.6
  (58 shorter events, 0.7 us)
Async XLA Ops:
  2.5 15.0 %collective-permute-start = (bf16[2,16,4096]{2,1,0:T(8,128)(2,1)}, bf16[2,16,4096]{2,1,0:T(8,128)(2,1)S(1)}, u32[]{:S(2)}, u32[]{:S(2)}) collective-permute-start(bf16[2,16,4096]{2,1,0:T(8,128)(2,1)} %normalize.1.refs_1_), channel_id=1, source_target_pairs={{0,2},{1,3},{2,0},{3,1},{4,6},{5,7},{6,4},{7,5},{8,10},{9,11},{10,... | collective-permute-start | bytes 786440 | tf_op jit(solution)/shard_map/ppermute | solution.py:260
  5.5 14.6 %collective-permute-start.1 = (bf16[2,16,4096]{2,1,0:T(8,128)(2,1)}, bf16[2,16,4096]{2,1,0:T(8,128)(2,1)S(1)}, u32[]{:S(2)}, u32[]{:S(2)}) collective-permute-start(bf16[2,16,4096]{2,1,0:T(8,128)(2,1)} %normalize.1.refs_1_), channel_id=1, source_target_pairs={{0,4},{1,5},{2,6},{3,7},{4,0},{5,1},{6,2},{7,3},{8,12},{9,13},{10,... | collective-permute-start | bytes 786440 | tf_op jit(solution)/shard_map/ppermute | solution.py:260
  8.1 12.0 %collective-permute-start.2 = (bf16[2,16,4096]{2,1,0:T(8,128)(2,1)}, bf16[2,16,4096]{2,1,0:T(8,128)(2,1)S(1)}, u32[]{:S(2)}, u32[]{:S(2)}) collective-permute-start(bf16[2,16,4096]{2,1,0:T(8,128)(2,1)} %normalize.1.refs_1_), channel_id=1, source_target_pairs={{0,8},{1,9},{2,10},{3,11},{4,12},{5,13},{6,14},{7,15},{8,0},{9,1},... | collective-permute-start | bytes 786440 | tf_op jit(solution)/shard_map/ppermute | solution.py:260
  9.6 13.0 %collective-permute-start.3 = (bf16[2,16,4096]{2,1,0:T(8,128)(2,1)}, bf16[2,16,4096]{2,1,0:T(8,128)(2,1)S(1)}, u32[]{:S(2)}, u32[]{:S(2)}) collective-permute-start(bf16[2,16,4096]{2,1,0:T(8,128)(2,1)} %normalize.1.refs_1_), channel_id=1, source_target_pairs={{0,16},{1,17},{2,18},{3,19},{4,20},{5,21},{6,22},{7,23},{8,24},{9,... | collective-permute-start | bytes 786440 | tf_op jit(solution)/shard_map/ppermute | solution.py:260
  11.1 11.5 %collective-permute-start.4 = (bf16[2,16,4096]{2,1,0:T(8,128)(2,1)}, bf16[2,16,4096]{2,1,0:T(8,128)(2,1)S(1)}, u32[]{:S(2)}, u32[]{:S(2)}) collective-permute-start(bf16[2,16,4096]{2,1,0:T(8,128)(2,1)} %normalize.1.refs_1_), channel_id=1, source_target_pairs={{0,24},{1,25},{2,26},{3,27},{4,28},{5,29},{6,30},{7,31},{8,16},{9,... | collective-permute-start | bytes 786440 | tf_op jit(solution)/shard_map/ppermute | solution.py:260
  17.5 5.1 %collective-permute-start.5 = (bf16[2,16,4096]{2,1,0:T(8,128)(2,1)}, bf16[2,16,4096]{2,1,0:T(8,128)(2,1)S(1)}, u32[]{:S(2)}, u32[]{:S(2)}) collective-permute-start(bf16[2,16,4096]{2,1,0:T(8,128)(2,1)} %normalize.1.refs_1_), channel_id=1, source_target_pairs={{0,1},{1,0},{2,3},{3,2},{4,5},{5,4},{6,7},{7,6},{8,9},{9,8},{10,11... | collective-permute-start | bytes 786440 | tf_op jit(solution)/shard_map/ppermute | solution.py:260
  20.0 2.6 %collective-permute-start.6 = (bf16[2,16,4096]{2,1,0:T(8,128)(2,1)S(1)}, bf16[2,16,4096]{2,1,0:T(8,128)(2,1)S(1)}, u32[]{:S(2)}, u32[]{:S(2)}) collective-permute-start(bf16[2,16,4096]{2,1,0:T(8,128)(2,1)S(1)} %collective-permute-done.refs_2_), channel_id=1, source_target_pairs={{0,1},{1,0},{2,3},{3,2},{4,5},{5,4},{6,7},{7,6},{8,9},{9,8},{10,11... | collective-permute-start | bytes 786440 | tf_op jit(solution)/shard_map/ppermute | solution.py:260
  20.1 47.1 %copy-start.10 = (bf16[2,16,4096]{2,1,0:T(8,128)(2,1)}, bf16[2,16,4096]{2,1,0:T(8,128)(2,1)S(1)}, u32[]{:S(2)}) copy-start(bf16[2,16,4096]{2,1,0:T(8,128)(2,1)S(1)} %collective-permute-done.2.refs_7_) | copy-start | bytes 786436
  20.1 8.7 %collective-permute-start.7 = (bf16[2,16,4096]{2,1,0:T(8,128)(2,1)S(1)}, bf16[2,16,4096]{2,1,0:T(8,128)(2,1)S(1)}, u32[]{:S(2)}, u32[]{:S(2)}) collective-permute-start(bf16[2,16,4096]{2,1,0:T(8,128)(2,1)S(1)} %collective-permute-done.1), channel_id=1, source_target_pairs={{0,2},{1,3},{2,0},{3,1},{4,6},{5,7},{6,4},{7,5},{8,10},{9,11},{10,... | collective-permute-start | bytes 786440 | tf_op jit(solution)/shard_map/ppermute | solution.py:260
  22.6 45.1 %copy-start.11 = (bf16[2,16,4096]{2,1,0:T(8,128)(2,1)}, bf16[2,16,4096]{2,1,0:T(8,128)(2,1)S(1)}, u32[]{:S(2)}) copy-start(bf16[2,16,4096]{2,1,0:T(8,128)(2,1)S(1)} %collective-permute-done.3.refs_8_) | copy-start | bytes 786436
  22.6 45.2 %copy-start.12 = (bf16[2,16,4096]{2,1,0:T(8,128)(2,1)}, bf16[2,16,4096]{2,1,0:T(8,128)(2,1)S(1)}, u32[]{:S(2)}) copy-start(bf16[2,16,4096]{2,1,0:T(8,128)(2,1)S(1)} %collective-permute-done.4.refs_9_) | copy-start | bytes 786436
  28.8 3.6 %collective-permute-start.8 = (bf16[2,32,4096]{2,1,0:T(8,128)(2,1)S(1)}, bf16[2,32,4096]{2,1,0:T(8,128)(2,1)S(1)}, u32[]{:S(2)}, u32[]{:S(2)}) collective-permute-start(bf16[2,32,4096]{2,1,0:T(8,128)(2,1)S(1)} %get-tuple-element.63.refs_3_), channel_id=1, source_target_pairs={{0,1},{1,0},{2,3},{3,2},{4,5},{5,4},{6,7},{7,6},{8,9},{9,8},{10,11... | collective-permute-start | bytes 1572872 | tf_op jit(solution)/shard_map/ppermute | solution.py:260
  28.9 29.5 %collective-permute-start.9 = (bf16[2,48,4096]{2,1,0:T(8,128)(2,1)S(1)}, bf16[2,48,4096]{2,1,0:T(8,128)(2,1)S(1)}, u32[]{:S(2)}, u32[]{:S(2)}) collective-permute-start(bf16[2,48,4096]{2,1,0:T(8,128)(2,1)S(1)} %get-tuple-element.62), channel_id=1, source_target_pairs={{0,8},{1,9},{2,10},{3,11},{4,12},{5,13},{6,14},{7,15},{8,0},{9,1},... | collective-permute-start | bytes 2359304 | tf_op jit(solution)/shard_map/ppermute | solution.py:260
  30.5 36.5 %collective-permute-start.10 = (bf16[2,48,4096]{2,1,0:T(8,128)(2,1)S(1)}, bf16[2,48,4096]{2,1,0:T(8,128)(2,1)S(1)}, u32[]{:S(2)}, u32[]{:S(2)}) collective-permute-start(bf16[2,48,4096]{2,1,0:T(8,128)(2,1)S(1)} %get-tuple-element.62), channel_id=1, source_target_pairs={{0,16},{1,17},{2,18},{3,19},{4,20},{5,21},{6,22},{7,23},{8,24},{9,... | collective-permute-start | bytes 2359304 | tf_op jit(solution)/shard_map/ppermute | solution.py:260
  32.0 34.9 %collective-permute-start.11 = (bf16[2,48,4096]{2,1,0:T(8,128)(2,1)S(1)}, bf16[2,48,4096]{2,1,0:T(8,128)(2,1)S(1)}, u32[]{:S(2)}, u32[]{:S(2)}) collective-permute-start(bf16[2,48,4096]{2,1,0:T(8,128)(2,1)S(1)} %get-tuple-element.62), channel_id=1, source_target_pairs={{0,24},{1,25},{2,26},{3,27},{4,28},{5,29},{6,30},{7,31},{8,16},{9,... | collective-permute-start | bytes 2359304 | tf_op jit(solution)/shard_map/ppermute | solution.py:260
  33.4 33.6 %copy-start.1 = (bf16[16,4096]{1,0:T(8,128)(2,1)S(1)}, bf16[16,4096]{1,0:T(8,128)(2,1)}, u32[]{:S(2)}) copy-start(bf16[16,4096]{1,0:T(8,128)(2,1)} %tokens.1) | copy-start | bytes 393220
  58.4 16.7 %copy-start.4 = (bf16[2,48,4096]{2,1,0:T(8,128)(2,1)}, bf16[2,48,4096]{2,1,0:T(8,128)(2,1)S(1)}, u32[]{:S(2)}) copy-start(bf16[2,48,4096]{2,1,0:T(8,128)(2,1)S(1)} %collective-permute-done.9.refs_1_) | copy-start | bytes 2359300
  66.9 8.2 %copy-start.5 = (bf16[2,48,4096]{2,1,0:T(8,128)(2,1)}, bf16[2,48,4096]{2,1,0:T(8,128)(2,1)S(1)}, u32[]{:S(2)}) copy-start(bf16[2,48,4096]{2,1,0:T(8,128)(2,1)S(1)} %collective-permute-done.10.refs_2_) | copy-start | bytes 2359300
  66.9 8.2 %copy-start.6 = (bf16[2,48,4096]{2,1,0:T(8,128)(2,1)}, bf16[2,48,4096]{2,1,0:T(8,128)(2,1)S(1)}, u32[]{:S(2)}) copy-start(bf16[2,48,4096]{2,1,0:T(8,128)(2,1)S(1)} %collective-permute-done.11.refs_3_) | copy-start | bytes 2359300
  66.9 2.7 %collective-permute-start.12 = (bf16[2,64,4096]{2,1,0:T(8,128)(2,1)S(1)}, bf16[2,64,4096]{2,1,0:T(8,128)(2,1)S(1)}, u32[]{:S(2)}, u32[]{:S(2)}) collective-permute-start(bf16[2,64,4096]{2,1,0:T(8,128)(2,1)S(1)} %get-tuple-element.37), channel_id=1, source_target_pairs={{0,1},{1,0},{2,3},{3,2},{4,5},{5,4},{6,7},{7,6},{8,9},{9,8},{10,11... | collective-permute-start | bytes 3145736 | tf_op jit(solution)/shard_map/ppermute | solution.py:260
  67.2 2.9 %collective-permute-start.19 = (bf16[2,16,4096]{2,1,0:T(8,128)(2,1)S(1)}, bf16[2,16,4096]{2,1,0:T(8,128)(2,1)S(1)}, u32[]{:S(2)}, u32[]{:S(2)}) collective-permute-start(bf16[2,16,4096]{2,1,0:T(8,128)(2,1)S(1)} %collective-permute-done.2.refs_7_), channel_id=1, source_target_pairs={{0,1},{1,0},{2,3},{3,2},{4,5},{5,4},{6,7},{7,6},{8,9},{9,8},{10,11... | collective-permute-start | bytes 786440 | tf_op jit(solution)/shard_map/ppermute | solution.py:260
  67.7 2.9 %collective-permute-start.20 = (bf16[2,16,4096]{2,1,0:T(8,128)(2,1)S(1)}, bf16[2,16,4096]{2,1,0:T(8,128)(2,1)S(1)}, u32[]{:S(2)}, u32[]{:S(2)}) collective-permute-start(bf16[2,16,4096]{2,1,0:T(8,128)(2,1)S(1)} %collective-permute-done.3.refs_8_), channel_id=1, source_target_pairs={{0,1},{1,0},{2,3},{3,2},{4,5},{5,4},{6,7},{7,6},{8,9},{9,8},{10,11... | collective-permute-start | bytes 786440 | tf_op jit(solution)/shard_map/ppermute | solution.py:260
  67.8 3.3 %collective-permute-start.21 = (bf16[2,16,4096]{2,1,0:T(8,128)(2,1)S(1)}, bf16[2,16,4096]{2,1,0:T(8,128)(2,1)S(1)}, u32[]{:S(2)}, u32[]{:S(2)}) collective-permute-start(bf16[2,16,4096]{2,1,0:T(8,128)(2,1)S(1)} %collective-permute-done.4.refs_9_), channel_id=1, source_target_pairs={{0,1},{1,0},{2,3},{3,2},{4,5},{5,4},{6,7},{7,6},{8,9},{9,8},{10,11... | collective-permute-start | bytes 786440 | tf_op jit(solution)/shard_map/ppermute | solution.py:260
  68.2 5.5 %collective-permute-start.16 = (bf16[2,48,4096]{2,1,0:T(8,128)(2,1)S(1)}, bf16[2,48,4096]{2,1,0:T(8,128)(2,1)S(1)}, u32[]{:S(2)}, u32[]{:S(2)}) collective-permute-start(bf16[2,48,4096]{2,1,0:T(8,128)(2,1)S(1)} %collective-permute-done.9.refs_1_), channel_id=1, source_target_pairs={{0,1},{1,0},{2,3},{3,2},{4,5},{5,4},{6,7},{7,6},{8,9},{9,8},{10,11... | collective-permute-start | bytes 2359304 | tf_op jit(solution)/shard_map/ppermute | solution.py:260
  69.6 5.5 %collective-permute-start.17 = (bf16[2,48,4096]{2,1,0:T(8,128)(2,1)S(1)}, bf16[2,48,4096]{2,1,0:T(8,128)(2,1)S(1)}, u32[]{:S(2)}, u32[]{:S(2)}) collective-permute-start(bf16[2,48,4096]{2,1,0:T(8,128)(2,1)S(1)} %collective-permute-done.10.refs_2_), channel_id=1, source_target_pairs={{0,1},{1,0},{2,3},{3,2},{4,5},{5,4},{6,7},{7,6},{8,9},{9,8},{10,11... | collective-permute-start | bytes 2359304 | tf_op jit(solution)/shard_map/ppermute | solution.py:260
  70.1 5.0 %copy-start.13 = (bf16[2,16,4096]{2,1,0:T(8,128)(2,1)}, bf16[2,16,4096]{2,1,0:T(8,128)(2,1)S(1)}, u32[]{:S(2)}) copy-start(bf16[2,16,4096]{2,1,0:T(8,128)(2,1)S(1)} %collective-permute-done.19.refs_10_) | copy-start | bytes 786436
  70.1 5.0 %collective-permute-start.18 = (bf16[2,48,4096]{2,1,0:T(8,128)(2,1)S(1)}, bf16[2,48,4096]{2,1,0:T(8,128)(2,1)S(1)}, u32[]{:S(2)}, u32[]{:S(2)}) collective-permute-start(bf16[2,48,4096]{2,1,0:T(8,128)(2,1)S(1)} %collective-permute-done.11.refs_3_), channel_id=1, source_target_pairs={{0,1},{1,0},{2,3},{3,2},{4,5},{5,4},{6,7},{7,6},{8,9},{9,8},{10,11... | collective-permute-start | bytes 2359304 | tf_op jit(solution)/shard_map/ppermute | solution.py:260
  70.6 42.7 %collective-permute-start.13 = (bf16[2,16,4096]{2,1,0:T(8,128)(2,1)S(1)}, bf16[2,16,4096]{2,1,0:T(8,128)(2,1)S(1)}, u32[]{:S(2)}, u32[]{:S(2)}) collective-permute-start(bf16[2,16,4096]{2,1,0:T(8,128)(2,1)S(1)} %get-tuple-element.59), channel_id=1, source_target_pairs={{0,2},{1,3},{2,0},{3,1},{4,6},{5,7},{6,4},{7,5},{8,10},{9,11},{10,... | collective-permute-start | bytes 786440 | tf_op jit(solution)/shard_map/ppermute | solution.py:260
  71.1 42.2 %collective-permute-start.14 = (bf16[2,16,4096]{2,1,0:T(8,128)(2,1)S(1)}, bf16[2,16,4096]{2,1,0:T(8,128)(2,1)S(1)}, u32[]{:S(2)}, u32[]{:S(2)}) collective-permute-start(bf16[2,16,4096]{2,1,0:T(8,128)(2,1)S(1)} %get-tuple-element.58), channel_id=1, source_target_pairs={{0,4},{1,5},{2,6},{3,7},{4,0},{5,1},{6,2},{7,3},{8,12},{9,13},{10,... | collective-permute-start | bytes 786440 | tf_op jit(solution)/shard_map/ppermute | solution.py:260
  73.7 39.6 %collective-permute-start.15 = (bf16[2,16,4096]{2,1,0:T(8,128)(2,1)S(1)}, bf16[2,16,4096]{2,1,0:T(8,128)(2,1)S(1)}, u32[]{:S(2)}, u32[]{:S(2)}) collective-permute-start(bf16[2,16,4096]{2,1,0:T(8,128)(2,1)S(1)} %get-tuple-element.57), channel_id=1, source_target_pairs={{0,6},{1,7},{2,4},{3,5},{4,2},{5,3},{6,0},{7,1},{8,14},{9,15},{10,... | collective-permute-start | bytes 786440 | tf_op jit(solution)/shard_map/ppermute | solution.py:260
  76.3 37.2 %copy-start.3 = (f32[4096]{0:T(1024)S(1)}, f32[4096]{0:T(1024)}, u32[]{:S(2)}) copy-start(f32[4096]{0:T(1024)} %param.7) | copy-start | bytes 49156
  76.3 37.5 %copy-start.2 = (bf16[16,4096]{1,0:T(8,128)(2,1)S(1)}, bf16[16,4096]{1,0:T(8,128)(2,1)}, u32[]{:S(2)}) copy-start(bf16[16,4096]{1,0:T(8,128)(2,1)} %cotangent.1) | copy-start | bytes 393220
  (6 other events, 13.0 us)

commit v10 on v9

--- a/solution.py
+++ b/solution.py
@@ -24,11 +24,14 @@
 CHUNK = 1024
 
 
+def project_back(grad_out_t, down_weight):
+    return jnp.dot(down_weight, grad_out_t, preferred_element_type=jnp.float32).T
+
+
 def project(normed, grad_out_t, gate_weight, up_weight, down_weight):
     gate = jnp.dot(normed, gate_weight, preferred_element_type=jnp.float32)
     lifted = jnp.dot(normed, up_weight, preferred_element_type=jnp.float32)
-    grad_hidden = jnp.dot(down_weight, grad_out_t, preferred_element_type=jnp.float32).T
-    return gate, lifted, grad_hidden
+    return gate, lifted, project_back(grad_out_t, down_weight)
 
 
 def activations(gate, lifted, grad_hidden):
@@ -45,11 +48,18 @@
 def pack(pieces, rows, arrived):
     copies, at = [], 0
     for i, piece in enumerate(pieces):
-        height = piece.shape[1]
-        copies.append(pltpu.make_async_copy(piece, rows.at[:, pl.ds(at, height)], arrived.at[i]))
-        at += height
-    for copy in copies:
+        here = pl.ds(at, piece.shape[1])
+        copies.append(
+            [pltpu.make_async_copy(piece.at[j], rows.at[j, here], arrived.at[j, i]) for j in (0, 1)]
+        )
+        at += piece.shape[1]
+    normed, grad_out = zip(*copies)
+    for copy in normed + grad_out:
         copy.start()
+    return normed, grad_out
+
+
+def wait(copies):
     for copy in copies:
         copy.wait()
 
@@ -89,7 +99,8 @@
 
     @pl.when(step == 0)
     def _():
-        pack(pieces, rows, arrived)
+        for copies in pack(pieces, rows, arrived):
+            wait(copies)
         width = columns.shape[2]
         columns[...] = rows[:, :, pl.ds(pl.multiple_of(replica[0] * width, 128), width)]
         grad_out_t[...] = rows[1].T
@@ -141,7 +152,7 @@
             pltpu.VMEM((depth, count), jnp.bfloat16),
             pltpu.VMEM((count, depth), jnp.float32),
             pltpu.VMEM((depth, count), jnp.float32),
-            pltpu.SemaphoreType.DMA((len(pieces),)),
+            pltpu.SemaphoreType.DMA((2, len(pieces))),
         ],
         compiler_params=pltpu.CompilerParams(vmem_limit_bytes=28 * 2**20),
         cost_estimate=pl.CostEstimate(
@@ -150,7 +161,7 @@
             transcendentals=count * hidden_units,
         ),
         name="own_rows",
-    )(replica, *pieces, *in_hbm(gate_weight, up_weight, down_weight))
+    )(replica, *in_hbm(pieces[0]), *pieces[1:], *in_hbm(gate_weight, up_weight, down_weight))
 
 
 def all_kernel(n_pieces, *refs):
@@ -161,16 +172,6 @@
     step, last = pl.program_id(0), pl.num_programs(0) - 1
     ahead = own_columns.shape[1]
     width = normed_t.shape[0]
-
-    @pl.when(step == 0)
-    def _():
-        columns = pl.ds(pl.multiple_of(replica[0] * width, 128), width)
-        pack(pieces, rows, arrived)
-        grad_out_t[...] = rows[1].T
-        normed_t[:, :ahead] = own_columns[0].T
-        normed_t[:, ahead:] = rows[0, :, columns].T
-        grad_out[:ahead] = own_columns[1]
-        grad_out[ahead:] = rows[1, :, columns]
 
     def weight_gradients():
         grad_gate[...] = jnp.dot(
@@ -183,16 +184,36 @@
             hidden[...].T, grad_out[...], preferred_element_type=jnp.float32
         ).astype(grad_down.dtype)
 
-    @pl.when(step < last)
+    def fill(gate, lifted, grad_hidden):
+        hidden[:ahead] = own_hidden[...]
+        grad_pre[:ahead] = own_grad_pre[...]
+        grad_lifted[:ahead] = own_grad_lifted[...]
+        hidden[ahead:], grad_pre[ahead:], grad_lifted[ahead:] = activations(
+            gate, lifted, grad_hidden
+        )
+
+    @pl.when(step == 0)
+    def _():
+        columns = pl.ds(pl.multiple_of(replica[0] * width, 128), width)
+        normed_copies, grad_out_copies = pack(pieces, rows, arrived)
+        normed_t[:, :ahead] = own_columns[0].T
+        grad_out[:ahead] = own_columns[1]
+        wait(normed_copies)
+        gate = jnp.dot(rows[0], gate_weight[...], preferred_element_type=jnp.float32)
+        lifted = jnp.dot(rows[0], up_weight[...], preferred_element_type=jnp.float32)
+        normed_t[:, ahead:] = rows[0, :, columns].T
+        wait(grad_out_copies)
+        grad_out_t[...] = rows[1].T
+        grad_out[ahead:] = rows[1, :, columns]
+        fill(gate, lifted, project_back(grad_out_t[...], down_weight[...]))
+
+    @pl.when((step > 0) & (step < last))
     def _():
         products = project(
             rows[0], grad_out_t[...], gate_weight[...], up_weight[...], down_weight[...]
         )
         weight_gradients()
-        hidden[:ahead] = own_hidden[...]
-        grad_pre[:ahead] = own_grad_pre[...]
-        grad_lifted[:ahead] = own_grad_lifted[...]
-        hidden[ahead:], grad_pre[ahead:], grad_lifted[ahead:] = activations(*products)
+        fill(*products)
 
     @pl.when(step == last)
     def _():
@@ -233,7 +254,7 @@
             pltpu.VMEM((count, TILE), jnp.bfloat16),
             pltpu.VMEM((count, TILE), jnp.bfloat16),
             pltpu.VMEM((count, TILE), jnp.bfloat16),
-            pltpu.SemaphoreType.DMA((len(pieces),)),
+            pltpu.SemaphoreType.DMA((2, len(pieces))),
         ],
         compiler_params=pltpu.CompilerParams(vmem_limit_bytes=32 * 2**20),
         cost_estimate=pl.CostEstimate(
@@ -269,20 +290,26 @@
     unit_input = expanded_hidden * reciprocal_root_mean
     unit0 = normalize(tokens, norm_scale_vector, cotangent)
     unit2, unit1 = swap(unit0, 0, 4), swap(unit0, 0, 2)
-    across = [swap(unit0, b, 0) for b in range(1, n_dp)]
+    across0 = [swap(unit0, 1, 0), swap(unit0, 2, 0)]
+    unit2, unit1, across0, far_unit0, again0 = lax.optimization_barrier(
+        (unit2, unit1, across0, swap(unit0, 0, 1), unit0)
+    )
     unit3 = swap(unit2, 0, 2)
-    far_units, far_across = far([unit0, unit1]), far(across)
-    across, far_units, unit3 = lax.optimization_barrier((across, far_units, unit3))
+    across1 = [swap(unit1, 1, 0), swap(unit1, 2, 0), swap(again0, 3, 0)]
+    far_unit1, far_across0 = swap(unit1, 0, 1), far(across0)
+    unit3, across1, far_unit1, far_across0 = lax.optimization_barrier(
+        (unit3, across1, far_unit1, far_across0)
+    )
     last = jnp.concatenate([unit2, unit3], axis=1)
     late = jnp.concatenate([unit1, unit2, unit3], axis=1)
-    own = [unit0, unit1, last] + far_units + [swap(last, 0, 1)]
-    rest = [swap(late, b, 0) for b in range(1, n_dp)]
+    own = [unit0, unit1, last, far_unit0, far_unit1, swap(last, 0, 1)]
+    rest = [swap(last, 1, 0), swap(last, 2, 0), swap(late, 3, 0)]
     *units, own_columns, kept, sent = own_rows(
         replica, n_dp, own, gate_weight, up_weight, down_weight
     )
     kept, sent, rest = lax.optimization_barrier((kept, sent, rest))
     pair = (kept.astype(jnp.float32) + swap(sent, 0, 1).astype(jnp.float32)).astype(jnp.bfloat16)
-    rest += far(rest) + across + far_across
+    rest += across1 + far(across1 + rest) + across0 + far_across0
     parts = [swap(pair[:, k * rows : (k + 1) * rows], 0, 2 * k) for k in range(1, n_tp // 2)]
     weight_gradients = all_rows(
         replica, rest, units, own_columns, gate_weight, up_weight, down_weight

time: 115 us -> 114 us (level)
  waiting for transfers between devices: 26.4 us -> 21 us
  starting transfers between devices: 19.5 us -> 23.9 us
    ppermute x22 -> x26, waiting for transfers between devices: 26.4 us -> 21 us  [swap(): return lax.ppermute(array, ('dp', 'tp'), pairs)]
    ppermute x22 -> x26, starting transfers between devices: 19.5 us -> 23.9 us  [swap(): return lax.ppermute(array, ('dp', 'tp'), pairs)]
    pallas_call x1, Pallas kernels: 37 us -> 34.8 us  [all_rows(): pl.pallas_call(functools.partial(all_kernel, len(pieces)), grid=(tiles +...]
    pallas_call x1, Pallas kernels: 25 us -> 27 us  [own_rows(): pl.pallas_call(functools.partial(own_kernel, len(pieces)), grid=(hidden_u...]
    unnamed x34 -> x41, local copies, waits for them, and re-layouts: 2.11 us -> 2.61 us
  transfers between devices with their start and end apart: 22 -> 26, of which waited for: 6 -> 7; matrix products, arithmetic and copies ran while one was open for 0% -> 0% of each run, Pallas kernels for 54% -> 54%
where the time goes in v10:
time: 114 us
  Pallas kernels  63.6 us (56%)
  starting transfers between devices  23.9 us (21%)
  waiting for transfers between devices  21 us (18%)
  local copies, waits for them, and re-layouts  2.68 us (2%)
  other arithmetic  1.61 us (1%)
    pallas_call x1, Pallas kernels, all_rows(): pl.pallas_call(functools.partial(all_kernel, len(pieces)), grid=(tiles +...  34.8 us
    pallas_call x1, Pallas kernels, own_rows(): pl.pallas_call(functools.partial(own_kernel, len(pieces)), grid=(hidden_u...  27 us
    ppermute x26, starting transfers between devices, swap(): return lax.ppermute(array, ('dp', 'tp'), pairs)  23.9 us
    ppermute x26, waiting for transfers between devices, swap(): return lax.ppermute(array, ('dp', 'tp'), pairs)  21 us
    unnamed x41, local copies, waits for them, and re-layouts  2.61 us
  transfers between devices with their start and end apart: 26, of which 7 were waited for; matrix products, arithmetic and copies ran while one was open for 0% of the time, Pallas kernels for 54%

profile of v10, /device:TPU:0, one launch (start us, length us, event | category | flops | bytes accessed | tf_op | source)
XLA Modules:
  0.0 113.7 jit_solution(462912194632164708)
XLA Ops:
  0.6 1.8 %normalize.1.refs_1_ = bf16[2,16,4096]{2,1,0:T(8,128)(2,1)} custom-call(bf16[16,4096]{1,0:T(8,128)(2,1)} %tokens.1, f32[1,4096]{1,0:T(1,128)} %bitcast.14, bf16[16,4096]{1,0:T(8,128)(2,1)} %cotangent.1), custom_call_target="tpu_custom_call" | custom-call | tf_op jit(solution)/shard_map/normalize/pallas_call | solution.py:86
  2.5 4.0 %collective-permute-start = (bf16[2,16,4096]{2,1,0:T(8,128)(2,1)}, bf16[2,16,4096]{2,1,0:T(8,128)(2,1)S(1)}, u32[]{:S(2)}, u32[]{:S(2)}) collective-permute-start(bf16[2,16,4096]{2,1,0:T(8,128)(2,1)} %normalize.1.refs_1_), channel_id=1, source_target_pairs={{0,4},{1,5},{2,6},{3,7},{4,0},{5,1},{6,2},{7,3},{8,12},{9,13},{10,... | collective-permute-start | bytes 786440 | tf_op jit(solution)/shard_map/ppermute | solution.py:281
  6.5 1.6 %collective-permute-start.1 = (bf16[2,16,4096]{2,1,0:T(8,128)(2,1)}, bf16[2,16,4096]{2,1,0:T(8,128)(2,1)S(1)}, u32[]{:S(2)}, u32[]{:S(2)}) collective-permute-start(bf16[2,16,4096]{2,1,0:T(8,128)(2,1)} %normalize.1.refs_1_), channel_id=1, source_target_pairs={{0,2},{1,3},{2,0},{3,1},{4,6},{5,7},{6,4},{7,5},{8,10},{9,11},{10,... | collective-permute-start | bytes 786440 | tf_op jit(solution)/shard_map/ppermute | solution.py:281
  8.1 1.5 %collective-permute-start.2 = (bf16[2,16,4096]{2,1,0:T(8,128)(2,1)}, bf16[2,16,4096]{2,1,0:T(8,128)(2,1)S(1)}, u32[]{:S(2)}, u32[]{:S(2)}) collective-permute-start(bf16[2,16,4096]{2,1,0:T(8,128)(2,1)} %normalize.1.refs_1_), channel_id=1, source_target_pairs={{0,8},{1,9},{2,10},{3,11},{4,12},{5,13},{6,14},{7,15},{8,0},{9,1},... | collective-permute-start | bytes 786440 | tf_op jit(solution)/shard_map/ppermute | solution.py:281
  9.6 1.5 %collective-permute-start.3 = (bf16[2,16,4096]{2,1,0:T(8,128)(2,1)}, bf16[2,16,4096]{2,1,0:T(8,128)(2,1)S(1)}, u32[]{:S(2)}, u32[]{:S(2)}) collective-permute-start(bf16[2,16,4096]{2,1,0:T(8,128)(2,1)} %normalize.1.refs_1_), channel_id=1, source_target_pairs={{0,16},{1,17},{2,18},{3,19},{4,20},{5,21},{6,22},{7,23},{8,24},{9,... | collective-permute-start | bytes 786440 | tf_op jit(solution)/shard_map/ppermute | solution.py:281
  11.1 7.6 %collective-permute-done = bf16[2,16,4096]{2,1,0:T(8,128)(2,1)S(1)} collective-permute-done((bf16[2,16,4096]{2,1,0:T(8,128)(2,1)}, bf16[2,16,4096]{2,1,0:T(8,128)(2,1)S(1)}, u32[]{:S(2)}, u32[]{:S(2)}) %collective-permute-start) | collective-permute-done | bytes 262176 | tf_op jit(solution)/shard_map/ppermute | solution.py:281
  19.0 1.6 %collective-permute-start.5 = (bf16[2,16,4096]{2,1,0:T(8,128)(2,1)S(1)}, bf16[2,16,4096]{2,1,0:T(8,128)(2,1)S(1)}, u32[]{:S(2)}, u32[]{:S(2)}) collective-permute-start(bf16[2,16,4096]{2,1,0:T(8,128)(2,1)S(1)} %collective-permute-done), channel_id=1, source_target_pairs={{0,2},{1,3},{2,0},{3,1},{4,6},{5,7},{6,4},{7,5},{8,10},{9,11},{10,... | collective-permute-start | bytes 786440 | tf_op jit(solution)/shard_map/ppermute | solution.py:281
  20.5 1.5 %collective-permute-start.6 = (bf16[2,16,4096]{2,1,0:T(8,128)(2,1)S(1)}, bf16[2,16,4096]{2,1,0:T(8,128)(2,1)S(1)}, u32[]{:S(2)}, u32[]{:S(2)}) collective-permute-start(bf16[2,16,4096]{2,1,0:T(8,128)(2,1)S(1)} %collective-permute-done.1.refs_2_), channel_id=1, source_target_pairs={{0,8},{1,9},{2,10},{3,11},{4,12},{5,13},{6,14},{7,15},{8,0},{9,1},... | collective-permute-start | bytes 786440 | tf_op jit(solution)/shard_map/ppermute | solution.py:281
  22.0 1.5 %collective-permute-start.7 = (bf16[2,16,4096]{2,1,0:T(8,128)(2,1)S(1)}, bf16[2,16,4096]{2,1,0:T(8,128)(2,1)S(1)}, u32[]{:S(2)}, u32[]{:S(2)}) collective-permute-start(bf16[2,16,4096]{2,1,0:T(8,128)(2,1)S(1)} %collective-permute-done.1.refs_2_), channel_id=1, source_target_pairs={{0,16},{1,17},{2,18},{3,19},{4,20},{5,21},{6,22},{7,23},{8,24},{9,... | collective-permute-start | bytes 786440 | tf_op jit(solution)/shard_map/ppermute | solution.py:281
  23.5 0.5 collective-permute-start.8
  24.0 2.3 %collective-permute-done.5 = bf16[2,16,4096]{2,1,0:T(8,128)(2,1)S(1)} collective-permute-done((bf16[2,16,4096]{2,1,0:T(8,128)(2,1)S(1)}, bf16[2,16,4096]{2,1,0:T(8,128)(2,1)S(1)}, u32[]{:S(2)}, u32[]{:S(2)}) %collective-permute-start.5) | collective-permute-done | bytes 262176 | tf_op jit(solution)/shard_map/ppermute | solution.py:281
  26.3 1.9 %collective-permute-done.6.refs_4_ = bf16[2,16,4096]{2,1,0:T(8,128)(2,1)S(1)} collective-permute-done((bf16[2,16,4096]{2,1,0:T(8,128)(2,1)S(1)}, bf16[2,16,4096]{2,1,0:T(8,128)(2,1)S(1)}, u32[]{:S(2)}, u32[]{:S(2)}) %collective-permute-start.6) | collective-permute-done | bytes 262176 | tf_op jit(solution)/shard_map/ppermute | solution.py:281
  28.2 6.1 %collective-permute-done.7.refs_5_ = bf16[2,16,4096]{2,1,0:T(8,128)(2,1)S(1)} collective-permute-done((bf16[2,16,4096]{2,1,0:T(8,128)(2,1)S(1)}, bf16[2,16,4096]{2,1,0:T(8,128)(2,1)S(1)}, u32[]{:S(2)}, u32[]{:S(2)}) %collective-permute-start.7) | collective-permute-done | bytes 262176 | tf_op jit(solution)/shard_map/ppermute | solution.py:281
  34.4 0.7 copy-done.13
  35.2 0.7 copy-done.16
  35.9 1.2 %collective-permute-start.13 = (bf16[2,32,4096]{2,1,0:T(8,128)(2,1)S(1)}, bf16[2,32,4096]{2,1,0:T(8,128)(2,1)S(1)}, u32[]{:S(2)}, u32[]{:S(2)}) collective-permute-start(bf16[2,32,4096]{2,1,0:T(8,128)(2,1)S(1)} %constant_dynamic-update-slice_fusion.refs_3_), channel_id=1, source_target_pairs={{0,8},{1,9},{2,10},{3,11},{4,12},{5,13},{6,14},{7,15},{8,0},{9,1},... | collective-permute-start | bytes 1572872 | tf_op jit(solution)/shard_map/ppermute | solution.py:281
  37.1 0.8 collective-permute-start.14
  38.0 1.5 %collective-permute-start.15 = (bf16[2,48,4096]{2,1,0:T(8,128)(2,1)S(1)}, bf16[2,48,4096]{2,1,0:T(8,128)(2,1)S(1)}, u32[]{:S(2)}, u32[]{:S(2)}) collective-permute-start(bf16[2,48,4096]{2,1,0:T(8,128)(2,1)S(1)} %pad_maximum_fusion), channel_id=1, source_target_pairs={{0,24},{1,25},{2,26},{3,27},{4,28},{5,29},{6,30},{7,31},{8,16},{9,... | collective-permute-start | bytes 2359304 | tf_op jit(solution)/shard_map/ppermute | solution.py:281
  39.5 27.0 %own_rows.1 = (bf16[128,1792]{1,0:T(8,128)(2,1)}, bf16[128,1792]{1,0:T(8,128)(2,1)}, bf16[128,1792]{1,0:T(8,128)(2,1)}, bf16[2,128,1024]{2,1,0:T(8,128)(2,1)}, b...) custom-call(s32[1]{0:T(128)} %bitcast.refs_0_, bf16[2,16,4096]{2,1,0:T(8,128)(2,1)} %normalize.1.refs_1_, ...), custom_call_target="tpu_custom_call" | custom-call | flops 11274289152 | bytes 44040192 | tf_op jit(solution)/shard_map/own_rows/pallas_call | solution.py:142
  66.6 1.5 %collective-permute-done.15.refs_3_ = bf16[2,48,4096]{2,1,0:T(8,128)(2,1)S(1)} collective-permute-done((bf16[2,48,4096]{2,1,0:T(8,128)(2,1)S(1)}, bf16[2,48,4096]{2,1,0:T(8,128)(2,1)S(1)}, u32[]{:S(2)}, u32[]{:S(2)}) %collective-permute-start.15) | collective-permute-done | bytes 786464 | tf_op jit(solution)/shard_map/ppermute | solution.py:281
  68.2 0.6 collective-permute-start.20
  68.9 0.4 collective-permute-start.22
  69.4 1.3 %collective-permute-done.16 = bf16[2,64,4096]{2,1,0:T(8,128)(2,1)S(1)} collective-permute-done((bf16[2,64,4096]{2,1,0:T(8,128)(2,1)S(1)}, bf16[2,64,4096]{2,1,0:T(8,128)(2,1)S(1)}, u32[]{:S(2)}, u32[]{:S(2)}) %collective-permute-start.16) | collective-permute-done | bytes 1048608 | tf_op jit(solution)/shard_map/ppermute | solution.py:281
  70.9 0.2 add_convert_fusion
  71.1 0.4 collective-permute-start.25
  71.7 0.4 collective-permute-start.17
  72.1 3.3 %collective-permute-start.18 = (bf16[2,16,4096]{2,1,0:T(8,128)(2,1)S(1)}, bf16[2,16,4096]{2,1,0:T(8,128)(2,1)S(1)}, u32[]{:S(2)}, u32[]{:S(2)}) collective-permute-start(bf16[2,16,4096]{2,1,0:T(8,128)(2,1)S(1)} %get-tuple-element.72), channel_id=1, source_target_pairs={{0,4},{1,5},{2,6},{3,7},{4,0},{5,1},{6,2},{7,3},{8,12},{9,13},{10,... | collective-permute-start | bytes 786440 | tf_op jit(solution)/shard_map/ppermute | solution.py:281
  75.4 1.2 %collective-permute-start.19 = (bf16[2,16,4096]{2,1,0:T(8,128)(2,1)S(1)}, bf16[2,16,4096]{2,1,0:T(8,128)(2,1)S(1)}, u32[]{:S(2)}, u32[]{:S(2)}) collective-permute-start(bf16[2,16,4096]{2,1,0:T(8,128)(2,1)S(1)} %get-tuple-element.71), channel_id=1, source_target_pairs={{0,6},{1,7},{2,4},{3,5},{4,2},{5,3},{6,0},{7,1},{8,14},{9,15},{10,... | collective-permute-start | bytes 786440 | tf_op jit(solution)/shard_map/ppermute | solution.py:281
  76.7 0.7 copy-done.8
  77.4 0.3 copy-done.4
  77.7 34.8 %all_rows.1 = (bf16[1024,1792]{1,0:T(8,128)(2,1)}, bf16[1024,1792]{1,0:T(8,128)(2,1)}, bf16[1792,1024]{1,0:T(8,128)(2,1)}) custom-call(s32[1]{0:T(128)} %bitcast.refs_0_, bf16[2,32,4096]{2,1,0:T(8,128)(2,1)} %copy-done.5, bf16[2,32,4096]{2,1,0:T(8,128)(2,1)} %copy-done.6, bf16[2,48,4096]{2,1,0:T(8,128)(2,1)} %copy-done.3, bf16[2,16,4096]{2,1,0:T(8,128)(2,1)} %copy-done.11, ...), custom_call_target="tpu_custom_call" | custom-call | flops 22548578304 | bytes 55050240 | tf_op jit(solution)/shard_map/all_rows/pallas_call | solution.py:232
  112.9 0.8 fusion.6
  (74 shorter events, 1.4 us)
Async XLA Ops:
  2.5 16.3 %collective-permute-start = (bf16[2,16,4096]{2,1,0:T(8,128)(2,1)}, bf16[2,16,4096]{2,1,0:T(8,128)(2,1)S(1)}, u32[]{:S(2)}, u32[]{:S(2)}) collective-permute-start(bf16[2,16,4096]{2,1,0:T(8,128)(2,1)} %normalize.1.refs_1_), channel_id=1, source_target_pairs={{0,4},{1,5},{2,6},{3,7},{4,0},{5,1},{6,2},{7,3},{8,12},{9,13},{10,... | collective-permute-start | bytes 786440 | tf_op jit(solution)/shard_map/ppermute | solution.py:281
  6.5 12.4 %collective-permute-start.1 = (bf16[2,16,4096]{2,1,0:T(8,128)(2,1)}, bf16[2,16,4096]{2,1,0:T(8,128)(2,1)S(1)}, u32[]{:S(2)}, u32[]{:S(2)}) collective-permute-start(bf16[2,16,4096]{2,1,0:T(8,128)(2,1)} %normalize.1.refs_1_), channel_id=1, source_target_pairs={{0,2},{1,3},{2,0},{3,1},{4,6},{5,7},{6,4},{7,5},{8,10},{9,11},{10,... | collective-permute-start | bytes 786440 | tf_op jit(solution)/shard_map/ppermute | solution.py:281
  8.1 10.9 %collective-permute-start.2 = (bf16[2,16,4096]{2,1,0:T(8,128)(2,1)}, bf16[2,16,4096]{2,1,0:T(8,128)(2,1)S(1)}, u32[]{:S(2)}, u32[]{:S(2)}) collective-permute-start(bf16[2,16,4096]{2,1,0:T(8,128)(2,1)} %normalize.1.refs_1_), channel_id=1, source_target_pairs={{0,8},{1,9},{2,10},{3,11},{4,12},{5,13},{6,14},{7,15},{8,0},{9,1},... | collective-permute-start | bytes 786440 | tf_op jit(solution)/shard_map/ppermute | solution.py:281
  9.6 9.4 %collective-permute-start.3 = (bf16[2,16,4096]{2,1,0:T(8,128)(2,1)}, bf16[2,16,4096]{2,1,0:T(8,128)(2,1)S(1)}, u32[]{:S(2)}, u32[]{:S(2)}) collective-permute-start(bf16[2,16,4096]{2,1,0:T(8,128)(2,1)} %normalize.1.refs_1_), channel_id=1, source_target_pairs={{0,16},{1,17},{2,18},{3,19},{4,20},{5,21},{6,22},{7,23},{8,24},{9,... | collective-permute-start | bytes 786440 | tf_op jit(solution)/shard_map/ppermute | solution.py:281
  11.1 7.9 %collective-permute-start.4 = (bf16[2,16,4096]{2,1,0:T(8,128)(2,1)}, bf16[2,16,4096]{2,1,0:T(8,128)(2,1)S(1)}, u32[]{:S(2)}, u32[]{:S(2)}) collective-permute-start(bf16[2,16,4096]{2,1,0:T(8,128)(2,1)} %normalize.1.refs_1_), channel_id=1, source_target_pairs={{0,1},{1,0},{2,3},{3,2},{4,5},{5,4},{6,7},{7,6},{8,9},{9,8},{10,11... | collective-permute-start | bytes 786440 | tf_op jit(solution)/shard_map/ppermute | solution.py:281
  18.9 47.6 %copy-start.9 = (bf16[2,16,4096]{2,1,0:T(8,128)(2,1)}, bf16[2,16,4096]{2,1,0:T(8,128)(2,1)S(1)}, u32[]{:S(2)}) copy-start(bf16[2,16,4096]{2,1,0:T(8,128)(2,1)S(1)} %collective-permute-done.2.refs_13_) | copy-start | bytes 786436
  18.9 47.6 %copy-start.10 = (bf16[2,16,4096]{2,1,0:T(8,128)(2,1)}, bf16[2,16,4096]{2,1,0:T(8,128)(2,1)S(1)}, u32[]{:S(2)}) copy-start(bf16[2,16,4096]{2,1,0:T(8,128)(2,1)S(1)} %collective-permute-done.3.refs_14_) | copy-start | bytes 786436
  19.0 7.3 %collective-permute-start.5 = (bf16[2,16,4096]{2,1,0:T(8,128)(2,1)S(1)}, bf16[2,16,4096]{2,1,0:T(8,128)(2,1)S(1)}, u32[]{:S(2)}, u32[]{:S(2)}) collective-permute-start(bf16[2,16,4096]{2,1,0:T(8,128)(2,1)S(1)} %collective-permute-done), channel_id=1, source_target_pairs={{0,2},{1,3},{2,0},{3,1},{4,6},{5,7},{6,4},{7,5},{8,10},{9,11},{10,... | collective-permute-start | bytes 786440 | tf_op jit(solution)/shard_map/ppermute | solution.py:281
  20.5 7.7 %collective-permute-start.6 = (bf16[2,16,4096]{2,1,0:T(8,128)(2,1)S(1)}, bf16[2,16,4096]{2,1,0:T(8,128)(2,1)S(1)}, u32[]{:S(2)}, u32[]{:S(2)}) collective-permute-start(bf16[2,16,4096]{2,1,0:T(8,128)(2,1)S(1)} %collective-permute-done.1.refs_2_), channel_id=1, source_target_pairs={{0,8},{1,9},{2,10},{3,11},{4,12},{5,13},{6,14},{7,15},{8,0},{9,1},... | collective-permute-start | bytes 786440 | tf_op jit(solution)/shard_map/ppermute | solution.py:281
  22.0 12.3 %collective-permute-start.7 = (bf16[2,16,4096]{2,1,0:T(8,128)(2,1)S(1)}, bf16[2,16,4096]{2,1,0:T(8,128)(2,1)S(1)}, u32[]{:S(2)}, u32[]{:S(2)}) collective-permute-start(bf16[2,16,4096]{2,1,0:T(8,128)(2,1)S(1)} %collective-permute-done.1.refs_2_), channel_id=1, source_target_pairs={{0,16},{1,17},{2,18},{3,19},{4,20},{5,21},{6,22},{7,23},{8,24},{9,... | collective-permute-start | bytes 786440 | tf_op jit(solution)/shard_map/ppermute | solution.py:281
  23.5 10.8 %collective-permute-start.9 = (bf16[2,16,4096]{2,1,0:T(8,128)(2,1)S(1)}, bf16[2,16,4096]{2,1,0:T(8,128)(2,1)S(1)}, u32[]{:S(2)}, u32[]{:S(2)}) collective-permute-start(bf16[2,16,4096]{2,1,0:T(8,128)(2,1)S(1)} %collective-permute-done.1.refs_2_), channel_id=1, source_target_pairs={{0,1},{1,0},{2,3},{3,2},{4,5},{5,4},{6,7},{7,6},{8,9},{9,8},{10,11... | collective-permute-start | bytes 786440 | tf_op jit(solution)/shard_map/ppermute | solution.py:281
  23.5 10.8 %collective-permute-start.8 = (bf16[2,16,4096]{2,1,0:T(8,128)(2,1)}, bf16[2,16,4096]{2,1,0:T(8,128)(2,1)S(1)}, u32[]{:S(2)}, u32[]{:S(2)}) collective-permute-start(bf16[2,16,4096]{2,1,0:T(8,128)(2,1)} %normalize.1.refs_1_), channel_id=1, source_target_pairs={{0,24},{1,25},{2,26},{3,27},{4,28},{5,29},{6,30},{7,31},{8,16},{9,... | collective-permute-start | bytes 786440 | tf_op jit(solution)/shard_map/ppermute | solution.py:281
  26.3 8.1 %collective-permute-start.10 = (bf16[2,16,4096]{2,1,0:T(8,128)(2,1)S(1)}, bf16[2,16,4096]{2,1,0:T(8,128)(2,1)S(1)}, u32[]{:S(2)}, u32[]{:S(2)}) collective-permute-start(bf16[2,16,4096]{2,1,0:T(8,128)(2,1)S(1)} %collective-permute-done.2.refs_13_), channel_id=1, source_target_pairs={{0,1},{1,0},{2,3},{3,2},{4,5},{5,4},{6,7},{7,6},{8,9},{9,8},{10,11... | collective-permute-start | bytes 786440 | tf_op jit(solution)/shard_map/ppermute | solution.py:281
  28.2 40.1 %copy-start.11 = (bf16[2,16,4096]{2,1,0:T(8,128)(2,1)}, bf16[2,16,4096]{2,1,0:T(8,128)(2,1)S(1)}, u32[]{:S(2)}) copy-start(bf16[2,16,4096]{2,1,0:T(8,128)(2,1)S(1)} %collective-permute-done.6.refs_4_) | copy-start | bytes 786436
  28.2 6.2 %collective-permute-start.11 = (bf16[2,16,4096]{2,1,0:T(8,128)(2,1)S(1)}, bf16[2,16,4096]{2,1,0:T(8,128)(2,1)S(1)}, u32[]{:S(2)}, u32[]{:S(2)}) collective-permute-start(bf16[2,16,4096]{2,1,0:T(8,128)(2,1)S(1)} %collective-permute-done.3.refs_14_), channel_id=1, source_target_pairs={{0,1},{1,0},{2,3},{3,2},{4,5},{5,4},{6,7},{7,6},{8,9},{9,8},{10,11... | collective-permute-start | bytes 786440 | tf_op jit(solution)/shard_map/ppermute | solution.py:281
  34.3 34.5 %copy-start.12 = (bf16[2,16,4096]{2,1,0:T(8,128)(2,1)}, bf16[2,16,4096]{2,1,0:T(8,128)(2,1)S(1)}, u32[]{:S(2)}) copy-start(bf16[2,16,4096]{2,1,0:T(8,128)(2,1)S(1)} %collective-permute-done.7.refs_5_) | copy-start | bytes 786436
  35.9 3.6 %collective-permute-start.12 = (bf16[2,32,4096]{2,1,0:T(8,128)(2,1)S(1)}, bf16[2,32,4096]{2,1,0:T(8,128)(2,1)S(1)}, u32[]{:S(2)}, u32[]{:S(2)}) collective-permute-start(bf16[2,32,4096]{2,1,0:T(8,128)(2,1)S(1)} %constant_dynamic-update-slice_fusion.refs_3_), channel_id=1, source_target_pairs={{0,1},{1,0},{2,3},{3,2},{4,5},{5,4},{6,7},{7,6},{8,9},{9,8},{10,11... | collective-permute-start | bytes 1572872 | tf_op jit(solution)/shard_map/ppermute | solution.py:281
  35.9 30.6 %collective-permute-start.13 = (bf16[2,32,4096]{2,1,0:T(8,128)(2,1)S(1)}, bf16[2,32,4096]{2,1,0:T(8,128)(2,1)S(1)}, u32[]{:S(2)}, u32[]{:S(2)}) collective-permute-start(bf16[2,32,4096]{2,1,0:T(8,128)(2,1)S(1)} %constant_dynamic-update-slice_fusion.refs_3_), channel_id=1, source_target_pairs={{0,8},{1,9},{2,10},{3,11},{4,12},{5,13},{6,14},{7,15},{8,0},{9,1},... | collective-permute-start | bytes 1572872 | tf_op jit(solution)/shard_map/ppermute | solution.py:281
  37.1 29.4 %collective-permute-start.14 = (bf16[2,32,4096]{2,1,0:T(8,128)(2,1)S(1)}, bf16[2,32,4096]{2,1,0:T(8,128)(2,1)S(1)}, u32[]{:S(2)}, u32[]{:S(2)}) collective-permute-start(bf16[2,32,4096]{2,1,0:T(8,128)(2,1)S(1)} %constant_dynamic-update-slice_fusion.refs_3_), channel_id=1, source_target_pairs={{0,16},{1,17},{2,18},{3,19},{4,20},{5,21},{6,22},{7,23},{8,24},{9,... | collective-permute-start | bytes 1572872 | tf_op jit(solution)/shard_map/ppermute | solution.py:281
  38.0 30.0 %collective-permute-start.15 = (bf16[2,48,4096]{2,1,0:T(8,128)(2,1)S(1)}, bf16[2,48,4096]{2,1,0:T(8,128)(2,1)S(1)}, u32[]{:S(2)}, u32[]{:S(2)}) collective-permute-start(bf16[2,48,4096]{2,1,0:T(8,128)(2,1)S(1)} %pad_maximum_fusion), channel_id=1, source_target_pairs={{0,24},{1,25},{2,26},{3,27},{4,28},{5,29},{6,30},{7,31},{8,16},{9,... | collective-permute-start | bytes 2359304 | tf_op jit(solution)/shard_map/ppermute | solution.py:281
  68.1 2.7 %collective-permute-start.16 = (bf16[2,64,4096]{2,1,0:T(8,128)(2,1)S(1)}, bf16[2,64,4096]{2,1,0:T(8,128)(2,1)S(1)}, u32[]{:S(2)}, u32[]{:S(2)}) collective-permute-start(bf16[2,64,4096]{2,1,0:T(8,128)(2,1)S(1)} %get-tuple-element.49), channel_id=1, source_target_pairs={{0,1},{1,0},{2,3},{3,2},{4,5},{5,4},{6,7},{7,6},{8,9},{9,8},{10,11... | collective-permute-start | bytes 3145736 | tf_op jit(solution)/shard_map/ppermute | solution.py:281
  68.2 2.9 %collective-permute-start.20 = (bf16[2,16,4096]{2,1,0:T(8,128)(2,1)S(1)}, bf16[2,16,4096]{2,1,0:T(8,128)(2,1)S(1)}, u32[]{:S(2)}, u32[]{:S(2)}) collective-permute-start(bf16[2,16,4096]{2,1,0:T(8,128)(2,1)S(1)} %collective-permute-done.6.refs_4_), channel_id=1, source_target_pairs={{0,1},{1,0},{2,3},{3,2},{4,5},{5,4},{6,7},{7,6},{8,9},{9,8},{10,11... | collective-permute-start | bytes 786440 | tf_op jit(solution)/shard_map/ppermute | solution.py:281
  68.8 2.9 %collective-permute-start.21 = (bf16[2,16,4096]{2,1,0:T(8,128)(2,1)S(1)}, bf16[2,16,4096]{2,1,0:T(8,128)(2,1)S(1)}, u32[]{:S(2)}, u32[]{:S(2)}) collective-permute-start(bf16[2,16,4096]{2,1,0:T(8,128)(2,1)S(1)} %collective-permute-done.7.refs_5_), channel_id=1, source_target_pairs={{0,1},{1,0},{2,3},{3,2},{4,5},{5,4},{6,7},{7,6},{8,9},{9,8},{10,11... | collective-permute-start | bytes 786440 | tf_op jit(solution)/shard_map/ppermute | solution.py:281
  68.9 3.2 %collective-permute-start.22 = (bf16[2,16,4096]{2,1,0:T(8,128)(2,1)S(1)}, bf16[2,16,4096]{2,1,0:T(8,128)(2,1)S(1)}, u32[]{:S(2)}, u32[]{:S(2)}) collective-permute-start(bf16[2,16,4096]{2,1,0:T(8,128)(2,1)S(1)} %copy-done.14), channel_id=1, source_target_pairs={{0,1},{1,0},{2,3},{3,2},{4,5},{5,4},{6,7},{7,6},{8,9},{9,8},{10,11... | collective-permute-start | bytes 786440 | tf_op jit(solution)/shard_map/ppermute | solution.py:281
  69.3 6.1 %collective-permute-start.23 = (bf16[2,32,4096]{2,1,0:T(8,128)(2,1)S(1)}, bf16[2,32,4096]{2,1,0:T(8,128)(2,1)S(1)}, u32[]{:S(2)}, u32[]{:S(2)}) collective-permute-start(bf16[2,32,4096]{2,1,0:T(8,128)(2,1)S(1)} %collective-permute-done.13.refs_1_), channel_id=1, source_target_pairs={{0,1},{1,0},{2,3},{3,2},{4,5},{5,4},{6,7},{7,6},{8,9},{9,8},{10,11... | collective-permute-start | bytes 1572872 | tf_op jit(solution)/shard_map/ppermute | solution.py:281
  70.7 5.9 %collective-permute-start.24 = (bf16[2,32,4096]{2,1,0:T(8,128)(2,1)S(1)}, bf16[2,32,4096]{2,1,0:T(8,128)(2,1)S(1)}, u32[]{:S(2)}, u32[]{:S(2)}) collective-permute-start(bf16[2,32,4096]{2,1,0:T(8,128)(2,1)S(1)} %collective-permute-done.14.refs_2_), channel_id=1, source_target_pairs={{0,1},{1,0},{2,3},{3,2},{4,5},{5,4},{6,7},{7,6},{8,9},{9,8},{10,11... | collective-permute-start | bytes 1572872 | tf_op jit(solution)/shard_map/ppermute | solution.py:281
  71.1 5.5 %collective-permute-start.25 = (bf16[2,48,4096]{2,1,0:T(8,128)(2,1)S(1)}, bf16[2,48,4096]{2,1,0:T(8,128)(2,1)S(1)}, u32[]{:S(2)}, u32[]{:S(2)}) collective-permute-start(bf16[2,48,4096]{2,1,0:T(8,128)(2,1)S(1)} %collective-permute-done.15.refs_3_), channel_id=1, source_target_pairs={{0,1},{1,0},{2,3},{3,2},{4,5},{5,4},{6,7},{7,6},{8,9},{9,8},{10,11... | collective-permute-start | bytes 2359304 | tf_op jit(solution)/shard_map/ppermute | solution.py:281
  71.7 40.8 %collective-permute-start.17 = (bf16[2,16,4096]{2,1,0:T(8,128)(2,1)S(1)}, bf16[2,16,4096]{2,1,0:T(8,128)(2,1)S(1)}, u32[]{:S(2)}, u32[]{:S(2)}) collective-permute-start(bf16[2,16,4096]{2,1,0:T(8,128)(2,1)S(1)} %get-tuple-element.73), channel_id=1, source_target_pairs={{0,2},{1,3},{2,0},{3,1},{4,6},{5,7},{6,4},{7,5},{8,10},{9,11},{10,... | collective-permute-start | bytes 786440 | tf_op jit(solution)/shard_map/ppermute | solution.py:281
  72.1 40.4 %collective-permute-start.18 = (bf16[2,16,4096]{2,1,0:T(8,128)(2,1)S(1)}, bf16[2,16,4096]{2,1,0:T(8,128)(2,1)S(1)}, u32[]{:S(2)}, u32[]{:S(2)}) collective-permute-start(bf16[2,16,4096]{2,1,0:T(8,128)(2,1)S(1)} %get-tuple-element.72), channel_id=1, source_target_pairs={{0,4},{1,5},{2,6},{3,7},{4,0},{5,1},{6,2},{7,3},{8,12},{9,13},{10,... | collective-permute-start | bytes 786440 | tf_op jit(solution)/shard_map/ppermute | solution.py:281
  75.4 37.1 %collective-permute-start.19 = (bf16[2,16,4096]{2,1,0:T(8,128)(2,1)S(1)}, bf16[2,16,4096]{2,1,0:T(8,128)(2,1)S(1)}, u32[]{:S(2)}, u32[]{:S(2)}) collective-permute-start(bf16[2,16,4096]{2,1,0:T(8,128)(2,1)S(1)} %get-tuple-element.71), channel_id=1, source_target_pairs={{0,6},{1,7},{2,4},{3,5},{4,2},{5,3},{6,0},{7,1},{8,14},{9,15},{10,... | collective-permute-start | bytes 786440 | tf_op jit(solution)/shard_map/ppermute | solution.py:281
  77.7 35.0 %copy-start.2 = (f32[4096]{0:T(1024)S(1)}, f32[4096]{0:T(1024)}, u32[]{:S(2)}) copy-start(f32[4096]{0:T(1024)} %param.7) | copy-start | bytes 49156
  77.7 35.2 %copy-start.1 = (bf16[16,4096]{1,0:T(8,128)(2,1)S(1)}, bf16[16,4096]{1,0:T(8,128)(2,1)}, u32[]{:S(2)}) copy-start(bf16[16,4096]{1,0:T(8,128)(2,1)} %cotangent.1) | copy-start | bytes 393220
  (14 other events, 92.1 us)

commit v11 on v10

--- a/solution.py
+++ b/solution.py
@@ -68,6 +68,10 @@
     return [pltpu.with_memory_space_constraint(array, pltpu.HBM) for array in arrays]
 
 
+def in_vmem(*arrays):
+    return [pltpu.with_memory_space_constraint(array, pltpu.VMEM) for array in arrays]
+
+
 def height(pieces):
     return sum(piece.shape[1] for piece in pieces)
 
@@ -85,7 +89,7 @@
 def normalize(tokens, norm_scale_vector, cotangent):
     return pl.pallas_call(
         norm_kernel,
-        out_shape=jax.ShapeDtypeStruct((2, *tokens.shape), jnp.bfloat16),
+        out_shape=pltpu.VMEM((2, *tokens.shape), jnp.bfloat16),
         name="normalize",
     )(*in_hbm(tokens, norm_scale_vector.reshape(1, -1), cotangent))
 
@@ -138,7 +142,7 @@
     whole = pl.BlockSpec((2, count // 2, depth), lambda i: (0, 0, 0))
     kept = jax.ShapeDtypeStruct((2, count // 2, depth), jnp.bfloat16)
     columns = (2, count, depth // n_dp)
-    unit = pltpu.HBM((count, hidden_units), jnp.bfloat16)
+    unit = pltpu.VMEM((count, hidden_units), jnp.bfloat16)
     return pl.pallas_call(
         functools.partial(own_kernel, len(pieces)),
         grid=(hidden_units // TILE,),
@@ -146,7 +150,7 @@
         + [pl.BlockSpec(memory_space=pl.ANY)] * len(pieces)
         + [tall, tall, wide],
         out_specs=[slim, slim, slim, pl.BlockSpec(columns, lambda i: (0, 0, 0)), whole, whole],
-        out_shape=[unit, unit, unit, pltpu.HBM(columns, jnp.bfloat16), kept, kept],
+        out_shape=[unit, unit, unit, pltpu.VMEM(columns, jnp.bfloat16), kept, kept],
         scratch_shapes=[
             pltpu.VMEM((2, count, depth), jnp.bfloat16),
             pltpu.VMEM((depth, count), jnp.bfloat16),
@@ -161,7 +165,7 @@
             transcendentals=count * hidden_units,
         ),
         name="own_rows",
-    )(replica, *in_hbm(pieces[0]), *pieces[1:], *in_hbm(gate_weight, up_weight, down_weight))
+    )(replica, *in_vmem(*pieces), *in_hbm(gate_weight, up_weight, down_weight))
 
 
 def all_kernel(n_pieces, *refs):
@@ -263,7 +267,11 @@
             transcendentals=behind * hidden_units,
         ),
         name="all_rows",
-    )(replica, *in_hbm(*pieces, *units, own_columns, gate_weight, up_weight, down_weight))
+    )(
+        replica,
+        *in_vmem(*pieces, *units, own_columns),
+        *in_hbm(gate_weight, up_weight, down_weight),
+    )
 
 
 def gather_tokens(tokens, norm_scale_vector, gate_weight, up_weight, down_weight, cotangent):
@@ -290,19 +298,17 @@
     unit_input = expanded_hidden * reciprocal_root_mean
     unit0 = normalize(tokens, norm_scale_vector, cotangent)
     unit2, unit1 = swap(unit0, 0, 4), swap(unit0, 0, 2)
-    across0 = [swap(unit0, 1, 0), swap(unit0, 2, 0)]
-    unit2, unit1, across0, far_unit0, again0 = lax.optimization_barrier(
-        (unit2, unit1, across0, swap(unit0, 0, 1), unit0)
-    )
+    across0 = [swap(unit0, b, 0) for b in range(1, n_dp)]
+    unit2, unit1, across0, again0 = lax.optimization_barrier((unit2, unit1, across0, unit0))
     unit3 = swap(unit2, 0, 2)
-    across1 = [swap(unit1, 1, 0), swap(unit1, 2, 0), swap(again0, 3, 0)]
-    far_unit1, far_across0 = swap(unit1, 0, 1), far(across0)
-    unit3, across1, far_unit1, far_across0 = lax.optimization_barrier(
-        (unit3, across1, far_unit1, far_across0)
+    across1 = [swap(unit1, 1, 0), swap(unit1, 2, 0)]
+    far_units, far_across0 = far([again0, unit1]), far(across0)
+    unit3, across1, far_units, far_across0 = lax.optimization_barrier(
+        (unit3, across1, far_units, far_across0)
     )
     last = jnp.concatenate([unit2, unit3], axis=1)
     late = jnp.concatenate([unit1, unit2, unit3], axis=1)
-    own = [unit0, unit1, last, far_unit0, far_unit1, swap(last, 0, 1)]
+    own = [unit0, unit1, last] + far_units + [swap(last, 0, 1)]
     rest = [swap(last, 1, 0), swap(last, 2, 0), swap(late, 3, 0)]
     *units, own_columns, kept, sent = own_rows(
         replica, n_dp, own, gate_weight, up_weight, down_weight

time: 114 us -> 110 us (0.965)
  waiting for transfers between devices: 21 us -> 18.7 us
  starting transfers between devices: 23.9 us -> 22 us
    pallas_call x1, Pallas kernels: 34.8 us -> 37.2 us  [all_rows(): pl.pallas_call(functools.partial(all_kernel, len(pieces)), grid=(tiles +...]
    ppermute x26, waiting for transfers between devices: 21 us -> 18.7 us  [swap(): return lax.ppermute(array, ('dp', 'tp'), pairs)]
    ppermute x26, starting transfers between devices: 23.9 us -> 22 us  [swap(): return lax.ppermute(array, ('dp', 'tp'), pairs)]
    pallas_call x1, Pallas kernels: 27 us -> 25.5 us  [own_rows(): pl.pallas_call(functools.partial(own_kernel, len(pieces)), grid=(hidden_u...]
    unnamed x41 -> x23, local copies, waits for them, and re-layouts: 2.61 us -> 2.11 us
  transfers between devices with their start and end apart: 26 -> 26, of which waited for: 7 -> 9; matrix products, arithmetic and copies ran while one was open for 0% -> 1% of each run, Pallas kernels for 54% -> 57%
where the time goes in v11:
time: 110 us
  Pallas kernels  63.8 us (58%)
  starting transfers between devices  22 us (20%)
  waiting for transfers between devices  18.7 us (17%)
  other arithmetic  2.64 us (2%)
  local copies, waits for them, and re-layouts  2.19 us (2%)
    pallas_call x1, Pallas kernels, all_rows(): pl.pallas_call(functools.partial(all_kernel, len(pieces)), grid=(tiles +...  37.2 us
    pallas_call x1, Pallas kernels, own_rows(): pl.pallas_call(functools.partial(own_kernel, len(pieces)), grid=(hidden_u...  25.5 us
    ppermute x26, starting transfers between devices, swap(): return lax.ppermute(array, ('dp', 'tp'), pairs)  22 us
    ppermute x26, waiting for transfers between devices, swap(): return lax.ppermute(array, ('dp', 'tp'), pairs)  18.7 us
  transfers between devices with their start and end apart: 26, of which 9 were waited for; matrix products, arithmetic and copies ran while one was open for 1% of the time, Pallas kernels for 57%

profile of v11, /device:TPU:0, one launch (start us, length us, event | category | flops | bytes accessed | tf_op | source)
XLA Modules:
  0.0 110.2 jit_solution(16453687403292627285)
XLA Ops:
  0.6 1.1 %normalize.1.refs_1_ = bf16[2,16,4096]{2,1,0:T(8,128)(2,1)S(1)} custom-call(bf16[16,4096]{1,0:T(8,128)(2,1)} %tokens.1, f32[1,4096]{1,0:T(1,128)} %bitcast.14, bf16[16,4096]{1,0:T(8,128)(2,1)} %cotangent.1), custom_call_target="tpu_custom_call" | custom-call | tf_op jit(solution)/shard_map/normalize/pallas_call | solution.py:90
  1.8 4.1 %collective-permute-start = (bf16[2,16,4096]{2,1,0:T(8,128)(2,1)S(1)}, bf16[2,16,4096]{2,1,0:T(8,128)(2,1)S(1)}, u32[]{:S(2)}, u32[]{:S(2)}) collective-permute-start(bf16[2,16,4096]{2,1,0:T(8,128)(2,1)S(1)} %normalize.1.refs_1_), channel_id=1, source_target_pairs={{0,4},{1,5},{2,6},{3,7},{4,0},{5,1},{6,2},{7,3},{8,12},{9,13},{10,... | collective-permute-start | bytes 786440 | tf_op jit(solution)/shard_map/ppermute | solution.py:289
  5.9 1.6 %collective-permute-start.1 = (bf16[2,16,4096]{2,1,0:T(8,128)(2,1)S(1)}, bf16[2,16,4096]{2,1,0:T(8,128)(2,1)S(1)}, u32[]{:S(2)}, u32[]{:S(2)}) collective-permute-start(bf16[2,16,4096]{2,1,0:T(8,128)(2,1)S(1)} %normalize.1.refs_1_), channel_id=1, source_target_pairs={{0,2},{1,3},{2,0},{3,1},{4,6},{5,7},{6,4},{7,5},{8,10},{9,11},{10,... | collective-permute-start | bytes 786440 | tf_op jit(solution)/shard_map/ppermute | solution.py:289
  7.4 1.5 %collective-permute-start.2 = (bf16[2,16,4096]{2,1,0:T(8,128)(2,1)S(1)}, bf16[2,16,4096]{2,1,0:T(8,128)(2,1)S(1)}, u32[]{:S(2)}, u32[]{:S(2)}) collective-permute-start(bf16[2,16,4096]{2,1,0:T(8,128)(2,1)S(1)} %normalize.1.refs_1_), channel_id=1, source_target_pairs={{0,8},{1,9},{2,10},{3,11},{4,12},{5,13},{6,14},{7,15},{8,0},{9,1},... | collective-permute-start | bytes 786440 | tf_op jit(solution)/shard_map/ppermute | solution.py:289
  8.9 1.5 %collective-permute-start.3 = (bf16[2,16,4096]{2,1,0:T(8,128)(2,1)S(1)}, bf16[2,16,4096]{2,1,0:T(8,128)(2,1)S(1)}, u32[]{:S(2)}, u32[]{:S(2)}) collective-permute-start(bf16[2,16,4096]{2,1,0:T(8,128)(2,1)S(1)} %normalize.1.refs_1_), channel_id=1, source_target_pairs={{0,16},{1,17},{2,18},{3,19},{4,20},{5,21},{6,22},{7,23},{8,24},{9,... | collective-permute-start | bytes 786440 | tf_op jit(solution)/shard_map/ppermute | solution.py:289
  10.5 0.5 collective-permute-start.4
  10.9 7.0 %collective-permute-done = bf16[2,16,4096]{2,1,0:T(8,128)(2,1)S(1)} collective-permute-done((bf16[2,16,4096]{2,1,0:T(8,128)(2,1)S(1)}, bf16[2,16,4096]{2,1,0:T(8,128)(2,1)S(1)}, u32[]{:S(2)}, u32[]{:S(2)}) %collective-permute-start) | collective-permute-done | bytes 262176 | tf_op jit(solution)/shard_map/ppermute | solution.py:289
  18.1 3.7 %collective-permute-done.3.refs_12_ = bf16[2,16,4096]{2,1,0:T(8,128)(2,1)S(1)} collective-permute-done((bf16[2,16,4096]{2,1,0:T(8,128)(2,1)S(1)}, bf16[2,16,4096]{2,1,0:T(8,128)(2,1)S(1)}, u32[]{:S(2)}, u32[]{:S(2)}) %collective-permute-start.3) | collective-permute-done | bytes 262176 | tf_op jit(solution)/shard_map/ppermute | solution.py:289
  21.8 0.5 collective-permute-start.5
  22.2 1.2 %collective-permute-start.6 = (bf16[2,16,4096]{2,1,0:T(8,128)(2,1)S(1)}, bf16[2,16,4096]{2,1,0:T(8,128)(2,1)S(1)}, u32[]{:S(2)}, u32[]{:S(2)}) collective-permute-start(bf16[2,16,4096]{2,1,0:T(8,128)(2,1)S(1)} %collective-permute-done.1.refs_2_), channel_id=1, source_target_pairs={{0,8},{1,9},{2,10},{3,11},{4,12},{5,13},{6,14},{7,15},{8,0},{9,1},... | collective-permute-start | bytes 786440 | tf_op jit(solution)/shard_map/ppermute | solution.py:289
  23.4 0.8 collective-permute-start.7
  24.3 0.5 collective-permute-start.8
  24.8 3.4 %collective-permute-done.5 = bf16[2,16,4096]{2,1,0:T(8,128)(2,1)S(1)} collective-permute-done((bf16[2,16,4096]{2,1,0:T(8,128)(2,1)S(1)}, bf16[2,16,4096]{2,1,0:T(8,128)(2,1)S(1)}, u32[]{:S(2)}, u32[]{:S(2)}) %collective-permute-start.5) | collective-permute-done | bytes 262176 | tf_op jit(solution)/shard_map/ppermute | solution.py:289
  28.1 0.4 collective-permute-done.6.refs_4_
  28.7 1.2 %collective-permute-done.7.refs_5_ = bf16[2,16,4096]{2,1,0:T(8,128)(2,1)S(1)} collective-permute-done((bf16[2,16,4096]{2,1,0:T(8,128)(2,1)S(1)}, bf16[2,16,4096]{2,1,0:T(8,128)(2,1)S(1)}, u32[]{:S(2)}, u32[]{:S(2)}) %collective-permute-start.7) | collective-permute-done | bytes 262176 | tf_op jit(solution)/shard_map/ppermute | solution.py:289
  29.9 0.7 copy-done
  30.6 0.7 copy-done.2
  31.4 0.7 copy-done.4
  32.1 0.4 collective-permute-start.13
  32.5 0.9 collective-permute-start.14
  33.4 1.5 %collective-permute-start.15 = (bf16[2,32,4096]{2,1,0:T(8,128)(2,1)S(1)}, bf16[2,32,4096]{2,1,0:T(8,128)(2,1)S(1)}, u32[]{:S(2)}, u32[]{:S(2)}) collective-permute-start(bf16[2,32,4096]{2,1,0:T(8,128)(2,1)S(1)} %constant_dynamic-update-slice_fusion.refs_3_), channel_id=1, source_target_pairs={{0,16},{1,17},{2,18},{3,19},{4,20},{5,21},{6,22},{7,23},{8,24},{9,... | collective-permute-start | bytes 1572872 | tf_op jit(solution)/shard_map/ppermute | solution.py:289
  34.8 1.1 pad_maximum_fusion
  35.9 1.2 %collective-permute-start.16 = (bf16[2,48,4096]{2,1,0:T(8,128)(2,1)S(1)}, bf16[2,48,4096]{2,1,0:T(8,128)(2,1)S(1)}, u32[]{:S(2)}, u32[]{:S(2)}) collective-permute-start(bf16[2,48,4096]{2,1,0:T(8,128)(2,1)S(1)} %pad_maximum_fusion), channel_id=1, source_target_pairs={{0,24},{1,25},{2,26},{3,27},{4,28},{5,29},{6,30},{7,31},{8,16},{9,... | collective-permute-start | bytes 2359304 | tf_op jit(solution)/shard_map/ppermute | solution.py:289
  37.1 25.5 %own_rows.1 = (bf16[128,1792]{1,0:T(8,128)(2,1)S(1)}, bf16[128,1792]{1,0:T(8,128)(2,1)S(1)}, bf16[128,1792]{1,0:T(8,128)(2,1)S(1)}, bf16[2,128,1024]{2,1,0:T(8,1...) custom-call(s32[1]{0:T(128)} %bitcast.refs_0_, ...), custom_call_target="tpu_custom_call" | custom-call | flops 11274289152 | bytes 44040192 | tf_op jit(solution)/shard_map/own_rows/pallas_call | solution.py:146
  62.6 1.5 %collective-permute-done.15.refs_2_ = bf16[2,32,4096]{2,1,0:T(8,128)(2,1)S(1)} collective-permute-done((bf16[2,32,4096]{2,1,0:T(8,128)(2,1)S(1)}, bf16[2,32,4096]{2,1,0:T(8,128)(2,1)S(1)}, u32[]{:S(2)}, u32[]{:S(2)}) %collective-permute-start.15) | collective-permute-done | bytes 524320 | tf_op jit(solution)/shard_map/ppermute | solution.py:289
  64.3 0.6 collective-permute-start.21
  65.5 1.3 %collective-permute-done.17 = bf16[2,64,4096]{2,1,0:T(8,128)(2,1)S(1)} collective-permute-done((bf16[2,64,4096]{2,1,0:T(8,128)(2,1)S(1)}, bf16[2,64,4096]{2,1,0:T(8,128)(2,1)S(1)}, u32[]{:S(2)}, u32[]{:S(2)}) %collective-permute-start.17) | collective-permute-done | bytes 1048608 | tf_op jit(solution)/shard_map/ppermute | solution.py:289
  67.2 1.3 %collective-permute-start.18 = (bf16[2,16,4096]{2,1,0:T(8,128)(2,1)S(1)}, bf16[2,16,4096]{2,1,0:T(8,128)(2,1)S(1)}, u32[]{:S(2)}, u32[]{:S(2)}) collective-permute-start(bf16[2,16,4096]{2,1,0:T(8,128)(2,1)S(1)} %get-tuple-element.75), channel_id=1, source_target_pairs={{0,2},{1,3},{2,0},{3,1},{4,6},{5,7},{6,4},{7,5},{8,10},{9,11},{10,... | collective-permute-start | bytes 786440 | tf_op jit(solution)/shard_map/ppermute | solution.py:289
  68.6 0.9 collective-permute-start.19
  69.5 2.2 %collective-permute-start.20 = (bf16[2,16,4096]{2,1,0:T(8,128)(2,1)S(1)}, bf16[2,16,4096]{2,1,0:T(8,128)(2,1)S(1)}, u32[]{:S(2)}, u32[]{:S(2)}) collective-permute-start(bf16[2,16,4096]{2,1,0:T(8,128)(2,1)S(1)} %get-tuple-element.73), channel_id=1, source_target_pairs={{0,6},{1,7},{2,4},{3,5},{4,2},{5,3},{6,0},{7,1},{8,14},{9,15},{10,... | collective-permute-start | bytes 786440 | tf_op jit(solution)/shard_map/ppermute | solution.py:289
  71.8 37.2 %all_rows.1 = (bf16[1024,1792]{1,0:T(8,128)(2,1)}, bf16[1024,1792]{1,0:T(8,128)(2,1)}, bf16[1792,1024]{1,0:T(8,128)(2,1)}) custom-call(s32[1]{0:T(128)} %bitcast.refs_0_, bf16[2,32,4096]{2,1,0:T(8,128)(2,1)S(1)} %collective-permute-done.14.refs_1_, bf16[2,32,4096]{2,1,0:T(8,128)(2,1)S(1)} %collective-permute-done.15.refs_2_, ...), custom_call_target="tpu_custom_call" | custom-call | flops 22548578304 | bytes 55050240 | tf_op jit(solution)/shard_map/all_rows/pallas_call | solution.py:236
  109.4 0.8 fusion.6
  (56 shorter events, 2.0 us)
Async XLA Ops:
  1.8 16.1 %collective-permute-start = (bf16[2,16,4096]{2,1,0:T(8,128)(2,1)S(1)}, bf16[2,16,4096]{2,1,0:T(8,128)(2,1)S(1)}, u32[]{:S(2)}, u32[]{:S(2)}) collective-permute-start(bf16[2,16,4096]{2,1,0:T(8,128)(2,1)S(1)} %normalize.1.refs_1_), channel_id=1, source_target_pairs={{0,4},{1,5},{2,6},{3,7},{4,0},{5,1},{6,2},{7,3},{8,12},{9,13},{10,... | collective-permute-start | bytes 786440 | tf_op jit(solution)/shard_map/ppermute | solution.py:289
  5.9 12.2 %collective-permute-start.1 = (bf16[2,16,4096]{2,1,0:T(8,128)(2,1)S(1)}, bf16[2,16,4096]{2,1,0:T(8,128)(2,1)S(1)}, u32[]{:S(2)}, u32[]{:S(2)}) collective-permute-start(bf16[2,16,4096]{2,1,0:T(8,128)(2,1)S(1)} %normalize.1.refs_1_), channel_id=1, source_target_pairs={{0,2},{1,3},{2,0},{3,1},{4,6},{5,7},{6,4},{7,5},{8,10},{9,11},{10,... | collective-permute-start | bytes 786440 | tf_op jit(solution)/shard_map/ppermute | solution.py:289
  7.4 10.6 %collective-permute-start.2 = (bf16[2,16,4096]{2,1,0:T(8,128)(2,1)S(1)}, bf16[2,16,4096]{2,1,0:T(8,128)(2,1)S(1)}, u32[]{:S(2)}, u32[]{:S(2)}) collective-permute-start(bf16[2,16,4096]{2,1,0:T(8,128)(2,1)S(1)} %normalize.1.refs_1_), channel_id=1, source_target_pairs={{0,8},{1,9},{2,10},{3,11},{4,12},{5,13},{6,14},{7,15},{8,0},{9,1},... | collective-permute-start | bytes 786440 | tf_op jit(solution)/shard_map/ppermute | solution.py:289
  8.9 12.8 %collective-permute-start.3 = (bf16[2,16,4096]{2,1,0:T(8,128)(2,1)S(1)}, bf16[2,16,4096]{2,1,0:T(8,128)(2,1)S(1)}, u32[]{:S(2)}, u32[]{:S(2)}) collective-permute-start(bf16[2,16,4096]{2,1,0:T(8,128)(2,1)S(1)} %normalize.1.refs_1_), channel_id=1, source_target_pairs={{0,16},{1,17},{2,18},{3,19},{4,20},{5,21},{6,22},{7,23},{8,24},{9,... | collective-permute-start | bytes 786440 | tf_op jit(solution)/shard_map/ppermute | solution.py:289
  10.5 11.3 %collective-permute-start.4 = (bf16[2,16,4096]{2,1,0:T(8,128)(2,1)S(1)}, bf16[2,16,4096]{2,1,0:T(8,128)(2,1)S(1)}, u32[]{:S(2)}, u32[]{:S(2)}) collective-permute-start(bf16[2,16,4096]{2,1,0:T(8,128)(2,1)S(1)} %normalize.1.refs_1_), channel_id=1, source_target_pairs={{0,24},{1,25},{2,26},{3,27},{4,28},{5,29},{6,30},{7,31},{8,16},{9,... | collective-permute-start | bytes 786440 | tf_op jit(solution)/shard_map/ppermute | solution.py:289
  17.9 14.6 %copy-start.7 = (bf16[2,16,4096]{2,1,0:T(8,128)(2,1)}, bf16[2,16,4096]{2,1,0:T(8,128)(2,1)S(1)}, u32[]{:S(2)}) copy-start(bf16[2,16,4096]{2,1,0:T(8,128)(2,1)S(1)} %collective-permute-done) | copy-start | bytes 786436
  21.8 6.4 %collective-permute-start.5 = (bf16[2,16,4096]{2,1,0:T(8,128)(2,1)S(1)}, bf16[2,16,4096]{2,1,0:T(8,128)(2,1)S(1)}, u32[]{:S(2)}, u32[]{:S(2)}) collective-permute-start(bf16[2,16,4096]{2,1,0:T(8,128)(2,1)S(1)} %collective-permute-done), channel_id=1, source_target_pairs={{0,2},{1,3},{2,0},{3,1},{4,6},{5,7},{6,4},{7,5},{8,10},{9,11},{10,... | collective-permute-start | bytes 786440 | tf_op jit(solution)/shard_map/ppermute | solution.py:289
  22.2 6.4 %collective-permute-start.6 = (bf16[2,16,4096]{2,1,0:T(8,128)(2,1)S(1)}, bf16[2,16,4096]{2,1,0:T(8,128)(2,1)S(1)}, u32[]{:S(2)}, u32[]{:S(2)}) collective-permute-start(bf16[2,16,4096]{2,1,0:T(8,128)(2,1)S(1)} %collective-permute-done.1.refs_2_), channel_id=1, source_target_pairs={{0,8},{1,9},{2,10},{3,11},{4,12},{5,13},{6,14},{7,15},{8,0},{9,1},... | collective-permute-start | bytes 786440 | tf_op jit(solution)/shard_map/ppermute | solution.py:289
  23.4 6.4 %collective-permute-start.7 = (bf16[2,16,4096]{2,1,0:T(8,128)(2,1)S(1)}, bf16[2,16,4096]{2,1,0:T(8,128)(2,1)S(1)}, u32[]{:S(2)}, u32[]{:S(2)}) collective-permute-start(bf16[2,16,4096]{2,1,0:T(8,128)(2,1)S(1)} %collective-permute-done.1.refs_2_), channel_id=1, source_target_pairs={{0,16},{1,17},{2,18},{3,19},{4,20},{5,21},{6,22},{7,23},{8,24},{9,... | collective-permute-start | bytes 786440 | tf_op jit(solution)/shard_map/ppermute | solution.py:289
  24.3 5.6 %collective-permute-start.9 = (bf16[2,16,4096]{2,1,0:T(8,128)(2,1)S(1)}, bf16[2,16,4096]{2,1,0:T(8,128)(2,1)S(1)}, u32[]{:S(2)}, u32[]{:S(2)}) collective-permute-start(bf16[2,16,4096]{2,1,0:T(8,128)(2,1)S(1)} %collective-permute-done.1.refs_2_), channel_id=1, source_target_pairs={{0,1},{1,0},{2,3},{3,2},{4,5},{5,4},{6,7},{7,6},{8,9},{9,8},{10,11... | collective-permute-start | bytes 786440 | tf_op jit(solution)/shard_map/ppermute | solution.py:289
  24.3 5.6 %collective-permute-start.8 = (bf16[2,16,4096]{2,1,0:T(8,128)(2,1)S(1)}, bf16[2,16,4096]{2,1,0:T(8,128)(2,1)S(1)}, u32[]{:S(2)}, u32[]{:S(2)}) collective-permute-start(bf16[2,16,4096]{2,1,0:T(8,128)(2,1)S(1)} %normalize.1.refs_1_), channel_id=1, source_target_pairs={{0,1},{1,0},{2,3},{3,2},{4,5},{5,4},{6,7},{7,6},{8,9},{9,8},{10,11... | collective-permute-start | bytes 786440 | tf_op jit(solution)/shard_map/ppermute | solution.py:289
  28.1 1.7 %collective-permute-start.10 = (bf16[2,16,4096]{2,1,0:T(8,128)(2,1)S(1)}, bf16[2,16,4096]{2,1,0:T(8,128)(2,1)S(1)}, u32[]{:S(2)}, u32[]{:S(2)}) collective-permute-start(bf16[2,16,4096]{2,1,0:T(8,128)(2,1)S(1)} %collective-permute-done.2.refs_11_), channel_id=1, source_target_pairs={{0,1},{1,0},{2,3},{3,2},{4,5},{5,4},{6,7},{7,6},{8,9},{9,8},{10,11... | collective-permute-start | bytes 786440 | tf_op jit(solution)/shard_map/ppermute | solution.py:289
  28.6 2.0 %collective-permute-start.11 = (bf16[2,16,4096]{2,1,0:T(8,128)(2,1)S(1)}, bf16[2,16,4096]{2,1,0:T(8,128)(2,1)S(1)}, u32[]{:S(2)}, u32[]{:S(2)}) collective-permute-start(bf16[2,16,4096]{2,1,0:T(8,128)(2,1)S(1)} %collective-permute-done.3.refs_12_), channel_id=1, source_target_pairs={{0,1},{1,0},{2,3},{3,2},{4,5},{5,4},{6,7},{7,6},{8,9},{9,8},{10,11... | collective-permute-start | bytes 786440 | tf_op jit(solution)/shard_map/ppermute | solution.py:289
  29.8 1.5 %collective-permute-start.12 = (bf16[2,16,4096]{2,1,0:T(8,128)(2,1)S(1)}, bf16[2,16,4096]{2,1,0:T(8,128)(2,1)S(1)}, u32[]{:S(2)}, u32[]{:S(2)}) collective-permute-start(bf16[2,16,4096]{2,1,0:T(8,128)(2,1)S(1)} %collective-permute-done.4.refs_13_), channel_id=1, source_target_pairs={{0,1},{1,0},{2,3},{3,2},{4,5},{5,4},{6,7},{7,6},{8,9},{9,8},{10,11... | collective-permute-start | bytes 786440 | tf_op jit(solution)/shard_map/ppermute | solution.py:289
  32.1 5.1 %collective-permute-start.13 = (bf16[2,32,4096]{2,1,0:T(8,128)(2,1)S(1)}, bf16[2,32,4096]{2,1,0:T(8,128)(2,1)S(1)}, u32[]{:S(2)}, u32[]{:S(2)}) collective-permute-start(bf16[2,32,4096]{2,1,0:T(8,128)(2,1)S(1)} %constant_dynamic-update-slice_fusion.refs_3_), channel_id=1, source_target_pairs={{0,1},{1,0},{2,3},{3,2},{4,5},{5,4},{6,7},{7,6},{8,9},{9,8},{10,11... | collective-permute-start | bytes 1572872 | tf_op jit(solution)/shard_map/ppermute | solution.py:289
  32.5 30.1 %collective-permute-start.14 = (bf16[2,32,4096]{2,1,0:T(8,128)(2,1)S(1)}, bf16[2,32,4096]{2,1,0:T(8,128)(2,1)S(1)}, u32[]{:S(2)}, u32[]{:S(2)}) collective-permute-start(bf16[2,32,4096]{2,1,0:T(8,128)(2,1)S(1)} %constant_dynamic-update-slice_fusion.refs_3_), channel_id=1, source_target_pairs={{0,8},{1,9},{2,10},{3,11},{4,12},{5,13},{6,14},{7,15},{8,0},{9,1},... | collective-permute-start | bytes 1572872 | tf_op jit(solution)/shard_map/ppermute | solution.py:289
  33.4 30.8 %collective-permute-start.15 = (bf16[2,32,4096]{2,1,0:T(8,128)(2,1)S(1)}, bf16[2,32,4096]{2,1,0:T(8,128)(2,1)S(1)}, u32[]{:S(2)}, u32[]{:S(2)}) collective-permute-start(bf16[2,32,4096]{2,1,0:T(8,128)(2,1)S(1)} %constant_dynamic-update-slice_fusion.refs_3_), channel_id=1, source_target_pairs={{0,16},{1,17},{2,18},{3,19},{4,20},{5,21},{6,22},{7,23},{8,24},{9,... | collective-permute-start | bytes 1572872 | tf_op jit(solution)/shard_map/ppermute | solution.py:289
  35.9 28.2 %collective-permute-start.16 = (bf16[2,48,4096]{2,1,0:T(8,128)(2,1)S(1)}, bf16[2,48,4096]{2,1,0:T(8,128)(2,1)S(1)}, u32[]{:S(2)}, u32[]{:S(2)}) collective-permute-start(bf16[2,48,4096]{2,1,0:T(8,128)(2,1)S(1)} %pad_maximum_fusion), channel_id=1, source_target_pairs={{0,24},{1,25},{2,26},{3,27},{4,28},{5,29},{6,30},{7,31},{8,16},{9,... | collective-permute-start | bytes 2359304 | tf_op jit(solution)/shard_map/ppermute | solution.py:289
  37.1 27.0 %copy-start.6 = (bf16[16,4096]{1,0:T(8,128)(2,1)S(1)}, bf16[16,4096]{1,0:T(8,128)(2,1)}, u32[]{:S(2)}) copy-start(bf16[16,4096]{1,0:T(8,128)(2,1)} %tokens.1) | copy-start | bytes 393220
  64.1 2.7 %collective-permute-start.17 = (bf16[2,64,4096]{2,1,0:T(8,128)(2,1)S(1)}, bf16[2,64,4096]{2,1,0:T(8,128)(2,1)S(1)}, u32[]{:S(2)}, u32[]{:S(2)}) collective-permute-start(bf16[2,64,4096]{2,1,0:T(8,128)(2,1)S(1)} %get-tuple-element.51), channel_id=1, source_target_pairs={{0,1},{1,0},{2,3},{3,2},{4,5},{5,4},{6,7},{7,6},{8,9},{9,8},{10,11... | collective-permute-start | bytes 3145736 | tf_op jit(solution)/shard_map/ppermute | solution.py:289
  64.3 7.4 %copy-start.1 = (bf16[2,16,4096]{2,1,0:T(8,128)(2,1)S(1)}, bf16[2,16,4096]{2,1,0:T(8,128)(2,1)}, u32[]{:S(2)}) copy-start(bf16[2,16,4096]{2,1,0:T(8,128)(2,1)} %copy-done) | copy-start | bytes 786436
  64.3 7.4 %copy-start.3 = (bf16[2,16,4096]{2,1,0:T(8,128)(2,1)S(1)}, bf16[2,16,4096]{2,1,0:T(8,128)(2,1)}, u32[]{:S(2)}) copy-start(bf16[2,16,4096]{2,1,0:T(8,128)(2,1)} %copy-done.2) | copy-start | bytes 786436
  64.3 2.9 %collective-permute-start.21 = (bf16[2,16,4096]{2,1,0:T(8,128)(2,1)S(1)}, bf16[2,16,4096]{2,1,0:T(8,128)(2,1)S(1)}, u32[]{:S(2)}, u32[]{:S(2)}) collective-permute-start(bf16[2,16,4096]{2,1,0:T(8,128)(2,1)S(1)} %collective-permute-done.6.refs_4_), channel_id=1, source_target_pairs={{0,1},{1,0},{2,3},{3,2},{4,5},{5,4},{6,7},{7,6},{8,9},{9,8},{10,11... | collective-permute-start | bytes 786440 | tf_op jit(solution)/shard_map/ppermute | solution.py:289
  64.9 3.7 %collective-permute-start.22 = (bf16[2,16,4096]{2,1,0:T(8,128)(2,1)S(1)}, bf16[2,16,4096]{2,1,0:T(8,128)(2,1)S(1)}, u32[]{:S(2)}, u32[]{:S(2)}) collective-permute-start(bf16[2,16,4096]{2,1,0:T(8,128)(2,1)S(1)} %collective-permute-done.7.refs_5_), channel_id=1, source_target_pairs={{0,1},{1,0},{2,3},{3,2},{4,5},{5,4},{6,7},{7,6},{8,9},{9,8},{10,11... | collective-permute-start | bytes 786440 | tf_op jit(solution)/shard_map/ppermute | solution.py:289
  65.0 4.5 %collective-permute-start.23 = (bf16[2,32,4096]{2,1,0:T(8,128)(2,1)S(1)}, bf16[2,32,4096]{2,1,0:T(8,128)(2,1)S(1)}, u32[]{:S(2)}, u32[]{:S(2)}) collective-permute-start(bf16[2,32,4096]{2,1,0:T(8,128)(2,1)S(1)} %collective-permute-done.14.refs_1_), channel_id=1, source_target_pairs={{0,1},{1,0},{2,3},{3,2},{4,5},{5,4},{6,7},{7,6},{8,9},{9,8},{10,11... | collective-permute-start | bytes 1572872 | tf_op jit(solution)/shard_map/ppermute | solution.py:289
  65.4 6.3 %collective-permute-start.24 = (bf16[2,32,4096]{2,1,0:T(8,128)(2,1)S(1)}, bf16[2,32,4096]{2,1,0:T(8,128)(2,1)S(1)}, u32[]{:S(2)}, u32[]{:S(2)}) collective-permute-start(bf16[2,32,4096]{2,1,0:T(8,128)(2,1)S(1)} %collective-permute-done.15.refs_2_), channel_id=1, source_target_pairs={{0,1},{1,0},{2,3},{3,2},{4,5},{5,4},{6,7},{7,6},{8,9},{9,8},{10,11... | collective-permute-start | bytes 1572872 | tf_op jit(solution)/shard_map/ppermute | solution.py:289
  66.8 4.9 %collective-permute-start.25 = (bf16[2,48,4096]{2,1,0:T(8,128)(2,1)S(1)}, bf16[2,48,4096]{2,1,0:T(8,128)(2,1)S(1)}, u32[]{:S(2)}, u32[]{:S(2)}) collective-permute-start(bf16[2,48,4096]{2,1,0:T(8,128)(2,1)S(1)} %collective-permute-done.16.refs_3_), channel_id=1, source_target_pairs={{0,1},{1,0},{2,3},{3,2},{4,5},{5,4},{6,7},{7,6},{8,9},{9,8},{10,11... | collective-permute-start | bytes 2359304 | tf_op jit(solution)/shard_map/ppermute | solution.py:289
  67.2 41.7 %collective-permute-start.18 = (bf16[2,16,4096]{2,1,0:T(8,128)(2,1)S(1)}, bf16[2,16,4096]{2,1,0:T(8,128)(2,1)S(1)}, u32[]{:S(2)}, u32[]{:S(2)}) collective-permute-start(bf16[2,16,4096]{2,1,0:T(8,128)(2,1)S(1)} %get-tuple-element.75), channel_id=1, source_target_pairs={{0,2},{1,3},{2,0},{3,1},{4,6},{5,7},{6,4},{7,5},{8,10},{9,11},{10,... | collective-permute-start | bytes 786440 | tf_op jit(solution)/shard_map/ppermute | solution.py:289
  68.6 40.4 %collective-permute-start.19 = (bf16[2,16,4096]{2,1,0:T(8,128)(2,1)S(1)}, bf16[2,16,4096]{2,1,0:T(8,128)(2,1)S(1)}, u32[]{:S(2)}, u32[]{:S(2)}) collective-permute-start(bf16[2,16,4096]{2,1,0:T(8,128)(2,1)S(1)} %get-tuple-element.74), channel_id=1, source_target_pairs={{0,4},{1,5},{2,6},{3,7},{4,0},{5,1},{6,2},{7,3},{8,12},{9,13},{10,... | collective-permute-start | bytes 786440 | tf_op jit(solution)/shard_map/ppermute | solution.py:289
  69.5 39.5 %collective-permute-start.20 = (bf16[2,16,4096]{2,1,0:T(8,128)(2,1)S(1)}, bf16[2,16,4096]{2,1,0:T(8,128)(2,1)S(1)}, u32[]{:S(2)}, u32[]{:S(2)}) collective-permute-start(bf16[2,16,4096]{2,1,0:T(8,128)(2,1)S(1)} %get-tuple-element.73), channel_id=1, source_target_pairs={{0,6},{1,7},{2,4},{3,5},{4,2},{5,3},{6,0},{7,1},{8,14},{9,15},{10,... | collective-permute-start | bytes 786440 | tf_op jit(solution)/shard_map/ppermute | solution.py:289
  71.8 37.4 %copy-start.10 = (f32[4096]{0:T(1024)S(1)}, f32[4096]{0:T(1024)}, u32[]{:S(2)}) copy-start(f32[4096]{0:T(1024)} %param.7) | copy-start | bytes 49156
  71.8 37.6 %copy-start.9 = (bf16[16,4096]{1,0:T(8,128)(2,1)S(1)}, bf16[16,4096]{1,0:T(8,128)(2,1)}, u32[]{:S(2)}) copy-start(bf16[16,4096]{1,0:T(8,128)(2,1)} %cotangent.1) | copy-start | bytes 393220
  (5 other events, 13.9 us)

commit v12 on v11

--- a/solution.py
+++ b/solution.py
@@ -45,23 +45,11 @@
     return hidden, grad_pre, grad_lifted
 
 
-def pack(pieces, rows, arrived):
-    copies, at = [], 0
-    for i, piece in enumerate(pieces):
-        here = pl.ds(at, piece.shape[1])
-        copies.append(
-            [pltpu.make_async_copy(piece.at[j], rows.at[j, here], arrived.at[j, i]) for j in (0, 1)]
-        )
+def pack(pieces, rows):
+    at = 0
+    for piece in pieces:
+        rows[:, at : at + piece.shape[1]] = piece[...]
         at += piece.shape[1]
-    normed, grad_out = zip(*copies)
-    for copy in normed + grad_out:
-        copy.start()
-    return normed, grad_out
-
-
-def wait(copies):
-    for copy in copies:
-        copy.wait()
 
 
 def in_hbm(*arrays):
@@ -96,67 +84,65 @@
 
 def own_kernel(n_pieces, *refs):
     replica, pieces, refs = refs[0], refs[1 : n_pieces + 1], refs[n_pieces + 1 :]
-    gate_weight, up_weight, down_weight, hidden, grad_pre, grad_lifted = refs[:6]
-    columns, kept, sent, rows, grad_out_t, out_sum, in_sum, arrived = refs[6:]
-    step = pl.program_id(0)
+    weights, refs = refs[:3], refs[3:]
+    columns, kept, sent, rows, grad_out_t, out_sum, in_sum = refs[3:]
     part = kept.shape[1]
 
-    @pl.when(step == 0)
-    def _():
-        for copies in pack(pieces, rows, arrived):
-            wait(copies)
+    def first():
+        pack(pieces, rows)
         width = columns.shape[2]
         columns[...] = rows[:, :, pl.ds(pl.multiple_of(replica[0] * width, 128), width)]
         grad_out_t[...] = rows[1].T
         out_sum[...] = jnp.zeros_like(out_sum)
         in_sum[...] = jnp.zeros_like(in_sum)
 
-    hidden[...], grad_pre[...], grad_lifted[...] = activations(
-        *project(rows[0], grad_out_t[...], gate_weight[...], up_weight[...], down_weight[...])
-    )
-    grad_pre_t, grad_lifted_t = grad_pre[...].T, grad_lifted[...].T
-    for at in range(0, out_sum.shape[1], CHUNK):
-        here = slice(at, at + CHUNK)
-        out_sum[:, here] += jnp.dot(
-            hidden[...], down_weight[:, here], preferred_element_type=jnp.float32
+    def body(gate_weight, up_weight, down_weight):
+        step = pl.program_id(0)
+        pl.when(step == 0)(first)
+        hidden, grad_pre, grad_lifted = activations(
+            *project(rows[0], grad_out_t[...], gate_weight[...], up_weight[...], down_weight[...])
         )
-        in_sum[here] += jnp.dot(
-            gate_weight[here], grad_pre_t, preferred_element_type=jnp.float32
-        ) + jnp.dot(up_weight[here], grad_lifted_t, preferred_element_type=jnp.float32)
-
-    @pl.when(step == pl.num_programs(0) - 1)
-    def _():
-        kept[0] = out_sum[:part].astype(kept.dtype)
-        sent[0] = out_sum[part:].astype(sent.dtype)
-        summed = in_sum[...].T
-        kept[1] = summed[:part].astype(kept.dtype)
-        sent[1] = summed[part:].astype(sent.dtype)
+        here = pl.ds(pl.multiple_of(step * TILE, TILE), TILE)
+        for ref, unit in zip(refs, (hidden, grad_pre, grad_lifted)):
+            ref[:, here] = unit
+        grad_pre_t, grad_lifted_t = grad_pre.T, grad_lifted.T
+        for at in range(0, out_sum.shape[1], CHUNK):
+            here = slice(at, at + CHUNK)
+            out_sum[:, here] += jnp.dot(
+                hidden, down_weight[:, here], preferred_element_type=jnp.float32
+            )
+            in_sum[here] += jnp.dot(
+                gate_weight[here], grad_pre_t, preferred_element_type=jnp.float32
+            ) + jnp.dot(up_weight[here], grad_lifted_t, preferred_element_type=jnp.float32)
+
+    depth, hidden_units = weights[0].shape
+    tall = pl.BlockSpec((depth, TILE), lambda i: (0, i))
+    wide = pl.BlockSpec((TILE, depth), lambda i: (i, 0))
+    pltpu.emit_pipeline(body, grid=(hidden_units // TILE,), in_specs=[tall, tall, wide])(*weights)
+    kept[0] = out_sum[:part].astype(kept.dtype)
+    sent[0] = out_sum[part:].astype(sent.dtype)
+    summed = in_sum[...].T
+    kept[1] = summed[:part].astype(kept.dtype)
+    sent[1] = summed[part:].astype(sent.dtype)
 
 
 def own_rows(replica, n_dp, pieces, gate_weight, up_weight, down_weight):
     depth, hidden_units = gate_weight.shape
     count = height(pieces)
-    tall = pl.BlockSpec((depth, TILE), lambda i: (0, i))
-    wide = pl.BlockSpec((TILE, depth), lambda i: (i, 0))
-    slim = pl.BlockSpec((count, TILE), lambda i: (0, i))
-    whole = pl.BlockSpec((2, count // 2, depth), lambda i: (0, 0, 0))
-    kept = jax.ShapeDtypeStruct((2, count // 2, depth), jnp.bfloat16)
+    half = pltpu.VMEM((2, count // 2, depth), jnp.bfloat16)
     columns = (2, count, depth // n_dp)
     unit = pltpu.VMEM((count, hidden_units), jnp.bfloat16)
     return pl.pallas_call(
         functools.partial(own_kernel, len(pieces)),
-        grid=(hidden_units // TILE,),
         in_specs=[pl.BlockSpec(memory_space=pltpu.SMEM)]
-        + [pl.BlockSpec(memory_space=pl.ANY)] * len(pieces)
-        + [tall, tall, wide],
-        out_specs=[slim, slim, slim, pl.BlockSpec(columns, lambda i: (0, 0, 0)), whole, whole],
-        out_shape=[unit, unit, unit, pltpu.VMEM(columns, jnp.bfloat16), kept, kept],
+        + [pl.BlockSpec(memory_space=pltpu.VMEM)] * len(pieces)
+        + [pl.BlockSpec(memory_space=pl.ANY)] * 3,
+        out_shape=[unit, unit, unit, pltpu.VMEM(columns, jnp.bfloat16), half, half],
         scratch_shapes=[
             pltpu.VMEM((2, count, depth), jnp.bfloat16),
             pltpu.VMEM((depth, count), jnp.bfloat16),
             pltpu.VMEM((count, depth), jnp.float32),
             pltpu.VMEM((depth, count), jnp.float32),
-            pltpu.SemaphoreType.DMA((2, len(pieces))),
         ],
         compiler_params=pltpu.CompilerParams(vmem_limit_bytes=28 * 2**20),
         cost_estimate=pl.CostEstimate(
@@ -171,13 +157,14 @@
 def all_kernel(n_pieces, *refs):
     replica, pieces, refs = refs[0], refs[1 : n_pieces + 1], refs[n_pieces + 1 :]
     own_hidden, own_grad_pre, own_grad_lifted, own_columns = refs[:4]
-    gate_weight, up_weight, down_weight, grad_gate, grad_up, grad_down = refs[4:10]
-    rows, normed_t, grad_out, grad_out_t, hidden, grad_pre, grad_lifted, arrived = refs[10:]
-    step, last = pl.program_id(0), pl.num_programs(0) - 1
+    weights, gradients = refs[4:7], refs[7:10]
+    rows, normed_t, grad_out, grad_out_t, hidden, grad_pre, grad_lifted = refs[10:]
+    depth, hidden_units = weights[0].shape
+    tiles = hidden_units // TILE
     ahead = own_columns.shape[1]
     width = normed_t.shape[0]
 
-    def weight_gradients():
+    def weight_gradients(grad_gate, grad_up, grad_down):
         grad_gate[...] = jnp.dot(
             normed_t[...], grad_pre[...], preferred_element_type=jnp.float32
         ).astype(grad_gate.dtype)
@@ -188,40 +175,56 @@
             hidden[...].T, grad_out[...], preferred_element_type=jnp.float32
         ).astype(grad_down.dtype)
 
-    def fill(gate, lifted, grad_hidden):
-        hidden[:ahead] = own_hidden[...]
-        grad_pre[:ahead] = own_grad_pre[...]
-        grad_lifted[:ahead] = own_grad_lifted[...]
+    def fill(step, gate, lifted, grad_hidden):
+        here = pl.ds(pl.multiple_of(step * TILE, TILE), TILE)
+        hidden[:ahead] = own_hidden[:, here]
+        grad_pre[:ahead] = own_grad_pre[:, here]
+        grad_lifted[:ahead] = own_grad_lifted[:, here]
         hidden[ahead:], grad_pre[ahead:], grad_lifted[ahead:] = activations(
             gate, lifted, grad_hidden
         )
 
-    @pl.when(step == 0)
-    def _():
-        columns = pl.ds(pl.multiple_of(replica[0] * width, 128), width)
-        normed_copies, grad_out_copies = pack(pieces, rows, arrived)
-        normed_t[:, :ahead] = own_columns[0].T
-        grad_out[:ahead] = own_columns[1]
-        wait(normed_copies)
-        gate = jnp.dot(rows[0], gate_weight[...], preferred_element_type=jnp.float32)
-        lifted = jnp.dot(rows[0], up_weight[...], preferred_element_type=jnp.float32)
-        normed_t[:, ahead:] = rows[0, :, columns].T
-        wait(grad_out_copies)
-        grad_out_t[...] = rows[1].T
-        grad_out[ahead:] = rows[1, :, columns]
-        fill(gate, lifted, project_back(grad_out_t[...], down_weight[...]))
-
-    @pl.when((step > 0) & (step < last))
-    def _():
-        products = project(
-            rows[0], grad_out_t[...], gate_weight[...], up_weight[...], down_weight[...]
-        )
-        weight_gradients()
-        fill(*products)
-
-    @pl.when(step == last)
-    def _():
-        weight_gradients()
+    def body(gate_weight, up_weight, down_weight, *outs):
+        step = pl.program_id(0)
+
+        @pl.when(step == 0)
+        def _():
+            columns = pl.ds(pl.multiple_of(replica[0] * width, 128), width)
+            pack(pieces, rows)
+            normed_t[:, :ahead] = own_columns[0].T
+            normed_t[:, ahead:] = rows[0, :, columns].T
+            grad_out[:ahead] = own_columns[1]
+            grad_out[ahead:] = rows[1, :, columns]
+            grad_out_t[...] = rows[1].T
+            fill(
+                0,
+                *project(
+                    rows[0], grad_out_t[...], gate_weight[...], up_weight[...], down_weight[...]
+                ),
+            )
+
+        @pl.when((step > 0) & (step < tiles))
+        def _():
+            products = project(
+                rows[0], grad_out_t[...], gate_weight[...], up_weight[...], down_weight[...]
+            )
+            weight_gradients(*outs)
+            fill(step, *products)
+
+        @pl.when(step == tiles)
+        def _():
+            weight_gradients(*outs)
+
+    tall = pl.BlockSpec((depth, TILE), lambda i: (0, jnp.minimum(i, tiles - 1)))
+    wide = pl.BlockSpec((TILE, depth), lambda i: (jnp.minimum(i, tiles - 1), 0))
+    tall_out = pl.BlockSpec((width, TILE), lambda i: (0, jnp.maximum(i - 1, 0)))
+    wide_out = pl.BlockSpec((TILE, width), lambda i: (jnp.maximum(i - 1, 0), 0))
+    pltpu.emit_pipeline(
+        body,
+        grid=(tiles + 1,),
+        in_specs=[tall, tall, wide],
+        out_specs=[tall_out, tall_out, wide_out],
+    )(*weights, *gradients)
 
 
 def all_rows(replica, pieces, units, own_columns, gate_weight, up_weight, down_weight):
@@ -229,22 +232,12 @@
     ahead, width = own_columns.shape[1:]
     behind = height(pieces)
     count = ahead + behind
-    tiles = hidden_units // TILE
-    tall = pl.BlockSpec((depth, TILE), lambda i: (0, jnp.minimum(i, tiles - 1)))
-    wide = pl.BlockSpec((TILE, depth), lambda i: (jnp.minimum(i, tiles - 1), 0))
-    slim = pl.BlockSpec((ahead, TILE), lambda i: (0, jnp.minimum(i, tiles - 1)))
     return pl.pallas_call(
         functools.partial(all_kernel, len(pieces)),
-        grid=(tiles + 1,),
         in_specs=[pl.BlockSpec(memory_space=pltpu.SMEM)]
-        + [pl.BlockSpec(memory_space=pl.ANY)] * len(pieces)
-        + [slim, slim, slim, pl.BlockSpec(own_columns.shape, lambda i: (0, 0, 0))]
-        + [tall, tall, wide],
-        out_specs=[
-            pl.BlockSpec((width, TILE), lambda i: (0, jnp.maximum(i - 1, 0))),
-            pl.BlockSpec((width, TILE), lambda i: (0, jnp.maximum(i - 1, 0))),
-            pl.BlockSpec((TILE, width), lambda i: (jnp.maximum(i - 1, 0), 0)),
-        ],
+        + [pl.BlockSpec(memory_space=pltpu.VMEM)] * (len(pieces) + 4)
+        + [pl.BlockSpec(memory_space=pl.ANY)] * 3,
+        out_specs=[pl.BlockSpec(memory_space=pl.ANY)] * 3,
         out_shape=[
             jax.ShapeDtypeStruct((width, hidden_units), jnp.bfloat16),
             jax.ShapeDtypeStruct((width, hidden_units), jnp.bfloat16),
@@ -258,7 +251,6 @@
             pltpu.VMEM((count, TILE), jnp.bfloat16),
             pltpu.VMEM((count, TILE), jnp.bfloat16),
             pltpu.VMEM((count, TILE), jnp.bfloat16),
-            pltpu.SemaphoreType.DMA((2, len(pieces))),
         ],
         compiler_params=pltpu.CompilerParams(vmem_limit_bytes=32 * 2**20),
         cost_estimate=pl.CostEstimate(

time: 110 us -> 105 us (0.955)
  Pallas kernels: 63.8 us -> 56.4 us
  waiting for transfers between devices: 18.7 us -> 20.5 us
    pallas_call x2, Pallas kernels: 62.7 us -> 55.3 us  [the longest x1 31.6 us: all_rows(): pl.pallas_call(functools.partial(all_kernel, len(pieces)), in_specs=[pl.B...]
    ppermute x26, waiting for transfers between devices: 18.7 us -> 20.5 us  [swap(): return lax.ppermute(array, ('dp', 'tp'), pairs)]
  transfers between devices with their start and end apart: 26 -> 26, of which waited for: 9 -> 9; matrix products, arithmetic and copies ran while one was open for 1% -> 1% of each run, Pallas kernels for 57% -> 53%
where the time goes in v12:
time: 105 us
  Pallas kernels  56.4 us (54%)
  starting transfers between devices  22 us (21%)
  waiting for transfers between devices  20.5 us (20%)
  other arithmetic  2.64 us (3%)
  local copies, waits for them, and re-layouts  2.19 us (2%)
    pallas_call x1, Pallas kernels, all_rows(): pl.pallas_call(functools.partial(all_kernel, len(pieces)), in_specs=[pl.B...  31.6 us
    pallas_call x1, Pallas kernels, own_rows(): pl.pallas_call(functools.partial(own_kernel, len(pieces)), in_specs=[pl.B...  23.7 us
    ppermute x26, starting transfers between devices, swap(): return lax.ppermute(array, ('dp', 'tp'), pairs)  22 us
    ppermute x26, waiting for transfers between devices, swap(): return lax.ppermute(array, ('dp', 'tp'), pairs)  20.5 us
    unnamed x23, local copies, waits for them, and re-layouts  2.11 us
  transfers between devices with their start and end apart: 26, of which 9 were waited for; matrix products, arithmetic and copies ran while one was open for 1% of the time, Pallas kernels for 53%

profile of v12, /device:TPU:0, one launch (start us, length us, event | category | flops | bytes accessed | tf_op | source)
XLA Modules:
  0.0 104.6 jit_solution(1852989928417138373)
XLA Ops:
  0.6 1.1 %normalize.1.refs_1_ = bf16[2,16,4096]{2,1,0:T(8,128)(2,1)S(1)} custom-call(bf16[16,4096]{1,0:T(8,128)(2,1)} %tokens.1, f32[1,4096]{1,0:T(1,128)} %bitcast.14, bf16[16,4096]{1,0:T(8,128)(2,1)} %cotangent.1), custom_call_target="tpu_custom_call" | custom-call | tf_op jit(solution)/shard_map/normalize/pallas_call | solution.py:78
  1.8 4.1 %collective-permute-start = (bf16[2,16,4096]{2,1,0:T(8,128)(2,1)S(1)}, bf16[2,16,4096]{2,1,0:T(8,128)(2,1)S(1)}, u32[]{:S(2)}, u32[]{:S(2)}) collective-permute-start(bf16[2,16,4096]{2,1,0:T(8,128)(2,1)S(1)} %normalize.1.refs_1_), channel_id=1, source_target_pairs={{0,4},{1,5},{2,6},{3,7},{4,0},{5,1},{6,2},{7,3},{8,12},{9,13},{10,... | collective-permute-start | bytes 786440 | tf_op jit(solution)/shard_map/ppermute | solution.py:281
  5.9 1.6 %collective-permute-start.1 = (bf16[2,16,4096]{2,1,0:T(8,128)(2,1)S(1)}, bf16[2,16,4096]{2,1,0:T(8,128)(2,1)S(1)}, u32[]{:S(2)}, u32[]{:S(2)}) collective-permute-start(bf16[2,16,4096]{2,1,0:T(8,128)(2,1)S(1)} %normalize.1.refs_1_), channel_id=1, source_target_pairs={{0,2},{1,3},{2,0},{3,1},{4,6},{5,7},{6,4},{7,5},{8,10},{9,11},{10,... | collective-permute-start | bytes 786440 | tf_op jit(solution)/shard_map/ppermute | solution.py:281
  7.4 1.5 %collective-permute-start.2 = (bf16[2,16,4096]{2,1,0:T(8,128)(2,1)S(1)}, bf16[2,16,4096]{2,1,0:T(8,128)(2,1)S(1)}, u32[]{:S(2)}, u32[]{:S(2)}) collective-permute-start(bf16[2,16,4096]{2,1,0:T(8,128)(2,1)S(1)} %normalize.1.refs_1_), channel_id=1, source_target_pairs={{0,8},{1,9},{2,10},{3,11},{4,12},{5,13},{6,14},{7,15},{8,0},{9,1},... | collective-permute-start | bytes 786440 | tf_op jit(solution)/shard_map/ppermute | solution.py:281
  8.9 1.5 %collective-permute-start.3 = (bf16[2,16,4096]{2,1,0:T(8,128)(2,1)S(1)}, bf16[2,16,4096]{2,1,0:T(8,128)(2,1)S(1)}, u32[]{:S(2)}, u32[]{:S(2)}) collective-permute-start(bf16[2,16,4096]{2,1,0:T(8,128)(2,1)S(1)} %normalize.1.refs_1_), channel_id=1, source_target_pairs={{0,16},{1,17},{2,18},{3,19},{4,20},{5,21},{6,22},{7,23},{8,24},{9,... | collective-permute-start | bytes 786440 | tf_op jit(solution)/shard_map/ppermute | solution.py:281
  10.5 0.5 collective-permute-start.4
  10.9 7.0 %collective-permute-done = bf16[2,16,4096]{2,1,0:T(8,128)(2,1)S(1)} collective-permute-done((bf16[2,16,4096]{2,1,0:T(8,128)(2,1)S(1)}, bf16[2,16,4096]{2,1,0:T(8,128)(2,1)S(1)}, u32[]{:S(2)}, u32[]{:S(2)}) %collective-permute-start) | collective-permute-done | bytes 262176 | tf_op jit(solution)/shard_map/ppermute | solution.py:281
  18.1 3.7 %collective-permute-done.3.refs_12_ = bf16[2,16,4096]{2,1,0:T(8,128)(2,1)S(1)} collective-permute-done((bf16[2,16,4096]{2,1,0:T(8,128)(2,1)S(1)}, bf16[2,16,4096]{2,1,0:T(8,128)(2,1)S(1)}, u32[]{:S(2)}, u32[]{:S(2)}) %collective-permute-start.3) | collective-permute-done | bytes 262176 | tf_op jit(solution)/shard_map/ppermute | solution.py:281
  21.8 0.5 collective-permute-start.5
  22.2 1.2 %collective-permute-start.6 = (bf16[2,16,4096]{2,1,0:T(8,128)(2,1)S(1)}, bf16[2,16,4096]{2,1,0:T(8,128)(2,1)S(1)}, u32[]{:S(2)}, u32[]{:S(2)}) collective-permute-start(bf16[2,16,4096]{2,1,0:T(8,128)(2,1)S(1)} %collective-permute-done.1.refs_2_), channel_id=1, source_target_pairs={{0,8},{1,9},{2,10},{3,11},{4,12},{5,13},{6,14},{7,15},{8,0},{9,1},... | collective-permute-start | bytes 786440 | tf_op jit(solution)/shard_map/ppermute | solution.py:281
  23.4 0.8 collective-permute-start.7
  24.3 0.5 collective-permute-start.8
  24.8 3.4 %collective-permute-done.5 = bf16[2,16,4096]{2,1,0:T(8,128)(2,1)S(1)} collective-permute-done((bf16[2,16,4096]{2,1,0:T(8,128)(2,1)S(1)}, bf16[2,16,4096]{2,1,0:T(8,128)(2,1)S(1)}, u32[]{:S(2)}, u32[]{:S(2)}) %collective-permute-start.5) | collective-permute-done | bytes 262176 | tf_op jit(solution)/shard_map/ppermute | solution.py:281
  28.1 0.4 collective-permute-done.6.refs_4_
  28.7 1.2 %collective-permute-done.7.refs_5_ = bf16[2,16,4096]{2,1,0:T(8,128)(2,1)S(1)} collective-permute-done((bf16[2,16,4096]{2,1,0:T(8,128)(2,1)S(1)}, bf16[2,16,4096]{2,1,0:T(8,128)(2,1)S(1)}, u32[]{:S(2)}, u32[]{:S(2)}) %collective-permute-start.7) | collective-permute-done | bytes 262176 | tf_op jit(solution)/shard_map/ppermute | solution.py:281
  29.9 0.7 copy-done
  30.6 0.7 copy-done.2
  31.4 0.7 copy-done.4
  32.1 0.4 collective-permute-start.13
  32.5 0.9 collective-permute-start.14
  33.4 1.5 %collective-permute-start.15 = (bf16[2,32,4096]{2,1,0:T(8,128)(2,1)S(1)}, bf16[2,32,4096]{2,1,0:T(8,128)(2,1)S(1)}, u32[]{:S(2)}, u32[]{:S(2)}) collective-permute-start(bf16[2,32,4096]{2,1,0:T(8,128)(2,1)S(1)} %constant_dynamic-update-slice_fusion.refs_3_), channel_id=1, source_target_pairs={{0,16},{1,17},{2,18},{3,19},{4,20},{5,21},{6,22},{7,23},{8,24},{9,... | collective-permute-start | bytes 1572872 | tf_op jit(solution)/shard_map/ppermute | solution.py:281
  34.8 1.1 %pad_maximum_fusion = bf16[2,48,4096]{2,1,0:T(8,128)(2,1)S(1)} fusion(bf16[2,16,4096]{2,1,0:T(8,128)(2,1)} %copy-done.8, bf16[2,16,4096]{2,1,0:T(8,128)(2,1)} %copy-done.7, bf16[2,16,4096]{2,1,0:T(8,128)(2,1)S(1)} %collective-permute-done.1.refs_2_), kind=kLoop, calls=%fused_computation.1 | loop fusion | flops 2359296 | bytes 1572864 | tf_op jit(solution)/shard_map/concatenate | solution.py:302
  35.9 1.2 %collective-permute-start.16 = (bf16[2,48,4096]{2,1,0:T(8,128)(2,1)S(1)}, bf16[2,48,4096]{2,1,0:T(8,128)(2,1)S(1)}, u32[]{:S(2)}, u32[]{:S(2)}) collective-permute-start(bf16[2,48,4096]{2,1,0:T(8,128)(2,1)S(1)} %pad_maximum_fusion), channel_id=1, source_target_pairs={{0,24},{1,25},{2,26},{3,27},{4,28},{5,29},{6,30},{7,31},{8,16},{9,... | collective-permute-start | bytes 2359304 | tf_op jit(solution)/shard_map/ppermute | solution.py:281
  37.1 23.7 %own_rows.1 = (bf16[128,1792]{1,0:T(8,128)(2,1)S(1)}, bf16[128,1792]{1,0:T(8,128)(2,1)S(1)}, bf16[128,1792]{1,0:T(8,128)(2,1)S(1)}, bf16[2,128,1024]{2,1,0:T(8,1...) custom-call(s32[1]{0:T(128)} %bitcast.refs_0_, ...), custom_call_target="tpu_custom_call" | custom-call | flops 11274289152 | bytes 44040192 | tf_op jit(solution)/shard_map/own_rows/pallas_call | solution.py:135
  60.9 3.3 %collective-permute-done.15.refs_2_ = bf16[2,32,4096]{2,1,0:T(8,128)(2,1)S(1)} collective-permute-done((bf16[2,32,4096]{2,1,0:T(8,128)(2,1)S(1)}, bf16[2,32,4096]{2,1,0:T(8,128)(2,1)S(1)}, u32[]{:S(2)}, u32[]{:S(2)}) %collective-permute-start.15) | collective-permute-done | bytes 524320 | tf_op jit(solution)/shard_map/ppermute | solution.py:281
  64.3 0.6 collective-permute-start.21
  65.5 1.3 %collective-permute-done.17 = bf16[2,64,4096]{2,1,0:T(8,128)(2,1)S(1)} collective-permute-done((bf16[2,64,4096]{2,1,0:T(8,128)(2,1)S(1)}, bf16[2,64,4096]{2,1,0:T(8,128)(2,1)S(1)}, u32[]{:S(2)}, u32[]{:S(2)}) %collective-permute-start.17) | collective-permute-done | bytes 1048608 | tf_op jit(solution)/shard_map/ppermute | solution.py:281
  67.2 1.3 %collective-permute-start.18 = (bf16[2,16,4096]{2,1,0:T(8,128)(2,1)S(1)}, bf16[2,16,4096]{2,1,0:T(8,128)(2,1)S(1)}, u32[]{:S(2)}, u32[]{:S(2)}) collective-permute-start(bf16[2,16,4096]{2,1,0:T(8,128)(2,1)S(1)} %get-tuple-element.75), channel_id=1, source_target_pairs={{0,2},{1,3},{2,0},{3,1},{4,6},{5,7},{6,4},{7,5},{8,10},{9,11},{10,... | collective-permute-start | bytes 786440 | tf_op jit(solution)/shard_map/ppermute | solution.py:281
  68.6 0.9 collective-permute-start.19
  69.5 2.2 %collective-permute-start.20 = (bf16[2,16,4096]{2,1,0:T(8,128)(2,1)S(1)}, bf16[2,16,4096]{2,1,0:T(8,128)(2,1)S(1)}, u32[]{:S(2)}, u32[]{:S(2)}) collective-permute-start(bf16[2,16,4096]{2,1,0:T(8,128)(2,1)S(1)} %get-tuple-element.73), channel_id=1, source_target_pairs={{0,6},{1,7},{2,4},{3,5},{4,2},{5,3},{6,0},{7,1},{8,14},{9,15},{10,... | collective-permute-start | bytes 786440 | tf_op jit(solution)/shard_map/ppermute | solution.py:281
  71.8 31.6 %all_rows.1 = (bf16[1024,1792]{1,0:T(8,128)(2,1)}, bf16[1024,1792]{1,0:T(8,128)(2,1)}, bf16[1792,1024]{1,0:T(8,128)(2,1)}) custom-call(s32[1]{0:T(128)} %bitcast.refs_0_, bf16[2,32,4096]{2,1,0:T(8,128)(2,1)S(1)} %collective-permute-done.14.refs_1_, bf16[2,32,4096]{2,1,0:T(8,128)(2,1)S(1)} %collective-permute-done.15.refs_2_, ...), custom_call_target="tpu_custom_call" | custom-call | flops 22548578304 | bytes 55050240 | tf_op jit(solution)/shard_map/all_rows/pallas_call | solution.py:235
  103.8 0.8 fusion.6
  (56 shorter events, 2.0 us)
Async XLA Ops:
  1.8 16.1 %collective-permute-start = (bf16[2,16,4096]{2,1,0:T(8,128)(2,1)S(1)}, bf16[2,16,4096]{2,1,0:T(8,128)(2,1)S(1)}, u32[]{:S(2)}, u32[]{:S(2)}) collective-permute-start(bf16[2,16,4096]{2,1,0:T(8,128)(2,1)S(1)} %normalize.1.refs_1_), channel_id=1, source_target_pairs={{0,4},{1,5},{2,6},{3,7},{4,0},{5,1},{6,2},{7,3},{8,12},{9,13},{10,... | collective-permute-start | bytes 786440 | tf_op jit(solution)/shard_map/ppermute | solution.py:281
  5.9 12.2 %collective-permute-start.1 = (bf16[2,16,4096]{2,1,0:T(8,128)(2,1)S(1)}, bf16[2,16,4096]{2,1,0:T(8,128)(2,1)S(1)}, u32[]{:S(2)}, u32[]{:S(2)}) collective-permute-start(bf16[2,16,4096]{2,1,0:T(8,128)(2,1)S(1)} %normalize.1.refs_1_), channel_id=1, source_target_pairs={{0,2},{1,3},{2,0},{3,1},{4,6},{5,7},{6,4},{7,5},{8,10},{9,11},{10,... | collective-permute-start | bytes 786440 | tf_op jit(solution)/shard_map/ppermute | solution.py:281
  7.4 10.6 %collective-permute-start.2 = (bf16[2,16,4096]{2,1,0:T(8,128)(2,1)S(1)}, bf16[2,16,4096]{2,1,0:T(8,128)(2,1)S(1)}, u32[]{:S(2)}, u32[]{:S(2)}) collective-permute-start(bf16[2,16,4096]{2,1,0:T(8,128)(2,1)S(1)} %normalize.1.refs_1_), channel_id=1, source_target_pairs={{0,8},{1,9},{2,10},{3,11},{4,12},{5,13},{6,14},{7,15},{8,0},{9,1},... | collective-permute-start | bytes 786440 | tf_op jit(solution)/shard_map/ppermute | solution.py:281
  8.9 12.8 %collective-permute-start.3 = (bf16[2,16,4096]{2,1,0:T(8,128)(2,1)S(1)}, bf16[2,16,4096]{2,1,0:T(8,128)(2,1)S(1)}, u32[]{:S(2)}, u32[]{:S(2)}) collective-permute-start(bf16[2,16,4096]{2,1,0:T(8,128)(2,1)S(1)} %normalize.1.refs_1_), channel_id=1, source_target_pairs={{0,16},{1,17},{2,18},{3,19},{4,20},{5,21},{6,22},{7,23},{8,24},{9,... | collective-permute-start | bytes 786440 | tf_op jit(solution)/shard_map/ppermute | solution.py:281
  10.5 11.3 %collective-permute-start.4 = (bf16[2,16,4096]{2,1,0:T(8,128)(2,1)S(1)}, bf16[2,16,4096]{2,1,0:T(8,128)(2,1)S(1)}, u32[]{:S(2)}, u32[]{:S(2)}) collective-permute-start(bf16[2,16,4096]{2,1,0:T(8,128)(2,1)S(1)} %normalize.1.refs_1_), channel_id=1, source_target_pairs={{0,24},{1,25},{2,26},{3,27},{4,28},{5,29},{6,30},{7,31},{8,16},{9,... | collective-permute-start | bytes 786440 | tf_op jit(solution)/shard_map/ppermute | solution.py:281
  17.9 14.6 %copy-start.7 = (bf16[2,16,4096]{2,1,0:T(8,128)(2,1)}, bf16[2,16,4096]{2,1,0:T(8,128)(2,1)S(1)}, u32[]{:S(2)}) copy-start(bf16[2,16,4096]{2,1,0:T(8,128)(2,1)S(1)} %collective-permute-done) | copy-start | bytes 786436
  21.8 6.4 %collective-permute-start.5 = (bf16[2,16,4096]{2,1,0:T(8,128)(2,1)S(1)}, bf16[2,16,4096]{2,1,0:T(8,128)(2,1)S(1)}, u32[]{:S(2)}, u32[]{:S(2)}) collective-permute-start(bf16[2,16,4096]{2,1,0:T(8,128)(2,1)S(1)} %collective-permute-done), channel_id=1, source_target_pairs={{0,2},{1,3},{2,0},{3,1},{4,6},{5,7},{6,4},{7,5},{8,10},{9,11},{10,... | collective-permute-start | bytes 786440 | tf_op jit(solution)/shard_map/ppermute | solution.py:281
  22.2 6.4 %collective-permute-start.6 = (bf16[2,16,4096]{2,1,0:T(8,128)(2,1)S(1)}, bf16[2,16,4096]{2,1,0:T(8,128)(2,1)S(1)}, u32[]{:S(2)}, u32[]{:S(2)}) collective-permute-start(bf16[2,16,4096]{2,1,0:T(8,128)(2,1)S(1)} %collective-permute-done.1.refs_2_), channel_id=1, source_target_pairs={{0,8},{1,9},{2,10},{3,11},{4,12},{5,13},{6,14},{7,15},{8,0},{9,1},... | collective-permute-start | bytes 786440 | tf_op jit(solution)/shard_map/ppermute | solution.py:281
  23.4 6.4 %collective-permute-start.7 = (bf16[2,16,4096]{2,1,0:T(8,128)(2,1)S(1)}, bf16[2,16,4096]{2,1,0:T(8,128)(2,1)S(1)}, u32[]{:S(2)}, u32[]{:S(2)}) collective-permute-start(bf16[2,16,4096]{2,1,0:T(8,128)(2,1)S(1)} %collective-permute-done.1.refs_2_), channel_id=1, source_target_pairs={{0,16},{1,17},{2,18},{3,19},{4,20},{5,21},{6,22},{7,23},{8,24},{9,... | collective-permute-start | bytes 786440 | tf_op jit(solution)/shard_map/ppermute | solution.py:281
  24.3 5.6 %collective-permute-start.9 = (bf16[2,16,4096]{2,1,0:T(8,128)(2,1)S(1)}, bf16[2,16,4096]{2,1,0:T(8,128)(2,1)S(1)}, u32[]{:S(2)}, u32[]{:S(2)}) collective-permute-start(bf16[2,16,4096]{2,1,0:T(8,128)(2,1)S(1)} %collective-permute-done.1.refs_2_), channel_id=1, source_target_pairs={{0,1},{1,0},{2,3},{3,2},{4,5},{5,4},{6,7},{7,6},{8,9},{9,8},{10,11... | collective-permute-start | bytes 786440 | tf_op jit(solution)/shard_map/ppermute | solution.py:281
  24.3 5.6 %collective-permute-start.8 = (bf16[2,16,4096]{2,1,0:T(8,128)(2,1)S(1)}, bf16[2,16,4096]{2,1,0:T(8,128)(2,1)S(1)}, u32[]{:S(2)}, u32[]{:S(2)}) collective-permute-start(bf16[2,16,4096]{2,1,0:T(8,128)(2,1)S(1)} %normalize.1.refs_1_), channel_id=1, source_target_pairs={{0,1},{1,0},{2,3},{3,2},{4,5},{5,4},{6,7},{7,6},{8,9},{9,8},{10,11... | collective-permute-start | bytes 786440 | tf_op jit(solution)/shard_map/ppermute | solution.py:281
  28.1 1.7 %collective-permute-start.10 = (bf16[2,16,4096]{2,1,0:T(8,128)(2,1)S(1)}, bf16[2,16,4096]{2,1,0:T(8,128)(2,1)S(1)}, u32[]{:S(2)}, u32[]{:S(2)}) collective-permute-start(bf16[2,16,4096]{2,1,0:T(8,128)(2,1)S(1)} %collective-permute-done.2.refs_11_), channel_id=1, source_target_pairs={{0,1},{1,0},{2,3},{3,2},{4,5},{5,4},{6,7},{7,6},{8,9},{9,8},{10,11... | collective-permute-start | bytes 786440 | tf_op jit(solution)/shard_map/ppermute | solution.py:281
  28.6 2.0 %collective-permute-start.11 = (bf16[2,16,4096]{2,1,0:T(8,128)(2,1)S(1)}, bf16[2,16,4096]{2,1,0:T(8,128)(2,1)S(1)}, u32[]{:S(2)}, u32[]{:S(2)}) collective-permute-start(bf16[2,16,4096]{2,1,0:T(8,128)(2,1)S(1)} %collective-permute-done.3.refs_12_), channel_id=1, source_target_pairs={{0,1},{1,0},{2,3},{3,2},{4,5},{5,4},{6,7},{7,6},{8,9},{9,8},{10,11... | collective-permute-start | bytes 786440 | tf_op jit(solution)/shard_map/ppermute | solution.py:281
  29.8 1.5 %collective-permute-start.12 = (bf16[2,16,4096]{2,1,0:T(8,128)(2,1)S(1)}, bf16[2,16,4096]{2,1,0:T(8,128)(2,1)S(1)}, u32[]{:S(2)}, u32[]{:S(2)}) collective-permute-start(bf16[2,16,4096]{2,1,0:T(8,128)(2,1)S(1)} %collective-permute-done.4.refs_13_), channel_id=1, source_target_pairs={{0,1},{1,0},{2,3},{3,2},{4,5},{5,4},{6,7},{7,6},{8,9},{9,8},{10,11... | collective-permute-start | bytes 786440 | tf_op jit(solution)/shard_map/ppermute | solution.py:281
  32.1 5.1 %collective-permute-start.13 = (bf16[2,32,4096]{2,1,0:T(8,128)(2,1)S(1)}, bf16[2,32,4096]{2,1,0:T(8,128)(2,1)S(1)}, u32[]{:S(2)}, u32[]{:S(2)}) collective-permute-start(bf16[2,32,4096]{2,1,0:T(8,128)(2,1)S(1)} %constant_dynamic-update-slice_fusion.refs_3_), channel_id=1, source_target_pairs={{0,1},{1,0},{2,3},{3,2},{4,5},{5,4},{6,7},{7,6},{8,9},{9,8},{10,11... | collective-permute-start | bytes 1572872 | tf_op jit(solution)/shard_map/ppermute | solution.py:281
  32.5 28.4 %collective-permute-start.14 = (bf16[2,32,4096]{2,1,0:T(8,128)(2,1)S(1)}, bf16[2,32,4096]{2,1,0:T(8,128)(2,1)S(1)}, u32[]{:S(2)}, u32[]{:S(2)}) collective-permute-start(bf16[2,32,4096]{2,1,0:T(8,128)(2,1)S(1)} %constant_dynamic-update-slice_fusion.refs_3_), channel_id=1, source_target_pairs={{0,8},{1,9},{2,10},{3,11},{4,12},{5,13},{6,14},{7,15},{8,0},{9,1},... | collective-permute-start | bytes 1572872 | tf_op jit(solution)/shard_map/ppermute | solution.py:281
  33.4 30.8 %collective-permute-start.15 = (bf16[2,32,4096]{2,1,0:T(8,128)(2,1)S(1)}, bf16[2,32,4096]{2,1,0:T(8,128)(2,1)S(1)}, u32[]{:S(2)}, u32[]{:S(2)}) collective-permute-start(bf16[2,32,4096]{2,1,0:T(8,128)(2,1)S(1)} %constant_dynamic-update-slice_fusion.refs_3_), channel_id=1, source_target_pairs={{0,16},{1,17},{2,18},{3,19},{4,20},{5,21},{6,22},{7,23},{8,24},{9,... | collective-permute-start | bytes 1572872 | tf_op jit(solution)/shard_map/ppermute | solution.py:281
  35.9 28.2 %collective-permute-start.16 = (bf16[2,48,4096]{2,1,0:T(8,128)(2,1)S(1)}, bf16[2,48,4096]{2,1,0:T(8,128)(2,1)S(1)}, u32[]{:S(2)}, u32[]{:S(2)}) collective-permute-start(bf16[2,48,4096]{2,1,0:T(8,128)(2,1)S(1)} %pad_maximum_fusion), channel_id=1, source_target_pairs={{0,24},{1,25},{2,26},{3,27},{4,28},{5,29},{6,30},{7,31},{8,16},{9,... | collective-permute-start | bytes 2359304 | tf_op jit(solution)/shard_map/ppermute | solution.py:281
  37.1 27.0 %copy-start.6 = (bf16[16,4096]{1,0:T(8,128)(2,1)S(1)}, bf16[16,4096]{1,0:T(8,128)(2,1)}, u32[]{:S(2)}) copy-start(bf16[16,4096]{1,0:T(8,128)(2,1)} %tokens.1) | copy-start | bytes 393220
  64.1 2.7 %collective-permute-start.17 = (bf16[2,64,4096]{2,1,0:T(8,128)(2,1)S(1)}, bf16[2,64,4096]{2,1,0:T(8,128)(2,1)S(1)}, u32[]{:S(2)}, u32[]{:S(2)}) collective-permute-start(bf16[2,64,4096]{2,1,0:T(8,128)(2,1)S(1)} %get-tuple-element.51), channel_id=1, source_target_pairs={{0,1},{1,0},{2,3},{3,2},{4,5},{5,4},{6,7},{7,6},{8,9},{9,8},{10,11... | collective-permute-start | bytes 3145736 | tf_op jit(solution)/shard_map/ppermute | solution.py:281
  64.3 7.4 %copy-start.1 = (bf16[2,16,4096]{2,1,0:T(8,128)(2,1)S(1)}, bf16[2,16,4096]{2,1,0:T(8,128)(2,1)}, u32[]{:S(2)}) copy-start(bf16[2,16,4096]{2,1,0:T(8,128)(2,1)} %copy-done) | copy-start | bytes 786436
  64.3 7.4 %copy-start.3 = (bf16[2,16,4096]{2,1,0:T(8,128)(2,1)S(1)}, bf16[2,16,4096]{2,1,0:T(8,128)(2,1)}, u32[]{:S(2)}) copy-start(bf16[2,16,4096]{2,1,0:T(8,128)(2,1)} %copy-done.2) | copy-start | bytes 786436
  64.3 2.9 %collective-permute-start.21 = (bf16[2,16,4096]{2,1,0:T(8,128)(2,1)S(1)}, bf16[2,16,4096]{2,1,0:T(8,128)(2,1)S(1)}, u32[]{:S(2)}, u32[]{:S(2)}) collective-permute-start(bf16[2,16,4096]{2,1,0:T(8,128)(2,1)S(1)} %collective-permute-done.6.refs_4_), channel_id=1, source_target_pairs={{0,1},{1,0},{2,3},{3,2},{4,5},{5,4},{6,7},{7,6},{8,9},{9,8},{10,11... | collective-permute-start | bytes 786440 | tf_op jit(solution)/shard_map/ppermute | solution.py:281
  64.9 3.7 %collective-permute-start.22 = (bf16[2,16,4096]{2,1,0:T(8,128)(2,1)S(1)}, bf16[2,16,4096]{2,1,0:T(8,128)(2,1)S(1)}, u32[]{:S(2)}, u32[]{:S(2)}) collective-permute-start(bf16[2,16,4096]{2,1,0:T(8,128)(2,1)S(1)} %collective-permute-done.7.refs_5_), channel_id=1, source_target_pairs={{0,1},{1,0},{2,3},{3,2},{4,5},{5,4},{6,7},{7,6},{8,9},{9,8},{10,11... | collective-permute-start | bytes 786440 | tf_op jit(solution)/shard_map/ppermute | solution.py:281
  65.0 4.5 %collective-permute-start.23 = (bf16[2,32,4096]{2,1,0:T(8,128)(2,1)S(1)}, bf16[2,32,4096]{2,1,0:T(8,128)(2,1)S(1)}, u32[]{:S(2)}, u32[]{:S(2)}) collective-permute-start(bf16[2,32,4096]{2,1,0:T(8,128)(2,1)S(1)} %collective-permute-done.14.refs_1_), channel_id=1, source_target_pairs={{0,1},{1,0},{2,3},{3,2},{4,5},{5,4},{6,7},{7,6},{8,9},{9,8},{10,11... | collective-permute-start | bytes 1572872 | tf_op jit(solution)/shard_map/ppermute | solution.py:281
  65.4 6.3 %collective-permute-start.24 = (bf16[2,32,4096]{2,1,0:T(8,128)(2,1)S(1)}, bf16[2,32,4096]{2,1,0:T(8,128)(2,1)S(1)}, u32[]{:S(2)}, u32[]{:S(2)}) collective-permute-start(bf16[2,32,4096]{2,1,0:T(8,128)(2,1)S(1)} %collective-permute-done.15.refs_2_), channel_id=1, source_target_pairs={{0,1},{1,0},{2,3},{3,2},{4,5},{5,4},{6,7},{7,6},{8,9},{9,8},{10,11... | collective-permute-start | bytes 1572872 | tf_op jit(solution)/shard_map/ppermute | solution.py:281
  66.8 4.9 %collective-permute-start.25 = (bf16[2,48,4096]{2,1,0:T(8,128)(2,1)S(1)}, bf16[2,48,4096]{2,1,0:T(8,128)(2,1)S(1)}, u32[]{:S(2)}, u32[]{:S(2)}) collective-permute-start(bf16[2,48,4096]{2,1,0:T(8,128)(2,1)S(1)} %collective-permute-done.16.refs_3_), channel_id=1, source_target_pairs={{0,1},{1,0},{2,3},{3,2},{4,5},{5,4},{6,7},{7,6},{8,9},{9,8},{10,11... | collective-permute-start | bytes 2359304 | tf_op jit(solution)/shard_map/ppermute | solution.py:281
  67.2 36.1 %collective-permute-start.18 = (bf16[2,16,4096]{2,1,0:T(8,128)(2,1)S(1)}, bf16[2,16,4096]{2,1,0:T(8,128)(2,1)S(1)}, u32[]{:S(2)}, u32[]{:S(2)}) collective-permute-start(bf16[2,16,4096]{2,1,0:T(8,128)(2,1)S(1)} %get-tuple-element.75), channel_id=1, source_target_pairs={{0,2},{1,3},{2,0},{3,1},{4,6},{5,7},{6,4},{7,5},{8,10},{9,11},{10,... | collective-permute-start | bytes 786440 | tf_op jit(solution)/shard_map/ppermute | solution.py:281
  68.6 34.8 %collective-permute-start.19 = (bf16[2,16,4096]{2,1,0:T(8,128)(2,1)S(1)}, bf16[2,16,4096]{2,1,0:T(8,128)(2,1)S(1)}, u32[]{:S(2)}, u32[]{:S(2)}) collective-permute-start(bf16[2,16,4096]{2,1,0:T(8,128)(2,1)S(1)} %get-tuple-element.74), channel_id=1, source_target_pairs={{0,4},{1,5},{2,6},{3,7},{4,0},{5,1},{6,2},{7,3},{8,12},{9,13},{10,... | collective-permute-start | bytes 786440 | tf_op jit(solution)/shard_map/ppermute | solution.py:281
  69.5 33.9 %collective-permute-start.20 = (bf16[2,16,4096]{2,1,0:T(8,128)(2,1)S(1)}, bf16[2,16,4096]{2,1,0:T(8,128)(2,1)S(1)}, u32[]{:S(2)}, u32[]{:S(2)}) collective-permute-start(bf16[2,16,4096]{2,1,0:T(8,128)(2,1)S(1)} %get-tuple-element.73), channel_id=1, source_target_pairs={{0,6},{1,7},{2,4},{3,5},{4,2},{5,3},{6,0},{7,1},{8,14},{9,15},{10,... | collective-permute-start | bytes 786440 | tf_op jit(solution)/shard_map/ppermute | solution.py:281
  71.8 31.8 %copy-start.10 = (f32[4096]{0:T(1024)S(1)}, f32[4096]{0:T(1024)}, u32[]{:S(2)}) copy-start(f32[4096]{0:T(1024)} %param.7) | copy-start | bytes 49156
  71.8 32.0 %copy-start.9 = (bf16[16,4096]{1,0:T(8,128)(2,1)S(1)}, bf16[16,4096]{1,0:T(8,128)(2,1)}, u32[]{:S(2)}) copy-start(bf16[16,4096]{1,0:T(8,128)(2,1)} %cotangent.1) | copy-start | bytes 393220
  (5 other events, 13.9 us)

commit v13 on v12

--- a/solution.py
+++ b/solution.py
@@ -290,24 +290,25 @@
     unit_input = expanded_hidden * reciprocal_root_mean
     unit0 = normalize(tokens, norm_scale_vector, cotangent)
     unit2, unit1 = swap(unit0, 0, 4), swap(unit0, 0, 2)
-    across0 = [swap(unit0, b, 0) for b in range(1, n_dp)]
-    unit2, unit1, across0, again0 = lax.optimization_barrier((unit2, unit1, across0, unit0))
+    across = [swap(unit0, 1, 0), swap(unit0, 2, 0)]
+    early = jnp.concatenate([unit0, unit1], axis=1)
+    unit2, unit1, across, early, again0 = lax.optimization_barrier(
+        (unit2, unit1, across, early, unit0)
+    )
     unit3 = swap(unit2, 0, 2)
     across1 = [swap(unit1, 1, 0), swap(unit1, 2, 0)]
-    far_units, far_across0 = far([again0, unit1]), far(across0)
-    unit3, across1, far_units, far_across0 = lax.optimization_barrier(
-        (unit3, across1, far_units, far_across0)
-    )
+    far_units = far([again0, unit1])
     last = jnp.concatenate([unit2, unit3], axis=1)
-    late = jnp.concatenate([unit1, unit2, unit3], axis=1)
+    across1, far_units, last = lax.optimization_barrier((across1, far_units, last))
     own = [unit0, unit1, last] + far_units + [swap(last, 0, 1)]
-    rest = [swap(last, 1, 0), swap(last, 2, 0), swap(late, 3, 0)]
+    rest = [swap(last, b, 0) for b in range(1, n_dp)] + [swap(early, 3, 0)]
     *units, own_columns, kept, sent = own_rows(
         replica, n_dp, own, gate_weight, up_weight, down_weight
     )
     kept, sent, rest = lax.optimization_barrier((kept, sent, rest))
     pair = (kept.astype(jnp.float32) + swap(sent, 0, 1).astype(jnp.float32)).astype(jnp.bfloat16)
-    rest += across1 + far(across1 + rest) + across0 + far_across0
+    rest += across + across1
+    rest += far(rest)
     parts = [swap(pair[:, k * rows : (k + 1) * rows], 0, 2 * k) for k in range(1, n_tp // 2)]
     weight_gradients = all_rows(
         replica, rest, units, own_columns, gate_weight, up_weight, down_weight

time: 105 us -> 107 us (1.019)
  waiting for transfers between devices: 20.5 us -> 23.1 us
  starting transfers between devices: 22 us -> 24.3 us
  local copies, waits for them, and re-layouts: 2.19 us -> 0.07 us
    ppermute x26, waiting for transfers between devices: 20.5 us -> 23.1 us  [swap(): return lax.ppermute(array, ('dp', 'tp'), pairs)]
    ppermute x26, starting transfers between devices: 22 us -> 24.3 us  [swap(): return lax.ppermute(array, ('dp', 'tp'), pairs)]
    unnamed x23 -> x6, local copies, waits for them, and re-layouts: 2.11 us -> 0.01 us
  transfers between devices with their start and end apart: 26 -> 26, of which waited for: 9 -> 9; matrix products, arithmetic and copies ran while one was open for 1% -> 1% of each run, Pallas kernels for 53% -> 52%
where the time goes in v13:
time: 107 us
  Pallas kernels  56.5 us (53%)
  starting transfers between devices  24.3 us (23%)
  waiting for transfers between devices  23.1 us (22%)
  other arithmetic  2.42 us (2%)
    pallas_call x1, Pallas kernels, all_rows(): pl.pallas_call(functools.partial(all_kernel, len(pieces)), in_specs=[pl.B...  31.6 us
    ppermute x26, starting transfers between devices, swap(): return lax.ppermute(array, ('dp', 'tp'), pairs)  24.3 us
    pallas_call x1, Pallas kernels, own_rows(): pl.pallas_call(functools.partial(own_kernel, len(pieces)), in_specs=[pl.B...  23.7 us
    ppermute x26, waiting for transfers between devices, swap(): return lax.ppermute(array, ('dp', 'tp'), pairs)  23.1 us
  transfers between devices with their start and end apart: 26, of which 9 were waited for; matrix products, arithmetic and copies ran while one was open for 1% of the time, Pallas kernels for 52%

profile of v13, /device:TPU:0, one launch (start us, length us, event | category | flops | bytes accessed | tf_op | source)
XLA Modules:
  0.0 107.2 jit_solution(17294178126062002940)
XLA Ops:
  0.6 1.1 %normalize.1.refs_1_ = bf16[2,16,4096]{2,1,0:T(8,128)(2,1)S(1)} custom-call(bf16[16,4096]{1,0:T(8,128)(2,1)} %tokens.1, f32[1,4096]{1,0:T(1,128)} %bitcast.14, bf16[16,4096]{1,0:T(8,128)(2,1)} %cotangent.1), custom_call_target="tpu_custom_call" | custom-call | tf_op jit(solution)/shard_map/normalize/pallas_call | solution.py:78
  1.8 3.1 %collective-permute-start.1 = (bf16[2,16,4096]{2,1,0:T(8,128)(2,1)S(1)}, bf16[2,16,4096]{2,1,0:T(8,128)(2,1)S(1)}, u32[]{:S(2)}, u32[]{:S(2)}) collective-permute-start(bf16[2,16,4096]{2,1,0:T(8,128)(2,1)S(1)} %normalize.1.refs_1_), channel_id=1, source_target_pairs={{0,2},{1,3},{2,0},{3,1},{4,6},{5,7},{6,4},{7,5},{8,10},{9,11},{10,... | collective-permute-start | bytes 786440 | tf_op jit(solution)/shard_map/ppermute | solution.py:281
  4.9 2.6 %collective-permute-start = (bf16[2,16,4096]{2,1,0:T(8,128)(2,1)S(1)}, bf16[2,16,4096]{2,1,0:T(8,128)(2,1)S(1)}, u32[]{:S(2)}, u32[]{:S(2)}) collective-permute-start(bf16[2,16,4096]{2,1,0:T(8,128)(2,1)S(1)} %normalize.1.refs_1_), channel_id=1, source_target_pairs={{0,4},{1,5},{2,6},{3,7},{4,0},{5,1},{6,2},{7,3},{8,12},{9,13},{10,... | collective-permute-start | bytes 786440 | tf_op jit(solution)/shard_map/ppermute | solution.py:281
  7.4 1.5 %collective-permute-start.2 = (bf16[2,16,4096]{2,1,0:T(8,128)(2,1)S(1)}, bf16[2,16,4096]{2,1,0:T(8,128)(2,1)S(1)}, u32[]{:S(2)}, u32[]{:S(2)}) collective-permute-start(bf16[2,16,4096]{2,1,0:T(8,128)(2,1)S(1)} %normalize.1.refs_1_), channel_id=1, source_target_pairs={{0,8},{1,9},{2,10},{3,11},{4,12},{5,13},{6,14},{7,15},{8,0},{9,1},... | collective-permute-start | bytes 786440 | tf_op jit(solution)/shard_map/ppermute | solution.py:281
  8.9 1.5 %collective-permute-start.3 = (bf16[2,16,4096]{2,1,0:T(8,128)(2,1)S(1)}, bf16[2,16,4096]{2,1,0:T(8,128)(2,1)S(1)}, u32[]{:S(2)}, u32[]{:S(2)}) collective-permute-start(bf16[2,16,4096]{2,1,0:T(8,128)(2,1)S(1)} %normalize.1.refs_1_), channel_id=1, source_target_pairs={{0,16},{1,17},{2,18},{3,19},{4,20},{5,21},{6,22},{7,23},{8,24},{9,... | collective-permute-start | bytes 786440 | tf_op jit(solution)/shard_map/ppermute | solution.py:281
  10.5 6.2 %collective-permute-done.1.refs_2_ = bf16[2,16,4096]{2,1,0:T(8,128)(2,1)S(1)} collective-permute-done((bf16[2,16,4096]{2,1,0:T(8,128)(2,1)S(1)}, bf16[2,16,4096]{2,1,0:T(8,128)(2,1)S(1)}, u32[]{:S(2)}, u32[]{:S(2)}) %collective-permute-start.1) | collective-permute-done | bytes 262176 | tf_op jit(solution)/shard_map/ppermute | solution.py:281
  16.7 0.8 pad_maximum_fusion
  17.5 1.7 %collective-permute-done = bf16[2,16,4096]{2,1,0:T(8,128)(2,1)S(1)} collective-permute-done((bf16[2,16,4096]{2,1,0:T(8,128)(2,1)S(1)}, bf16[2,16,4096]{2,1,0:T(8,128)(2,1)S(1)}, u32[]{:S(2)}, u32[]{:S(2)}) %collective-permute-start) | collective-permute-done | bytes 262176 | tf_op jit(solution)/shard_map/ppermute | solution.py:281
  19.2 0.5 collective-permute-start.8
  19.6 1.5 %collective-permute-start.4 = (bf16[2,16,4096]{2,1,0:T(8,128)(2,1)S(1)}, bf16[2,16,4096]{2,1,0:T(8,128)(2,1)S(1)}, u32[]{:S(2)}, u32[]{:S(2)}) collective-permute-start(bf16[2,16,4096]{2,1,0:T(8,128)(2,1)S(1)} %collective-permute-done.1.refs_2_), channel_id=1, source_target_pairs={{0,8},{1,9},{2,10},{3,11},{4,12},{5,13},{6,14},{7,15},{8,0},{9,1},... | collective-permute-start | bytes 786440 | tf_op jit(solution)/shard_map/ppermute | solution.py:281
  21.1 1.5 %collective-permute-start.5 = (bf16[2,16,4096]{2,1,0:T(8,128)(2,1)S(1)}, bf16[2,16,4096]{2,1,0:T(8,128)(2,1)S(1)}, u32[]{:S(2)}, u32[]{:S(2)}) collective-permute-start(bf16[2,16,4096]{2,1,0:T(8,128)(2,1)S(1)} %collective-permute-done.1.refs_2_), channel_id=1, source_target_pairs={{0,16},{1,17},{2,18},{3,19},{4,20},{5,21},{6,22},{7,23},{8,24},{9,... | collective-permute-start | bytes 786440 | tf_op jit(solution)/shard_map/ppermute | solution.py:281
  22.7 0.5 collective-permute-start.6
  23.2 2.4 %collective-permute-done.8 = bf16[2,16,4096]{2,1,0:T(8,128)(2,1)S(1)} collective-permute-done((bf16[2,16,4096]{2,1,0:T(8,128)(2,1)S(1)}, bf16[2,16,4096]{2,1,0:T(8,128)(2,1)S(1)}, u32[]{:S(2)}, u32[]{:S(2)}) %collective-permute-start.8) | collective-permute-done | bytes 262176 | tf_op jit(solution)/shard_map/ppermute | solution.py:281
  25.6 0.9 collective-permute-done.4.refs_7_
  26.5 1.2 %collective-permute-done.5.refs_8_ = bf16[2,16,4096]{2,1,0:T(8,128)(2,1)S(1)} collective-permute-done((bf16[2,16,4096]{2,1,0:T(8,128)(2,1)S(1)}, bf16[2,16,4096]{2,1,0:T(8,128)(2,1)S(1)}, u32[]{:S(2)}, u32[]{:S(2)}) %collective-permute-start.5) | collective-permute-done | bytes 262176 | tf_op jit(solution)/shard_map/ppermute | solution.py:281
  27.7 1.6 %collective-permute-start.13 = (bf16[2,32,4096]{2,1,0:T(8,128)(2,1)}, bf16[2,32,4096]{2,1,0:T(8,128)(2,1)S(1)}, u32[]{:S(2)}, u32[]{:S(2)}) collective-permute-start(bf16[2,32,4096]{2,1,0:T(8,128)(2,1)} %pad_maximum_fusion), channel_id=1, source_target_pairs={{0,24},{1,25},{2,26},{3,27},{4,28},{5,29},{6,30},{7,31},{8,16},{9,... | collective-permute-start | bytes 1572872 | tf_op jit(solution)/shard_map/ppermute | solution.py:281
  29.3 1.5 %collective-permute-start.10 = (bf16[2,32,4096]{2,1,0:T(8,128)(2,1)S(1)}, bf16[2,32,4096]{2,1,0:T(8,128)(2,1)S(1)}, u32[]{:S(2)}, u32[]{:S(2)}) collective-permute-start(bf16[2,32,4096]{2,1,0:T(8,128)(2,1)S(1)} %pad_maximum_fusion.1.refs_3_), channel_id=1, source_target_pairs={{0,8},{1,9},{2,10},{3,11},{4,12},{5,13},{6,14},{7,15},{8,0},{9,1},... | collective-permute-start | bytes 1572872 | tf_op jit(solution)/shard_map/ppermute | solution.py:281
  30.8 0.5 collective-permute-start.11
  31.3 1.5 %collective-permute-start.12 = (bf16[2,32,4096]{2,1,0:T(8,128)(2,1)S(1)}, bf16[2,32,4096]{2,1,0:T(8,128)(2,1)S(1)}, u32[]{:S(2)}, u32[]{:S(2)}) collective-permute-start(bf16[2,32,4096]{2,1,0:T(8,128)(2,1)S(1)} %pad_maximum_fusion.1.refs_3_), channel_id=1, source_target_pairs={{0,24},{1,25},{2,26},{3,27},{4,28},{5,29},{6,30},{7,31},{8,16},{9,... | collective-permute-start | bytes 1572872 | tf_op jit(solution)/shard_map/ppermute | solution.py:281
  32.8 23.7 %own_rows.1 = (bf16[128,1792]{1,0:T(8,128)(2,1)S(1)}, bf16[128,1792]{1,0:T(8,128)(2,1)S(1)}, bf16[128,1792]{1,0:T(8,128)(2,1)S(1)}, bf16[2,128,1024]{2,1,0:T(8,1...) custom-call(s32[1]{0:T(128)} %bitcast.refs_0_, ...), custom_call_target="tpu_custom_call" | custom-call | flops 11274289152 | bytes 44040192 | tf_op jit(solution)/shard_map/own_rows/pallas_call | solution.py:135
  56.5 9.2 %collective-permute-done.12.refs_3_ = bf16[2,32,4096]{2,1,0:T(8,128)(2,1)S(1)} collective-permute-done((bf16[2,32,4096]{2,1,0:T(8,128)(2,1)S(1)}, bf16[2,32,4096]{2,1,0:T(8,128)(2,1)S(1)}, u32[]{:S(2)}, u32[]{:S(2)}) %collective-permute-start.12) | collective-permute-done | bytes 524320 | tf_op jit(solution)/shard_map/ppermute | solution.py:281
  65.8 0.6 collective-permute-start.22
  66.5 0.4 collective-permute-start.24
  67.0 1.3 %collective-permute-done.14 = bf16[2,64,4096]{2,1,0:T(8,128)(2,1)S(1)} collective-permute-done((bf16[2,64,4096]{2,1,0:T(8,128)(2,1)S(1)}, bf16[2,64,4096]{2,1,0:T(8,128)(2,1)S(1)}, u32[]{:S(2)}, u32[]{:S(2)}) %collective-permute-start.14) | collective-permute-done | bytes 1048608 | tf_op jit(solution)/shard_map/ppermute | solution.py:281
  68.5 0.2 add_convert_fusion
  68.7 0.4 collective-permute-start.19
  69.5 0.2 collective-permute-start.21
  69.8 1.4 %collective-permute-start.15 = (bf16[2,16,4096]{2,1,0:T(8,128)(2,1)S(1)}, bf16[2,16,4096]{2,1,0:T(8,128)(2,1)S(1)}, u32[]{:S(2)}, u32[]{:S(2)}) collective-permute-start(bf16[2,16,4096]{2,1,0:T(8,128)(2,1)S(1)} %get-tuple-element.71), channel_id=1, source_target_pairs={{0,2},{1,3},{2,0},{3,1},{4,6},{5,7},{6,4},{7,5},{8,10},{9,11},{10,... | collective-permute-start | bytes 786440 | tf_op jit(solution)/shard_map/ppermute | solution.py:281
  71.2 1.8 %collective-permute-start.16 = (bf16[2,16,4096]{2,1,0:T(8,128)(2,1)S(1)}, bf16[2,16,4096]{2,1,0:T(8,128)(2,1)S(1)}, u32[]{:S(2)}, u32[]{:S(2)}) collective-permute-start(bf16[2,16,4096]{2,1,0:T(8,128)(2,1)S(1)} %get-tuple-element.70), channel_id=1, source_target_pairs={{0,4},{1,5},{2,6},{3,7},{4,0},{5,1},{6,2},{7,3},{8,12},{9,13},{10,... | collective-permute-start | bytes 786440 | tf_op jit(solution)/shard_map/ppermute | solution.py:281
  73.0 1.4 %collective-permute-start.17 = (bf16[2,16,4096]{2,1,0:T(8,128)(2,1)S(1)}, bf16[2,16,4096]{2,1,0:T(8,128)(2,1)S(1)}, u32[]{:S(2)}, u32[]{:S(2)}) collective-permute-start(bf16[2,16,4096]{2,1,0:T(8,128)(2,1)S(1)} %get-tuple-element.69), channel_id=1, source_target_pairs={{0,6},{1,7},{2,4},{3,5},{4,2},{5,3},{6,0},{7,1},{8,14},{9,15},{10,... | collective-permute-start | bytes 786440 | tf_op jit(solution)/shard_map/ppermute | solution.py:281
  74.4 31.6 %all_rows.1 = (bf16[1024,1792]{1,0:T(8,128)(2,1)}, bf16[1024,1792]{1,0:T(8,128)(2,1)}, bf16[1792,1024]{1,0:T(8,128)(2,1)}) custom-call(s32[1]{0:T(128)} %bitcast.refs_0_, bf16[2,32,4096]{2,1,0:T(8,128)(2,1)S(1)} %collective-permute-done.10.refs_1_, bf16[2,32,4096]{2,1,0:T(8,128)(2,1)S(1)} %collective-permute-done.11.refs_2_, ...), custom_call_target="tpu_custom_call" | custom-call | flops 22548578304 | bytes 55050240 | tf_op jit(solution)/shard_map/all_rows/pallas_call | solution.py:235
  106.4 0.8 fusion.6
  (39 shorter events, 1.3 us)
Async XLA Ops:
  1.8 14.9 %collective-permute-start.1 = (bf16[2,16,4096]{2,1,0:T(8,128)(2,1)S(1)}, bf16[2,16,4096]{2,1,0:T(8,128)(2,1)S(1)}, u32[]{:S(2)}, u32[]{:S(2)}) collective-permute-start(bf16[2,16,4096]{2,1,0:T(8,128)(2,1)S(1)} %normalize.1.refs_1_), channel_id=1, source_target_pairs={{0,2},{1,3},{2,0},{3,1},{4,6},{5,7},{6,4},{7,5},{8,10},{9,11},{10,... | collective-permute-start | bytes 786440 | tf_op jit(solution)/shard_map/ppermute | solution.py:281
  4.9 14.3 %collective-permute-start = (bf16[2,16,4096]{2,1,0:T(8,128)(2,1)S(1)}, bf16[2,16,4096]{2,1,0:T(8,128)(2,1)S(1)}, u32[]{:S(2)}, u32[]{:S(2)}) collective-permute-start(bf16[2,16,4096]{2,1,0:T(8,128)(2,1)S(1)} %normalize.1.refs_1_), channel_id=1, source_target_pairs={{0,4},{1,5},{2,6},{3,7},{4,0},{5,1},{6,2},{7,3},{8,12},{9,13},{10,... | collective-permute-start | bytes 786440 | tf_op jit(solution)/shard_map/ppermute | solution.py:281
  7.4 11.7 %collective-permute-start.2 = (bf16[2,16,4096]{2,1,0:T(8,128)(2,1)S(1)}, bf16[2,16,4096]{2,1,0:T(8,128)(2,1)S(1)}, u32[]{:S(2)}, u32[]{:S(2)}) collective-permute-start(bf16[2,16,4096]{2,1,0:T(8,128)(2,1)S(1)} %normalize.1.refs_1_), channel_id=1, source_target_pairs={{0,8},{1,9},{2,10},{3,11},{4,12},{5,13},{6,14},{7,15},{8,0},{9,1},... | collective-permute-start | bytes 786440 | tf_op jit(solution)/shard_map/ppermute | solution.py:281
  8.9 10.3 %collective-permute-start.3 = (bf16[2,16,4096]{2,1,0:T(8,128)(2,1)S(1)}, bf16[2,16,4096]{2,1,0:T(8,128)(2,1)S(1)}, u32[]{:S(2)}, u32[]{:S(2)}) collective-permute-start(bf16[2,16,4096]{2,1,0:T(8,128)(2,1)S(1)} %normalize.1.refs_1_), channel_id=1, source_target_pairs={{0,16},{1,17},{2,18},{3,19},{4,20},{5,21},{6,22},{7,23},{8,24},{9,... | collective-permute-start | bytes 786440 | tf_op jit(solution)/shard_map/ppermute | solution.py:281
  19.2 6.4 %collective-permute-start.8 = (bf16[2,16,4096]{2,1,0:T(8,128)(2,1)S(1)}, bf16[2,16,4096]{2,1,0:T(8,128)(2,1)S(1)}, u32[]{:S(2)}, u32[]{:S(2)}) collective-permute-start(bf16[2,16,4096]{2,1,0:T(8,128)(2,1)S(1)} %collective-permute-done), channel_id=1, source_target_pairs={{0,2},{1,3},{2,0},{3,1},{4,6},{5,7},{6,4},{7,5},{8,10},{9,11},{10,... | collective-permute-start | bytes 786440 | tf_op jit(solution)/shard_map/ppermute | solution.py:281
  19.6 6.8 %collective-permute-start.4 = (bf16[2,16,4096]{2,1,0:T(8,128)(2,1)S(1)}, bf16[2,16,4096]{2,1,0:T(8,128)(2,1)S(1)}, u32[]{:S(2)}, u32[]{:S(2)}) collective-permute-start(bf16[2,16,4096]{2,1,0:T(8,128)(2,1)S(1)} %collective-permute-done.1.refs_2_), channel_id=1, source_target_pairs={{0,8},{1,9},{2,10},{3,11},{4,12},{5,13},{6,14},{7,15},{8,0},{9,1},... | collective-permute-start | bytes 786440 | tf_op jit(solution)/shard_map/ppermute | solution.py:281
  21.1 6.6 %collective-permute-start.5 = (bf16[2,16,4096]{2,1,0:T(8,128)(2,1)S(1)}, bf16[2,16,4096]{2,1,0:T(8,128)(2,1)S(1)}, u32[]{:S(2)}, u32[]{:S(2)}) collective-permute-start(bf16[2,16,4096]{2,1,0:T(8,128)(2,1)S(1)} %collective-permute-done.1.refs_2_), channel_id=1, source_target_pairs={{0,16},{1,17},{2,18},{3,19},{4,20},{5,21},{6,22},{7,23},{8,24},{9,... | collective-permute-start | bytes 786440 | tf_op jit(solution)/shard_map/ppermute | solution.py:281
  22.7 5.0 %collective-permute-start.7 = (bf16[2,16,4096]{2,1,0:T(8,128)(2,1)S(1)}, bf16[2,16,4096]{2,1,0:T(8,128)(2,1)S(1)}, u32[]{:S(2)}, u32[]{:S(2)}) collective-permute-start(bf16[2,16,4096]{2,1,0:T(8,128)(2,1)S(1)} %collective-permute-done.1.refs_2_), channel_id=1, source_target_pairs={{0,1},{1,0},{2,3},{3,2},{4,5},{5,4},{6,7},{7,6},{8,9},{9,8},{10,11... | collective-permute-start | bytes 786440 | tf_op jit(solution)/shard_map/ppermute | solution.py:281
  22.7 5.0 %collective-permute-start.6 = (bf16[2,16,4096]{2,1,0:T(8,128)(2,1)S(1)}, bf16[2,16,4096]{2,1,0:T(8,128)(2,1)S(1)}, u32[]{:S(2)}, u32[]{:S(2)}) collective-permute-start(bf16[2,16,4096]{2,1,0:T(8,128)(2,1)S(1)} %normalize.1.refs_1_), channel_id=1, source_target_pairs={{0,1},{1,0},{2,3},{3,2},{4,5},{5,4},{6,7},{7,6},{8,9},{9,8},{10,11... | collective-permute-start | bytes 786440 | tf_op jit(solution)/shard_map/ppermute | solution.py:281
  27.7 5.1 %collective-permute-start.9 = (bf16[2,32,4096]{2,1,0:T(8,128)(2,1)S(1)}, bf16[2,32,4096]{2,1,0:T(8,128)(2,1)S(1)}, u32[]{:S(2)}, u32[]{:S(2)}) collective-permute-start(bf16[2,32,4096]{2,1,0:T(8,128)(2,1)S(1)} %pad_maximum_fusion.1.refs_3_), channel_id=1, source_target_pairs={{0,1},{1,0},{2,3},{3,2},{4,5},{5,4},{6,7},{7,6},{8,9},{9,8},{10,11... | collective-permute-start | bytes 1572872 | tf_op jit(solution)/shard_map/ppermute | solution.py:281
  27.7 28.8 %collective-permute-start.13 = (bf16[2,32,4096]{2,1,0:T(8,128)(2,1)}, bf16[2,32,4096]{2,1,0:T(8,128)(2,1)S(1)}, u32[]{:S(2)}, u32[]{:S(2)}) collective-permute-start(bf16[2,32,4096]{2,1,0:T(8,128)(2,1)} %pad_maximum_fusion), channel_id=1, source_target_pairs={{0,24},{1,25},{2,26},{3,27},{4,28},{5,29},{6,30},{7,31},{8,16},{9,... | collective-permute-start | bytes 1572872 | tf_op jit(solution)/shard_map/ppermute | solution.py:281
  29.3 27.2 %collective-permute-start.10 = (bf16[2,32,4096]{2,1,0:T(8,128)(2,1)S(1)}, bf16[2,32,4096]{2,1,0:T(8,128)(2,1)S(1)}, u32[]{:S(2)}, u32[]{:S(2)}) collective-permute-start(bf16[2,32,4096]{2,1,0:T(8,128)(2,1)S(1)} %pad_maximum_fusion.1.refs_3_), channel_id=1, source_target_pairs={{0,8},{1,9},{2,10},{3,11},{4,12},{5,13},{6,14},{7,15},{8,0},{9,1},... | collective-permute-start | bytes 1572872 | tf_op jit(solution)/shard_map/ppermute | solution.py:281
  30.8 25.8 %collective-permute-start.11 = (bf16[2,32,4096]{2,1,0:T(8,128)(2,1)S(1)}, bf16[2,32,4096]{2,1,0:T(8,128)(2,1)S(1)}, u32[]{:S(2)}, u32[]{:S(2)}) collective-permute-start(bf16[2,32,4096]{2,1,0:T(8,128)(2,1)S(1)} %pad_maximum_fusion.1.refs_3_), channel_id=1, source_target_pairs={{0,16},{1,17},{2,18},{3,19},{4,20},{5,21},{6,22},{7,23},{8,24},{9,... | collective-permute-start | bytes 1572872 | tf_op jit(solution)/shard_map/ppermute | solution.py:281
  31.3 34.4 %collective-permute-start.12 = (bf16[2,32,4096]{2,1,0:T(8,128)(2,1)S(1)}, bf16[2,32,4096]{2,1,0:T(8,128)(2,1)S(1)}, u32[]{:S(2)}, u32[]{:S(2)}) collective-permute-start(bf16[2,32,4096]{2,1,0:T(8,128)(2,1)S(1)} %pad_maximum_fusion.1.refs_3_), channel_id=1, source_target_pairs={{0,24},{1,25},{2,26},{3,27},{4,28},{5,29},{6,30},{7,31},{8,16},{9,... | collective-permute-start | bytes 1572872 | tf_op jit(solution)/shard_map/ppermute | solution.py:281
  32.8 32.9 %copy-start = (bf16[16,4096]{1,0:T(8,128)(2,1)S(1)}, bf16[16,4096]{1,0:T(8,128)(2,1)}, u32[]{:S(2)}) copy-start(bf16[16,4096]{1,0:T(8,128)(2,1)} %tokens.1) | copy-start | bytes 393220
  65.7 2.7 %collective-permute-start.14 = (bf16[2,64,4096]{2,1,0:T(8,128)(2,1)S(1)}, bf16[2,64,4096]{2,1,0:T(8,128)(2,1)S(1)}, u32[]{:S(2)}, u32[]{:S(2)}) collective-permute-start(bf16[2,64,4096]{2,1,0:T(8,128)(2,1)S(1)} %get-tuple-element.47), channel_id=1, source_target_pairs={{0,1},{1,0},{2,3},{3,2},{4,5},{5,4},{6,7},{7,6},{8,9},{9,8},{10,11... | collective-permute-start | bytes 3145736 | tf_op jit(solution)/shard_map/ppermute | solution.py:281
  65.8 2.9 %collective-permute-start.22 = (bf16[2,16,4096]{2,1,0:T(8,128)(2,1)S(1)}, bf16[2,16,4096]{2,1,0:T(8,128)(2,1)S(1)}, u32[]{:S(2)}, u32[]{:S(2)}) collective-permute-start(bf16[2,16,4096]{2,1,0:T(8,128)(2,1)S(1)} %collective-permute-done.2.refs_5_), channel_id=1, source_target_pairs={{0,1},{1,0},{2,3},{3,2},{4,5},{5,4},{6,7},{7,6},{8,9},{9,8},{10,11... | collective-permute-start | bytes 786440 | tf_op jit(solution)/shard_map/ppermute | solution.py:281
  66.4 2.8 %collective-permute-start.23 = (bf16[2,16,4096]{2,1,0:T(8,128)(2,1)S(1)}, bf16[2,16,4096]{2,1,0:T(8,128)(2,1)S(1)}, u32[]{:S(2)}, u32[]{:S(2)}) collective-permute-start(bf16[2,16,4096]{2,1,0:T(8,128)(2,1)S(1)} %collective-permute-done.3.refs_6_), channel_id=1, source_target_pairs={{0,1},{1,0},{2,3},{3,2},{4,5},{5,4},{6,7},{7,6},{8,9},{9,8},{10,11... | collective-permute-start | bytes 786440 | tf_op jit(solution)/shard_map/ppermute | solution.py:281
  66.5 3.0 %collective-permute-start.24 = (bf16[2,16,4096]{2,1,0:T(8,128)(2,1)S(1)}, bf16[2,16,4096]{2,1,0:T(8,128)(2,1)S(1)}, u32[]{:S(2)}, u32[]{:S(2)}) collective-permute-start(bf16[2,16,4096]{2,1,0:T(8,128)(2,1)S(1)} %collective-permute-done.4.refs_7_), channel_id=1, source_target_pairs={{0,1},{1,0},{2,3},{3,2},{4,5},{5,4},{6,7},{7,6},{8,9},{9,8},{10,11... | collective-permute-start | bytes 786440 | tf_op jit(solution)/shard_map/ppermute | solution.py:281
  66.9 2.9 %collective-permute-start.25 = (bf16[2,16,4096]{2,1,0:T(8,128)(2,1)S(1)}, bf16[2,16,4096]{2,1,0:T(8,128)(2,1)S(1)}, u32[]{:S(2)}, u32[]{:S(2)}) collective-permute-start(bf16[2,16,4096]{2,1,0:T(8,128)(2,1)S(1)} %collective-permute-done.5.refs_8_), channel_id=1, source_target_pairs={{0,1},{1,0},{2,3},{3,2},{4,5},{5,4},{6,7},{7,6},{8,9},{9,8},{10,11... | collective-permute-start | bytes 786440 | tf_op jit(solution)/shard_map/ppermute | solution.py:281
  68.3 2.9 %collective-permute-start.18 = (bf16[2,32,4096]{2,1,0:T(8,128)(2,1)S(1)}, bf16[2,32,4096]{2,1,0:T(8,128)(2,1)S(1)}, u32[]{:S(2)}, u32[]{:S(2)}) collective-permute-start(bf16[2,32,4096]{2,1,0:T(8,128)(2,1)S(1)} %collective-permute-done.10.refs_1_), channel_id=1, source_target_pairs={{0,1},{1,0},{2,3},{3,2},{4,5},{5,4},{6,7},{7,6},{8,9},{9,8},{10,11... | collective-permute-start | bytes 1572872 | tf_op jit(solution)/shard_map/ppermute | solution.py:281
  68.7 4.3 %collective-permute-start.19 = (bf16[2,32,4096]{2,1,0:T(8,128)(2,1)S(1)}, bf16[2,32,4096]{2,1,0:T(8,128)(2,1)S(1)}, u32[]{:S(2)}, u32[]{:S(2)}) collective-permute-start(bf16[2,32,4096]{2,1,0:T(8,128)(2,1)S(1)} %collective-permute-done.11.refs_2_), channel_id=1, source_target_pairs={{0,1},{1,0},{2,3},{3,2},{4,5},{5,4},{6,7},{7,6},{8,9},{9,8},{10,11... | collective-permute-start | bytes 1572872 | tf_op jit(solution)/shard_map/ppermute | solution.py:281
  69.2 5.2 %collective-permute-start.20 = (bf16[2,32,4096]{2,1,0:T(8,128)(2,1)S(1)}, bf16[2,32,4096]{2,1,0:T(8,128)(2,1)S(1)}, u32[]{:S(2)}, u32[]{:S(2)}) collective-permute-start(bf16[2,32,4096]{2,1,0:T(8,128)(2,1)S(1)} %collective-permute-done.12.refs_3_), channel_id=1, source_target_pairs={{0,1},{1,0},{2,3},{3,2},{4,5},{5,4},{6,7},{7,6},{8,9},{9,8},{10,11... | collective-permute-start | bytes 1572872 | tf_op jit(solution)/shard_map/ppermute | solution.py:281
  69.5 4.9 %collective-permute-start.21 = (bf16[2,32,4096]{2,1,0:T(8,128)(2,1)S(1)}, bf16[2,32,4096]{2,1,0:T(8,128)(2,1)S(1)}, u32[]{:S(2)}, u32[]{:S(2)}) collective-permute-start(bf16[2,32,4096]{2,1,0:T(8,128)(2,1)S(1)} %collective-permute-done.13.refs_4_), channel_id=1, source_target_pairs={{0,1},{1,0},{2,3},{3,2},{4,5},{5,4},{6,7},{7,6},{8,9},{9,8},{10,11... | collective-permute-start | bytes 1572872 | tf_op jit(solution)/shard_map/ppermute | solution.py:281
  69.8 36.1 %collective-permute-start.15 = (bf16[2,16,4096]{2,1,0:T(8,128)(2,1)S(1)}, bf16[2,16,4096]{2,1,0:T(8,128)(2,1)S(1)}, u32[]{:S(2)}, u32[]{:S(2)}) collective-permute-start(bf16[2,16,4096]{2,1,0:T(8,128)(2,1)S(1)} %get-tuple-element.71), channel_id=1, source_target_pairs={{0,2},{1,3},{2,0},{3,1},{4,6},{5,7},{6,4},{7,5},{8,10},{9,11},{10,... | collective-permute-start | bytes 786440 | tf_op jit(solution)/shard_map/ppermute | solution.py:281
  71.2 34.8 %collective-permute-start.16 = (bf16[2,16,4096]{2,1,0:T(8,128)(2,1)S(1)}, bf16[2,16,4096]{2,1,0:T(8,128)(2,1)S(1)}, u32[]{:S(2)}, u32[]{:S(2)}) collective-permute-start(bf16[2,16,4096]{2,1,0:T(8,128)(2,1)S(1)} %get-tuple-element.70), channel_id=1, source_target_pairs={{0,4},{1,5},{2,6},{3,7},{4,0},{5,1},{6,2},{7,3},{8,12},{9,13},{10,... | collective-permute-start | bytes 786440 | tf_op jit(solution)/shard_map/ppermute | solution.py:281
  73.0 33.0 %collective-permute-start.17 = (bf16[2,16,4096]{2,1,0:T(8,128)(2,1)S(1)}, bf16[2,16,4096]{2,1,0:T(8,128)(2,1)S(1)}, u32[]{:S(2)}, u32[]{:S(2)}) collective-permute-start(bf16[2,16,4096]{2,1,0:T(8,128)(2,1)S(1)} %get-tuple-element.69), channel_id=1, source_target_pairs={{0,6},{1,7},{2,4},{3,5},{4,2},{5,3},{6,0},{7,1},{8,14},{9,15},{10,... | collective-permute-start | bytes 786440 | tf_op jit(solution)/shard_map/ppermute | solution.py:281
  74.4 31.8 %copy-start.2 = (f32[4096]{0:T(1024)S(1)}, f32[4096]{0:T(1024)}, u32[]{:S(2)}) copy-start(f32[4096]{0:T(1024)} %param.7) | copy-start | bytes 49156
  74.4 32.0 %copy-start.1 = (bf16[16,4096]{1,0:T(8,128)(2,1)S(1)}, bf16[16,4096]{1,0:T(8,128)(2,1)}, u32[]{:S(2)}) copy-start(bf16[16,4096]{1,0:T(8,128)(2,1)} %cotangent.1) | copy-start | bytes 393220

commit v14 on v13

--- a/solution.py
+++ b/solution.py
@@ -82,11 +82,11 @@
     )(*in_hbm(tokens, norm_scale_vector.reshape(1, -1), cotangent))
 
 
-def own_kernel(n_pieces, *refs):
+def first_kernel(n_pieces, *refs):
     replica, pieces, refs = refs[0], refs[1 : n_pieces + 1], refs[n_pieces + 1 :]
     weights, refs = refs[:3], refs[3:]
     columns, kept, sent, rows, grad_out_t, out_sum, in_sum = refs[3:]
-    part = kept.shape[1]
+    part, own = kept.shape[1], out_sum.shape[0]
 
     def first():
         pack(pieces, rows)
@@ -105,11 +105,11 @@
         here = pl.ds(pl.multiple_of(step * TILE, TILE), TILE)
         for ref, unit in zip(refs, (hidden, grad_pre, grad_lifted)):
             ref[:, here] = unit
-        grad_pre_t, grad_lifted_t = grad_pre.T, grad_lifted.T
+        grad_pre_t, grad_lifted_t = grad_pre[:own].T, grad_lifted[:own].T
         for at in range(0, out_sum.shape[1], CHUNK):
             here = slice(at, at + CHUNK)
             out_sum[:, here] += jnp.dot(
-                hidden, down_weight[:, here], preferred_element_type=jnp.float32
+                hidden[:own], down_weight[:, here], preferred_element_type=jnp.float32
             )
             in_sum[here] += jnp.dot(
                 gate_weight[here], grad_pre_t, preferred_element_type=jnp.float32
@@ -126,14 +126,15 @@
     sent[1] = summed[part:].astype(sent.dtype)
 
 
-def own_rows(replica, n_dp, pieces, gate_weight, up_weight, down_weight):
+def first_rows(replica, n_dp, own_pieces, more_pieces, gate_weight, up_weight, down_weight):
     depth, hidden_units = gate_weight.shape
-    count = height(pieces)
-    half = pltpu.VMEM((2, count // 2, depth), jnp.bfloat16)
+    pieces = own_pieces + more_pieces
+    own, count = height(own_pieces), height(pieces)
+    half = pltpu.VMEM((2, own // 2, depth), jnp.bfloat16)
     columns = (2, count, depth // n_dp)
     unit = pltpu.VMEM((count, hidden_units), jnp.bfloat16)
     return pl.pallas_call(
-        functools.partial(own_kernel, len(pieces)),
+        functools.partial(first_kernel, len(pieces)),
         in_specs=[pl.BlockSpec(memory_space=pltpu.SMEM)]
         + [pl.BlockSpec(memory_space=pltpu.VMEM)] * len(pieces)
         + [pl.BlockSpec(memory_space=pl.ANY)] * 3,
@@ -141,16 +142,16 @@
         scratch_shapes=[
             pltpu.VMEM((2, count, depth), jnp.bfloat16),
             pltpu.VMEM((depth, count), jnp.bfloat16),
-            pltpu.VMEM((count, depth), jnp.float32),
-            pltpu.VMEM((depth, count), jnp.float32),
+            pltpu.VMEM((own, depth), jnp.float32),
+            pltpu.VMEM((depth, own), jnp.float32),
         ],
-        compiler_params=pltpu.CompilerParams(vmem_limit_bytes=28 * 2**20),
+        compiler_params=pltpu.CompilerParams(vmem_limit_bytes=32 * 2**20),
         cost_estimate=pl.CostEstimate(
-            flops=12 * count * depth * hidden_units,
+            flops=6 * (count + own) * depth * hidden_units,
             bytes_accessed=6 * depth * hidden_units,
             transcendentals=count * hidden_units,
         ),
-        name="own_rows",
+        name="first_rows",
     )(replica, *in_vmem(*pieces), *in_hbm(gate_weight, up_weight, down_weight))
 
 
@@ -297,21 +298,23 @@
     )
     unit3 = swap(unit2, 0, 2)
     across1 = [swap(unit1, 1, 0), swap(unit1, 2, 0)]
-    far_units = far([again0, unit1])
+    far_units, far_across = far([again0, unit1]), far(across)
     last = jnp.concatenate([unit2, unit3], axis=1)
-    across1, far_units, last = lax.optimization_barrier((across1, far_units, last))
+    across1, far_units, far_across, last = lax.optimization_barrier(
+        (across1, far_units, far_across, last)
+    )
     own = [unit0, unit1, last] + far_units + [swap(last, 0, 1)]
+    more = across + across1 + far_across + far(across1)
     rest = [swap(last, b, 0) for b in range(1, n_dp)] + [swap(early, 3, 0)]
-    *units, own_columns, kept, sent = own_rows(
-        replica, n_dp, own, gate_weight, up_weight, down_weight
+    *units, columns, kept, sent = first_rows(
+        replica, n_dp, own, more, gate_weight, up_weight, down_weight
     )
     kept, sent, rest = lax.optimization_barrier((kept, sent, rest))
     pair = (kept.astype(jnp.float32) + swap(sent, 0, 1).astype(jnp.float32)).astype(jnp.bfloat16)
-    rest += across + across1
     rest += far(rest)
     parts = [swap(pair[:, k * rows : (k + 1) * rows], 0, 2 * k) for k in range(1, n_tp // 2)]
     weight_gradients = all_rows(
-        replica, rest, units, own_columns, gate_weight, up_weight, down_weight
+        replica, rest, units, columns, gate_weight, up_weight, down_weight
     )
     parts, weight_gradients = lax.optimization_barrier((parts, weight_gradients))
     total = pair[:, :rows].astype(jnp.float32) + sum(part.astype(jnp.float32) for part in parts)

time: 107 us -> 106 us (level)
  waiting for transfers between devices: 23.1 us -> 14.7 us
  Pallas kernels: 56.5 us -> 62.5 us
  local copies, waits for them, and re-layouts: 0.07 us -> 1.72 us
    pallas_call x1, Pallas kernels: 23.7 us -> 36 us  [first_rows(): pl.pallas_call(functools.partial(first_kernel, len(pieces)), in_specs=[pl...]
    ppermute x26, waiting for transfers between devices: 23.1 us -> 14.7 us  [swap(): return lax.ppermute(array, ('dp', 'tp'), pairs)]
    pallas_call x1, Pallas kernels: 31.6 us -> 25.5 us  [all_rows(): pl.pallas_call(functools.partial(all_kernel, len(pieces)), in_specs=[pl.B...]
    unnamed x6 -> x10, local copies, waits for them, and re-layouts: 0.01 us -> 1.67 us
  transfers between devices with their start and end apart: 26 -> 26, of which waited for: 9 -> 7; matrix products, arithmetic and copies ran while one was open for 1% -> 1% of each run, Pallas kernels for 52% -> 58%
where the time goes in v14:
time: 106 us
  Pallas kernels  62.5 us (59%)
  starting transfers between devices  24 us (23%)
  waiting for transfers between devices  14.7 us (14%)
  other arithmetic  2.42 us (2%)
  local copies, waits for them, and re-layouts  1.72 us (2%)
    pallas_call x1, Pallas kernels, first_rows(): pl.pallas_call(functools.partial(first_kernel, len(pieces)), in_specs=[pl...  36 us
    pallas_call x1, Pallas kernels, all_rows(): pl.pallas_call(functools.partial(all_kernel, len(pieces)), in_specs=[pl.B...  25.5 us
    ppermute x26, starting transfers between devices, swap(): return lax.ppermute(array, ('dp', 'tp'), pairs)  24 us
    ppermute x26, waiting for transfers between devices, swap(): return lax.ppermute(array, ('dp', 'tp'), pairs)  14.7 us
  transfers between devices with their start and end apart: 26, of which 7 were waited for; matrix products, arithmetic and copies ran while one was open for 1% of the time, Pallas kernels for 58%

profile of v14, /device:TPU:0, one launch (start us, length us, event | category | flops | bytes accessed | tf_op | source)
XLA Modules:
  0.0 106.1 jit_solution(2747783929765818139)
XLA Ops:
  0.6 1.1 %normalize.1.refs_1_ = bf16[2,16,4096]{2,1,0:T(8,128)(2,1)S(1)} custom-call(bf16[16,4096]{1,0:T(8,128)(2,1)} %tokens.1, f32[1,4096]{1,0:T(1,128)} %bitcast.14, bf16[16,4096]{1,0:T(8,128)(2,1)} %cotangent.1), custom_call_target="tpu_custom_call" | custom-call | tf_op jit(solution)/shard_map/normalize/pallas_call | solution.py:78
  1.8 3.1 %collective-permute-start.1 = (bf16[2,16,4096]{2,1,0:T(8,128)(2,1)S(1)}, bf16[2,16,4096]{2,1,0:T(8,128)(2,1)S(1)}, u32[]{:S(2)}, u32[]{:S(2)}) collective-permute-start(bf16[2,16,4096]{2,1,0:T(8,128)(2,1)S(1)} %normalize.1.refs_1_), channel_id=1, source_target_pairs={{0,2},{1,3},{2,0},{3,1},{4,6},{5,7},{6,4},{7,5},{8,10},{9,11},{10,... | collective-permute-start | bytes 786440 | tf_op jit(solution)/shard_map/ppermute | solution.py:282
  4.9 2.6 %collective-permute-start = (bf16[2,16,4096]{2,1,0:T(8,128)(2,1)S(1)}, bf16[2,16,4096]{2,1,0:T(8,128)(2,1)S(1)}, u32[]{:S(2)}, u32[]{:S(2)}) collective-permute-start(bf16[2,16,4096]{2,1,0:T(8,128)(2,1)S(1)} %normalize.1.refs_1_), channel_id=1, source_target_pairs={{0,4},{1,5},{2,6},{3,7},{4,0},{5,1},{6,2},{7,3},{8,12},{9,13},{10,... | collective-permute-start | bytes 786440 | tf_op jit(solution)/shard_map/ppermute | solution.py:282
  7.4 1.5 %collective-permute-start.2 = (bf16[2,16,4096]{2,1,0:T(8,128)(2,1)S(1)}, bf16[2,16,4096]{2,1,0:T(8,128)(2,1)S(1)}, u32[]{:S(2)}, u32[]{:S(2)}) collective-permute-start(bf16[2,16,4096]{2,1,0:T(8,128)(2,1)S(1)} %normalize.1.refs_1_), channel_id=1, source_target_pairs={{0,8},{1,9},{2,10},{3,11},{4,12},{5,13},{6,14},{7,15},{8,0},{9,1},... | collective-permute-start | bytes 786440 | tf_op jit(solution)/shard_map/ppermute | solution.py:282
  8.9 1.5 %collective-permute-start.3 = (bf16[2,16,4096]{2,1,0:T(8,128)(2,1)S(1)}, bf16[2,16,4096]{2,1,0:T(8,128)(2,1)S(1)}, u32[]{:S(2)}, u32[]{:S(2)}) collective-permute-start(bf16[2,16,4096]{2,1,0:T(8,128)(2,1)S(1)} %normalize.1.refs_1_), channel_id=1, source_target_pairs={{0,16},{1,17},{2,18},{3,19},{4,20},{5,21},{6,22},{7,23},{8,24},{9,... | collective-permute-start | bytes 786440 | tf_op jit(solution)/shard_map/ppermute | solution.py:282
  10.5 6.2 %collective-permute-done.1.refs_2_ = bf16[2,16,4096]{2,1,0:T(8,128)(2,1)S(1)} collective-permute-done((bf16[2,16,4096]{2,1,0:T(8,128)(2,1)S(1)}, bf16[2,16,4096]{2,1,0:T(8,128)(2,1)S(1)}, u32[]{:S(2)}, u32[]{:S(2)}) %collective-permute-start.1) | collective-permute-done | bytes 262176 | tf_op jit(solution)/shard_map/ppermute | solution.py:282
  16.7 0.8 pad_maximum_fusion
  17.5 1.7 %collective-permute-done = bf16[2,16,4096]{2,1,0:T(8,128)(2,1)S(1)} collective-permute-done((bf16[2,16,4096]{2,1,0:T(8,128)(2,1)S(1)}, bf16[2,16,4096]{2,1,0:T(8,128)(2,1)S(1)}, u32[]{:S(2)}, u32[]{:S(2)}) %collective-permute-start) | collective-permute-done | bytes 262176 | tf_op jit(solution)/shard_map/ppermute | solution.py:282
  19.2 1.5 %collective-permute-start.4 = (bf16[2,16,4096]{2,1,0:T(8,128)(2,1)S(1)}, bf16[2,16,4096]{2,1,0:T(8,128)(2,1)S(1)}, u32[]{:S(2)}, u32[]{:S(2)}) collective-permute-start(bf16[2,16,4096]{2,1,0:T(8,128)(2,1)S(1)} %collective-permute-done.1.refs_2_), channel_id=1, source_target_pairs={{0,8},{1,9},{2,10},{3,11},{4,12},{5,13},{6,14},{7,15},{8,0},{9,1},... | collective-permute-start | bytes 786440 | tf_op jit(solution)/shard_map/ppermute | solution.py:282
  20.7 0.4 collective-permute-start.10
  21.1 1.5 %collective-permute-start.5 = (bf16[2,16,4096]{2,1,0:T(8,128)(2,1)S(1)}, bf16[2,16,4096]{2,1,0:T(8,128)(2,1)S(1)}, u32[]{:S(2)}, u32[]{:S(2)}) collective-permute-start(bf16[2,16,4096]{2,1,0:T(8,128)(2,1)S(1)} %collective-permute-done.1.refs_2_), channel_id=1, source_target_pairs={{0,16},{1,17},{2,18},{3,19},{4,20},{5,21},{6,22},{7,23},{8,24},{9,... | collective-permute-start | bytes 786440 | tf_op jit(solution)/shard_map/ppermute | solution.py:282
  22.7 0.5 collective-permute-start.6
  23.2 2.4 %collective-permute-done.4.refs_9_ = bf16[2,16,4096]{2,1,0:T(8,128)(2,1)S(1)} collective-permute-done((bf16[2,16,4096]{2,1,0:T(8,128)(2,1)S(1)}, bf16[2,16,4096]{2,1,0:T(8,128)(2,1)S(1)}, u32[]{:S(2)}, u32[]{:S(2)}) %collective-permute-start.4) | collective-permute-done | bytes 262176 | tf_op jit(solution)/shard_map/ppermute | solution.py:282
  25.6 1.5 %collective-permute-done.10 = bf16[2,16,4096]{2,1,0:T(8,128)(2,1)S(1)} collective-permute-done((bf16[2,16,4096]{2,1,0:T(8,128)(2,1)S(1)}, bf16[2,16,4096]{2,1,0:T(8,128)(2,1)S(1)}, u32[]{:S(2)}, u32[]{:S(2)}) %collective-permute-start.10) | collective-permute-done | bytes 262176 | tf_op jit(solution)/shard_map/ppermute | solution.py:282
  27.1 0.6 collective-permute-done.5.refs_10_
  27.7 0.9 collective-permute-done.9.refs_12_
  28.6 0.7 copy-done
  29.4 0.4 collective-permute-start.12
  29.9 1.5 %collective-permute-start.17 = (bf16[2,32,4096]{2,1,0:T(8,128)(2,1)}, bf16[2,32,4096]{2,1,0:T(8,128)(2,1)S(1)}, u32[]{:S(2)}, u32[]{:S(2)}) collective-permute-start(bf16[2,32,4096]{2,1,0:T(8,128)(2,1)} %pad_maximum_fusion), channel_id=1, source_target_pairs={{0,24},{1,25},{2,26},{3,27},{4,28},{5,29},{6,30},{7,31},{8,16},{9,... | collective-permute-start | bytes 1572872 | tf_op jit(solution)/shard_map/ppermute | solution.py:282
  31.5 1.5 %collective-permute-start.14 = (bf16[2,32,4096]{2,1,0:T(8,128)(2,1)S(1)}, bf16[2,32,4096]{2,1,0:T(8,128)(2,1)S(1)}, u32[]{:S(2)}, u32[]{:S(2)}) collective-permute-start(bf16[2,32,4096]{2,1,0:T(8,128)(2,1)S(1)} %pad_maximum_fusion.1.refs_3_), channel_id=1, source_target_pairs={{0,8},{1,9},{2,10},{3,11},{4,12},{5,13},{6,14},{7,15},{8,0},{9,1},... | collective-permute-start | bytes 1572872 | tf_op jit(solution)/shard_map/ppermute | solution.py:282
  32.9 0.5 collective-permute-start.15
  33.5 1.5 %collective-permute-start.16 = (bf16[2,32,4096]{2,1,0:T(8,128)(2,1)S(1)}, bf16[2,32,4096]{2,1,0:T(8,128)(2,1)S(1)}, u32[]{:S(2)}, u32[]{:S(2)}) collective-permute-start(bf16[2,32,4096]{2,1,0:T(8,128)(2,1)S(1)} %pad_maximum_fusion.1.refs_3_), channel_id=1, source_target_pairs={{0,24},{1,25},{2,26},{3,27},{4,28},{5,29},{6,30},{7,31},{8,16},{9,... | collective-permute-start | bytes 1572872 | tf_op jit(solution)/shard_map/ppermute | solution.py:282
  35.0 0.9 copy-done.1
  35.9 36.0 %first_rows.1 = (bf16[256,1792]{1,0:T(8,128)(2,1)S(1)}, bf16[256,1792]{1,0:T(8,128)(2,1)S(1)}, bf16[256,1792]{1,0:T(8,128)(2,1)S(1)}, bf16[2,256,1024]{2,1,0:T(8...) custom-call(s32[1]{0:T(128)} %bitcast.refs_0_, ...), custom_call_target="tpu_custom_call" | custom-call | flops 16911433728 | bytes 44040192 | tf_op jit(solution)/shard_map/first_rows/pallas_call | solution.py:136
  72.2 0.6 collective-permute-start.22
  72.8 0.4 collective-permute-start.24
  73.3 1.3 %collective-permute-done.18 = bf16[2,64,4096]{2,1,0:T(8,128)(2,1)S(1)} collective-permute-done((bf16[2,64,4096]{2,1,0:T(8,128)(2,1)S(1)}, bf16[2,64,4096]{2,1,0:T(8,128)(2,1)S(1)}, u32[]{:S(2)}, u32[]{:S(2)}) %collective-permute-start.18) | collective-permute-done | bytes 1048608 | tf_op jit(solution)/shard_map/ppermute | solution.py:282
  75.0 1.1 %collective-permute-start.19 = (bf16[2,16,4096]{2,1,0:T(8,128)(2,1)S(1)}, bf16[2,16,4096]{2,1,0:T(8,128)(2,1)S(1)}, u32[]{:S(2)}, u32[]{:S(2)}) collective-permute-start(bf16[2,16,4096]{2,1,0:T(8,128)(2,1)S(1)} %get-tuple-element.75), channel_id=1, source_target_pairs={{0,2},{1,3},{2,0},{3,1},{4,6},{5,7},{6,4},{7,5},{8,10},{9,11},{10,... | collective-permute-start | bytes 786440 | tf_op jit(solution)/shard_map/ppermute | solution.py:282
  76.1 2.0 %collective-permute-start.20 = (bf16[2,16,4096]{2,1,0:T(8,128)(2,1)S(1)}, bf16[2,16,4096]{2,1,0:T(8,128)(2,1)S(1)}, u32[]{:S(2)}, u32[]{:S(2)}) collective-permute-start(bf16[2,16,4096]{2,1,0:T(8,128)(2,1)S(1)} %get-tuple-element.74), channel_id=1, source_target_pairs={{0,4},{1,5},{2,6},{3,7},{4,0},{5,1},{6,2},{7,3},{8,12},{9,13},{10,... | collective-permute-start | bytes 786440 | tf_op jit(solution)/shard_map/ppermute | solution.py:282
  78.1 1.3 %collective-permute-start.21 = (bf16[2,16,4096]{2,1,0:T(8,128)(2,1)S(1)}, bf16[2,16,4096]{2,1,0:T(8,128)(2,1)S(1)}, u32[]{:S(2)}, u32[]{:S(2)}) collective-permute-start(bf16[2,16,4096]{2,1,0:T(8,128)(2,1)S(1)} %get-tuple-element.73), channel_id=1, source_target_pairs={{0,6},{1,7},{2,4},{3,5},{4,2},{5,3},{6,0},{7,1},{8,14},{9,15},{10,... | collective-permute-start | bytes 786440 | tf_op jit(solution)/shard_map/ppermute | solution.py:282
  79.4 25.5 %all_rows.1 = (bf16[1024,1792]{1,0:T(8,128)(2,1)}, bf16[1024,1792]{1,0:T(8,128)(2,1)}, bf16[1792,1024]{1,0:T(8,128)(2,1)}) custom-call(s32[1]{0:T(128)} %bitcast.refs_0_, bf16[2,32,4096]{2,1,0:T(8,128)(2,1)S(1)} %collective-permute-done.14.refs_1_, bf16[2,32,4096]{2,1,0:T(8,128)(2,1)S(1)} %collective-permute-done.15.refs_2_, ...), custom_call_target="tpu_custom_call" | custom-call | flops 16911433728 | bytes 55050240 | tf_op jit(solution)/shard_map/all_rows/pallas_call | solution.py:236
  105.3 0.8 fusion.6
  (43 shorter events, 1.4 us)
Async XLA Ops:
  1.8 14.9 %collective-permute-start.1 = (bf16[2,16,4096]{2,1,0:T(8,128)(2,1)S(1)}, bf16[2,16,4096]{2,1,0:T(8,128)(2,1)S(1)}, u32[]{:S(2)}, u32[]{:S(2)}) collective-permute-start(bf16[2,16,4096]{2,1,0:T(8,128)(2,1)S(1)} %normalize.1.refs_1_), channel_id=1, source_target_pairs={{0,2},{1,3},{2,0},{3,1},{4,6},{5,7},{6,4},{7,5},{8,10},{9,11},{10,... | collective-permute-start | bytes 786440 | tf_op jit(solution)/shard_map/ppermute | solution.py:282
  4.9 14.3 %collective-permute-start = (bf16[2,16,4096]{2,1,0:T(8,128)(2,1)S(1)}, bf16[2,16,4096]{2,1,0:T(8,128)(2,1)S(1)}, u32[]{:S(2)}, u32[]{:S(2)}) collective-permute-start(bf16[2,16,4096]{2,1,0:T(8,128)(2,1)S(1)} %normalize.1.refs_1_), channel_id=1, source_target_pairs={{0,4},{1,5},{2,6},{3,7},{4,0},{5,1},{6,2},{7,3},{8,12},{9,13},{10,... | collective-permute-start | bytes 786440 | tf_op jit(solution)/shard_map/ppermute | solution.py:282
  7.4 11.7 %collective-permute-start.2 = (bf16[2,16,4096]{2,1,0:T(8,128)(2,1)S(1)}, bf16[2,16,4096]{2,1,0:T(8,128)(2,1)S(1)}, u32[]{:S(2)}, u32[]{:S(2)}) collective-permute-start(bf16[2,16,4096]{2,1,0:T(8,128)(2,1)S(1)} %normalize.1.refs_1_), channel_id=1, source_target_pairs={{0,8},{1,9},{2,10},{3,11},{4,12},{5,13},{6,14},{7,15},{8,0},{9,1},... | collective-permute-start | bytes 786440 | tf_op jit(solution)/shard_map/ppermute | solution.py:282
  8.9 10.3 %collective-permute-start.3 = (bf16[2,16,4096]{2,1,0:T(8,128)(2,1)S(1)}, bf16[2,16,4096]{2,1,0:T(8,128)(2,1)S(1)}, u32[]{:S(2)}, u32[]{:S(2)}) collective-permute-start(bf16[2,16,4096]{2,1,0:T(8,128)(2,1)S(1)} %normalize.1.refs_1_), channel_id=1, source_target_pairs={{0,16},{1,17},{2,18},{3,19},{4,20},{5,21},{6,22},{7,23},{8,24},{9,... | collective-permute-start | bytes 786440 | tf_op jit(solution)/shard_map/ppermute | solution.py:282
  19.2 6.4 %collective-permute-start.4 = (bf16[2,16,4096]{2,1,0:T(8,128)(2,1)S(1)}, bf16[2,16,4096]{2,1,0:T(8,128)(2,1)S(1)}, u32[]{:S(2)}, u32[]{:S(2)}) collective-permute-start(bf16[2,16,4096]{2,1,0:T(8,128)(2,1)S(1)} %collective-permute-done.1.refs_2_), channel_id=1, source_target_pairs={{0,8},{1,9},{2,10},{3,11},{4,12},{5,13},{6,14},{7,15},{8,0},{9,1},... | collective-permute-start | bytes 786440 | tf_op jit(solution)/shard_map/ppermute | solution.py:282
  20.7 6.4 %collective-permute-start.10 = (bf16[2,16,4096]{2,1,0:T(8,128)(2,1)S(1)}, bf16[2,16,4096]{2,1,0:T(8,128)(2,1)S(1)}, u32[]{:S(2)}, u32[]{:S(2)}) collective-permute-start(bf16[2,16,4096]{2,1,0:T(8,128)(2,1)S(1)} %collective-permute-done), channel_id=1, source_target_pairs={{0,2},{1,3},{2,0},{3,1},{4,6},{5,7},{6,4},{7,5},{8,10},{9,11},{10,... | collective-permute-start | bytes 786440 | tf_op jit(solution)/shard_map/ppermute | solution.py:282
  21.1 6.6 %collective-permute-start.5 = (bf16[2,16,4096]{2,1,0:T(8,128)(2,1)S(1)}, bf16[2,16,4096]{2,1,0:T(8,128)(2,1)S(1)}, u32[]{:S(2)}, u32[]{:S(2)}) collective-permute-start(bf16[2,16,4096]{2,1,0:T(8,128)(2,1)S(1)} %collective-permute-done.1.refs_2_), channel_id=1, source_target_pairs={{0,16},{1,17},{2,18},{3,19},{4,20},{5,21},{6,22},{7,23},{8,24},{9,... | collective-permute-start | bytes 786440 | tf_op jit(solution)/shard_map/ppermute | solution.py:282
  22.7 5.0 %collective-permute-start.7 = (bf16[2,16,4096]{2,1,0:T(8,128)(2,1)S(1)}, bf16[2,16,4096]{2,1,0:T(8,128)(2,1)S(1)}, u32[]{:S(2)}, u32[]{:S(2)}) collective-permute-start(bf16[2,16,4096]{2,1,0:T(8,128)(2,1)S(1)} %collective-permute-done.1.refs_2_), channel_id=1, source_target_pairs={{0,1},{1,0},{2,3},{3,2},{4,5},{5,4},{6,7},{7,6},{8,9},{9,8},{10,11... | collective-permute-start | bytes 786440 | tf_op jit(solution)/shard_map/ppermute | solution.py:282
  22.7 5.0 %collective-permute-start.6 = (bf16[2,16,4096]{2,1,0:T(8,128)(2,1)S(1)}, bf16[2,16,4096]{2,1,0:T(8,128)(2,1)S(1)}, u32[]{:S(2)}, u32[]{:S(2)}) collective-permute-start(bf16[2,16,4096]{2,1,0:T(8,128)(2,1)S(1)} %normalize.1.refs_1_), channel_id=1, source_target_pairs={{0,1},{1,0},{2,3},{3,2},{4,5},{5,4},{6,7},{7,6},{8,9},{9,8},{10,11... | collective-permute-start | bytes 786440 | tf_op jit(solution)/shard_map/ppermute | solution.py:282
  25.6 2.1 %collective-permute-start.8 = (bf16[2,16,4096]{2,1,0:T(8,128)(2,1)S(1)}, bf16[2,16,4096]{2,1,0:T(8,128)(2,1)S(1)}, u32[]{:S(2)}, u32[]{:S(2)}) collective-permute-start(bf16[2,16,4096]{2,1,0:T(8,128)(2,1)S(1)} %collective-permute-done.2.refs_7_), channel_id=1, source_target_pairs={{0,1},{1,0},{2,3},{3,2},{4,5},{5,4},{6,7},{7,6},{8,9},{9,8},{10,11... | collective-permute-start | bytes 786440 | tf_op jit(solution)/shard_map/ppermute | solution.py:282
  27.1 1.5 %collective-permute-start.9 = (bf16[2,16,4096]{2,1,0:T(8,128)(2,1)S(1)}, bf16[2,16,4096]{2,1,0:T(8,128)(2,1)S(1)}, u32[]{:S(2)}, u32[]{:S(2)}) collective-permute-start(bf16[2,16,4096]{2,1,0:T(8,128)(2,1)S(1)} %collective-permute-done.3.refs_8_), channel_id=1, source_target_pairs={{0,1},{1,0},{2,3},{3,2},{4,5},{5,4},{6,7},{7,6},{8,9},{9,8},{10,11... | collective-permute-start | bytes 786440 | tf_op jit(solution)/shard_map/ppermute | solution.py:282
  28.6 0.7 copy-start
  29.3 5.7 %collective-permute-start.11 = (bf16[2,32,4096]{2,1,0:T(8,128)(2,1)S(1)}, bf16[2,32,4096]{2,1,0:T(8,128)(2,1)S(1)}, u32[]{:S(2)}, u32[]{:S(2)}) collective-permute-start(bf16[2,32,4096]{2,1,0:T(8,128)(2,1)S(1)} %pad_maximum_fusion.1.refs_3_), channel_id=1, source_target_pairs={{0,1},{1,0},{2,3},{3,2},{4,5},{5,4},{6,7},{7,6},{8,9},{9,8},{10,11... | collective-permute-start | bytes 1572872 | tf_op jit(solution)/shard_map/ppermute | solution.py:282
  29.4 3.5 %collective-permute-start.12 = (bf16[2,16,4096]{2,1,0:T(8,128)(2,1)S(1)}, bf16[2,16,4096]{2,1,0:T(8,128)(2,1)}, u32[]{:S(2)}, u32[]{:S(2)}) collective-permute-start(bf16[2,16,4096]{2,1,0:T(8,128)(2,1)S(1)} %collective-permute-done.4.refs_9_), channel_id=1, source_target_pairs={{0,1},{1,0},{2,3},{3,2},{4,5},{5,4},{6,7},{7,6},{8,9},{9,8},{10,11... | collective-permute-start | bytes 786440 | tf_op jit(solution)/shard_map/ppermute | solution.py:282
  29.8 3.6 %collective-permute-start.13 = (bf16[2,16,4096]{2,1,0:T(8,128)(2,1)S(1)}, bf16[2,16,4096]{2,1,0:T(8,128)(2,1)}, u32[]{:S(2)}, u32[]{:S(2)}) collective-permute-start(bf16[2,16,4096]{2,1,0:T(8,128)(2,1)S(1)} %collective-permute-done.5.refs_10_), channel_id=1, source_target_pairs={{0,1},{1,0},{2,3},{3,2},{4,5},{5,4},{6,7},{7,6},{8,9},{9,8},{10,11... | collective-permute-start | bytes 786440 | tf_op jit(solution)/shard_map/ppermute | solution.py:282
  29.9 41.9 %collective-permute-start.17 = (bf16[2,32,4096]{2,1,0:T(8,128)(2,1)}, bf16[2,32,4096]{2,1,0:T(8,128)(2,1)S(1)}, u32[]{:S(2)}, u32[]{:S(2)}) collective-permute-start(bf16[2,32,4096]{2,1,0:T(8,128)(2,1)} %pad_maximum_fusion), channel_id=1, source_target_pairs={{0,24},{1,25},{2,26},{3,27},{4,28},{5,29},{6,30},{7,31},{8,16},{9,... | collective-permute-start | bytes 1572872 | tf_op jit(solution)/shard_map/ppermute | solution.py:282
  31.5 40.4 %collective-permute-start.14 = (bf16[2,32,4096]{2,1,0:T(8,128)(2,1)S(1)}, bf16[2,32,4096]{2,1,0:T(8,128)(2,1)S(1)}, u32[]{:S(2)}, u32[]{:S(2)}) collective-permute-start(bf16[2,32,4096]{2,1,0:T(8,128)(2,1)S(1)} %pad_maximum_fusion.1.refs_3_), channel_id=1, source_target_pairs={{0,8},{1,9},{2,10},{3,11},{4,12},{5,13},{6,14},{7,15},{8,0},{9,1},... | collective-permute-start | bytes 1572872 | tf_op jit(solution)/shard_map/ppermute | solution.py:282
  32.9 38.9 %collective-permute-start.15 = (bf16[2,32,4096]{2,1,0:T(8,128)(2,1)S(1)}, bf16[2,32,4096]{2,1,0:T(8,128)(2,1)S(1)}, u32[]{:S(2)}, u32[]{:S(2)}) collective-permute-start(bf16[2,32,4096]{2,1,0:T(8,128)(2,1)S(1)} %pad_maximum_fusion.1.refs_3_), channel_id=1, source_target_pairs={{0,16},{1,17},{2,18},{3,19},{4,20},{5,21},{6,22},{7,23},{8,24},{9,... | collective-permute-start | bytes 1572872 | tf_op jit(solution)/shard_map/ppermute | solution.py:282
  33.5 38.4 %collective-permute-start.16 = (bf16[2,32,4096]{2,1,0:T(8,128)(2,1)S(1)}, bf16[2,32,4096]{2,1,0:T(8,128)(2,1)S(1)}, u32[]{:S(2)}, u32[]{:S(2)}) collective-permute-start(bf16[2,32,4096]{2,1,0:T(8,128)(2,1)S(1)} %pad_maximum_fusion.1.refs_3_), channel_id=1, source_target_pairs={{0,24},{1,25},{2,26},{3,27},{4,28},{5,29},{6,30},{7,31},{8,16},{9,... | collective-permute-start | bytes 1572872 | tf_op jit(solution)/shard_map/ppermute | solution.py:282
  35.0 1.0 copy-start.1
  35.9 36.1 %copy-start.2 = (bf16[16,4096]{1,0:T(8,128)(2,1)S(1)}, bf16[16,4096]{1,0:T(8,128)(2,1)}, u32[]{:S(2)}) copy-start(bf16[16,4096]{1,0:T(8,128)(2,1)} %tokens.1) | copy-start | bytes 393220
  71.9 2.7 %collective-permute-start.18 = (bf16[2,64,4096]{2,1,0:T(8,128)(2,1)S(1)}, bf16[2,64,4096]{2,1,0:T(8,128)(2,1)S(1)}, u32[]{:S(2)}, u32[]{:S(2)}) collective-permute-start(bf16[2,64,4096]{2,1,0:T(8,128)(2,1)S(1)} %get-tuple-element.55), channel_id=1, source_target_pairs={{0,1},{1,0},{2,3},{3,2},{4,5},{5,4},{6,7},{7,6},{8,9},{9,8},{10,11... | collective-permute-start | bytes 3145736 | tf_op jit(solution)/shard_map/ppermute | solution.py:282
  72.2 3.9 %collective-permute-start.22 = (bf16[2,32,4096]{2,1,0:T(8,128)(2,1)S(1)}, bf16[2,32,4096]{2,1,0:T(8,128)(2,1)S(1)}, u32[]{:S(2)}, u32[]{:S(2)}) collective-permute-start(bf16[2,32,4096]{2,1,0:T(8,128)(2,1)S(1)} %collective-permute-done.14.refs_1_), channel_id=1, source_target_pairs={{0,1},{1,0},{2,3},{3,2},{4,5},{5,4},{6,7},{7,6},{8,9},{9,8},{10,11... | collective-permute-start | bytes 1572872 | tf_op jit(solution)/shard_map/ppermute | solution.py:282
  72.7 5.4 %collective-permute-start.23 = (bf16[2,32,4096]{2,1,0:T(8,128)(2,1)S(1)}, bf16[2,32,4096]{2,1,0:T(8,128)(2,1)S(1)}, u32[]{:S(2)}, u32[]{:S(2)}) collective-permute-start(bf16[2,32,4096]{2,1,0:T(8,128)(2,1)S(1)} %collective-permute-done.15.refs_2_), channel_id=1, source_target_pairs={{0,1},{1,0},{2,3},{3,2},{4,5},{5,4},{6,7},{7,6},{8,9},{9,8},{10,11... | collective-permute-start | bytes 1572872 | tf_op jit(solution)/shard_map/ppermute | solution.py:282
  72.8 6.6 %collective-permute-start.24 = (bf16[2,32,4096]{2,1,0:T(8,128)(2,1)S(1)}, bf16[2,32,4096]{2,1,0:T(8,128)(2,1)S(1)}, u32[]{:S(2)}, u32[]{:S(2)}) collective-permute-start(bf16[2,32,4096]{2,1,0:T(8,128)(2,1)S(1)} %collective-permute-done.16.refs_3_), channel_id=1, source_target_pairs={{0,1},{1,0},{2,3},{3,2},{4,5},{5,4},{6,7},{7,6},{8,9},{9,8},{10,11... | collective-permute-start | bytes 1572872 | tf_op jit(solution)/shard_map/ppermute | solution.py:282
  73.2 6.2 %collective-permute-start.25 = (bf16[2,32,4096]{2,1,0:T(8,128)(2,1)S(1)}, bf16[2,32,4096]{2,1,0:T(8,128)(2,1)S(1)}, u32[]{:S(2)}, u32[]{:S(2)}) collective-permute-start(bf16[2,32,4096]{2,1,0:T(8,128)(2,1)S(1)} %collective-permute-done.17.refs_4_), channel_id=1, source_target_pairs={{0,1},{1,0},{2,3},{3,2},{4,5},{5,4},{6,7},{7,6},{8,9},{9,8},{10,11... | collective-permute-start | bytes 1572872 | tf_op jit(solution)/shard_map/ppermute | solution.py:282
  75.0 29.9 %collective-permute-start.19 = (bf16[2,16,4096]{2,1,0:T(8,128)(2,1)S(1)}, bf16[2,16,4096]{2,1,0:T(8,128)(2,1)S(1)}, u32[]{:S(2)}, u32[]{:S(2)}) collective-permute-start(bf16[2,16,4096]{2,1,0:T(8,128)(2,1)S(1)} %get-tuple-element.75), channel_id=1, source_target_pairs={{0,2},{1,3},{2,0},{3,1},{4,6},{5,7},{6,4},{7,5},{8,10},{9,11},{10,... | collective-permute-start | bytes 786440 | tf_op jit(solution)/shard_map/ppermute | solution.py:282
  76.1 28.8 %collective-permute-start.20 = (bf16[2,16,4096]{2,1,0:T(8,128)(2,1)S(1)}, bf16[2,16,4096]{2,1,0:T(8,128)(2,1)S(1)}, u32[]{:S(2)}, u32[]{:S(2)}) collective-permute-start(bf16[2,16,4096]{2,1,0:T(8,128)(2,1)S(1)} %get-tuple-element.74), channel_id=1, source_target_pairs={{0,4},{1,5},{2,6},{3,7},{4,0},{5,1},{6,2},{7,3},{8,12},{9,13},{10,... | collective-permute-start | bytes 786440 | tf_op jit(solution)/shard_map/ppermute | solution.py:282
  78.1 26.8 %collective-permute-start.21 = (bf16[2,16,4096]{2,1,0:T(8,128)(2,1)S(1)}, bf16[2,16,4096]{2,1,0:T(8,128)(2,1)S(1)}, u32[]{:S(2)}, u32[]{:S(2)}) collective-permute-start(bf16[2,16,4096]{2,1,0:T(8,128)(2,1)S(1)} %get-tuple-element.73), channel_id=1, source_target_pairs={{0,6},{1,7},{2,4},{3,5},{4,2},{5,3},{6,0},{7,1},{8,14},{9,15},{10,... | collective-permute-start | bytes 786440 | tf_op jit(solution)/shard_map/ppermute | solution.py:282
  79.4 25.6 %copy-start.4 = (f32[4096]{0:T(1024)S(1)}, f32[4096]{0:T(1024)}, u32[]{:S(2)}) copy-start(f32[4096]{0:T(1024)} %param.7) | copy-start | bytes 49156
  79.4 25.9 %copy-start.3 = (bf16[16,4096]{1,0:T(8,128)(2,1)S(1)}, bf16[16,4096]{1,0:T(8,128)(2,1)}, u32[]{:S(2)}) copy-start(bf16[16,4096]{1,0:T(8,128)(2,1)} %cotangent.1) | copy-start | bytes 393220

commit v15 on v13

--- a/solution.py
+++ b/solution.py
@@ -82,14 +82,16 @@
     )(*in_hbm(tokens, norm_scale_vector.reshape(1, -1), cotangent))
 
 
-def own_kernel(n_pieces, *refs):
+def own_kernel(n_pieces, n_more, *refs):
     replica, pieces, refs = refs[0], refs[1 : n_pieces + 1], refs[n_pieces + 1 :]
+    more, refs = refs[:n_more], refs[n_more:]
     weights, refs = refs[:3], refs[3:]
-    columns, kept, sent, rows, grad_out_t, out_sum, in_sum = refs[3:]
+    columns, kept, sent, packed, rows, grad_out_t, out_sum, in_sum = refs[3:]
     part = kept.shape[1]
 
     def first():
         pack(pieces, rows)
+        pack(more, packed)
         width = columns.shape[2]
         columns[...] = rows[:, :, pl.ds(pl.multiple_of(replica[0] * width, 128), width)]
         grad_out_t[...] = rows[1].T
@@ -126,18 +128,26 @@
     sent[1] = summed[part:].astype(sent.dtype)
 
 
-def own_rows(replica, n_dp, pieces, gate_weight, up_weight, down_weight):
+def own_rows(replica, n_dp, pieces, more, gate_weight, up_weight, down_weight):
     depth, hidden_units = gate_weight.shape
     count = height(pieces)
     half = pltpu.VMEM((2, count // 2, depth), jnp.bfloat16)
     columns = (2, count, depth // n_dp)
     unit = pltpu.VMEM((count, hidden_units), jnp.bfloat16)
     return pl.pallas_call(
-        functools.partial(own_kernel, len(pieces)),
+        functools.partial(own_kernel, len(pieces), len(more)),
         in_specs=[pl.BlockSpec(memory_space=pltpu.SMEM)]
-        + [pl.BlockSpec(memory_space=pltpu.VMEM)] * len(pieces)
+        + [pl.BlockSpec(memory_space=pltpu.VMEM)] * (len(pieces) + len(more))
         + [pl.BlockSpec(memory_space=pl.ANY)] * 3,
-        out_shape=[unit, unit, unit, pltpu.VMEM(columns, jnp.bfloat16), half, half],
+        out_shape=[
+            unit,
+            unit,
+            unit,
+            pltpu.VMEM(columns, jnp.bfloat16),
+            half,
+            half,
+            pltpu.VMEM((2, height(more), depth), jnp.bfloat16),
+        ],
         scratch_shapes=[
             pltpu.VMEM((2, count, depth), jnp.bfloat16),
             pltpu.VMEM((depth, count), jnp.bfloat16),
@@ -151,7 +161,7 @@
             transcendentals=count * hidden_units,
         ),
         name="own_rows",
-    )(replica, *in_vmem(*pieces), *in_hbm(gate_weight, up_weight, down_weight))
+    )(replica, *in_vmem(*pieces, *more), *in_hbm(gate_weight, up_weight, down_weight))
 
 
 def all_kernel(n_pieces, *refs):
@@ -290,24 +300,21 @@
     unit_input = expanded_hidden * reciprocal_root_mean
     unit0 = normalize(tokens, norm_scale_vector, cotangent)
     unit2, unit1 = swap(unit0, 0, 4), swap(unit0, 0, 2)
-    across = [swap(unit0, 1, 0), swap(unit0, 2, 0)]
-    early = jnp.concatenate([unit0, unit1], axis=1)
-    unit2, unit1, across, early, again0 = lax.optimization_barrier(
-        (unit2, unit1, across, early, unit0)
-    )
+    across = [swap(unit0, b, 0) for b in range(1, n_dp)]
+    unit2, unit1, across, again0 = lax.optimization_barrier((unit2, unit1, across, unit0))
     unit3 = swap(unit2, 0, 2)
     across1 = [swap(unit1, 1, 0), swap(unit1, 2, 0)]
     far_units = far([again0, unit1])
     last = jnp.concatenate([unit2, unit3], axis=1)
     across1, far_units, last = lax.optimization_barrier((across1, far_units, last))
     own = [unit0, unit1, last] + far_units + [swap(last, 0, 1)]
-    rest = [swap(last, b, 0) for b in range(1, n_dp)] + [swap(early, 3, 0)]
-    *units, own_columns, kept, sent = own_rows(
-        replica, n_dp, own, gate_weight, up_weight, down_weight
+    rest = [swap(last, b, 0) for b in range(1, n_dp)] + [swap(unit1, 3, 0)]
+    *units, own_columns, kept, sent, packed = own_rows(
+        replica, n_dp, own, across + across1, gate_weight, up_weight, down_weight
     )
     kept, sent, rest = lax.optimization_barrier((kept, sent, rest))
     pair = (kept.astype(jnp.float32) + swap(sent, 0, 1).astype(jnp.float32)).astype(jnp.bfloat16)
-    rest += across + across1
+    rest += [packed]
     rest += far(rest)
     parts = [swap(pair[:, k * rows : (k + 1) * rows], 0, 2 * k) for k in range(1, n_tp // 2)]
     weight_gradients = all_rows(

time: 107 us -> 105 us (0.981)
  starting transfers between devices: 24.3 us -> 23.2 us
    ppermute x26 -> x24, starting transfers between devices: 24.3 us -> 23.2 us  [swap(): return lax.ppermute(array, ('dp', 'tp'), pairs)]
    ppermute x26 -> x24, waiting for transfers between devices: 23.1 us -> 22.4 us  [swap(): return lax.ppermute(array, ('dp', 'tp'), pairs)]
  transfers between devices with their start and end apart: 26 -> 24, of which waited for: 9 -> 9; matrix products, arithmetic and copies ran while one was open for 1% -> 0% of each run, Pallas kernels for 52% -> 53%
where the time goes in v15:
time: 105 us; the launch traced here: 104 us
  Pallas kernels  56.4 us (54%)
  starting transfers between devices  23.2 us (22%)
  waiting for transfers between devices  22.4 us (21%)
  other arithmetic  1.59 us (2%)
    pallas_call x1, Pallas kernels, all_rows(): pl.pallas_call(functools.partial(all_kernel, len(pieces)), in_specs=[pl.B...  31.5 us
    pallas_call x1, Pallas kernels, own_rows(): pl.pallas_call(functools.partial(own_kernel, len(pieces), len(more)), in_...  23.8 us
    ppermute x24, starting transfers between devices, swap(): return lax.ppermute(array, ('dp', 'tp'), pairs)  23.2 us
    ppermute x24, waiting for transfers between devices, swap(): return lax.ppermute(array, ('dp', 'tp'), pairs)  22.4 us
  transfers between devices with their start and end apart: 24, of which 9 were waited for; matrix products, arithmetic and copies ran while one was open for 0% of the time, Pallas kernels for 53%

profile of v15, /device:TPU:0, one launch (start us, length us, event | category | flops | bytes accessed | tf_op | source)
XLA Modules:
  0.0 104.4 jit_solution(147451792640679176)
XLA Ops:
  0.6 1.1 %normalize.1.refs_1_ = bf16[2,16,4096]{2,1,0:T(8,128)(2,1)S(1)} custom-call(bf16[16,4096]{1,0:T(8,128)(2,1)} %tokens.1, f32[1,4096]{1,0:T(1,128)} %bitcast.14, bf16[16,4096]{1,0:T(8,128)(2,1)} %cotangent.1), custom_call_target="tpu_custom_call" | custom-call | tf_op jit(solution)/shard_map/normalize/pallas_call | solution.py:78
  1.8 4.1 %collective-permute-start = (bf16[2,16,4096]{2,1,0:T(8,128)(2,1)S(1)}, bf16[2,16,4096]{2,1,0:T(8,128)(2,1)S(1)}, u32[]{:S(2)}, u32[]{:S(2)}) collective-permute-start(bf16[2,16,4096]{2,1,0:T(8,128)(2,1)S(1)} %normalize.1.refs_1_), channel_id=1, source_target_pairs={{0,4},{1,5},{2,6},{3,7},{4,0},{5,1},{6,2},{7,3},{8,12},{9,13},{10,... | collective-permute-start | bytes 786440 | tf_op jit(solution)/shard_map/ppermute | solution.py:291
  5.9 1.6 %collective-permute-start.1 = (bf16[2,16,4096]{2,1,0:T(8,128)(2,1)S(1)}, bf16[2,16,4096]{2,1,0:T(8,128)(2,1)S(1)}, u32[]{:S(2)}, u32[]{:S(2)}) collective-permute-start(bf16[2,16,4096]{2,1,0:T(8,128)(2,1)S(1)} %normalize.1.refs_1_), channel_id=1, source_target_pairs={{0,2},{1,3},{2,0},{3,1},{4,6},{5,7},{6,4},{7,5},{8,10},{9,11},{10,... | collective-permute-start | bytes 786440 | tf_op jit(solution)/shard_map/ppermute | solution.py:291
  7.4 1.5 %collective-permute-start.2 = (bf16[2,16,4096]{2,1,0:T(8,128)(2,1)S(1)}, bf16[2,16,4096]{2,1,0:T(8,128)(2,1)S(1)}, u32[]{:S(2)}, u32[]{:S(2)}) collective-permute-start(bf16[2,16,4096]{2,1,0:T(8,128)(2,1)S(1)} %normalize.1.refs_1_), channel_id=1, source_target_pairs={{0,8},{1,9},{2,10},{3,11},{4,12},{5,13},{6,14},{7,15},{8,0},{9,1},... | collective-permute-start | bytes 786440 | tf_op jit(solution)/shard_map/ppermute | solution.py:291
  8.9 1.5 %collective-permute-start.3 = (bf16[2,16,4096]{2,1,0:T(8,128)(2,1)S(1)}, bf16[2,16,4096]{2,1,0:T(8,128)(2,1)S(1)}, u32[]{:S(2)}, u32[]{:S(2)}) collective-permute-start(bf16[2,16,4096]{2,1,0:T(8,128)(2,1)S(1)} %normalize.1.refs_1_), channel_id=1, source_target_pairs={{0,16},{1,17},{2,18},{3,19},{4,20},{5,21},{6,22},{7,23},{8,24},{9,... | collective-permute-start | bytes 786440 | tf_op jit(solution)/shard_map/ppermute | solution.py:291
  10.5 0.5 collective-permute-start.4
  10.9 7.0 %collective-permute-done = bf16[2,16,4096]{2,1,0:T(8,128)(2,1)S(1)} collective-permute-done((bf16[2,16,4096]{2,1,0:T(8,128)(2,1)S(1)}, bf16[2,16,4096]{2,1,0:T(8,128)(2,1)S(1)}, u32[]{:S(2)}, u32[]{:S(2)}) %collective-permute-start) | collective-permute-done | bytes 262176 | tf_op jit(solution)/shard_map/ppermute | solution.py:291
  18.1 3.7 %collective-permute-done.3.refs_8_ = bf16[2,16,4096]{2,1,0:T(8,128)(2,1)S(1)} collective-permute-done((bf16[2,16,4096]{2,1,0:T(8,128)(2,1)S(1)}, bf16[2,16,4096]{2,1,0:T(8,128)(2,1)S(1)}, u32[]{:S(2)}, u32[]{:S(2)}) %collective-permute-start.3) | collective-permute-done | bytes 262176 | tf_op jit(solution)/shard_map/ppermute | solution.py:291
  21.8 0.5 collective-permute-start.9
  22.2 1.2 %collective-permute-start.5 = (bf16[2,16,4096]{2,1,0:T(8,128)(2,1)S(1)}, bf16[2,16,4096]{2,1,0:T(8,128)(2,1)S(1)}, u32[]{:S(2)}, u32[]{:S(2)}) collective-permute-start(bf16[2,16,4096]{2,1,0:T(8,128)(2,1)S(1)} %collective-permute-done.1.refs_2_), channel_id=1, source_target_pairs={{0,8},{1,9},{2,10},{3,11},{4,12},{5,13},{6,14},{7,15},{8,0},{9,1},... | collective-permute-start | bytes 786440 | tf_op jit(solution)/shard_map/ppermute | solution.py:291
  23.4 0.8 collective-permute-start.6
  24.3 0.5 collective-permute-start.7
  24.8 3.4 %collective-permute-done.9 = bf16[2,16,4096]{2,1,0:T(8,128)(2,1)S(1)} collective-permute-done((bf16[2,16,4096]{2,1,0:T(8,128)(2,1)S(1)}, bf16[2,16,4096]{2,1,0:T(8,128)(2,1)S(1)}, u32[]{:S(2)}, u32[]{:S(2)}) %collective-permute-start.9) | collective-permute-done | bytes 262176 | tf_op jit(solution)/shard_map/ppermute | solution.py:291
  28.2 0.4 collective-permute-done.5.refs_10_
  28.6 1.2 %collective-permute-done.6.refs_11_ = bf16[2,16,4096]{2,1,0:T(8,128)(2,1)S(1)} collective-permute-done((bf16[2,16,4096]{2,1,0:T(8,128)(2,1)S(1)}, bf16[2,16,4096]{2,1,0:T(8,128)(2,1)S(1)}, u32[]{:S(2)}, u32[]{:S(2)}) %collective-permute-start.6) | collective-permute-done | bytes 262176 | tf_op jit(solution)/shard_map/ppermute | solution.py:291
  29.8 1.8 %collective-permute-start.14 = (bf16[2,16,4096]{2,1,0:T(8,128)(2,1)S(1)}, bf16[2,16,4096]{2,1,0:T(8,128)(2,1)S(1)}, u32[]{:S(2)}, u32[]{:S(2)}) collective-permute-start(bf16[2,16,4096]{2,1,0:T(8,128)(2,1)S(1)} %collective-permute-done.1.refs_2_), channel_id=1, source_target_pairs={{0,24},{1,25},{2,26},{3,27},{4,28},{5,29},{6,30},{7,31},{8,16},{9,... | collective-permute-start | bytes 786440 | tf_op jit(solution)/shard_map/ppermute | solution.py:291
  31.7 0.5 collective-permute-start.11
  32.2 1.2 %collective-permute-start.12 = (bf16[2,32,4096]{2,1,0:T(8,128)(2,1)S(1)}, bf16[2,32,4096]{2,1,0:T(8,128)(2,1)S(1)}, u32[]{:S(2)}, u32[]{:S(2)}) collective-permute-start(bf16[2,32,4096]{2,1,0:T(8,128)(2,1)S(1)} %pad_maximum_fusion.refs_3_), channel_id=1, source_target_pairs={{0,16},{1,17},{2,18},{3,19},{4,20},{5,21},{6,22},{7,23},{8,24},{9,... | collective-permute-start | bytes 1572872 | tf_op jit(solution)/shard_map/ppermute | solution.py:291
  33.4 1.7 %collective-permute-start.13 = (bf16[2,32,4096]{2,1,0:T(8,128)(2,1)S(1)}, bf16[2,32,4096]{2,1,0:T(8,128)(2,1)S(1)}, u32[]{:S(2)}, u32[]{:S(2)}) collective-permute-start(bf16[2,32,4096]{2,1,0:T(8,128)(2,1)S(1)} %pad_maximum_fusion.refs_3_), channel_id=1, source_target_pairs={{0,24},{1,25},{2,26},{3,27},{4,28},{5,29},{6,30},{7,31},{8,16},{9,... | collective-permute-start | bytes 1572872 | tf_op jit(solution)/shard_map/ppermute | solution.py:291
  35.2 23.8 %own_rows.1 = (bf16[128,1792]{1,0:T(8,128)(2,1)S(1)}, bf16[128,1792]{1,0:T(8,128)(2,1)S(1)}, bf16[128,1792]{1,0:T(8,128)(2,1)S(1)}, bf16[2,128,1024]{2,1,0:T(8,1...) custom-call(s32[1]{0:T(128)} %bitcast.refs_0_, ...), custom_call_target="tpu_custom_call" | custom-call | flops 11274289152 | bytes 44040192 | tf_op jit(solution)/shard_map/own_rows/pallas_call | solution.py:137
  59.0 3.0 %collective-permute-done.13.refs_3_ = bf16[2,32,4096]{2,1,0:T(8,128)(2,1)S(1)} collective-permute-done((bf16[2,32,4096]{2,1,0:T(8,128)(2,1)S(1)}, bf16[2,32,4096]{2,1,0:T(8,128)(2,1)S(1)}, u32[]{:S(2)}, u32[]{:S(2)}) %collective-permute-start.13) | collective-permute-done | bytes 524320 | tf_op jit(solution)/shard_map/ppermute | solution.py:291
  62.1 0.6 collective-permute-start.19
  62.8 0.4 collective-permute-start.21
  63.3 1.3 %collective-permute-done.15 = bf16[2,64,4096]{2,1,0:T(8,128)(2,1)S(1)} collective-permute-done((bf16[2,64,4096]{2,1,0:T(8,128)(2,1)S(1)}, bf16[2,64,4096]{2,1,0:T(8,128)(2,1)S(1)}, u32[]{:S(2)}, u32[]{:S(2)}) %collective-permute-start.15) | collective-permute-done | bytes 1048608 | tf_op jit(solution)/shard_map/ppermute | solution.py:291
  64.8 0.2 add_convert_fusion
  65.1 2.2 %collective-permute-done.22.refs_9_ = bf16[2,16,4096]{2,1,0:T(8,128)(2,1)S(1)} collective-permute-done((bf16[2,16,4096]{2,1,0:T(8,128)(2,1)S(1)}, bf16[2,16,4096]{2,1,0:T(8,128)(2,1)S(1)}, u32[]{:S(2)}, u32[]{:S(2)}) %collective-permute-start.22) | collective-permute-done | bytes 262176 | tf_op jit(solution)/shard_map/ppermute | solution.py:291
  67.3 1.6 %collective-permute-start.16 = (bf16[2,16,4096]{2,1,0:T(8,128)(2,1)S(1)}, bf16[2,16,4096]{2,1,0:T(8,128)(2,1)S(1)}, u32[]{:S(2)}, u32[]{:S(2)}) collective-permute-start(bf16[2,16,4096]{2,1,0:T(8,128)(2,1)S(1)} %get-tuple-element.73), channel_id=1, source_target_pairs={{0,2},{1,3},{2,0},{3,1},{4,6},{5,7},{6,4},{7,5},{8,10},{9,11},{10,... | collective-permute-start | bytes 786440 | tf_op jit(solution)/shard_map/ppermute | solution.py:291
  68.8 0.4 collective-permute-start.17
  69.2 2.5 %collective-permute-start.18 = (bf16[2,16,4096]{2,1,0:T(8,128)(2,1)S(1)}, bf16[2,16,4096]{2,1,0:T(8,128)(2,1)S(1)}, u32[]{:S(2)}, u32[]{:S(2)}) collective-permute-start(bf16[2,16,4096]{2,1,0:T(8,128)(2,1)S(1)} %get-tuple-element.71), channel_id=1, source_target_pairs={{0,6},{1,7},{2,4},{3,5},{4,2},{5,3},{6,0},{7,1},{8,14},{9,15},{10,... | collective-permute-start | bytes 786440 | tf_op jit(solution)/shard_map/ppermute | solution.py:291
  71.7 31.5 %all_rows.1 = (bf16[1024,1792]{1,0:T(8,128)(2,1)}, bf16[1024,1792]{1,0:T(8,128)(2,1)}, bf16[1792,1024]{1,0:T(8,128)(2,1)}) custom-call(s32[1]{0:T(128)} %bitcast.refs_0_, bf16[2,32,4096]{2,1,0:T(8,128)(2,1)S(1)} %collective-permute-done.11.refs_1_, bf16[2,32,4096]{2,1,0:T(8,128)(2,1)S(1)} %collective-permute-done.12.refs_2_, ...), custom_call_target="tpu_custom_call" | custom-call | flops 22548578304 | bytes 55050240 | tf_op jit(solution)/shard_map/all_rows/pallas_call | solution.py:245
  103.3 0.2 fusion.2
  103.6 0.8 fusion.6
  (34 shorter events, 0.9 us)
Async XLA Ops:
  1.8 16.1 %collective-permute-start = (bf16[2,16,4096]{2,1,0:T(8,128)(2,1)S(1)}, bf16[2,16,4096]{2,1,0:T(8,128)(2,1)S(1)}, u32[]{:S(2)}, u32[]{:S(2)}) collective-permute-start(bf16[2,16,4096]{2,1,0:T(8,128)(2,1)S(1)} %normalize.1.refs_1_), channel_id=1, source_target_pairs={{0,4},{1,5},{2,6},{3,7},{4,0},{5,1},{6,2},{7,3},{8,12},{9,13},{10,... | collective-permute-start | bytes 786440 | tf_op jit(solution)/shard_map/ppermute | solution.py:291
  5.9 12.2 %collective-permute-start.1 = (bf16[2,16,4096]{2,1,0:T(8,128)(2,1)S(1)}, bf16[2,16,4096]{2,1,0:T(8,128)(2,1)S(1)}, u32[]{:S(2)}, u32[]{:S(2)}) collective-permute-start(bf16[2,16,4096]{2,1,0:T(8,128)(2,1)S(1)} %normalize.1.refs_1_), channel_id=1, source_target_pairs={{0,2},{1,3},{2,0},{3,1},{4,6},{5,7},{6,4},{7,5},{8,10},{9,11},{10,... | collective-permute-start | bytes 786440 | tf_op jit(solution)/shard_map/ppermute | solution.py:291
  7.4 10.6 %collective-permute-start.2 = (bf16[2,16,4096]{2,1,0:T(8,128)(2,1)S(1)}, bf16[2,16,4096]{2,1,0:T(8,128)(2,1)S(1)}, u32[]{:S(2)}, u32[]{:S(2)}) collective-permute-start(bf16[2,16,4096]{2,1,0:T(8,128)(2,1)S(1)} %normalize.1.refs_1_), channel_id=1, source_target_pairs={{0,8},{1,9},{2,10},{3,11},{4,12},{5,13},{6,14},{7,15},{8,0},{9,1},... | collective-permute-start | bytes 786440 | tf_op jit(solution)/shard_map/ppermute | solution.py:291
  8.9 12.8 %collective-permute-start.3 = (bf16[2,16,4096]{2,1,0:T(8,128)(2,1)S(1)}, bf16[2,16,4096]{2,1,0:T(8,128)(2,1)S(1)}, u32[]{:S(2)}, u32[]{:S(2)}) collective-permute-start(bf16[2,16,4096]{2,1,0:T(8,128)(2,1)S(1)} %normalize.1.refs_1_), channel_id=1, source_target_pairs={{0,16},{1,17},{2,18},{3,19},{4,20},{5,21},{6,22},{7,23},{8,24},{9,... | collective-permute-start | bytes 786440 | tf_op jit(solution)/shard_map/ppermute | solution.py:291
  10.5 11.3 %collective-permute-start.4 = (bf16[2,16,4096]{2,1,0:T(8,128)(2,1)S(1)}, bf16[2,16,4096]{2,1,0:T(8,128)(2,1)S(1)}, u32[]{:S(2)}, u32[]{:S(2)}) collective-permute-start(bf16[2,16,4096]{2,1,0:T(8,128)(2,1)S(1)} %normalize.1.refs_1_), channel_id=1, source_target_pairs={{0,24},{1,25},{2,26},{3,27},{4,28},{5,29},{6,30},{7,31},{8,16},{9,... | collective-permute-start | bytes 786440 | tf_op jit(solution)/shard_map/ppermute | solution.py:291
  21.8 6.4 %collective-permute-start.9 = (bf16[2,16,4096]{2,1,0:T(8,128)(2,1)S(1)}, bf16[2,16,4096]{2,1,0:T(8,128)(2,1)S(1)}, u32[]{:S(2)}, u32[]{:S(2)}) collective-permute-start(bf16[2,16,4096]{2,1,0:T(8,128)(2,1)S(1)} %collective-permute-done), channel_id=1, source_target_pairs={{0,2},{1,3},{2,0},{3,1},{4,6},{5,7},{6,4},{7,5},{8,10},{9,11},{10,... | collective-permute-start | bytes 786440 | tf_op jit(solution)/shard_map/ppermute | solution.py:291
  22.2 6.4 %collective-permute-start.5 = (bf16[2,16,4096]{2,1,0:T(8,128)(2,1)S(1)}, bf16[2,16,4096]{2,1,0:T(8,128)(2,1)S(1)}, u32[]{:S(2)}, u32[]{:S(2)}) collective-permute-start(bf16[2,16,4096]{2,1,0:T(8,128)(2,1)S(1)} %collective-permute-done.1.refs_2_), channel_id=1, source_target_pairs={{0,8},{1,9},{2,10},{3,11},{4,12},{5,13},{6,14},{7,15},{8,0},{9,1},... | collective-permute-start | bytes 786440 | tf_op jit(solution)/shard_map/ppermute | solution.py:291
  23.4 6.4 %collective-permute-start.6 = (bf16[2,16,4096]{2,1,0:T(8,128)(2,1)S(1)}, bf16[2,16,4096]{2,1,0:T(8,128)(2,1)S(1)}, u32[]{:S(2)}, u32[]{:S(2)}) collective-permute-start(bf16[2,16,4096]{2,1,0:T(8,128)(2,1)S(1)} %collective-permute-done.1.refs_2_), channel_id=1, source_target_pairs={{0,16},{1,17},{2,18},{3,19},{4,20},{5,21},{6,22},{7,23},{8,24},{9,... | collective-permute-start | bytes 786440 | tf_op jit(solution)/shard_map/ppermute | solution.py:291
  24.3 5.6 %collective-permute-start.8 = (bf16[2,16,4096]{2,1,0:T(8,128)(2,1)S(1)}, bf16[2,16,4096]{2,1,0:T(8,128)(2,1)S(1)}, u32[]{:S(2)}, u32[]{:S(2)}) collective-permute-start(bf16[2,16,4096]{2,1,0:T(8,128)(2,1)S(1)} %collective-permute-done.1.refs_2_), channel_id=1, source_target_pairs={{0,1},{1,0},{2,3},{3,2},{4,5},{5,4},{6,7},{7,6},{8,9},{9,8},{10,11... | collective-permute-start | bytes 786440 | tf_op jit(solution)/shard_map/ppermute | solution.py:291
  24.3 5.5 %collective-permute-start.7 = (bf16[2,16,4096]{2,1,0:T(8,128)(2,1)S(1)}, bf16[2,16,4096]{2,1,0:T(8,128)(2,1)S(1)}, u32[]{:S(2)}, u32[]{:S(2)}) collective-permute-start(bf16[2,16,4096]{2,1,0:T(8,128)(2,1)S(1)} %normalize.1.refs_1_), channel_id=1, source_target_pairs={{0,1},{1,0},{2,3},{3,2},{4,5},{5,4},{6,7},{7,6},{8,9},{9,8},{10,11... | collective-permute-start | bytes 786440 | tf_op jit(solution)/shard_map/ppermute | solution.py:291
  29.8 5.3 %collective-permute-start.10 = (bf16[2,32,4096]{2,1,0:T(8,128)(2,1)S(1)}, bf16[2,32,4096]{2,1,0:T(8,128)(2,1)S(1)}, u32[]{:S(2)}, u32[]{:S(2)}) collective-permute-start(bf16[2,32,4096]{2,1,0:T(8,128)(2,1)S(1)} %pad_maximum_fusion.refs_3_), channel_id=1, source_target_pairs={{0,1},{1,0},{2,3},{3,2},{4,5},{5,4},{6,7},{7,6},{8,9},{9,8},{10,11... | collective-permute-start | bytes 1572872 | tf_op jit(solution)/shard_map/ppermute | solution.py:291
  29.8 29.1 %collective-permute-start.14 = (bf16[2,16,4096]{2,1,0:T(8,128)(2,1)S(1)}, bf16[2,16,4096]{2,1,0:T(8,128)(2,1)S(1)}, u32[]{:S(2)}, u32[]{:S(2)}) collective-permute-start(bf16[2,16,4096]{2,1,0:T(8,128)(2,1)S(1)} %collective-permute-done.1.refs_2_), channel_id=1, source_target_pairs={{0,24},{1,25},{2,26},{3,27},{4,28},{5,29},{6,30},{7,31},{8,16},{9,... | collective-permute-start | bytes 786440 | tf_op jit(solution)/shard_map/ppermute | solution.py:291
  31.7 27.3 %collective-permute-start.11 = (bf16[2,32,4096]{2,1,0:T(8,128)(2,1)S(1)}, bf16[2,32,4096]{2,1,0:T(8,128)(2,1)S(1)}, u32[]{:S(2)}, u32[]{:S(2)}) collective-permute-start(bf16[2,32,4096]{2,1,0:T(8,128)(2,1)S(1)} %pad_maximum_fusion.refs_3_), channel_id=1, source_target_pairs={{0,8},{1,9},{2,10},{3,11},{4,12},{5,13},{6,14},{7,15},{8,0},{9,1},... | collective-permute-start | bytes 1572872 | tf_op jit(solution)/shard_map/ppermute | solution.py:291
  32.2 26.8 %collective-permute-start.12 = (bf16[2,32,4096]{2,1,0:T(8,128)(2,1)S(1)}, bf16[2,32,4096]{2,1,0:T(8,128)(2,1)S(1)}, u32[]{:S(2)}, u32[]{:S(2)}) collective-permute-start(bf16[2,32,4096]{2,1,0:T(8,128)(2,1)S(1)} %pad_maximum_fusion.refs_3_), channel_id=1, source_target_pairs={{0,16},{1,17},{2,18},{3,19},{4,20},{5,21},{6,22},{7,23},{8,24},{9,... | collective-permute-start | bytes 1572872 | tf_op jit(solution)/shard_map/ppermute | solution.py:291
  33.4 28.6 %collective-permute-start.13 = (bf16[2,32,4096]{2,1,0:T(8,128)(2,1)S(1)}, bf16[2,32,4096]{2,1,0:T(8,128)(2,1)S(1)}, u32[]{:S(2)}, u32[]{:S(2)}) collective-permute-start(bf16[2,32,4096]{2,1,0:T(8,128)(2,1)S(1)} %pad_maximum_fusion.refs_3_), channel_id=1, source_target_pairs={{0,24},{1,25},{2,26},{3,27},{4,28},{5,29},{6,30},{7,31},{8,16},{9,... | collective-permute-start | bytes 1572872 | tf_op jit(solution)/shard_map/ppermute | solution.py:291
  35.1 26.8 %copy-start = (bf16[16,4096]{1,0:T(8,128)(2,1)S(1)}, bf16[16,4096]{1,0:T(8,128)(2,1)}, u32[]{:S(2)}) copy-start(bf16[16,4096]{1,0:T(8,128)(2,1)} %tokens.1) | copy-start | bytes 393220
  62.0 2.7 %collective-permute-start.15 = (bf16[2,64,4096]{2,1,0:T(8,128)(2,1)S(1)}, bf16[2,64,4096]{2,1,0:T(8,128)(2,1)S(1)}, u32[]{:S(2)}, u32[]{:S(2)}) collective-permute-start(bf16[2,64,4096]{2,1,0:T(8,128)(2,1)S(1)} %get-tuple-element.52), channel_id=1, source_target_pairs={{0,1},{1,0},{2,3},{3,2},{4,5},{5,4},{6,7},{7,6},{8,9},{9,8},{10,11... | collective-permute-start | bytes 3145736 | tf_op jit(solution)/shard_map/ppermute | solution.py:291
  62.1 6.7 %collective-permute-start.19 = (bf16[2,32,4096]{2,1,0:T(8,128)(2,1)S(1)}, bf16[2,32,4096]{2,1,0:T(8,128)(2,1)S(1)}, u32[]{:S(2)}, u32[]{:S(2)}) collective-permute-start(bf16[2,32,4096]{2,1,0:T(8,128)(2,1)S(1)} %collective-permute-done.11.refs_1_), channel_id=1, source_target_pairs={{0,1},{1,0},{2,3},{3,2},{4,5},{5,4},{6,7},{7,6},{8,9},{9,8},{10,11... | collective-permute-start | bytes 1572872 | tf_op jit(solution)/shard_map/ppermute | solution.py:291
  62.7 6.5 %collective-permute-start.20 = (bf16[2,32,4096]{2,1,0:T(8,128)(2,1)S(1)}, bf16[2,32,4096]{2,1,0:T(8,128)(2,1)S(1)}, u32[]{:S(2)}, u32[]{:S(2)}) collective-permute-start(bf16[2,32,4096]{2,1,0:T(8,128)(2,1)S(1)} %collective-permute-done.12.refs_2_), channel_id=1, source_target_pairs={{0,1},{1,0},{2,3},{3,2},{4,5},{5,4},{6,7},{7,6},{8,9},{9,8},{10,11... | collective-permute-start | bytes 1572872 | tf_op jit(solution)/shard_map/ppermute | solution.py:291
  62.8 8.9 %collective-permute-start.21 = (bf16[2,32,4096]{2,1,0:T(8,128)(2,1)S(1)}, bf16[2,32,4096]{2,1,0:T(8,128)(2,1)S(1)}, u32[]{:S(2)}, u32[]{:S(2)}) collective-permute-start(bf16[2,32,4096]{2,1,0:T(8,128)(2,1)S(1)} %collective-permute-done.13.refs_3_), channel_id=1, source_target_pairs={{0,1},{1,0},{2,3},{3,2},{4,5},{5,4},{6,7},{7,6},{8,9},{9,8},{10,11... | collective-permute-start | bytes 1572872 | tf_op jit(solution)/shard_map/ppermute | solution.py:291
  63.2 4.0 %collective-permute-start.22 = (bf16[2,16,4096]{2,1,0:T(8,128)(2,1)S(1)}, bf16[2,16,4096]{2,1,0:T(8,128)(2,1)S(1)}, u32[]{:S(2)}, u32[]{:S(2)}) collective-permute-start(bf16[2,16,4096]{2,1,0:T(8,128)(2,1)S(1)} %collective-permute-done.14.refs_4_), channel_id=1, source_target_pairs={{0,1},{1,0},{2,3},{3,2},{4,5},{5,4},{6,7},{7,6},{8,9},{9,8},{10,11... | collective-permute-start | bytes 786440 | tf_op jit(solution)/shard_map/ppermute | solution.py:291
  64.6 7.0 %collective-permute-start.23 = (bf16[2,80,4096]{2,1,0:T(8,128)(2,1)S(1)}, bf16[2,80,4096]{2,1,0:T(8,128)(2,1)S(1)}, u32[]{:S(2)}, u32[]{:S(2)}) collective-permute-start(bf16[2,80,4096]{2,1,0:T(8,128)(2,1)S(1)} %get-tuple-element.57.refs_5_), channel_id=1, source_target_pairs={{0,1},{1,0},{2,3},{3,2},{4,5},{5,4},{6,7},{7,6},{8,9},{9,8},{10,11... | collective-permute-start | bytes 3932168 | tf_op jit(solution)/shard_map/ppermute | solution.py:291
  67.3 35.9 %collective-permute-start.16 = (bf16[2,16,4096]{2,1,0:T(8,128)(2,1)S(1)}, bf16[2,16,4096]{2,1,0:T(8,128)(2,1)S(1)}, u32[]{:S(2)}, u32[]{:S(2)}) collective-permute-start(bf16[2,16,4096]{2,1,0:T(8,128)(2,1)S(1)} %get-tuple-element.73), channel_id=1, source_target_pairs={{0,2},{1,3},{2,0},{3,1},{4,6},{5,7},{6,4},{7,5},{8,10},{9,11},{10,... | collective-permute-start | bytes 786440 | tf_op jit(solution)/shard_map/ppermute | solution.py:291
  68.8 34.3 %collective-permute-start.17 = (bf16[2,16,4096]{2,1,0:T(8,128)(2,1)S(1)}, bf16[2,16,4096]{2,1,0:T(8,128)(2,1)S(1)}, u32[]{:S(2)}, u32[]{:S(2)}) collective-permute-start(bf16[2,16,4096]{2,1,0:T(8,128)(2,1)S(1)} %get-tuple-element.72), channel_id=1, source_target_pairs={{0,4},{1,5},{2,6},{3,7},{4,0},{5,1},{6,2},{7,3},{8,12},{9,13},{10,... | collective-permute-start | bytes 786440 | tf_op jit(solution)/shard_map/ppermute | solution.py:291
  69.2 34.0 %collective-permute-start.18 = (bf16[2,16,4096]{2,1,0:T(8,128)(2,1)S(1)}, bf16[2,16,4096]{2,1,0:T(8,128)(2,1)S(1)}, u32[]{:S(2)}, u32[]{:S(2)}) collective-permute-start(bf16[2,16,4096]{2,1,0:T(8,128)(2,1)S(1)} %get-tuple-element.71), channel_id=1, source_target_pairs={{0,6},{1,7},{2,4},{3,5},{4,2},{5,3},{6,0},{7,1},{8,14},{9,15},{10,... | collective-permute-start | bytes 786440 | tf_op jit(solution)/shard_map/ppermute | solution.py:291
  71.7 31.7 %copy-start.2 = (f32[4096]{0:T(1024)S(1)}, f32[4096]{0:T(1024)}, u32[]{:S(2)}) copy-start(f32[4096]{0:T(1024)} %param.7) | copy-start | bytes 49156
  71.7 31.9 %copy-start.1 = (bf16[16,4096]{1,0:T(8,128)(2,1)S(1)}, bf16[16,4096]{1,0:T(8,128)(2,1)}, u32[]{:S(2)}) copy-start(bf16[16,4096]{1,0:T(8,128)(2,1)} %cotangent.1) | copy-start | bytes 393220

commit v16 on v15

--- a/solution.py
+++ b/solution.py
@@ -304,18 +304,20 @@
     unit2, unit1, across, again0 = lax.optimization_barrier((unit2, unit1, across, unit0))
     unit3 = swap(unit2, 0, 2)
     across1 = [swap(unit1, 1, 0), swap(unit1, 2, 0)]
-    far_units = far([again0, unit1])
+    far_units, far_across = far([again0, unit1]), far(across)
     last = jnp.concatenate([unit2, unit3], axis=1)
-    across1, far_units, last = lax.optimization_barrier((across1, far_units, last))
+    last, across1, far_units, far_across = lax.optimization_barrier(
+        (last, across1, far_units, far_across)
+    )
+    more = across + far_across + across1 + far(across1)
     own = [unit0, unit1, last] + far_units + [swap(last, 0, 1)]
     rest = [swap(last, b, 0) for b in range(1, n_dp)] + [swap(unit1, 3, 0)]
     *units, own_columns, kept, sent, packed = own_rows(
-        replica, n_dp, own, across + across1, gate_weight, up_weight, down_weight
+        replica, n_dp, own, more, gate_weight, up_weight, down_weight
     )
     kept, sent, rest = lax.optimization_barrier((kept, sent, rest))
     pair = (kept.astype(jnp.float32) + swap(sent, 0, 1).astype(jnp.float32)).astype(jnp.bfloat16)
-    rest += [packed]
-    rest += far(rest)
+    rest += far(rest) + [packed]
     parts = [swap(pair[:, k * rows : (k + 1) * rows], 0, 2 * k) for k in range(1, n_tp // 2)]
     weight_gradients = all_rows(
         replica, rest, units, own_columns, gate_weight, up_weight, down_weight

time: 105 us -> 108 us (1.029)
  local copies, waits for them, and re-layouts: 0.07 us -> 5.02 us
  waiting for transfers between devices: 22.4 us -> 17.9 us
  starting transfers between devices: 23.2 us -> 25.2 us
  Pallas kernels: 56.4 us -> 57.5 us
    unnamed x6 -> x18, local copies, waits for them, and re-layouts: 0.01 us -> 4.97 us
    ppermute x24 -> x28, waiting for transfers between devices: 22.4 us -> 17.9 us  [swap(): return lax.ppermute(array, ('dp', 'tp'), pairs)]
    ppermute x24 -> x28, starting transfers between devices: 23.2 us -> 25.2 us  [swap(): return lax.ppermute(array, ('dp', 'tp'), pairs)]
    pallas_call x1, Pallas kernels: 23.8 us -> 24.9 us  [own_rows(): pl.pallas_call(functools.partial(own_kernel, len(pieces), len(more)), in_...]
  transfers between devices with their start and end apart: 24 -> 28, of which waited for: 9 -> 8; matrix products, arithmetic and copies ran while one was open for 0% -> 0% of each run, Pallas kernels for 53% -> 52%
where the time goes in v16:
time: 108 us
  Pallas kernels  57.5 us (53%)
  starting transfers between devices  25.2 us (23%)
  waiting for transfers between devices  17.9 us (17%)
  local copies, waits for them, and re-layouts  5.02 us (5%)
  other arithmetic  1.59 us (1%)
    pallas_call x1, Pallas kernels, all_rows(): pl.pallas_call(functools.partial(all_kernel, len(pieces)), in_specs=[pl.B...  31.5 us
    ppermute x28, starting transfers between devices, swap(): return lax.ppermute(array, ('dp', 'tp'), pairs)  25.2 us
    pallas_call x1, Pallas kernels, own_rows(): pl.pallas_call(functools.partial(own_kernel, len(pieces), len(more)), in_...  24.9 us
    ppermute x28, waiting for transfers between devices, swap(): return lax.ppermute(array, ('dp', 'tp'), pairs)  17.9 us
    unnamed x18, local copies, waits for them, and re-layouts  4.97 us
  transfers between devices with their start and end apart: 28, of which 8 were waited for; matrix products, arithmetic and copies ran while one was open for 0% of the time, Pallas kernels for 52%

profile of v16, /device:TPU:0, one launch (start us, length us, event | category | flops | bytes accessed | tf_op | source)
XLA Modules:
  0.0 108.1 jit_solution(10804620225890275715)
XLA Ops:
  0.6 1.1 %normalize.1.refs_1_ = bf16[2,16,4096]{2,1,0:T(8,128)(2,1)S(1)} custom-call(bf16[16,4096]{1,0:T(8,128)(2,1)} %tokens.1, f32[1,4096]{1,0:T(1,128)} %bitcast.14, bf16[16,4096]{1,0:T(8,128)(2,1)} %cotangent.1), custom_call_target="tpu_custom_call" | custom-call | tf_op jit(solution)/shard_map/normalize/pallas_call | solution.py:78
  1.8 4.1 %collective-permute-start = (bf16[2,16,4096]{2,1,0:T(8,128)(2,1)S(1)}, bf16[2,16,4096]{2,1,0:T(8,128)(2,1)S(1)}, u32[]{:S(2)}, u32[]{:S(2)}) collective-permute-start(bf16[2,16,4096]{2,1,0:T(8,128)(2,1)S(1)} %normalize.1.refs_1_), channel_id=1, source_target_pairs={{0,4},{1,5},{2,6},{3,7},{4,0},{5,1},{6,2},{7,3},{8,12},{9,13},{10,... | collective-permute-start | bytes 786440 | tf_op jit(solution)/shard_map/ppermute | solution.py:291
  5.9 1.6 %collective-permute-start.1 = (bf16[2,16,4096]{2,1,0:T(8,128)(2,1)S(1)}, bf16[2,16,4096]{2,1,0:T(8,128)(2,1)S(1)}, u32[]{:S(2)}, u32[]{:S(2)}) collective-permute-start(bf16[2,16,4096]{2,1,0:T(8,128)(2,1)S(1)} %normalize.1.refs_1_), channel_id=1, source_target_pairs={{0,2},{1,3},{2,0},{3,1},{4,6},{5,7},{6,4},{7,5},{8,10},{9,11},{10,... | collective-permute-start | bytes 786440 | tf_op jit(solution)/shard_map/ppermute | solution.py:291
  7.4 1.5 %collective-permute-start.2 = (bf16[2,16,4096]{2,1,0:T(8,128)(2,1)S(1)}, bf16[2,16,4096]{2,1,0:T(8,128)(2,1)S(1)}, u32[]{:S(2)}, u32[]{:S(2)}) collective-permute-start(bf16[2,16,4096]{2,1,0:T(8,128)(2,1)S(1)} %normalize.1.refs_1_), channel_id=1, source_target_pairs={{0,8},{1,9},{2,10},{3,11},{4,12},{5,13},{6,14},{7,15},{8,0},{9,1},... | collective-permute-start | bytes 786440 | tf_op jit(solution)/shard_map/ppermute | solution.py:291
  8.9 1.5 %collective-permute-start.3 = (bf16[2,16,4096]{2,1,0:T(8,128)(2,1)S(1)}, bf16[2,16,4096]{2,1,0:T(8,128)(2,1)S(1)}, u32[]{:S(2)}, u32[]{:S(2)}) collective-permute-start(bf16[2,16,4096]{2,1,0:T(8,128)(2,1)S(1)} %normalize.1.refs_1_), channel_id=1, source_target_pairs={{0,16},{1,17},{2,18},{3,19},{4,20},{5,21},{6,22},{7,23},{8,24},{9,... | collective-permute-start | bytes 786440 | tf_op jit(solution)/shard_map/ppermute | solution.py:291
  10.5 0.5 collective-permute-start.4
  10.9 7.0 %collective-permute-done = bf16[2,16,4096]{2,1,0:T(8,128)(2,1)S(1)} collective-permute-done((bf16[2,16,4096]{2,1,0:T(8,128)(2,1)S(1)}, bf16[2,16,4096]{2,1,0:T(8,128)(2,1)S(1)}, u32[]{:S(2)}, u32[]{:S(2)}) %collective-permute-start) | collective-permute-done | bytes 262176 | tf_op jit(solution)/shard_map/ppermute | solution.py:291
  18.1 3.7 %collective-permute-done.3.refs_8_ = bf16[2,16,4096]{2,1,0:T(8,128)(2,1)S(1)} collective-permute-done((bf16[2,16,4096]{2,1,0:T(8,128)(2,1)S(1)}, bf16[2,16,4096]{2,1,0:T(8,128)(2,1)S(1)}, u32[]{:S(2)}, u32[]{:S(2)}) %collective-permute-start.3) | collective-permute-done | bytes 262176 | tf_op jit(solution)/shard_map/ppermute | solution.py:291
  22.2 1.2 %collective-permute-start.6 = (bf16[2,16,4096]{2,1,0:T(8,128)(2,1)S(1)}, bf16[2,16,4096]{2,1,0:T(8,128)(2,1)S(1)}, u32[]{:S(2)}, u32[]{:S(2)}) collective-permute-start(bf16[2,16,4096]{2,1,0:T(8,128)(2,1)S(1)} %collective-permute-done.1.refs_2_), channel_id=1, source_target_pairs={{0,8},{1,9},{2,10},{3,11},{4,12},{5,13},{6,14},{7,15},{8,0},{9,1},... | collective-permute-start | bytes 786440 | tf_op jit(solution)/shard_map/ppermute | solution.py:291
  23.4 0.8 collective-permute-start.7
  24.3 0.5 collective-permute-start.8
  24.8 3.4 %collective-permute-done.5 = bf16[2,16,4096]{2,1,0:T(8,128)(2,1)S(1)} collective-permute-done((bf16[2,16,4096]{2,1,0:T(8,128)(2,1)S(1)}, bf16[2,16,4096]{2,1,0:T(8,128)(2,1)S(1)}, u32[]{:S(2)}, u32[]{:S(2)}) %collective-permute-start.5) | collective-permute-done | bytes 262176 | tf_op jit(solution)/shard_map/ppermute | solution.py:291
  28.7 1.2 %collective-permute-done.7.refs_14_ = bf16[2,16,4096]{2,1,0:T(8,128)(2,1)S(1)} collective-permute-done((bf16[2,16,4096]{2,1,0:T(8,128)(2,1)S(1)}, bf16[2,16,4096]{2,1,0:T(8,128)(2,1)S(1)}, u32[]{:S(2)}, u32[]{:S(2)}) %collective-permute-start.7) | collective-permute-done | bytes 262176 | tf_op jit(solution)/shard_map/ppermute | solution.py:291
  29.9 0.7 copy-done
  30.6 0.7 copy-done.2
  31.4 0.7 copy-done.4
  33.0 1.8 %collective-permute-start.19 = (bf16[2,16,4096]{2,1,0:T(8,128)(2,1)S(1)}, bf16[2,16,4096]{2,1,0:T(8,128)(2,1)S(1)}, u32[]{:S(2)}, u32[]{:S(2)}) collective-permute-start(bf16[2,16,4096]{2,1,0:T(8,128)(2,1)S(1)} %collective-permute-done.1.refs_2_), channel_id=1, source_target_pairs={{0,24},{1,25},{2,26},{3,27},{4,28},{5,29},{6,30},{7,31},{8,16},{9,... | collective-permute-start | bytes 786440 | tf_op jit(solution)/shard_map/ppermute | solution.py:291
  34.8 0.7 collective-permute-start.16
  35.4 1.1 %collective-permute-start.17 = (bf16[2,32,4096]{2,1,0:T(8,128)(2,1)S(1)}, bf16[2,32,4096]{2,1,0:T(8,128)(2,1)S(1)}, u32[]{:S(2)}, u32[]{:S(2)}) collective-permute-start(bf16[2,32,4096]{2,1,0:T(8,128)(2,1)S(1)} %pad_maximum_fusion.refs_3_), channel_id=1, source_target_pairs={{0,16},{1,17},{2,18},{3,19},{4,20},{5,21},{6,22},{7,23},{8,24},{9,... | collective-permute-start | bytes 1572872 | tf_op jit(solution)/shard_map/ppermute | solution.py:291
  36.5 1.8 %collective-permute-start.18 = (bf16[2,32,4096]{2,1,0:T(8,128)(2,1)S(1)}, bf16[2,32,4096]{2,1,0:T(8,128)(2,1)S(1)}, u32[]{:S(2)}, u32[]{:S(2)}) collective-permute-start(bf16[2,32,4096]{2,1,0:T(8,128)(2,1)S(1)} %pad_maximum_fusion.refs_3_), channel_id=1, source_target_pairs={{0,24},{1,25},{2,26},{3,27},{4,28},{5,29},{6,30},{7,31},{8,16},{9,... | collective-permute-start | bytes 1572872 | tf_op jit(solution)/shard_map/ppermute | solution.py:291
  38.3 0.9 copy-done.1
  39.2 0.9 copy-done.3
  40.2 0.9 copy-done.5
  41.1 24.9 %own_rows.1 = (bf16[128,1792]{1,0:T(8,128)(2,1)S(1)}, bf16[128,1792]{1,0:T(8,128)(2,1)S(1)}, bf16[128,1792]{1,0:T(8,128)(2,1)S(1)}, bf16[2,128,1024]{2,1,0:T(8,1...) custom-call(s32[1]{0:T(128)} %bitcast.refs_0_, ...), custom_call_target="tpu_custom_call" | custom-call | flops 11274289152 | bytes 44040192 | tf_op jit(solution)/shard_map/own_rows/pallas_call | solution.py:137
  66.3 0.6 collective-permute-start.24
  67.5 1.3 %collective-permute-done.20 = bf16[2,64,4096]{2,1,0:T(8,128)(2,1)S(1)} collective-permute-done((bf16[2,64,4096]{2,1,0:T(8,128)(2,1)S(1)}, bf16[2,64,4096]{2,1,0:T(8,128)(2,1)S(1)}, u32[]{:S(2)}, u32[]{:S(2)}) %collective-permute-start.20) | collective-permute-done | bytes 1048608 | tf_op jit(solution)/shard_map/ppermute | solution.py:291
  69.1 1.6 %collective-permute-start.21 = (bf16[2,16,4096]{2,1,0:T(8,128)(2,1)S(1)}, bf16[2,16,4096]{2,1,0:T(8,128)(2,1)S(1)}, u32[]{:S(2)}, u32[]{:S(2)}) collective-permute-start(bf16[2,16,4096]{2,1,0:T(8,128)(2,1)S(1)} %get-tuple-element.79), channel_id=1, source_target_pairs={{0,2},{1,3},{2,0},{3,1},{4,6},{5,7},{6,4},{7,5},{8,10},{9,11},{10,... | collective-permute-start | bytes 786440 | tf_op jit(solution)/shard_map/ppermute | solution.py:291
  70.8 0.7 collective-permute-done.27.refs_8_
  71.4 1.2 %collective-permute-start.22 = (bf16[2,16,4096]{2,1,0:T(8,128)(2,1)S(1)}, bf16[2,16,4096]{2,1,0:T(8,128)(2,1)S(1)}, u32[]{:S(2)}, u32[]{:S(2)}) collective-permute-start(bf16[2,16,4096]{2,1,0:T(8,128)(2,1)S(1)} %get-tuple-element.78), channel_id=1, source_target_pairs={{0,4},{1,5},{2,6},{3,7},{4,0},{5,1},{6,2},{7,3},{8,12},{9,13},{10,... | collective-permute-start | bytes 786440 | tf_op jit(solution)/shard_map/ppermute | solution.py:291
  72.6 2.7 %collective-permute-start.23 = (bf16[2,16,4096]{2,1,0:T(8,128)(2,1)S(1)}, bf16[2,16,4096]{2,1,0:T(8,128)(2,1)S(1)}, u32[]{:S(2)}, u32[]{:S(2)}) collective-permute-start(bf16[2,16,4096]{2,1,0:T(8,128)(2,1)S(1)} %get-tuple-element.77), channel_id=1, source_target_pairs={{0,6},{1,7},{2,4},{3,5},{4,2},{5,3},{6,0},{7,1},{8,14},{9,15},{10,... | collective-permute-start | bytes 786440 | tf_op jit(solution)/shard_map/ppermute | solution.py:291
  75.4 31.5 %all_rows.1 = (bf16[1024,1792]{1,0:T(8,128)(2,1)}, bf16[1024,1792]{1,0:T(8,128)(2,1)}, bf16[1792,1024]{1,0:T(8,128)(2,1)}) custom-call(s32[1]{0:T(128)} %bitcast.refs_0_, bf16[2,32,4096]{2,1,0:T(8,128)(2,1)S(1)} %collective-permute-done.16.refs_1_, bf16[2,32,4096]{2,1,0:T(8,128)(2,1)S(1)} %collective-permute-done.17.refs_2_, ...), custom_call_target="tpu_custom_call" | custom-call | flops 22548578304 | bytes 55050240 | tf_op jit(solution)/shard_map/all_rows/pallas_call | solution.py:245
  107.3 0.8 fusion.6
  (54 shorter events, 3.8 us)
Async XLA Ops:
  1.8 16.1 %collective-permute-start = (bf16[2,16,4096]{2,1,0:T(8,128)(2,1)S(1)}, bf16[2,16,4096]{2,1,0:T(8,128)(2,1)S(1)}, u32[]{:S(2)}, u32[]{:S(2)}) collective-permute-start(bf16[2,16,4096]{2,1,0:T(8,128)(2,1)S(1)} %normalize.1.refs_1_), channel_id=1, source_target_pairs={{0,4},{1,5},{2,6},{3,7},{4,0},{5,1},{6,2},{7,3},{8,12},{9,13},{10,... | collective-permute-start | bytes 786440 | tf_op jit(solution)/shard_map/ppermute | solution.py:291
  5.9 12.2 %collective-permute-start.1 = (bf16[2,16,4096]{2,1,0:T(8,128)(2,1)S(1)}, bf16[2,16,4096]{2,1,0:T(8,128)(2,1)S(1)}, u32[]{:S(2)}, u32[]{:S(2)}) collective-permute-start(bf16[2,16,4096]{2,1,0:T(8,128)(2,1)S(1)} %normalize.1.refs_1_), channel_id=1, source_target_pairs={{0,2},{1,3},{2,0},{3,1},{4,6},{5,7},{6,4},{7,5},{8,10},{9,11},{10,... | collective-permute-start | bytes 786440 | tf_op jit(solution)/shard_map/ppermute | solution.py:291
  7.4 10.6 %collective-permute-start.2 = (bf16[2,16,4096]{2,1,0:T(8,128)(2,1)S(1)}, bf16[2,16,4096]{2,1,0:T(8,128)(2,1)S(1)}, u32[]{:S(2)}, u32[]{:S(2)}) collective-permute-start(bf16[2,16,4096]{2,1,0:T(8,128)(2,1)S(1)} %normalize.1.refs_1_), channel_id=1, source_target_pairs={{0,8},{1,9},{2,10},{3,11},{4,12},{5,13},{6,14},{7,15},{8,0},{9,1},... | collective-permute-start | bytes 786440 | tf_op jit(solution)/shard_map/ppermute | solution.py:291
  8.9 12.8 %collective-permute-start.3 = (bf16[2,16,4096]{2,1,0:T(8,128)(2,1)S(1)}, bf16[2,16,4096]{2,1,0:T(8,128)(2,1)S(1)}, u32[]{:S(2)}, u32[]{:S(2)}) collective-permute-start(bf16[2,16,4096]{2,1,0:T(8,128)(2,1)S(1)} %normalize.1.refs_1_), channel_id=1, source_target_pairs={{0,16},{1,17},{2,18},{3,19},{4,20},{5,21},{6,22},{7,23},{8,24},{9,... | collective-permute-start | bytes 786440 | tf_op jit(solution)/shard_map/ppermute | solution.py:291
  10.5 11.3 %collective-permute-start.4 = (bf16[2,16,4096]{2,1,0:T(8,128)(2,1)S(1)}, bf16[2,16,4096]{2,1,0:T(8,128)(2,1)S(1)}, u32[]{:S(2)}, u32[]{:S(2)}) collective-permute-start(bf16[2,16,4096]{2,1,0:T(8,128)(2,1)S(1)} %normalize.1.refs_1_), channel_id=1, source_target_pairs={{0,24},{1,25},{2,26},{3,27},{4,28},{5,29},{6,30},{7,31},{8,16},{9,... | collective-permute-start | bytes 786440 | tf_op jit(solution)/shard_map/ppermute | solution.py:291
  21.8 6.4 %collective-permute-start.5 = (bf16[2,16,4096]{2,1,0:T(8,128)(2,1)S(1)}, bf16[2,16,4096]{2,1,0:T(8,128)(2,1)S(1)}, u32[]{:S(2)}, u32[]{:S(2)}) collective-permute-start(bf16[2,16,4096]{2,1,0:T(8,128)(2,1)S(1)} %collective-permute-done), channel_id=1, source_target_pairs={{0,2},{1,3},{2,0},{3,1},{4,6},{5,7},{6,4},{7,5},{8,10},{9,11},{10,... | collective-permute-start | bytes 786440 | tf_op jit(solution)/shard_map/ppermute | solution.py:291
  22.2 6.4 %collective-permute-start.6 = (bf16[2,16,4096]{2,1,0:T(8,128)(2,1)S(1)}, bf16[2,16,4096]{2,1,0:T(8,128)(2,1)S(1)}, u32[]{:S(2)}, u32[]{:S(2)}) collective-permute-start(bf16[2,16,4096]{2,1,0:T(8,128)(2,1)S(1)} %collective-permute-done.1.refs_2_), channel_id=1, source_target_pairs={{0,8},{1,9},{2,10},{3,11},{4,12},{5,13},{6,14},{7,15},{8,0},{9,1},... | collective-permute-start | bytes 786440 | tf_op jit(solution)/shard_map/ppermute | solution.py:291
  23.4 6.4 %collective-permute-start.7 = (bf16[2,16,4096]{2,1,0:T(8,128)(2,1)S(1)}, bf16[2,16,4096]{2,1,0:T(8,128)(2,1)S(1)}, u32[]{:S(2)}, u32[]{:S(2)}) collective-permute-start(bf16[2,16,4096]{2,1,0:T(8,128)(2,1)S(1)} %collective-permute-done.1.refs_2_), channel_id=1, source_target_pairs={{0,16},{1,17},{2,18},{3,19},{4,20},{5,21},{6,22},{7,23},{8,24},{9,... | collective-permute-start | bytes 786440 | tf_op jit(solution)/shard_map/ppermute | solution.py:291
  24.3 5.6 %collective-permute-start.9 = (bf16[2,16,4096]{2,1,0:T(8,128)(2,1)S(1)}, bf16[2,16,4096]{2,1,0:T(8,128)(2,1)S(1)}, u32[]{:S(2)}, u32[]{:S(2)}) collective-permute-start(bf16[2,16,4096]{2,1,0:T(8,128)(2,1)S(1)} %collective-permute-done.1.refs_2_), channel_id=1, source_target_pairs={{0,1},{1,0},{2,3},{3,2},{4,5},{5,4},{6,7},{7,6},{8,9},{9,8},{10,11... | collective-permute-start | bytes 786440 | tf_op jit(solution)/shard_map/ppermute | solution.py:291
  24.3 5.6 %collective-permute-start.8 = (bf16[2,16,4096]{2,1,0:T(8,128)(2,1)S(1)}, bf16[2,16,4096]{2,1,0:T(8,128)(2,1)S(1)}, u32[]{:S(2)}, u32[]{:S(2)}) collective-permute-start(bf16[2,16,4096]{2,1,0:T(8,128)(2,1)S(1)} %normalize.1.refs_1_), channel_id=1, source_target_pairs={{0,1},{1,0},{2,3},{3,2},{4,5},{5,4},{6,7},{7,6},{8,9},{9,8},{10,11... | collective-permute-start | bytes 786440 | tf_op jit(solution)/shard_map/ppermute | solution.py:291
  28.1 1.7 %collective-permute-start.10 = (bf16[2,16,4096]{2,1,0:T(8,128)(2,1)S(1)}, bf16[2,16,4096]{2,1,0:T(8,128)(2,1)S(1)}, u32[]{:S(2)}, u32[]{:S(2)}) collective-permute-start(bf16[2,16,4096]{2,1,0:T(8,128)(2,1)S(1)} %collective-permute-done.2.refs_7_), channel_id=1, source_target_pairs={{0,1},{1,0},{2,3},{3,2},{4,5},{5,4},{6,7},{7,6},{8,9},{9,8},{10,11... | collective-permute-start | bytes 786440 | tf_op jit(solution)/shard_map/ppermute | solution.py:291
  28.6 2.0 %collective-permute-start.11 = (bf16[2,16,4096]{2,1,0:T(8,128)(2,1)S(1)}, bf16[2,16,4096]{2,1,0:T(8,128)(2,1)S(1)}, u32[]{:S(2)}, u32[]{:S(2)}) collective-permute-start(bf16[2,16,4096]{2,1,0:T(8,128)(2,1)S(1)} %collective-permute-done.3.refs_8_), channel_id=1, source_target_pairs={{0,1},{1,0},{2,3},{3,2},{4,5},{5,4},{6,7},{7,6},{8,9},{9,8},{10,11... | collective-permute-start | bytes 786440 | tf_op jit(solution)/shard_map/ppermute | solution.py:291
  29.8 1.5 %collective-permute-start.12 = (bf16[2,16,4096]{2,1,0:T(8,128)(2,1)S(1)}, bf16[2,16,4096]{2,1,0:T(8,128)(2,1)S(1)}, u32[]{:S(2)}, u32[]{:S(2)}) collective-permute-start(bf16[2,16,4096]{2,1,0:T(8,128)(2,1)S(1)} %collective-permute-done.4.refs_9_), channel_id=1, source_target_pairs={{0,1},{1,0},{2,3},{3,2},{4,5},{5,4},{6,7},{7,6},{8,9},{9,8},{10,11... | collective-permute-start | bytes 786440 | tf_op jit(solution)/shard_map/ppermute | solution.py:291
  32.1 6.2 %collective-permute-start.13 = (bf16[2,32,4096]{2,1,0:T(8,128)(2,1)S(1)}, bf16[2,32,4096]{2,1,0:T(8,128)(2,1)S(1)}, u32[]{:S(2)}, u32[]{:S(2)}) collective-permute-start(bf16[2,32,4096]{2,1,0:T(8,128)(2,1)S(1)} %pad_maximum_fusion.refs_3_), channel_id=1, source_target_pairs={{0,1},{1,0},{2,3},{3,2},{4,5},{5,4},{6,7},{7,6},{8,9},{9,8},{10,11... | collective-permute-start | bytes 1572872 | tf_op jit(solution)/shard_map/ppermute | solution.py:291
  32.5 2.9 %collective-permute-start.14 = (bf16[2,16,4096]{2,1,0:T(8,128)(2,1)S(1)}, bf16[2,16,4096]{2,1,0:T(8,128)(2,1)}, u32[]{:S(2)}, u32[]{:S(2)}) collective-permute-start(bf16[2,16,4096]{2,1,0:T(8,128)(2,1)S(1)} %collective-permute-done.6.refs_13_), channel_id=1, source_target_pairs={{0,1},{1,0},{2,3},{3,2},{4,5},{5,4},{6,7},{7,6},{8,9},{9,8},{10,11... | collective-permute-start | bytes 786440 | tf_op jit(solution)/shard_map/ppermute | solution.py:291
  32.6 4.0 %collective-permute-start.15 = (bf16[2,16,4096]{2,1,0:T(8,128)(2,1)S(1)}, bf16[2,16,4096]{2,1,0:T(8,128)(2,1)}, u32[]{:S(2)}, u32[]{:S(2)}) collective-permute-start(bf16[2,16,4096]{2,1,0:T(8,128)(2,1)S(1)} %collective-permute-done.7.refs_14_), channel_id=1, source_target_pairs={{0,1},{1,0},{2,3},{3,2},{4,5},{5,4},{6,7},{7,6},{8,9},{9,8},{10,11... | collective-permute-start | bytes 786440 | tf_op jit(solution)/shard_map/ppermute | solution.py:291
  33.0 33.0 %collective-permute-start.19 = (bf16[2,16,4096]{2,1,0:T(8,128)(2,1)S(1)}, bf16[2,16,4096]{2,1,0:T(8,128)(2,1)S(1)}, u32[]{:S(2)}, u32[]{:S(2)}) collective-permute-start(bf16[2,16,4096]{2,1,0:T(8,128)(2,1)S(1)} %collective-permute-done.1.refs_2_), channel_id=1, source_target_pairs={{0,24},{1,25},{2,26},{3,27},{4,28},{5,29},{6,30},{7,31},{8,16},{9,... | collective-permute-start | bytes 786440 | tf_op jit(solution)/shard_map/ppermute | solution.py:291
  34.8 31.3 %collective-permute-start.16 = (bf16[2,32,4096]{2,1,0:T(8,128)(2,1)S(1)}, bf16[2,32,4096]{2,1,0:T(8,128)(2,1)S(1)}, u32[]{:S(2)}, u32[]{:S(2)}) collective-permute-start(bf16[2,32,4096]{2,1,0:T(8,128)(2,1)S(1)} %pad_maximum_fusion.refs_3_), channel_id=1, source_target_pairs={{0,8},{1,9},{2,10},{3,11},{4,12},{5,13},{6,14},{7,15},{8,0},{9,1},... | collective-permute-start | bytes 1572872 | tf_op jit(solution)/shard_map/ppermute | solution.py:291
  35.4 30.6 %collective-permute-start.17 = (bf16[2,32,4096]{2,1,0:T(8,128)(2,1)S(1)}, bf16[2,32,4096]{2,1,0:T(8,128)(2,1)S(1)}, u32[]{:S(2)}, u32[]{:S(2)}) collective-permute-start(bf16[2,32,4096]{2,1,0:T(8,128)(2,1)S(1)} %pad_maximum_fusion.refs_3_), channel_id=1, source_target_pairs={{0,16},{1,17},{2,18},{3,19},{4,20},{5,21},{6,22},{7,23},{8,24},{9,... | collective-permute-start | bytes 1572872 | tf_op jit(solution)/shard_map/ppermute | solution.py:291
  36.5 29.5 %collective-permute-start.18 = (bf16[2,32,4096]{2,1,0:T(8,128)(2,1)S(1)}, bf16[2,32,4096]{2,1,0:T(8,128)(2,1)S(1)}, u32[]{:S(2)}, u32[]{:S(2)}) collective-permute-start(bf16[2,32,4096]{2,1,0:T(8,128)(2,1)S(1)} %pad_maximum_fusion.refs_3_), channel_id=1, source_target_pairs={{0,24},{1,25},{2,26},{3,27},{4,28},{5,29},{6,30},{7,31},{8,16},{9,... | collective-permute-start | bytes 1572872 | tf_op jit(solution)/shard_map/ppermute | solution.py:291
  38.3 1.0 copy-start.1
  41.1 25.0 %copy-start.6 = (bf16[16,4096]{1,0:T(8,128)(2,1)S(1)}, bf16[16,4096]{1,0:T(8,128)(2,1)}, u32[]{:S(2)}) copy-start(bf16[16,4096]{1,0:T(8,128)(2,1)} %tokens.1) | copy-start | bytes 393220
  66.1 2.7 %collective-permute-start.20 = (bf16[2,64,4096]{2,1,0:T(8,128)(2,1)S(1)}, bf16[2,64,4096]{2,1,0:T(8,128)(2,1)S(1)}, u32[]{:S(2)}, u32[]{:S(2)}) collective-permute-start(bf16[2,64,4096]{2,1,0:T(8,128)(2,1)S(1)} %get-tuple-element.58), channel_id=1, source_target_pairs={{0,1},{1,0},{2,3},{3,2},{4,5},{5,4},{6,7},{7,6},{8,9},{9,8},{10,11... | collective-permute-start | bytes 3145736 | tf_op jit(solution)/shard_map/ppermute | solution.py:291
  66.3 6.3 %collective-permute-start.24 = (bf16[2,32,4096]{2,1,0:T(8,128)(2,1)S(1)}, bf16[2,32,4096]{2,1,0:T(8,128)(2,1)S(1)}, u32[]{:S(2)}, u32[]{:S(2)}) collective-permute-start(bf16[2,32,4096]{2,1,0:T(8,128)(2,1)S(1)} %collective-permute-done.16.refs_1_), channel_id=1, source_target_pairs={{0,1},{1,0},{2,3},{3,2},{4,5},{5,4},{6,7},{7,6},{8,9},{9,8},{10,11... | collective-permute-start | bytes 1572872 | tf_op jit(solution)/shard_map/ppermute | solution.py:291
  66.9 8.5 %collective-permute-start.25 = (bf16[2,32,4096]{2,1,0:T(8,128)(2,1)S(1)}, bf16[2,32,4096]{2,1,0:T(8,128)(2,1)S(1)}, u32[]{:S(2)}, u32[]{:S(2)}) collective-permute-start(bf16[2,32,4096]{2,1,0:T(8,128)(2,1)S(1)} %collective-permute-done.17.refs_2_), channel_id=1, source_target_pairs={{0,1},{1,0},{2,3},{3,2},{4,5},{5,4},{6,7},{7,6},{8,9},{9,8},{10,11... | collective-permute-start | bytes 1572872 | tf_op jit(solution)/shard_map/ppermute | solution.py:291
  66.9 8.4 %collective-permute-start.26 = (bf16[2,32,4096]{2,1,0:T(8,128)(2,1)S(1)}, bf16[2,32,4096]{2,1,0:T(8,128)(2,1)S(1)}, u32[]{:S(2)}, u32[]{:S(2)}) collective-permute-start(bf16[2,32,4096]{2,1,0:T(8,128)(2,1)S(1)} %collective-permute-done.18.refs_3_), channel_id=1, source_target_pairs={{0,1},{1,0},{2,3},{3,2},{4,5},{5,4},{6,7},{7,6},{8,9},{9,8},{10,11... | collective-permute-start | bytes 1572872 | tf_op jit(solution)/shard_map/ppermute | solution.py:291
  67.4 4.0 %collective-permute-start.27 = (bf16[2,16,4096]{2,1,0:T(8,128)(2,1)S(1)}, bf16[2,16,4096]{2,1,0:T(8,128)(2,1)S(1)}, u32[]{:S(2)}, u32[]{:S(2)}) collective-permute-start(bf16[2,16,4096]{2,1,0:T(8,128)(2,1)S(1)} %collective-permute-done.19.refs_4_), channel_id=1, source_target_pairs={{0,1},{1,0},{2,3},{3,2},{4,5},{5,4},{6,7},{7,6},{8,9},{9,8},{10,11... | collective-permute-start | bytes 786440 | tf_op jit(solution)/shard_map/ppermute | solution.py:291
  69.1 37.8 %collective-permute-start.21 = (bf16[2,16,4096]{2,1,0:T(8,128)(2,1)S(1)}, bf16[2,16,4096]{2,1,0:T(8,128)(2,1)S(1)}, u32[]{:S(2)}, u32[]{:S(2)}) collective-permute-start(bf16[2,16,4096]{2,1,0:T(8,128)(2,1)S(1)} %get-tuple-element.79), channel_id=1, source_target_pairs={{0,2},{1,3},{2,0},{3,1},{4,6},{5,7},{6,4},{7,5},{8,10},{9,11},{10,... | collective-permute-start | bytes 786440 | tf_op jit(solution)/shard_map/ppermute | solution.py:291
  71.4 35.5 %collective-permute-start.22 = (bf16[2,16,4096]{2,1,0:T(8,128)(2,1)S(1)}, bf16[2,16,4096]{2,1,0:T(8,128)(2,1)S(1)}, u32[]{:S(2)}, u32[]{:S(2)}) collective-permute-start(bf16[2,16,4096]{2,1,0:T(8,128)(2,1)S(1)} %get-tuple-element.78), channel_id=1, source_target_pairs={{0,4},{1,5},{2,6},{3,7},{4,0},{5,1},{6,2},{7,3},{8,12},{9,13},{10,... | collective-permute-start | bytes 786440 | tf_op jit(solution)/shard_map/ppermute | solution.py:291
  72.6 34.3 %collective-permute-start.23 = (bf16[2,16,4096]{2,1,0:T(8,128)(2,1)S(1)}, bf16[2,16,4096]{2,1,0:T(8,128)(2,1)S(1)}, u32[]{:S(2)}, u32[]{:S(2)}) collective-permute-start(bf16[2,16,4096]{2,1,0:T(8,128)(2,1)S(1)} %get-tuple-element.77), channel_id=1, source_target_pairs={{0,6},{1,7},{2,4},{3,5},{4,2},{5,3},{6,0},{7,1},{8,14},{9,15},{10,... | collective-permute-start | bytes 786440 | tf_op jit(solution)/shard_map/ppermute | solution.py:291
  75.4 31.7 %copy-start.8 = (f32[4096]{0:T(1024)S(1)}, f32[4096]{0:T(1024)}, u32[]{:S(2)}) copy-start(f32[4096]{0:T(1024)} %param.7) | copy-start | bytes 49156
  75.4 31.9 %copy-start.7 = (bf16[16,4096]{1,0:T(8,128)(2,1)S(1)}, bf16[16,4096]{1,0:T(8,128)(2,1)}, u32[]{:S(2)}) copy-start(bf16[16,4096]{1,0:T(8,128)(2,1)} %cotangent.1) | copy-start | bytes 393220
  (5 other events, 4.0 us)

commit v17 on v15

--- a/solution.py
+++ b/solution.py
@@ -313,9 +313,10 @@
         replica, n_dp, own, across + across1, gate_weight, up_weight, down_weight
     )
     kept, sent, rest = lax.optimization_barrier((kept, sent, rest))
-    pair = (kept.astype(jnp.float32) + swap(sent, 0, 1).astype(jnp.float32)).astype(jnp.bfloat16)
-    rest += [packed]
-    rest += far(rest)
+    came, far_packed = far([sent, packed])
+    pair = (kept.astype(jnp.float32) + came.astype(jnp.float32)).astype(jnp.bfloat16)
+    pair, far_packed = lax.optimization_barrier((pair, far_packed))
+    rest += far(rest) + [packed, far_packed]
     parts = [swap(pair[:, k * rows : (k + 1) * rows], 0, 2 * k) for k in range(1, n_tp // 2)]
     weight_gradients = all_rows(
         replica, rest, units, own_columns, gate_weight, up_weight, down_weight

time: 105 us -> 106 us (level)
  starting transfers between devices: 23.2 us -> 24.4 us
    ppermute x24, starting transfers between devices: 23.2 us -> 24.4 us  [swap(): return lax.ppermute(array, ('dp', 'tp'), pairs)]
  transfers between devices with their start and end apart: 24 -> 24, of which waited for: 9 -> 10; matrix products, arithmetic and copies ran while one was open for 0% -> 0% of each run, Pallas kernels for 53% -> 52%
where the time goes in v17:
time: 106 us
  Pallas kernels  56.4 us (53%)
  starting transfers between devices  24.4 us (23%)
  waiting for transfers between devices  22.6 us (21%)
  other arithmetic  1.59 us (2%)
    pallas_call x1, Pallas kernels, all_rows(): pl.pallas_call(functools.partial(all_kernel, len(pieces)), in_specs=[pl.B...  31.5 us
    ppermute x24, starting transfers between devices, swap(): return lax.ppermute(array, ('dp', 'tp'), pairs)  24.4 us
    pallas_call x1, Pallas kernels, own_rows(): pl.pallas_call(functools.partial(own_kernel, len(pieces), len(more)), in_...  23.8 us
    ppermute x24, waiting for transfers between devices, swap(): return lax.ppermute(array, ('dp', 'tp'), pairs)  22.6 us
  transfers between devices with their start and end apart: 24, of which 10 were waited for; matrix products, arithmetic and copies ran while one was open for 0% of the time, Pallas kernels for 52%

profile of v17, /device:TPU:0, one launch (start us, length us, event | category | flops | bytes accessed | tf_op | source)
XLA Modules:
  0.0 105.8 jit_solution(5123834770305398575)
XLA Ops:
  0.6 1.1 %normalize.1.refs_1_ = bf16[2,16,4096]{2,1,0:T(8,128)(2,1)S(1)} custom-call(bf16[16,4096]{1,0:T(8,128)(2,1)} %tokens.1, f32[1,4096]{1,0:T(1,128)} %bitcast.14, bf16[16,4096]{1,0:T(8,128)(2,1)} %cotangent.1), custom_call_target="tpu_custom_call" | custom-call | tf_op jit(solution)/shard_map/normalize/pallas_call | solution.py:78
  1.8 4.1 %collective-permute-start = (bf16[2,16,4096]{2,1,0:T(8,128)(2,1)S(1)}, bf16[2,16,4096]{2,1,0:T(8,128)(2,1)S(1)}, u32[]{:S(2)}, u32[]{:S(2)}) collective-permute-start(bf16[2,16,4096]{2,1,0:T(8,128)(2,1)S(1)} %normalize.1.refs_1_), channel_id=1, source_target_pairs={{0,4},{1,5},{2,6},{3,7},{4,0},{5,1},{6,2},{7,3},{8,12},{9,13},{10,... | collective-permute-start | bytes 786440 | tf_op jit(solution)/shard_map/ppermute | solution.py:291
  5.9 1.6 %collective-permute-start.1 = (bf16[2,16,4096]{2,1,0:T(8,128)(2,1)S(1)}, bf16[2,16,4096]{2,1,0:T(8,128)(2,1)S(1)}, u32[]{:S(2)}, u32[]{:S(2)}) collective-permute-start(bf16[2,16,4096]{2,1,0:T(8,128)(2,1)S(1)} %normalize.1.refs_1_), channel_id=1, source_target_pairs={{0,2},{1,3},{2,0},{3,1},{4,6},{5,7},{6,4},{7,5},{8,10},{9,11},{10,... | collective-permute-start | bytes 786440 | tf_op jit(solution)/shard_map/ppermute | solution.py:291
  7.4 1.5 %collective-permute-start.2 = (bf16[2,16,4096]{2,1,0:T(8,128)(2,1)S(1)}, bf16[2,16,4096]{2,1,0:T(8,128)(2,1)S(1)}, u32[]{:S(2)}, u32[]{:S(2)}) collective-permute-start(bf16[2,16,4096]{2,1,0:T(8,128)(2,1)S(1)} %normalize.1.refs_1_), channel_id=1, source_target_pairs={{0,8},{1,9},{2,10},{3,11},{4,12},{5,13},{6,14},{7,15},{8,0},{9,1},... | collective-permute-start | bytes 786440 | tf_op jit(solution)/shard_map/ppermute | solution.py:291
  8.9 1.5 %collective-permute-start.3 = (bf16[2,16,4096]{2,1,0:T(8,128)(2,1)S(1)}, bf16[2,16,4096]{2,1,0:T(8,128)(2,1)S(1)}, u32[]{:S(2)}, u32[]{:S(2)}) collective-permute-start(bf16[2,16,4096]{2,1,0:T(8,128)(2,1)S(1)} %normalize.1.refs_1_), channel_id=1, source_target_pairs={{0,16},{1,17},{2,18},{3,19},{4,20},{5,21},{6,22},{7,23},{8,24},{9,... | collective-permute-start | bytes 786440 | tf_op jit(solution)/shard_map/ppermute | solution.py:291
  10.5 0.5 collective-permute-start.4
  10.9 7.0 %collective-permute-done = bf16[2,16,4096]{2,1,0:T(8,128)(2,1)S(1)} collective-permute-done((bf16[2,16,4096]{2,1,0:T(8,128)(2,1)S(1)}, bf16[2,16,4096]{2,1,0:T(8,128)(2,1)S(1)}, u32[]{:S(2)}, u32[]{:S(2)}) %collective-permute-start) | collective-permute-done | bytes 262176 | tf_op jit(solution)/shard_map/ppermute | solution.py:291
  18.1 3.7 %collective-permute-done.3.refs_8_ = bf16[2,16,4096]{2,1,0:T(8,128)(2,1)S(1)} collective-permute-done((bf16[2,16,4096]{2,1,0:T(8,128)(2,1)S(1)}, bf16[2,16,4096]{2,1,0:T(8,128)(2,1)S(1)}, u32[]{:S(2)}, u32[]{:S(2)}) %collective-permute-start.3) | collective-permute-done | bytes 262176 | tf_op jit(solution)/shard_map/ppermute | solution.py:291
  21.8 0.5 collective-permute-start.9
  22.2 1.2 %collective-permute-start.5 = (bf16[2,16,4096]{2,1,0:T(8,128)(2,1)S(1)}, bf16[2,16,4096]{2,1,0:T(8,128)(2,1)S(1)}, u32[]{:S(2)}, u32[]{:S(2)}) collective-permute-start(bf16[2,16,4096]{2,1,0:T(8,128)(2,1)S(1)} %collective-permute-done.1.refs_2_), channel_id=1, source_target_pairs={{0,8},{1,9},{2,10},{3,11},{4,12},{5,13},{6,14},{7,15},{8,0},{9,1},... | collective-permute-start | bytes 786440 | tf_op jit(solution)/shard_map/ppermute | solution.py:291
  23.4 0.8 collective-permute-start.6
  24.3 0.5 collective-permute-start.7
  24.8 3.4 %collective-permute-done.9 = bf16[2,16,4096]{2,1,0:T(8,128)(2,1)S(1)} collective-permute-done((bf16[2,16,4096]{2,1,0:T(8,128)(2,1)S(1)}, bf16[2,16,4096]{2,1,0:T(8,128)(2,1)S(1)}, u32[]{:S(2)}, u32[]{:S(2)}) %collective-permute-start.9) | collective-permute-done | bytes 262176 | tf_op jit(solution)/shard_map/ppermute | solution.py:291
  28.2 0.4 collective-permute-done.5.refs_10_
  28.6 1.2 %collective-permute-done.6.refs_11_ = bf16[2,16,4096]{2,1,0:T(8,128)(2,1)S(1)} collective-permute-done((bf16[2,16,4096]{2,1,0:T(8,128)(2,1)S(1)}, bf16[2,16,4096]{2,1,0:T(8,128)(2,1)S(1)}, u32[]{:S(2)}, u32[]{:S(2)}) %collective-permute-start.6) | collective-permute-done | bytes 262176 | tf_op jit(solution)/shard_map/ppermute | solution.py:291
  29.8 1.8 %collective-permute-start.14 = (bf16[2,16,4096]{2,1,0:T(8,128)(2,1)S(1)}, bf16[2,16,4096]{2,1,0:T(8,128)(2,1)S(1)}, u32[]{:S(2)}, u32[]{:S(2)}) collective-permute-start(bf16[2,16,4096]{2,1,0:T(8,128)(2,1)S(1)} %collective-permute-done.1.refs_2_), channel_id=1, source_target_pairs={{0,24},{1,25},{2,26},{3,27},{4,28},{5,29},{6,30},{7,31},{8,16},{9,... | collective-permute-start | bytes 786440 | tf_op jit(solution)/shard_map/ppermute | solution.py:291
  31.7 0.5 collective-permute-start.11
  32.2 1.2 %collective-permute-start.12 = (bf16[2,32,4096]{2,1,0:T(8,128)(2,1)S(1)}, bf16[2,32,4096]{2,1,0:T(8,128)(2,1)S(1)}, u32[]{:S(2)}, u32[]{:S(2)}) collective-permute-start(bf16[2,32,4096]{2,1,0:T(8,128)(2,1)S(1)} %pad_maximum_fusion.refs_3_), channel_id=1, source_target_pairs={{0,16},{1,17},{2,18},{3,19},{4,20},{5,21},{6,22},{7,23},{8,24},{9,... | collective-permute-start | bytes 1572872 | tf_op jit(solution)/shard_map/ppermute | solution.py:291
  33.4 1.7 %collective-permute-start.13 = (bf16[2,32,4096]{2,1,0:T(8,128)(2,1)S(1)}, bf16[2,32,4096]{2,1,0:T(8,128)(2,1)S(1)}, u32[]{:S(2)}, u32[]{:S(2)}) collective-permute-start(bf16[2,32,4096]{2,1,0:T(8,128)(2,1)S(1)} %pad_maximum_fusion.refs_3_), channel_id=1, source_target_pairs={{0,24},{1,25},{2,26},{3,27},{4,28},{5,29},{6,30},{7,31},{8,16},{9,... | collective-permute-start | bytes 1572872 | tf_op jit(solution)/shard_map/ppermute | solution.py:291
  35.2 23.8 %own_rows.1 = (bf16[128,1792]{1,0:T(8,128)(2,1)S(1)}, bf16[128,1792]{1,0:T(8,128)(2,1)S(1)}, bf16[128,1792]{1,0:T(8,128)(2,1)S(1)}, bf16[2,128,1024]{2,1,0:T(8,1...) custom-call(s32[1]{0:T(128)} %bitcast.refs_0_, ...), custom_call_target="tpu_custom_call" | custom-call | flops 11274289152 | bytes 44040192 | tf_op jit(solution)/shard_map/own_rows/pallas_call | solution.py:137
  59.0 3.0 %collective-permute-done.13.refs_3_ = bf16[2,32,4096]{2,1,0:T(8,128)(2,1)S(1)} collective-permute-done((bf16[2,32,4096]{2,1,0:T(8,128)(2,1)S(1)}, bf16[2,32,4096]{2,1,0:T(8,128)(2,1)S(1)}, u32[]{:S(2)}, u32[]{:S(2)}) %collective-permute-start.13) | collective-permute-done | bytes 524320 | tf_op jit(solution)/shard_map/ppermute | solution.py:291
  62.0 0.5 collective-permute-start.16
  62.7 0.5 collective-permute-start.21
  63.3 1.3 %collective-permute-done.15 = bf16[2,64,4096]{2,1,0:T(8,128)(2,1)S(1)} collective-permute-done((bf16[2,64,4096]{2,1,0:T(8,128)(2,1)S(1)}, bf16[2,64,4096]{2,1,0:T(8,128)(2,1)S(1)}, u32[]{:S(2)}, u32[]{:S(2)}) %collective-permute-start.15) | collective-permute-done | bytes 1048608 | tf_op jit(solution)/shard_map/ppermute | solution.py:291
  64.8 0.2 add_convert_fusion
  65.0 1.5 %collective-permute-done.16.refs_10_ = bf16[2,80,4096]{2,1,0:T(8,128)(2,1)S(1)} collective-permute-done((bf16[2,80,4096]{2,1,0:T(8,128)(2,1)S(1)}, bf16[2,80,4096]{2,1,0:T(8,128)(2,1)S(1)}, u32[]{:S(2)}, u32[]{:S(2)}) %collective-permute-start.16) | collective-permute-done | bytes 1310752 | tf_op jit(solution)/shard_map/ppermute | solution.py:291
  66.6 1.6 %collective-permute-start.17 = (bf16[2,16,4096]{2,1,0:T(8,128)(2,1)S(1)}, bf16[2,16,4096]{2,1,0:T(8,128)(2,1)S(1)}, u32[]{:S(2)}, u32[]{:S(2)}) collective-permute-start(bf16[2,16,4096]{2,1,0:T(8,128)(2,1)S(1)} %get-tuple-element.77), channel_id=1, source_target_pairs={{0,2},{1,3},{2,0},{3,1},{4,6},{5,7},{6,4},{7,5},{8,10},{9,11},{10,... | collective-permute-start | bytes 786440 | tf_op jit(solution)/shard_map/ppermute | solution.py:291
  68.2 0.9 collective-permute-done.23.refs_8_
  69.1 1.3 %collective-permute-start.18 = (bf16[2,16,4096]{2,1,0:T(8,128)(2,1)S(1)}, bf16[2,16,4096]{2,1,0:T(8,128)(2,1)S(1)}, u32[]{:S(2)}, u32[]{:S(2)}) collective-permute-start(bf16[2,16,4096]{2,1,0:T(8,128)(2,1)S(1)} %get-tuple-element.76), channel_id=1, source_target_pairs={{0,4},{1,5},{2,6},{3,7},{4,0},{5,1},{6,2},{7,3},{8,12},{9,13},{10,... | collective-permute-start | bytes 786440 | tf_op jit(solution)/shard_map/ppermute | solution.py:291
  70.5 2.6 %collective-permute-start.19 = (bf16[2,16,4096]{2,1,0:T(8,128)(2,1)S(1)}, bf16[2,16,4096]{2,1,0:T(8,128)(2,1)S(1)}, u32[]{:S(2)}, u32[]{:S(2)}) collective-permute-start(bf16[2,16,4096]{2,1,0:T(8,128)(2,1)S(1)} %get-tuple-element.75), channel_id=1, source_target_pairs={{0,6},{1,7},{2,4},{3,5},{4,2},{5,3},{6,0},{7,1},{8,14},{9,15},{10,... | collective-permute-start | bytes 786440 | tf_op jit(solution)/shard_map/ppermute | solution.py:291
  73.1 31.5 %all_rows.1 = (bf16[1024,1792]{1,0:T(8,128)(2,1)}, bf16[1024,1792]{1,0:T(8,128)(2,1)}, bf16[1792,1024]{1,0:T(8,128)(2,1)}) custom-call(s32[1]{0:T(128)} %bitcast.refs_0_, bf16[2,32,4096]{2,1,0:T(8,128)(2,1)S(1)} %collective-permute-done.11.refs_1_, bf16[2,32,4096]{2,1,0:T(8,128)(2,1)S(1)} %collective-permute-done.12.refs_2_, ...), custom_call_target="tpu_custom_call" | custom-call | flops 22548578304 | bytes 55050240 | tf_op jit(solution)/shard_map/all_rows/pallas_call | solution.py:245
  105.0 0.8 fusion.6
  (34 shorter events, 1.1 us)
Async XLA Ops:
  1.8 16.1 %collective-permute-start = (bf16[2,16,4096]{2,1,0:T(8,128)(2,1)S(1)}, bf16[2,16,4096]{2,1,0:T(8,128)(2,1)S(1)}, u32[]{:S(2)}, u32[]{:S(2)}) collective-permute-start(bf16[2,16,4096]{2,1,0:T(8,128)(2,1)S(1)} %normalize.1.refs_1_), channel_id=1, source_target_pairs={{0,4},{1,5},{2,6},{3,7},{4,0},{5,1},{6,2},{7,3},{8,12},{9,13},{10,... | collective-permute-start | bytes 786440 | tf_op jit(solution)/shard_map/ppermute | solution.py:291
  5.9 12.2 %collective-permute-start.1 = (bf16[2,16,4096]{2,1,0:T(8,128)(2,1)S(1)}, bf16[2,16,4096]{2,1,0:T(8,128)(2,1)S(1)}, u32[]{:S(2)}, u32[]{:S(2)}) collective-permute-start(bf16[2,16,4096]{2,1,0:T(8,128)(2,1)S(1)} %normalize.1.refs_1_), channel_id=1, source_target_pairs={{0,2},{1,3},{2,0},{3,1},{4,6},{5,7},{6,4},{7,5},{8,10},{9,11},{10,... | collective-permute-start | bytes 786440 | tf_op jit(solution)/shard_map/ppermute | solution.py:291
  7.4 10.6 %collective-permute-start.2 = (bf16[2,16,4096]{2,1,0:T(8,128)(2,1)S(1)}, bf16[2,16,4096]{2,1,0:T(8,128)(2,1)S(1)}, u32[]{:S(2)}, u32[]{:S(2)}) collective-permute-start(bf16[2,16,4096]{2,1,0:T(8,128)(2,1)S(1)} %normalize.1.refs_1_), channel_id=1, source_target_pairs={{0,8},{1,9},{2,10},{3,11},{4,12},{5,13},{6,14},{7,15},{8,0},{9,1},... | collective-permute-start | bytes 786440 | tf_op jit(solution)/shard_map/ppermute | solution.py:291
  8.9 12.8 %collective-permute-start.3 = (bf16[2,16,4096]{2,1,0:T(8,128)(2,1)S(1)}, bf16[2,16,4096]{2,1,0:T(8,128)(2,1)S(1)}, u32[]{:S(2)}, u32[]{:S(2)}) collective-permute-start(bf16[2,16,4096]{2,1,0:T(8,128)(2,1)S(1)} %normalize.1.refs_1_), channel_id=1, source_target_pairs={{0,16},{1,17},{2,18},{3,19},{4,20},{5,21},{6,22},{7,23},{8,24},{9,... | collective-permute-start | bytes 786440 | tf_op jit(solution)/shard_map/ppermute | solution.py:291
  10.5 11.3 %collective-permute-start.4 = (bf16[2,16,4096]{2,1,0:T(8,128)(2,1)S(1)}, bf16[2,16,4096]{2,1,0:T(8,128)(2,1)S(1)}, u32[]{:S(2)}, u32[]{:S(2)}) collective-permute-start(bf16[2,16,4096]{2,1,0:T(8,128)(2,1)S(1)} %normalize.1.refs_1_), channel_id=1, source_target_pairs={{0,24},{1,25},{2,26},{3,27},{4,28},{5,29},{6,30},{7,31},{8,16},{9,... | collective-permute-start | bytes 786440 | tf_op jit(solution)/shard_map/ppermute | solution.py:291
  21.8 6.4 %collective-permute-start.9 = (bf16[2,16,4096]{2,1,0:T(8,128)(2,1)S(1)}, bf16[2,16,4096]{2,1,0:T(8,128)(2,1)S(1)}, u32[]{:S(2)}, u32[]{:S(2)}) collective-permute-start(bf16[2,16,4096]{2,1,0:T(8,128)(2,1)S(1)} %collective-permute-done), channel_id=1, source_target_pairs={{0,2},{1,3},{2,0},{3,1},{4,6},{5,7},{6,4},{7,5},{8,10},{9,11},{10,... | collective-permute-start | bytes 786440 | tf_op jit(solution)/shard_map/ppermute | solution.py:291
  22.2 6.4 %collective-permute-start.5 = (bf16[2,16,4096]{2,1,0:T(8,128)(2,1)S(1)}, bf16[2,16,4096]{2,1,0:T(8,128)(2,1)S(1)}, u32[]{:S(2)}, u32[]{:S(2)}) collective-permute-start(bf16[2,16,4096]{2,1,0:T(8,128)(2,1)S(1)} %collective-permute-done.1.refs_2_), channel_id=1, source_target_pairs={{0,8},{1,9},{2,10},{3,11},{4,12},{5,13},{6,14},{7,15},{8,0},{9,1},... | collective-permute-start | bytes 786440 | tf_op jit(solution)/shard_map/ppermute | solution.py:291
  23.4 6.4 %collective-permute-start.6 = (bf16[2,16,4096]{2,1,0:T(8,128)(2,1)S(1)}, bf16[2,16,4096]{2,1,0:T(8,128)(2,1)S(1)}, u32[]{:S(2)}, u32[]{:S(2)}) collective-permute-start(bf16[2,16,4096]{2,1,0:T(8,128)(2,1)S(1)} %collective-permute-done.1.refs_2_), channel_id=1, source_target_pairs={{0,16},{1,17},{2,18},{3,19},{4,20},{5,21},{6,22},{7,23},{8,24},{9,... | collective-permute-start | bytes 786440 | tf_op jit(solution)/shard_map/ppermute | solution.py:291
  24.3 5.6 %collective-permute-start.8 = (bf16[2,16,4096]{2,1,0:T(8,128)(2,1)S(1)}, bf16[2,16,4096]{2,1,0:T(8,128)(2,1)S(1)}, u32[]{:S(2)}, u32[]{:S(2)}) collective-permute-start(bf16[2,16,4096]{2,1,0:T(8,128)(2,1)S(1)} %collective-permute-done.1.refs_2_), channel_id=1, source_target_pairs={{0,1},{1,0},{2,3},{3,2},{4,5},{5,4},{6,7},{7,6},{8,9},{9,8},{10,11... | collective-permute-start | bytes 786440 | tf_op jit(solution)/shard_map/ppermute | solution.py:291
  24.3 5.6 %collective-permute-start.7 = (bf16[2,16,4096]{2,1,0:T(8,128)(2,1)S(1)}, bf16[2,16,4096]{2,1,0:T(8,128)(2,1)S(1)}, u32[]{:S(2)}, u32[]{:S(2)}) collective-permute-start(bf16[2,16,4096]{2,1,0:T(8,128)(2,1)S(1)} %normalize.1.refs_1_), channel_id=1, source_target_pairs={{0,1},{1,0},{2,3},{3,2},{4,5},{5,4},{6,7},{7,6},{8,9},{9,8},{10,11... | collective-permute-start | bytes 786440 | tf_op jit(solution)/shard_map/ppermute | solution.py:291
  29.8 5.3 %collective-permute-start.10 = (bf16[2,32,4096]{2,1,0:T(8,128)(2,1)S(1)}, bf16[2,32,4096]{2,1,0:T(8,128)(2,1)S(1)}, u32[]{:S(2)}, u32[]{:S(2)}) collective-permute-start(bf16[2,32,4096]{2,1,0:T(8,128)(2,1)S(1)} %pad_maximum_fusion.refs_3_), channel_id=1, source_target_pairs={{0,1},{1,0},{2,3},{3,2},{4,5},{5,4},{6,7},{7,6},{8,9},{9,8},{10,11... | collective-permute-start | bytes 1572872 | tf_op jit(solution)/shard_map/ppermute | solution.py:291
  29.8 29.1 %collective-permute-start.14 = (bf16[2,16,4096]{2,1,0:T(8,128)(2,1)S(1)}, bf16[2,16,4096]{2,1,0:T(8,128)(2,1)S(1)}, u32[]{:S(2)}, u32[]{:S(2)}) collective-permute-start(bf16[2,16,4096]{2,1,0:T(8,128)(2,1)S(1)} %collective-permute-done.1.refs_2_), channel_id=1, source_target_pairs={{0,24},{1,25},{2,26},{3,27},{4,28},{5,29},{6,30},{7,31},{8,16},{9,... | collective-permute-start | bytes 786440 | tf_op jit(solution)/shard_map/ppermute | solution.py:291
  31.7 27.3 %collective-permute-start.11 = (bf16[2,32,4096]{2,1,0:T(8,128)(2,1)S(1)}, bf16[2,32,4096]{2,1,0:T(8,128)(2,1)S(1)}, u32[]{:S(2)}, u32[]{:S(2)}) collective-permute-start(bf16[2,32,4096]{2,1,0:T(8,128)(2,1)S(1)} %pad_maximum_fusion.refs_3_), channel_id=1, source_target_pairs={{0,8},{1,9},{2,10},{3,11},{4,12},{5,13},{6,14},{7,15},{8,0},{9,1},... | collective-permute-start | bytes 1572872 | tf_op jit(solution)/shard_map/ppermute | solution.py:291
  32.2 26.8 %collective-permute-start.12 = (bf16[2,32,4096]{2,1,0:T(8,128)(2,1)S(1)}, bf16[2,32,4096]{2,1,0:T(8,128)(2,1)S(1)}, u32[]{:S(2)}, u32[]{:S(2)}) collective-permute-start(bf16[2,32,4096]{2,1,0:T(8,128)(2,1)S(1)} %pad_maximum_fusion.refs_3_), channel_id=1, source_target_pairs={{0,16},{1,17},{2,18},{3,19},{4,20},{5,21},{6,22},{7,23},{8,24},{9,... | collective-permute-start | bytes 1572872 | tf_op jit(solution)/shard_map/ppermute | solution.py:291
  33.4 28.6 %collective-permute-start.13 = (bf16[2,32,4096]{2,1,0:T(8,128)(2,1)S(1)}, bf16[2,32,4096]{2,1,0:T(8,128)(2,1)S(1)}, u32[]{:S(2)}, u32[]{:S(2)}) collective-permute-start(bf16[2,32,4096]{2,1,0:T(8,128)(2,1)S(1)} %pad_maximum_fusion.refs_3_), channel_id=1, source_target_pairs={{0,24},{1,25},{2,26},{3,27},{4,28},{5,29},{6,30},{7,31},{8,16},{9,... | collective-permute-start | bytes 1572872 | tf_op jit(solution)/shard_map/ppermute | solution.py:291
  35.1 27.3 %copy-start = (bf16[16,4096]{1,0:T(8,128)(2,1)S(1)}, bf16[16,4096]{1,0:T(8,128)(2,1)}, u32[]{:S(2)}) copy-start(bf16[16,4096]{1,0:T(8,128)(2,1)} %tokens.1) | copy-start | bytes 393220
  62.0 2.7 %collective-permute-start.15 = (bf16[2,64,4096]{2,1,0:T(8,128)(2,1)S(1)}, bf16[2,64,4096]{2,1,0:T(8,128)(2,1)S(1)}, u32[]{:S(2)}, u32[]{:S(2)}) collective-permute-start(bf16[2,64,4096]{2,1,0:T(8,128)(2,1)S(1)} %get-tuple-element.54), channel_id=1, source_target_pairs={{0,1},{1,0},{2,3},{3,2},{4,5},{5,4},{6,7},{7,6},{8,9},{9,8},{10,11... | collective-permute-start | bytes 3145736 | tf_op jit(solution)/shard_map/ppermute | solution.py:291
  62.0 4.5 %collective-permute-start.16 = (bf16[2,80,4096]{2,1,0:T(8,128)(2,1)S(1)}, bf16[2,80,4096]{2,1,0:T(8,128)(2,1)S(1)}, u32[]{:S(2)}, u32[]{:S(2)}) collective-permute-start(bf16[2,80,4096]{2,1,0:T(8,128)(2,1)S(1)} %get-tuple-element.55.refs_9_), channel_id=1, source_target_pairs={{0,1},{1,0},{2,3},{3,2},{4,5},{5,4},{6,7},{7,6},{8,9},{9,8},{10,11... | collective-permute-start | bytes 3932168 | tf_op jit(solution)/shard_map/ppermute | solution.py:291
  62.6 7.8 %collective-permute-start.20 = (bf16[2,32,4096]{2,1,0:T(8,128)(2,1)S(1)}, bf16[2,32,4096]{2,1,0:T(8,128)(2,1)S(1)}, u32[]{:S(2)}, u32[]{:S(2)}) collective-permute-start(bf16[2,32,4096]{2,1,0:T(8,128)(2,1)S(1)} %collective-permute-done.11.refs_1_), channel_id=1, source_target_pairs={{0,1},{1,0},{2,3},{3,2},{4,5},{5,4},{6,7},{7,6},{8,9},{9,8},{10,11... | collective-permute-start | bytes 1572872 | tf_op jit(solution)/shard_map/ppermute | solution.py:291
  62.7 10.4 %collective-permute-start.21 = (bf16[2,32,4096]{2,1,0:T(8,128)(2,1)S(1)}, bf16[2,32,4096]{2,1,0:T(8,128)(2,1)S(1)}, u32[]{:S(2)}, u32[]{:S(2)}) collective-permute-start(bf16[2,32,4096]{2,1,0:T(8,128)(2,1)S(1)} %collective-permute-done.12.refs_2_), channel_id=1, source_target_pairs={{0,1},{1,0},{2,3},{3,2},{4,5},{5,4},{6,7},{7,6},{8,9},{9,8},{10,11... | collective-permute-start | bytes 1572872 | tf_op jit(solution)/shard_map/ppermute | solution.py:291
  63.2 9.9 %collective-permute-start.22 = (bf16[2,32,4096]{2,1,0:T(8,128)(2,1)S(1)}, bf16[2,32,4096]{2,1,0:T(8,128)(2,1)S(1)}, u32[]{:S(2)}, u32[]{:S(2)}) collective-permute-start(bf16[2,32,4096]{2,1,0:T(8,128)(2,1)S(1)} %collective-permute-done.13.refs_3_), channel_id=1, source_target_pairs={{0,1},{1,0},{2,3},{3,2},{4,5},{5,4},{6,7},{7,6},{8,9},{9,8},{10,11... | collective-permute-start | bytes 1572872 | tf_op jit(solution)/shard_map/ppermute | solution.py:291
  64.6 4.5 %collective-permute-start.23 = (bf16[2,16,4096]{2,1,0:T(8,128)(2,1)S(1)}, bf16[2,16,4096]{2,1,0:T(8,128)(2,1)S(1)}, u32[]{:S(2)}, u32[]{:S(2)}) collective-permute-start(bf16[2,16,4096]{2,1,0:T(8,128)(2,1)S(1)} %collective-permute-done.14.refs_4_), channel_id=1, source_target_pairs={{0,1},{1,0},{2,3},{3,2},{4,5},{5,4},{6,7},{7,6},{8,9},{9,8},{10,11... | collective-permute-start | bytes 786440 | tf_op jit(solution)/shard_map/ppermute | solution.py:291
  66.6 38.0 %collective-permute-start.17 = (bf16[2,16,4096]{2,1,0:T(8,128)(2,1)S(1)}, bf16[2,16,4096]{2,1,0:T(8,128)(2,1)S(1)}, u32[]{:S(2)}, u32[]{:S(2)}) collective-permute-start(bf16[2,16,4096]{2,1,0:T(8,128)(2,1)S(1)} %get-tuple-element.77), channel_id=1, source_target_pairs={{0,2},{1,3},{2,0},{3,1},{4,6},{5,7},{6,4},{7,5},{8,10},{9,11},{10,... | collective-permute-start | bytes 786440 | tf_op jit(solution)/shard_map/ppermute | solution.py:291
  69.1 35.5 %collective-permute-start.18 = (bf16[2,16,4096]{2,1,0:T(8,128)(2,1)S(1)}, bf16[2,16,4096]{2,1,0:T(8,128)(2,1)S(1)}, u32[]{:S(2)}, u32[]{:S(2)}) collective-permute-start(bf16[2,16,4096]{2,1,0:T(8,128)(2,1)S(1)} %get-tuple-element.76), channel_id=1, source_target_pairs={{0,4},{1,5},{2,6},{3,7},{4,0},{5,1},{6,2},{7,3},{8,12},{9,13},{10,... | collective-permute-start | bytes 786440 | tf_op jit(solution)/shard_map/ppermute | solution.py:291
  70.5 34.1 %collective-permute-start.19 = (bf16[2,16,4096]{2,1,0:T(8,128)(2,1)S(1)}, bf16[2,16,4096]{2,1,0:T(8,128)(2,1)S(1)}, u32[]{:S(2)}, u32[]{:S(2)}) collective-permute-start(bf16[2,16,4096]{2,1,0:T(8,128)(2,1)S(1)} %get-tuple-element.75), channel_id=1, source_target_pairs={{0,6},{1,7},{2,4},{3,5},{4,2},{5,3},{6,0},{7,1},{8,14},{9,15},{10,... | collective-permute-start | bytes 786440 | tf_op jit(solution)/shard_map/ppermute | solution.py:291
  73.1 31.7 %copy-start.2 = (f32[4096]{0:T(1024)S(1)}, f32[4096]{0:T(1024)}, u32[]{:S(2)}) copy-start(f32[4096]{0:T(1024)} %param.7) | copy-start | bytes 49156
  73.1 31.9 %copy-start.1 = (bf16[16,4096]{1,0:T(8,128)(2,1)S(1)}, bf16[16,4096]{1,0:T(8,128)(2,1)}, u32[]{:S(2)}) copy-start(bf16[16,4096]{1,0:T(8,128)(2,1)} %cotangent.1) | copy-start | bytes 393220
